TPU v7x, 32 devices: a whole 2x2x4 slice. The times are simulated.
32 devices in a mesh: seq: 8 (over z, y), mem: 4 (over x, core).
Axes of the slice: x: 2, y: 2, z: 4, core: 2. Of those that a mesh axis runs over, the one named last changes fastest.
Arguments:
- inputs: bfloat16 [2, 8192, 1024], P(None, ('seq', 'mem')), may hold values from -6 to 6
- memory: bfloat16 [2, 8, 588, 1024], P(None, 'seq', 'mem'), may hold values from -6 to 6
- page_ids: int32 [2, 8192], replicated, may hold values from 0 to 7, as said below
- memory_length: int32 [2, 8], replicated, may hold values from 147 to 588, as said below
- cotangent: bfloat16 [2, 8192, 1024], P(None, ('seq', 'mem')), may hold values from -6 to 6
- gain_self: bfloat16 [1024], P(('seq', 'mem')), may hold values from 0.25 to 1.75
- self_query: bfloat16 [1024, 1024], P(('seq', 'mem')), may hold values from -0.25 to 0.25
- self_key: bfloat16 [1024, 1024], P(('seq', 'mem')), may hold values from -0.1875 to 0.1875
- self_value: bfloat16 [1024, 1024], P(('seq', 'mem')), may hold values from -0.1875 to 0.1875
- self_out: bfloat16 [1024, 1024], P(('seq', 'mem')), may hold values from -1.5 to 1.5
- gain_cross: bfloat16 [1024], P(('seq', 'mem')), may hold values from 0.25 to 1.75
- cross_query: bfloat16 [1024, 1024], P(('seq', 'mem')), may hold values from -0.25 to 0.25
- cross_key: bfloat16 [1024, 1024], P(('seq', 'mem')), may hold values from -0.1875 to 0.1875
- cross_value: bfloat16 [1024, 1024], P(('seq', 'mem')), may hold values from -0.1875 to 0.1875
- cross_out: bfloat16 [1024, 1024], P(('seq', 'mem')), may hold values from -1.5 to 1.5
- gain_mlp: bfloat16 [1024], P(('seq', 'mem')), may hold values from 0.25 to 1.75
- mlp_in: bfloat16 [4096, 1024], P(('seq', 'mem')), may hold values from -0.1875 to 0.1875
- mlp_out: bfloat16 [4096, 1024], P(('seq', 'mem')), may hold values from -0.1875 to 0.1875
Outputs:
- output: bfloat16 [2, 8192, 1024], P(None, ('seq', 'mem'))
- grad_inputs: float32 [2, 8192, 1024], P(None, ('seq', 'mem'))
- grad_memory: float32 [2, 8, 588, 1024], P(None, 'seq', 'mem')
- grad_gain_self: float32 [1024], P(('seq', 'mem'))
- grad_self_query: float32 [1024, 1024], P(('seq', 'mem'))
- grad_self_key: float32 [1024, 1024], P(('seq', 'mem'))
- grad_self_value: float32 [1024, 1024], P(('seq', 'mem'))
- grad_self_out: float32 [1024, 1024], P(('seq', 'mem'))
- grad_gain_cross: float32 [1024], P(('seq', 'mem'))
- grad_cross_query: float32 [1024, 1024], P(('seq', 'mem'))
- grad_cross_key: float32 [1024, 1024], P(('seq', 'mem'))
- grad_cross_value: float32 [1024, 1024], P(('seq', 'mem'))
- grad_cross_out: float32 [1024, 1024], P(('seq', 'mem'))
- grad_gain_mlp: float32 [1024], P(('seq', 'mem'))
- grad_mlp_in: float32 [4096, 1024], P(('seq', 'mem'))
- grad_mlp_out: float32 [4096, 1024], P(('seq', 'mem'))
Inputs may be any that keep to these rules, and one draw needn't show every extreme that they name: `page_ids`: in each micro-batch page numbers never fall along the tokens. Cut the tokens into blocks of 1024: block 0 holds only page 0; block g (g >= 1) begins with tokens of page g - 1 and holds the first token of page g, and all its later tokens belong to page g. Each value is 147 or 588; the rows of a page's memory from memory_length on are padding.
All inputs are finite; a program needn't handle non-finite values.
Results may differ from a plain program's by a relative error of at most 0.04.
Values may be sent and summed in bfloat16 or wider, within the bound.
No kernel may reach another device: no remote copies, remote signals or barrier semaphores. Data moves between devices by JAX's collectives and lax.ppermute only.
A program may use at most 320 MiB of HBM per device.

v0:
```python
import jax
import jax.numpy as jnp
from jax import lax
from jax.sharding import PartitionSpec as P

D = 1024
H = 16
HEAD = 64
MICRO = 2


def shifted(block, axis, distance):
    devices = range(lax.axis_size(axis))
    route = [(i - distance, i) for i in devices if i - distance in devices]
    return lax.ppermute(block, axis, route)


def normalize(tensor):
    average = jnp.mean(tensor, axis=-1, keepdims=True)
    centered = tensor - average
    variance = jnp.mean(centered * centered, axis=-1, keepdims=True)
    return centered * lax.rsqrt(variance + 1e-05)


def layer_norm(tensor, scales):
    return normalize(tensor) * scales


def exact_gelu(tensor):
    return jax.nn.gelu(tensor, approximate=False)


def product(left, right):
    return jnp.dot(left, right, preferred_element_type=jnp.float32)


def product_t(left, right):
    return lax.dot_general(
        left, right, (((1,), (1,)), ((), ())), preferred_element_type=jnp.float32
    )


def outer_sum(left, right):
    return lax.dot_general(
        left, right, (((0,), (0,)), ((), ())), preferred_element_type=jnp.float32
    )


def split_heads(tensor):
    row_count = tensor.shape[0]
    block_width = min(4, H) * HEAD
    return tensor.reshape(row_count, D // block_width, block_width).transpose(1, 0, 2)


def join_heads(tensor):
    return tensor.transpose(1, 0, 2).reshape(tensor.shape[1], D)


def block_scores(queries, key_rows):
    row_count = queries.shape[0]
    key_count = key_rows.shape[0]
    head_count = queries.shape[1] // HEAD
    return (
        jnp.einsum(
            "rhd,khd->hrk",
            queries.reshape(row_count, head_count, HEAD),
            key_rows.reshape(key_count, head_count, HEAD),
            preferred_element_type=jnp.float32,
        )
        * 0.125
    )


def block_max(queries, key_rows, allowed):
    scores = block_scores(queries, key_rows)
    return jnp.max(jnp.where(allowed[None], scores, -1e30), axis=-1)


def block_sums(queries, key_rows, values, allowed, rowmax):
    row_count = queries.shape[0]
    key_count = key_rows.shape[0]
    head_count = queries.shape[1] // HEAD
    scores = block_scores(queries, key_rows)
    weights = jnp.where(allowed[None], jnp.exp(scores - rowmax[:, :, None]), 0.0)
    summed = jnp.einsum(
        "hrk,khd->rhd",
        weights.astype(jnp.bfloat16),
        values.reshape(key_count, head_count, HEAD),
        preferred_element_type=jnp.float32,
    )
    return (summed.reshape(row_count, head_count * HEAD), jnp.sum(weights, axis=-1))


def block_grads(queries, key_rows, values, allowed, rowmax, grad_summed, grad_totals):
    row_count = queries.shape[0]
    key_count = key_rows.shape[0]
    head_count = queries.shape[1] // HEAD
    query_heads = queries.reshape(row_count, head_count, HEAD)
    key_heads = key_rows.reshape(key_count, head_count, HEAD)
    grad_heads = grad_summed.reshape(row_count, head_count, HEAD)
    scores = (
        jnp.einsum("rhd,khd->hrk", query_heads, key_heads, preferred_element_type=jnp.float32)
        * 0.125
    )
    weights = jnp.where(allowed[None], jnp.exp(scores - rowmax[:, :, None]), 0.0)
    grad_weights = jnp.einsum(
        "rhd,khd->hrk",
        grad_heads,
        values.reshape(key_count, head_count, HEAD),
        preferred_element_type=jnp.float32,
    )
    grad_scores = (weights * (grad_weights + grad_totals[:, :, None])).astype(jnp.bfloat16)
    grad_query = (
        jnp.einsum("hrk,khd->rhd", grad_scores, key_heads, preferred_element_type=jnp.float32)
        * 0.125
    )
    grad_key = (
        jnp.einsum("hrk,rhd->khd", grad_scores, query_heads, preferred_element_type=jnp.float32)
        * 0.125
    )
    grad_value = jnp.einsum(
        "hrk,rhd->khd", weights.astype(jnp.bfloat16), grad_heads, preferred_element_type=jnp.float32
    )
    return (
        grad_query.reshape(row_count, -1),
        grad_key.reshape(key_count, -1),
        grad_value.reshape(key_count, -1),
    )


def attend_max(queries, key_rows, allowed):
    return lax.map(
        lambda pieces: block_max(pieces[0], pieces[1], allowed),
        (split_heads(queries), split_heads(key_rows)),
    )


def attend_sums(queries, key_rows, values, allowed, rowmax):
    summed, totals = lax.map(
        lambda pieces: block_sums(pieces[0], pieces[1], pieces[2], allowed, pieces[3]),
        (split_heads(queries), split_heads(key_rows), split_heads(values), rowmax),
    )
    return (join_heads(summed), totals)


def attend_grads(queries, key_rows, values, allowed, rowmax, grad_summed, grad_totals):
    grad_query, grad_key, grad_value = lax.map(
        lambda pieces: block_grads(
            pieces[0], pieces[1], pieces[2], allowed, pieces[3], pieces[4], pieces[5]
        ),
        (
            split_heads(queries),
            split_heads(key_rows),
            split_heads(values),
            rowmax,
            split_heads(grad_summed),
            grad_totals,
        ),
    )
    return (join_heads(grad_query), join_heads(grad_key), join_heads(grad_value))


def divide_heads(summed, totals):
    row_count = summed.shape[0]
    per_head = totals.reshape(H, row_count).T
    return (summed.reshape(row_count, H, HEAD) / per_head[:, :, None]).reshape(row_count, D)


def softmax_back(grad_low, attn_raw, totals):
    row_count = grad_low.shape[0]
    per_head = totals.reshape(H, row_count).T
    grad_full = grad_low.astype(jnp.float32).reshape(row_count, H, HEAD)
    grad_summed = (grad_full / per_head[:, :, None]).reshape(row_count, D).astype(jnp.bfloat16)
    grad_totals = -jnp.sum(grad_full * attn_raw.reshape(row_count, H, HEAD), axis=-1) / per_head
    return (grad_summed, grad_totals.T.reshape(totals.shape))


def shards(
    inputs,
    memory,
    page_ids,
    memory_length,
    cotangent,
    gain_self,
    self_query,
    self_key,
    self_value,
    self_out,
    gain_cross,
    cross_query,
    cross_key,
    cross_value,
    cross_out,
    gain_mlp,
    mlp_in,
    mlp_out,
):
    seq_index = lax.axis_index("seq")
    mem_index = lax.axis_index("mem")
    mem_count = lax.axis_size("mem")
    tok_rows = inputs.shape[1]
    group = tok_rows * mem_count
    mem_dev = memory.shape[2]
    group_start = seq_index * group
    own_offset = mem_index * tok_rows
    own_start = group_start + own_offset

    def own_slice(tensor):
        return lax.dynamic_slice_in_dim(tensor, own_offset, tok_rows, 0)

    out_list = []
    grad_x_list = []
    grad_mem_list = []
    accumulated = None
    for micro_index in range(MICRO):
        fetch_attention_part = (
            lax.all_gather(gain_self, ("seq", "mem"), axis=0, tiled=True),
            lax.all_gather(self_query, ("seq", "mem"), axis=0, tiled=True),
            lax.all_gather(self_key, ("seq", "mem"), axis=0, tiled=True),
            lax.all_gather(self_value, ("seq", "mem"), axis=0, tiled=True),
            lax.all_gather(self_out, ("seq", "mem"), axis=0, tiled=True),
            lax.all_gather(gain_cross, ("seq", "mem"), axis=0, tiled=True),
            lax.all_gather(cross_query, ("seq", "mem"), axis=0, tiled=True),
            lax.all_gather(cross_key, ("seq", "mem"), axis=0, tiled=True),
            lax.all_gather(cross_value, ("seq", "mem"), axis=0, tiled=True),
            lax.all_gather(cross_out, ("seq", "mem"), axis=0, tiled=True),
            lax.all_gather(gain_mlp, ("seq", "mem"), axis=0, tiled=True),
        )
        fetch_hidden_part = (
            lax.all_gather(mlp_in, "seq", axis=0, tiled=True),
            lax.all_gather(mlp_out, "seq", axis=0, tiled=True),
        )
        weights = tuple(fetch_attention_part) + tuple(fetch_hidden_part)
        (
            gain_one,
            query_full,
            key_full,
            value_full,
            out_full,
            gain_two,
            cquery_full,
            ckey_full,
            cvalue_full,
            cout_full,
            gain_three,
            inner_part,
            outer_part,
        ) = weights
        x_rows = inputs[micro_index].astype(jnp.float32)
        page_row = page_ids[micro_index]
        normed_one, norm_one_back = jax.vjp(layer_norm, x_rows, gain_one.astype(jnp.float32))
        low_one = normed_one.astype(jnp.bfloat16)
        queries = product(low_one, query_full).astype(jnp.bfloat16)
        key_local = product(low_one, key_full).astype(jnp.bfloat16)
        value_local = product(low_one, value_full).astype(jnp.bfloat16)
        key_group = lax.all_gather(key_local, "mem", axis=0, tiled=True)
        value_group = lax.all_gather(value_local, "mem", axis=0, tiled=True)
        memory_flat = memory[micro_index].reshape(mem_dev, D)
        memory_keys = product(memory_flat, ckey_full).astype(jnp.bfloat16)
        memory_values = product(memory_flat, cvalue_full).astype(jnp.bfloat16)
        key_prev, value_prev, prev_keys, prev_values = shifted(
            (key_group, value_group, memory_keys, memory_values), "seq", 1
        )
        keys_all = jnp.concatenate([key_prev, key_group], axis=0)
        values_all = jnp.concatenate([value_prev, value_group], axis=0)
        ids_padded = jnp.concatenate([-jnp.ones((group,), jnp.int32), page_row], axis=0)
        key_ids = lax.dynamic_slice_in_dim(ids_padded, group_start, 2 * group, 0)
        query_ids = lax.dynamic_slice_in_dim(page_row, own_start, tok_rows, 0)
        query_pos = own_start + jnp.arange(tok_rows, dtype=jnp.int32)
        key_pos = group_start - group + jnp.arange(2 * group, dtype=jnp.int32)
        self_mask = (key_ids[None, :] == query_ids[:, None]) & (
            key_pos[None, :] <= query_pos[:, None]
        )
        self_max = attend_max(queries, keys_all, self_mask)
        self_sum, self_tot = attend_sums(queries, keys_all, values_all, self_mask, self_max)
        self_raw = divide_heads(self_sum, self_tot)
        self_low = self_raw.astype(jnp.bfloat16)
        after_self = x_rows + product(self_low, out_full)
        gain_two_f = gain_two.astype(jnp.float32)
        normed_two, norm_two_back = jax.vjp(layer_norm, after_self, gain_two_f)
        low_two_own = normed_two.astype(jnp.bfloat16)
        self_group = lax.all_gather(
            after_self.astype(jnp.bfloat16), "mem", axis=0, tiled=True
        ).astype(after_self.dtype)
        top_group = lax.all_gather(
            cotangent[micro_index].astype(jnp.float32).astype(jnp.bfloat16),
            "mem",
            axis=0,
            tiled=True,
        ).astype(jnp.float32)
        low_two = layer_norm(self_group, gain_two_f).astype(jnp.bfloat16)
        cross_q = product(low_two, cquery_full).astype(jnp.bfloat16)
        cross_keys = jnp.concatenate([prev_keys, memory_keys], axis=0)
        cross_values = jnp.concatenate([prev_values, memory_values], axis=0)
        length_padded = jnp.concatenate(
            [jnp.zeros((1,), jnp.int32), memory_length[micro_index]], axis=0
        )
        page_lens = lax.dynamic_slice_in_dim(length_padded, seq_index, 2, 0)
        key_page = seq_index - 1 + jnp.repeat(jnp.arange(2, dtype=jnp.int32), mem_dev)
        key_place = mem_index * mem_dev + jnp.tile(jnp.arange(mem_dev, dtype=jnp.int32), 2)
        key_live = key_place < jnp.repeat(page_lens, mem_dev)
        group_ids = lax.dynamic_slice_in_dim(page_row, group_start, group, 0)
        cross_mask = (group_ids[:, None] == key_page[None, :]) & key_live[None, :]
        local_max = attend_max(cross_q, cross_keys, cross_mask)
        cross_max = lax.pmax(local_max.astype(jnp.bfloat16), "mem").astype(local_max.dtype)
        part_sum, part_tot = attend_sums(cross_q, cross_keys, cross_values, cross_mask, cross_max)
        cross_sum = lax.psum(part_sum.astype(jnp.bfloat16), "mem").astype(jnp.float32)
        cross_tot = lax.psum(part_tot.astype(jnp.bfloat16), "mem").astype(jnp.float32)
        cross_raw = divide_heads(cross_sum, cross_tot)
        cross_low = cross_raw.astype(jnp.bfloat16)
        after_cross = self_group + product(cross_low, cout_full)
        gain_three_f = gain_three.astype(jnp.float32)
        plain_three, plain_back = jax.vjp(normalize, after_cross)
        low_three = (plain_three * gain_three_f).astype(jnp.bfloat16)
        hidden_pre = product_t(low_three, inner_part)
        activ, gelu_back = jax.vjp(exact_gelu, hidden_pre)
        act_low = activ.astype(jnp.bfloat16)
        hidden_rows = lax.psum_scatter(
            product(act_low, outer_part).astype(jnp.bfloat16),
            "mem",
            scatter_dimension=0,
            tiled=True,
        ).astype(jnp.float32)
        out_rows = (own_slice(after_cross) + hidden_rows).astype(jnp.bfloat16)
        grad_low = top_group.astype(jnp.bfloat16)
        grad_outer = outer_sum(act_low, grad_low)
        (grad_pre,) = gelu_back(product_t(grad_low, outer_part))
        pre_low = grad_pre.astype(jnp.bfloat16)
        grad_inner = outer_sum(pre_low, low_three)
        grad_plain = lax.psum(product(pre_low, inner_part).astype(jnp.bfloat16), "mem").astype(
            jnp.float32
        )
        grad_gain_three = jnp.sum(own_slice(grad_plain) * own_slice(plain_three), axis=0)
        (grad_ac_norm,) = plain_back(grad_plain * gain_three_f)
        grad_after_cross = top_group + grad_ac_norm
        cross_branch = grad_after_cross.astype(jnp.bfloat16)
        grad_cout = outer_sum(own_slice(cross_low), own_slice(cross_branch))
        cross_result_grad = product_t(cross_branch, cout_full).astype(jnp.bfloat16)
        cross_gsum, cross_gtot = softmax_back(cross_result_grad, cross_raw, cross_tot)
        cq_part, ck_part, cv_part = attend_grads(
            cross_q, cross_keys, cross_values, cross_mask, cross_max, cross_gsum, cross_gtot
        )
        grad_cq = lax.psum_scatter(
            cq_part.astype(jnp.bfloat16), "mem", scatter_dimension=0, tiled=True
        )
        grad_cquery = outer_sum(low_two_own, grad_cq)
        grad_as_norm, grad_gain_two = norm_two_back(product_t(grad_cq, cquery_full))
        grad_after_self = own_slice(grad_after_cross) + grad_as_norm
        self_branch = grad_after_self.astype(jnp.bfloat16)
        grad_out_w = outer_sum(self_low, self_branch)
        self_result_grad = product_t(self_branch, out_full).astype(jnp.bfloat16)
        self_gsum, self_gtot = softmax_back(self_result_grad, self_raw, self_tot)
        grad_q_full, grad_k_all, grad_v_all = attend_grads(
            queries, keys_all, values_all, self_mask, self_max, self_gsum, self_gtot
        )
        back_k = shifted(grad_k_all[:group].astype(jnp.bfloat16), "seq", -1).astype(jnp.float32)
        back_v = shifted(grad_v_all[:group].astype(jnp.bfloat16), "seq", -1).astype(jnp.float32)
        back_mkeys = shifted(ck_part[:mem_dev].astype(jnp.bfloat16), "seq", -1).astype(jnp.float32)
        back_mvalues = shifted(cv_part[:mem_dev].astype(jnp.bfloat16), "seq", -1).astype(
            jnp.float32
        )
        own_ck = (ck_part[mem_dev:] + back_mkeys).astype(jnp.bfloat16)
        own_cv = (cv_part[mem_dev:] + back_mvalues).astype(jnp.bfloat16)
        grad_ckey = outer_sum(memory_flat, own_ck)
        grad_cvalue = outer_sum(memory_flat, own_cv)
        grad_mem = (product_t(own_ck, ckey_full) + product_t(own_cv, cvalue_full)).reshape(
            1, mem_dev, D
        )
        grad_k_own = lax.psum_scatter(
            (grad_k_all[group:] + back_k).astype(jnp.bfloat16),
            "mem",
            scatter_dimension=0,
            tiled=True,
        )
        grad_v_own = lax.psum_scatter(
            (grad_v_all[group:] + back_v).astype(jnp.bfloat16),
            "mem",
            scatter_dimension=0,
            tiled=True,
        )
        grad_q_low = grad_q_full.astype(jnp.bfloat16)
        grad_query_w = outer_sum(low_one, grad_q_low)
        grad_key_w = outer_sum(low_one, grad_k_own)
        grad_value_w = outer_sum(low_one, grad_v_own)
        grad_normed = (
            product_t(grad_q_low, query_full)
            + product_t(grad_k_own, key_full)
            + product_t(grad_v_own, value_full)
        )
        grad_x_norm, grad_gain_one = norm_one_back(grad_normed)
        grad_x = grad_after_self + grad_x_norm
        full_grads = (
            grad_gain_one,
            grad_query_w,
            grad_key_w,
            grad_value_w,
            grad_out_w,
            grad_gain_two,
            grad_cquery,
            grad_ckey,
            grad_cvalue,
            grad_cout,
            grad_gain_three,
            grad_inner,
            grad_outer,
        )
        out_rows, grad_x, grad_mem, full_grads = (out_rows, grad_x, grad_mem, full_grads)
        out_list.append(out_rows)
        grad_x_list.append(grad_x)
        grad_mem_list.append(grad_mem)
        attention_part = (
            lax.psum_scatter(full_grads[0], ("seq", "mem"), scatter_dimension=0, tiled=True),
            lax.psum_scatter(full_grads[1], ("seq", "mem"), scatter_dimension=0, tiled=True),
            lax.psum_scatter(full_grads[2], ("seq", "mem"), scatter_dimension=0, tiled=True),
            lax.psum_scatter(full_grads[3], ("seq", "mem"), scatter_dimension=0, tiled=True),
            lax.psum_scatter(full_grads[4], ("seq", "mem"), scatter_dimension=0, tiled=True),
            lax.psum_scatter(full_grads[5], ("seq", "mem"), scatter_dimension=0, tiled=True),
            lax.psum_scatter(full_grads[6], ("seq", "mem"), scatter_dimension=0, tiled=True),
            lax.psum_scatter(full_grads[7], ("seq", "mem"), scatter_dimension=0, tiled=True),
            lax.psum_scatter(full_grads[8], ("seq", "mem"), scatter_dimension=0, tiled=True),
            lax.psum_scatter(full_grads[9], ("seq", "mem"), scatter_dimension=0, tiled=True),
            lax.psum_scatter(full_grads[10], ("seq", "mem"), scatter_dimension=0, tiled=True),
        )
        hidden_part = (
            lax.psum_scatter(
                full_grads[11].astype(jnp.bfloat16), "seq", scatter_dimension=0, tiled=True
            ).astype(jnp.float32),
            lax.psum_scatter(
                full_grads[12].astype(jnp.bfloat16), "seq", scatter_dimension=0, tiled=True
            ).astype(jnp.float32),
        )
        term_grads = tuple(attention_part) + tuple(hidden_part)
        if accumulated is None:
            accumulated = term_grads
        else:
            accumulated = jax.tree.map(lambda left, right: left + right, accumulated, term_grads)
    return (
        jnp.stack(out_list),
        jnp.stack(grad_x_list),
        jnp.stack(grad_mem_list),
        accumulated[0],
        accumulated[1],
        accumulated[2],
        accumulated[3],
        accumulated[4],
        accumulated[5],
        accumulated[6],
        accumulated[7],
        accumulated[8],
        accumulated[9],
        accumulated[10],
        accumulated[11],
        accumulated[12],
    )


def solution(mesh):
    placed = (
        P(None, ("seq", "mem"), None),
        P(None, "seq", "mem", None),
        P(),
        P(),
        P(None, ("seq", "mem"), None),
        P(("seq", "mem")),
        P(("seq", "mem"), None),
        P(("seq", "mem"), None),
        P(("seq", "mem"), None),
        P(("seq", "mem"), None),
        P(("seq", "mem")),
        P(("seq", "mem"), None),
        P(("seq", "mem"), None),
        P(("seq", "mem"), None),
        P(("seq", "mem"), None),
        P(("seq", "mem")),
        P(("seq", "mem"), None),
        P(("seq", "mem"), None),
    )
    return jax.shard_map(
        shards,
        mesh=mesh,
        in_specs=placed,
        out_specs=(
            P(None, ("seq", "mem"), None),
            P(None, ("seq", "mem"), None),
            P(None, "seq", "mem", None),
            P(("seq", "mem")),
            P(("seq", "mem"), None),
            P(("seq", "mem"), None),
            P(("seq", "mem"), None),
            P(("seq", "mem"), None),
            P(("seq", "mem")),
            P(("seq", "mem"), None),
            P(("seq", "mem"), None),
            P(("seq", "mem"), None),
            P(("seq", "mem"), None),
            P(("seq", "mem")),
            P(("seq", "mem"), None),
            P(("seq", "mem"), None),
        ),
        check_vma=False,
    )
```

profile of v0, /device:TPU:0, one launch (start us, length us, event | category | flops | bytes accessed | tf_op | source)
XLA Modules:
  0.0 3167.8 jit_solution(3443266203922773605)
XLA Ops:
  11.3 42.2 %all-reduce.9 = (bf16[1024]{0:T(1024)(128)(2,1)S(1)}, bf16[1024]{0:T(1024)(128)(2,1)S(1)}, bf16[1024]{0:T(1024)(128)(2,1)}) all-reduce(bf16[1024]{0:T(1024)(128)(2,1)S(1)} %dynamic-update-slice, bf16[1024]{0:T(1024)(128)(2,1)S(1)} %dynamic-update-slice.1, ...), channel_id=1, replica_groups=mesh['seq'=8,'mem'=4] {'seq','mem'}, use_global_device_ids=true, to_apply=%add.2 | all-reduce | flops 3072 | bytes 12288
  74.2 54.0 %all-gather.21.cloned.1.call-done = bf16[1024,1024]{1,0:T(8,128)(2,1)} async-done(((bf16[32,1024]{1,0:T(8,128)(2,1)}), bf16[1024,1024]{1,0:T(8,128)(2,1)}) %all-gather.21.cloned.1.call-update) | async-done | bytes 2097168 | tf_op jit(solution)/shard_map/all_gather | solution.py:220
  156.6 57.5 %all-gather.25.cloned.1.call-done = bf16[1024,1024]{1,0:T(8,128)(2,1)} async-done(((bf16[32,1024]{1,0:T(8,128)(2,1)}), bf16[1024,1024]{1,0:T(8,128)(2,1)}) %all-gather.25.cloned.1.call-update) | async-done | bytes 2097168 | tf_op jit(solution)/shard_map/all_gather | solution.py:218
  400.4 45.4 %all-gather.35.cloned.1.call-done = bf16[1024,1024]{1,0:T(8,128)(2,1)} async-done(((bf16[32,1024]{1,0:T(8,128)(2,1)}), bf16[1024,1024]{1,0:T(8,128)(2,1)}) %all-gather.35.cloned.1.call-update) | async-done | bytes 2097168 | tf_op jit(solution)/shard_map/all_gather | solution.py:225
  734.5 87.1 %all-reduce.23.cloned.1.call-done = (bf16[1024,1024]{0,1:T(8,128)(2,1)}, bf16[1024,1024]{0,1:T(8,128)(2,1)}) async-done(((bf16[1024,1024]{0,1:T(8,128)(2,1)}, bf16[1024,1024]{0,1:T(8,128)(2,1)}), (bf16[1024,1024]{0,1:T(8,128)(2,1)}, bf16[1024,1024]{0,1:T(8,128)(2,1)})) %all-reduce.23.cloned.1.call-update) | async-done | bytes 4194320 | tf_op jit(solution)/shard_map/psum | solution.py:307
  825.1 56.1 %all-gather.41.cloned.1.call-done = bf16[1024,1024]{1,0:T(8,128)(2,1)} async-done(((bf16[32,1024]{1,0:T(8,128)(2,1)}), bf16[1024,1024]{1,0:T(8,128)(2,1)}) %all-gather.41.cloned.1.call-update) | async-done | bytes 2097168 | tf_op jit(solution)/shard_map/all_gather | solution.py:226
  954.9 51.5 %all-gather.45.cloned.1.call-done = bf16[1024,1024]{1,0:T(8,128)(2,1)} async-done(((bf16[128,1024]{1,0:T(8,128)(2,1)}), bf16[1024,1024]{1,0:T(8,128)(2,1)}) %all-gather.45.cloned.1.call-update) | async-done | bytes 2097168 | tf_op jit(solution)/shard_map/all_gather | solution.py:231
  1048.1 84.3 %all-reduce.21.cloned.1.call-done = (bf16[1024,1024]{1,0:T(8,128)(2,1)}, bf16[1024,1024]{1,0:T(8,128)(2,1)}) async-done(((bf16[1024,1024]{1,0:T(8,128)(2,1)}, bf16[1024,1024]{1,0:T(8,128)(2,1)}), (bf16[1024,1024]{1,0:T(8,128)(2,1)}, bf16[1024,1024]{1,0:T(8,128)(2,1)})) %all-reduce.21.cloned.1.call-update) | async-done | bytes 4194320 | tf_op jit(solution)/shard_map/psum | solution.py:330
  1302.0 65.1 %while.167 = (s32[]{:T(128)}, bf16[4,256,256]{1,2,0:T(8,128)(2,1)S(1)}, f32[4,2048,256]{1,2,0:T(8,128)}, f32[4,2048,256]{1,2,0:T(8,128)}, bf16[4,2048,256]{1,2,0...) while((s32[]{:T(128)}, ...), condition=%wide.region_75.76_spmd.clone, body=%wide.region_74.75_spmd.clone.sunk | while | flops 1365377024 | bytes 60734620 | solution.py:147
  1434.7 65.0 %while.165 = (s32[]{:T(128)}, bf16[4,256,256]{1,2,0:T(8,128)(2,1)S(1)}, f32[4,2048,256]{1,2,0:T(8,128)}, f32[4,2048,256]{1,2,0:T(8,128)}, bf16[4,2048,256]{1,2,0...) while((s32[]{:T(128)}, ...), condition=%wide.region_57.58_spmd.clone, body=%wide.region_56.57_spmd.clone.sunk | while | flops 1365377024 | bytes 60734620 | solution.py:147
  1506.4 45.2 %collective-permute-done.9 = bf16[1024,1024]{0,1:T(8,128)(2,1)S(1)} collective-permute-done((bf16[1024,1024]{0,1:T(8,128)(2,1)S(1)}, bf16[1024,1024]{0,1:T(8,128)(2,1)S(1)}, u32[]{:S(2)}, u32[]{:S(2)}) %collective-permute-start.9) | collective-permute-done | bytes 2097184 | tf_op jit(solution)/shard_map/ppermute | solution.py:15
  1560.6 44.2 %collective-permute-done.10 = bf16[1024,1024]{0,1:T(8,128)(2,1)S(1)} collective-permute-done((bf16[1024,1024]{0,1:T(8,128)(2,1)S(1)}, bf16[1024,1024]{0,1:T(8,128)(2,1)S(1)}, u32[]{:S(2)}, u32[]{:S(2)}) %collective-permute-start.10) | collective-permute-done | bytes 2097184 | tf_op jit(solution)/shard_map/ppermute | solution.py:15
  1614.4 42.9 %collective-permute-done.8 = bf16[1024,1024]{0,1:T(8,128)(2,1)S(1)} collective-permute-done((bf16[1024,1024]{0,1:T(8,128)(2,1)S(1)}, bf16[1024,1024]{0,1:T(8,128)(2,1)S(1)}, u32[]{:S(2)}, u32[]{:S(2)}) %collective-permute-start.8) | collective-permute-done | bytes 2097184 | tf_op jit(solution)/shard_map/ppermute | solution.py:15
  1830.7 70.0 %reduce-scatter.43.cloned.1.call-done = bf16[128,1024]{1,0:T(8,128)(2,1)} async-done(((bf16[1024,1024]{1,0:T(8,128)(2,1)}), bf16[128,1024]{1,0:T(8,128)(2,1)}) %reduce-scatter.43.cloned.1.call-update) | async-done | bytes 262160 | tf_op jit(solution)/shard_map/reduce_scatter | solution.py:425
  1902.6 68.2 %reduce-scatter.45.cloned.1.call-done = bf16[128,1024]{1,0:T(8,128)(2,1)} async-done(((bf16[1024,1024]{1,0:T(8,128)(2,1)}), bf16[128,1024]{1,0:T(8,128)(2,1)}) %reduce-scatter.45.cloned.1.call-update) | async-done | bytes 262160 | tf_op jit(solution)/shard_map/reduce_scatter | solution.py:428
  1970.8 70.5 %reduce-scatter.47.cloned.1.call-done = bf16[128,1024]{1,0:T(8,128)(2,1)} async-done(((bf16[1024,1024]{1,0:T(8,128)(2,1)}), bf16[128,1024]{1,0:T(8,128)(2,1)}) %reduce-scatter.47.cloned.1.call-update) | async-done | bytes 262160 | tf_op jit(solution)/shard_map/reduce_scatter | solution.py:428
  2097.5 86.4 %reduce-scatter.59.cloned.1.call-done = f32[32,1024]{1,0:T(8,128)} async-done(((f32[1024,1024]{1,0:T(8,128)}), f32[32,1024]{1,0:T(8,128)}) %reduce-scatter.59.cloned.1.call-update) | async-done | bytes 131088 | tf_op jit(solution)/shard_map/reduce_scatter | solution.py:421
  2183.9 139.5 %reduce-scatter.63.cloned.1.call-done = f32[32,1024]{1,0:T(8,128)} async-done(((f32[1024,1024]{1,0:T(8,128)}), f32[32,1024]{1,0:T(8,128)}) %reduce-scatter.63.cloned.1.call-update) | async-done | bytes 131088
  2323.5 139.2 %reduce-scatter.61.cloned.1.call-done = f32[32,1024]{1,0:T(8,128)} async-done(((f32[1024,1024]{1,0:T(8,128)}), f32[32,1024]{1,0:T(8,128)}) %reduce-scatter.61.cloned.1.call-update) | async-done | bytes 131088
  2462.7 139.7 %reduce-scatter.57.cloned.1.call-done = f32[32,1024]{1,0:T(8,128)} async-done(((f32[1024,1024]{1,0:T(8,128)}), f32[32,1024]{1,0:T(8,128)}) %reduce-scatter.57.cloned.1.call-update) | async-done | bytes 131088 | tf_op jit(solution)/shard_map/reduce_scatter | solution.py:418
  2602.4 139.7 %reduce-scatter.55.cloned.1.call-done = f32[32,1024]{1,0:T(8,128)} async-done(((f32[1024,1024]{1,0:T(8,128)}), f32[32,1024]{1,0:T(8,128)}) %reduce-scatter.55.cloned.1.call-update) | async-done | bytes 131088 | tf_op jit(solution)/shard_map/reduce_scatter | solution.py:416
  2742.1 139.6 %reduce-scatter.49.cloned.1.call-done = f32[32,1024]{1,0:T(8,128)} async-done(((f32[1024,1024]{1,0:T(8,128)}), f32[32,1024]{1,0:T(8,128)}) %reduce-scatter.49.cloned.1.call-update) | async-done | bytes 131088 | tf_op jit(solution)/shard_map/reduce_scatter | solution.py:413
  2881.8 139.6 %reduce-scatter.53.cloned.1.call-done = f32[32,1024]{1,0:T(8,128)} async-done(((f32[1024,1024]{1,0:T(8,128)}), f32[32,1024]{1,0:T(8,128)}) %reduce-scatter.53.cloned.1.call-update) | async-done | bytes 131088 | tf_op jit(solution)/shard_map/reduce_scatter | solution.py:415
  3021.3 139.5 %reduce-scatter.51.cloned.1.call-done = f32[32,1024]{1,0:T(8,128)} async-done(((f32[1024,1024]{1,0:T(8,128)}), f32[32,1024]{1,0:T(8,128)}) %reduce-scatter.51.cloned.1.call-update) | async-done | bytes 131088 | tf_op jit(solution)/shard_map/reduce_scatter | solution.py:414
  (1132 shorter events, 1502.5 us)
Async XLA Ops:
  133.6 252.9 %all-gather.39.cloned.1.call-start = ((), (), s32[]{:S(2)}) async-start(), calls=%async_computation.29 | async-start | bytes 2162688 | tf_op jit(solution)/shard_map/all_gather | solution.py:224
  134.3 311.4 %all-gather.35.cloned.1.call-start = ((), (), s32[]{:S(2)}) async-start(), calls=%async_computation.27 | async-start | bytes 2162688 | tf_op jit(solution)/shard_map/all_gather | solution.py:225
  135.1 334.3 %all-gather.47.cloned.1.call-start = ((), (), s32[]{:S(2)}) async-start(), calls=%async_computation.34 | async-start | bytes 2621440 | tf_op jit(solution)/shard_map/all_gather | solution.py:257
  219.9 349.1 %all-gather.33.cloned.1.call-start = ((), (), s32[]{:S(2)}) async-start(), calls=%async_computation.26 | async-start | bytes 2621440 | tf_op jit(solution)/shard_map/all_gather | solution.py:282
  337.5 235.8 %all-gather.37.cloned.1.call-start = ((), (), s32[]{:S(2)}) async-start(), calls=%async_computation.28 | async-start | bytes 2162688 | tf_op jit(solution)/shard_map/all_gather | solution.py:223
  338.1 255.3 %all-gather.51.cloned.1.call-start = ((), (), s32[]{:S(2)}) async-start(), calls=%async_computation.36 | async-start | bytes 2621440 | tf_op jit(solution)/shard_map/all_gather | solution.py:282
  702.8 228.7 %all-gather.43.cloned.1.call-start = ((), (), s32[]{:S(2)}) async-start(), calls=%async_computation.31 | async-start | bytes 2359296 | tf_op jit(solution)/shard_map/all_gather | solution.py:230
  703.4 251.5 %all-gather.55.cloned.1.call-start = ((), (), s32[]{:S(2)}) async-start(), calls=%async_computation.49 | async-start | bytes 2621440 | tf_op jit(solution)/shard_map/all_gather | solution.py:285
  704.5 301.9 %all-gather.45.cloned.1.call-start = ((), (), s32[]{:S(2)}) async-start(), calls=%async_computation.32 | async-start | bytes 2359296 | tf_op jit(solution)/shard_map/all_gather | solution.py:231
  705.1 330.3 %all-gather.53.cloned.1.call-start = ((), (), s32[]{:S(2)}) async-start(), calls=%async_computation.48 | async-start | bytes 2621440 | tf_op jit(solution)/shard_map/all_gather | solution.py:285
  705.8 426.6 %all-reduce.21.cloned.1.call-start = ((), (), s32[]{:S(2)}) async-start(), calls=%async_computation.59 | async-start | bytes 8388608 | tf_op jit(solution)/shard_map/psum | solution.py:330
  1251.0 538.6 %reduce-scatter.39.cloned.1.call-start = ((), (), s32[]{:S(2)}) async-start(), calls=%async_computation.43 | async-start | bytes 2621440 | tf_op jit(solution)/shard_map/reduce_scatter | solution.py:375
  1425.8 367.7 %reduce-scatter.33.cloned.1.call-start = ((), (), s32[]{:S(2)}) async-start(), calls=%async_computation.40 | async-start | bytes 2621440 | tf_op jit(solution)/shard_map/reduce_scatter | solution.py:375
  1553.7 245.3 %reduce-scatter.37.cloned.1.call-start = ((), (), s32[]{:S(2)}) async-start(), calls=%async_computation.42 | async-start | bytes 2621440 | tf_op jit(solution)/shard_map/reduce_scatter | solution.py:369
  1684.1 286.7 %reduce-scatter.45.cloned.1.call-start = ((), (), s32[]{:S(2)}) async-start(), calls=%async_computation.46 | async-start | bytes 2359296 | tf_op jit(solution)/shard_map/reduce_scatter | solution.py:428
  1690.4 350.9 %reduce-scatter.47.cloned.1.call-start = ((), (), s32[]{:S(2)}) async-start(), calls=%async_computation.47 | async-start | bytes 2359296 | tf_op jit(solution)/shard_map/reduce_scatter | solution.py:428
  1696.0 487.9 %reduce-scatter.59.cloned.1.call-start = ((), (), s32[]{:S(2)}) async-start(), calls=%async_computation.55 | async-start | bytes 4325376 | tf_op jit(solution)/shard_map/reduce_scatter | solution.py:421
  1702.0 621.4 %reduce-scatter.63.cloned.1.call-start = ((), (), s32[]{:S(2)}) async-start(), calls=%async_computation.57 | async-start | bytes 4325376
  1738.3 724.4 %reduce-scatter.61.cloned.1.call-start = ((), (), s32[]{:S(2)}) async-start(), calls=%async_computation.56 | async-start | bytes 4325376
  1772.5 829.8 %reduce-scatter.57.cloned.1.call-start = ((), (), s32[]{:S(2)}) async-start(), calls=%async_computation.54 | async-start | bytes 4325376 | tf_op jit(solution)/shard_map/reduce_scatter | solution.py:418
  1778.6 963.5 %reduce-scatter.55.cloned.1.call-start = ((), (), s32[]{:S(2)}) async-start(), calls=%async_computation.53 | async-start | bytes 4325376 | tf_op jit(solution)/shard_map/reduce_scatter | solution.py:416
  1784.4 1097.3 %reduce-scatter.49.cloned.1.call-start = ((), (), s32[]{:S(2)}) async-start(), calls=%async_computation.50 | async-start | bytes 4325376 | tf_op jit(solution)/shard_map/reduce_scatter | solution.py:413
  1789.5 1231.8 %reduce-scatter.53.cloned.1.call-start = ((), (), s32[]{:S(2)}) async-start(), calls=%async_computation.52 | async-start | bytes 4325376 | tf_op jit(solution)/shard_map/reduce_scatter | solution.py:415
  1798.8 1362.1 %reduce-scatter.51.cloned.1.call-start = ((), (), s32[]{:S(2)}) async-start(), calls=%async_computation.51 | async-start | bytes 4325376 | tf_op jit(solution)/shard_map/reduce_scatter | solution.py:414
  (199 other events, 8798.1 us)
Sparse Core Ops, SparseCore 0:
  10.9 59.1 all-gather.26
  72.9 55.2 all-gather.20
  154.5 59.5 all-gather.24
  240.6 59.5 all-gather.30
  327.1 59.3 all-gather.38
  389.3 56.3 all-gather.34
  496.7 56.7 all-gather.36
  735.8 85.6 all-reduce.22
  824.7 56.4 all-gather.40
  883.4 48.1 all-gather.42
  957.1 49.2 all-gather.44
  1048.2 84.1 all-reduce.20
  1762.9 67.8 reduce-scatter.40
  1834.3 66.3 reduce-scatter.42
  1904.1 66.6 reduce-scatter.44
  1974.3 66.8 reduce-scatter.46
  2044.1 139.7 reduce-scatter.58
  2186.6 136.7 reduce-scatter.62
  2326.2 136.4 reduce-scatter.60
  2465.5 136.7 reduce-scatter.56
  2605.1 136.9 reduce-scatter.54
  2745.0 136.7 reduce-scatter.48
  2884.6 136.7 reduce-scatter.52
  3024.2 136.6 reduce-scatter.50
  (18 shorter events, 489.3 us)
where the time goes:
time: 3180 us; the launch traced here: 3170 us
  waiting for transfers between devices  2180 us (69%)
  matrix products  404 us (13%)
  local copies, waits for them, and re-layouts  301 us (9%)
  other arithmetic  128 us (4%)
  blocking collectives  82.3 us (3%)
  starting transfers between devices  53 us (2%)
    unnamed x44, waiting for transfers between devices  286 us
    ppermute x16, waiting for transfers between devices, shifted(): return lax.ppermute(block, axis, route)  247 us
    reduce_scatter x1, waiting for transfers between devices, shards(): lax.psum_scatter(full_grads[4], ('seq', 'mem'), scatter_dimension=0, tile...  140 us
    reduce_scatter x1, waiting for transfers between devices, shards(): lax.psum_scatter(full_grads[6], ('seq', 'mem'), scatter_dimension=0, tile...  140 us
    reduce_scatter x1, waiting for transfers between devices, shards(): lax.psum_scatter(full_grads[1], ('seq', 'mem'), scatter_dimension=0, tile...  140 us
    reduce_scatter x1, waiting for transfers between devices, shards(): lax.psum_scatter(full_grads[3], ('seq', 'mem'), scatter_dimension=0, tile...  140 us
    reduce_scatter x1, waiting for transfers between devices, shards(): lax.psum_scatter(full_grads[2], ('seq', 'mem'), scatter_dimension=0, tile...  140 us
    reduce_scatter x2, waiting for transfers between devices, shards(): lax.psum_scatter(full_grads[12].astype(jnp.bfloat16), 'seq', scatter_dime...  139 us
  transfers between devices with their start and end apart: 58, of which 39 were waited for; matrix products, arithmetic and copies ran while one was open for 18% of the time, Pallas kernels for 0%

commit v1 on v0

v1 whole, which is shorter than its diff:
```python
import functools
import jax
import jax.numpy as jnp
import numpy as np
from jax import lax
from jax.experimental import pallas as pl
from jax.experimental.pallas import tpu as pltpu
from jax.sharding import PartitionSpec as P

HEAD = 64
BF = jnp.bfloat16
F32 = jnp.float32
LOWEST = -1e30


def head_lanes(rows, width):
    return lax.broadcasted_iota(jnp.int32, (rows, width), 1) // HEAD


def one_head(block, lanes, head):
    return jnp.where(lanes == head, block, jnp.zeros_like(block))


def dot_nt(left, right):
    return lax.dot_general(left, right, (((1,), (1,)), ((), ())), preferred_element_type=F32)


def dot_nn(left, right):
    return lax.dot_general(left, right, (((1,), (0,)), ((), ())), preferred_element_type=F32)


def dot_tn(left, right):
    return lax.dot_general(left, right, (((0,), (0,)), ((), ())), preferred_element_type=F32)


def self_range(p, rows, blocks, spill, prev_spill):
    first = jnp.where(p * rows < spill, prev_spill // rows, blocks + spill // rows)
    return first, blocks + p + 1


def self_allowed(query, key, extent, spill, prev_spill):
    first = jnp.where(query < spill, prev_spill, extent + spill)
    return (key >= first) & (key <= extent + query)


def cross_allowed(query, place, side, spill, length, me, padded, real):
    part = place // padded
    inner = place - part * padded
    row = (part ^ me) * real + inner
    return (inner < real) & (row < length) & ((query < spill) == (side == 0))


def self_forward_kernel(rows, blocks, heads, sc, qkv, kvp, o_ref, lse_ref, k_scr, v_scr, s_scr, mx, tot):
    width = heads * HEAD
    extent = rows * blocks
    me, spill, prev_spill = sc[0], sc[1], sc[2]
    lanes = head_lanes(rows, width)

    def place(b):
        return pl.multiple_of((b ^ me) * rows, rows)

    first_used, _ = self_range(0, rows, blocks, spill, prev_spill)

    @pl.loop(first_used, 2 * blocks)
    def _(kb):
        def fill(keys, values):
            k_scr[kb] = keys
            for h in range(heads):
                v_scr[kb, h * rows : (h + 1) * rows, :] = one_head(values, lanes, h)

        @pl.when(kb < blocks)
        def _():
            at = pl.ds(place(kb), rows)
            fill(kvp[at, 0:width], kvp[at, width : 2 * width])

        @pl.when(kb >= blocks)
        def _():
            at = pl.ds(place(kb - blocks), rows)
            fill(qkv[at, width : 2 * width], qkv[at, 2 * width : 3 * width])

    @pl.loop(0, blocks)
    def _(p):
        q = qkv[pl.ds(place(p), rows), 0:width] * jnp.asarray(0.125, BF)
        mx[...] = jnp.full(mx.shape, LOWEST, F32)
        tot[...] = jnp.zeros(tot.shape, F32)
        first, last = self_range(p, rows, blocks, spill, prev_spill)
        query = p * rows + lax.broadcasted_iota(jnp.int32, (rows, 1), 0)

        @pl.loop(first, last)
        def _(kb):
            key = kb * rows + lax.broadcasted_iota(jnp.int32, (1, rows), 1)
            allowed = self_allowed(query, key, extent, spill, prev_spill)
            k = k_scr[kb]
            for h in range(heads):
                s = dot_nt(one_head(q, lanes, h), k)
                s = jnp.where(allowed, s, LOWEST)
                s_scr[kb, h] = s
                mx[h] = jnp.maximum(mx[h], s)

        for h in range(heads):
            mx[h, :, 0:1] = jnp.max(mx[h], axis=1, keepdims=True)

        def weigh(kb, acc):
            parts = []
            for h in range(heads):
                e = jnp.exp(s_scr[kb, h] - mx[h, :, 0:1])
                tot[h] += e
                parts.append(e.astype(BF))
            return acc + dot_nn(jnp.concatenate(parts, axis=1), v_scr[kb])

        acc = lax.fori_loop(first, last, weigh, jnp.zeros((rows, width), F32))
        finish(p, place(p), rows, heads, acc, mx, tot, lanes, o_ref, lse_ref)


def finish(p, start, rows, heads, acc, mx, tot, lanes, o_ref, lse_ref):
    over = jnp.zeros((rows, 128), F32)
    inverse = jnp.zeros(acc.shape, F32)
    slim = lax.broadcasted_iota(jnp.int32, (rows, 128), 1)
    for h in range(heads):
        total = jnp.sum(tot[h], axis=1, keepdims=True)
        inverse = jnp.where(lanes == h, 1.0 / total, inverse)
        over = jnp.where(slim == h, mx[h, :, 0:1] + jnp.log(total), over)
    o_ref[pl.ds(start, rows), :] = (acc * inverse).astype(BF)
    lse_ref[:, pl.ds(pl.multiple_of(p * rows, rows), rows)] = over.T[0:8, :]


def cross_forward_kernel(rows, blocks, heads, padded, real, sc, q_ref, kv0, kv1, o_ref, lse_ref, v_scr, s_scr, mx, tot):
    width = heads * HEAD
    keys = kv0.shape[0]
    me, spill = sc[0], sc[1]
    lanes = head_lanes(rows, width)
    key_lanes = head_lanes(keys, width)
    kvs = (kv0, kv1)

    def place(b):
        return pl.multiple_of((b ^ me) * rows, rows)

    for side in range(2):
        values = kvs[side][:, width : 2 * width]
        for h in range(heads):
            v_scr[side, h * keys : (h + 1) * keys, :] = one_head(values, key_lanes, h)
    spot = lax.broadcasted_iota(jnp.int32, (1, keys), 1)

    @pl.loop(0, blocks)
    def _(p):
        q = q_ref[pl.ds(place(p), rows), :] * jnp.asarray(0.125, BF)
        mx[...] = jnp.full(mx.shape, LOWEST, F32)
        tot[...] = jnp.zeros(tot.shape, F32)
        query = p * rows + lax.broadcasted_iota(jnp.int32, (rows, 1), 0)
        reads = (p * rows < spill, (p + 1) * rows > spill)
        for side in range(2):

            @pl.when(reads[side])
            def _():
                allowed = cross_allowed(query, spot, side, spill, sc[2 + side], me, padded, real)
                k = kvs[side][:, 0:width]
                for h in range(heads):
                    s = dot_nt(one_head(q, lanes, h), k)
                    s = jnp.where(allowed, s, LOWEST)
                    s_scr[side, h] = s
                    mx[h] = jnp.maximum(mx[h], jnp.max(s, axis=1, keepdims=True))

        def weigh(side, acc):
            parts = []
            for h in range(heads):
                e = jnp.exp(s_scr[side, h] - mx[h, :, 0:1])
                tot[h] += e
                parts.append(e.astype(BF))
            return acc + dot_nn(jnp.concatenate(parts, axis=1), v_scr[side])

        first = jnp.where(reads[0], 0, 1)
        last = jnp.where(reads[1], 2, 1)
        acc = lax.fori_loop(first, last, weigh, jnp.zeros((rows, width), F32))
        finish(p, place(p), rows, heads, acc, mx, tot, lanes, o_ref, lse_ref)


def spread(p, at, rows, heads, q, g, o_ref, lse_ref, lanes, q_cat, g_cat, stat):
    weighted = (g.astype(F32) * o_ref[at, :].astype(F32)).T
    for h in range(heads):
        q_cat[h * rows : (h + 1) * rows, :] = one_head(q, lanes, h)
        g_cat[h * rows : (h + 1) * rows, :] = one_head(g, lanes, h)
        stat[heads + h : heads + h + 1, :] = jnp.sum(weighted[h * HEAD : (h + 1) * HEAD, :], axis=0, keepdims=True)
    stat[0:heads, :] = lse_ref[0:heads, pl.ds(pl.multiple_of(p * rows, rows), rows)]


def back_block(rows, heads, k, v, allowed, q_cat, g_cat, stat, w_scr, ds_wide, ds_tall):
    count = k.shape[0]
    for h in range(heads):
        span = slice(h * rows, (h + 1) * rows)
        s = dot_nt(k, q_cat[span, :])
        e = jnp.where(allowed, jnp.exp(s - stat[h : h + 1, :]), 0.0)
        de = dot_nt(v, g_cat[span, :])
        ds = (e * (de - stat[heads + h : heads + h + 1, :])).astype(BF)
        w_scr[:, span] = e.astype(BF)
        ds_wide[:, span] = ds
        ds_tall[h * count : (h + 1) * count, :] = ds


def self_backward_kernel(rows, blocks, heads, sc, qkv, kvp, o_ref, g_ref, lse_ref, dq_ref, dkv_ref, dprev_ref,
                         kv_scr, k_cat, dkv_scr, q_cat, g_cat, stat, w_scr, ds_wide, ds_tall):
    width = heads * HEAD
    extent = rows * blocks
    me, spill, prev_spill = sc[0], sc[1], sc[2]
    lanes = head_lanes(rows, width)

    def place(b):
        return pl.multiple_of((b ^ me) * rows, rows)

    first_used, _ = self_range(0, rows, blocks, spill, prev_spill)

    @pl.loop(0, 2 * blocks)
    def _(kb):
        dkv_scr[kb] = jnp.zeros(dkv_scr.shape[1:], F32)

    @pl.loop(first_used, 2 * blocks)
    def _(kb):
        def fill(pair):
            kv_scr[kb] = pair
            scaled = pair[:, 0:width] * jnp.asarray(0.125, BF)
            for h in range(heads):
                k_cat[kb, h * rows : (h + 1) * rows, :] = one_head(scaled, lanes, h)

        @pl.when(kb < blocks)
        def _():
            fill(kvp[pl.ds(place(kb), rows), :])

        @pl.when(kb >= blocks)
        def _():
            fill(qkv[pl.ds(place(kb - blocks), rows), width : 3 * width])

    @pl.loop(0, blocks)
    def _(p):
        at = pl.ds(place(p), rows)
        q = qkv[at, 0:width] * jnp.asarray(0.125, BF)
        g = g_ref[at, :]
        spread(p, at, rows, heads, q, g, o_ref, lse_ref, lanes, q_cat, g_cat, stat)
        first, last = self_range(p, rows, blocks, spill, prev_spill)
        query = p * rows + lax.broadcasted_iota(jnp.int32, (1, rows), 1)

        def step(kb, dq):
            key = kb * rows + lax.broadcasted_iota(jnp.int32, (rows, 1), 0)
            allowed = self_allowed(query, key, extent, spill, prev_spill)
            back_block(rows, heads, kv_scr[kb, :, 0:width], kv_scr[kb, :, width : 2 * width], allowed,
                       q_cat, g_cat, stat, w_scr, ds_wide, ds_tall)
            dkv_scr[kb, :, 0:width] += dot_nn(ds_wide[...], q_cat[...])
            dkv_scr[kb, :, width : 2 * width] += dot_nn(w_scr[...], g_cat[...])
            return dq + dot_tn(ds_tall[...], k_cat[kb])

        dq = lax.fori_loop(first, last, step, jnp.zeros((rows, width), F32))
        dq_ref[at, :] = dq.astype(BF)

    @pl.loop(0, blocks)
    def _(b):
        at = pl.ds(place(b), rows)
        dprev_ref[at, :] = dkv_scr[b].astype(BF)
        dkv_ref[at, :] = dkv_scr[blocks + b].astype(BF)


def cross_backward_kernel(rows, blocks, heads, padded, real, pieces, sc, q_ref, kv0, kv1, o_ref, g_ref, lse_ref,
                          dq_ref, dkv0_ref, dkv1_ref, k_cat, dkv_scr, q_cat, g_cat, stat, w_scr, ds_wide, ds_tall):
    width = heads * HEAD
    keys = kv0.shape[0]
    step_keys = keys // pieces
    me, spill = sc[0], sc[1]
    lanes = head_lanes(rows, width)
    key_lanes = head_lanes(step_keys, width)
    kvs = (kv0, kv1)

    def place(b):
        return pl.multiple_of((b ^ me) * rows, rows)

    dkv_scr[...] = jnp.zeros(dkv_scr.shape, F32)
    for side in range(2):
        for piece in range(pieces):
            scaled = kvs[side][piece * step_keys : (piece + 1) * step_keys, 0:width] * jnp.asarray(0.125, BF)
            for h in range(heads):
                k_cat[side * pieces + piece, h * step_keys : (h + 1) * step_keys, :] = one_head(scaled, key_lanes, h)

    @pl.loop(0, blocks)
    def _(p):
        at = pl.ds(place(p), rows)
        q = q_ref[at, :] * jnp.asarray(0.125, BF)
        spread(p, at, rows, heads, q, g_ref[at, :], o_ref, lse_ref, lanes, q_cat, g_cat, stat)
        query = p * rows + lax.broadcasted_iota(jnp.int32, (1, rows), 1)
        reads = (p * rows < spill, (p + 1) * rows > spill)
        first = jnp.where(reads[0], 0, pieces)
        last = jnp.where(reads[1], 2 * pieces, pieces)

        def step(kb, dq):
            side = kb // pieces
            at_key = pl.ds(pl.multiple_of((kb - side * pieces) * step_keys, step_keys), step_keys)
            spot = (kb - side * pieces) * step_keys + lax.broadcasted_iota(jnp.int32, (step_keys, 1), 0)
            length = jnp.where(side == 0, sc[2], sc[3])
            allowed = cross_allowed(query, spot, side, spill, length, me, padded, real)
            is_prev = side == 0
            pair = jnp.where(is_prev, kv0[at_key, :], kv1[at_key, :])
            back_block(rows, heads, pair[:, 0:width], pair[:, width : 2 * width], allowed,
                       q_cat, g_cat, stat, w_scr, ds_wide, ds_tall)
            dkv_scr[kb, :, 0:width] += dot_nn(ds_wide[...], q_cat[...])
            dkv_scr[kb, :, width : 2 * width] += dot_nn(w_scr[...], g_cat[...])
            return dq + dot_tn(ds_tall[...], k_cat[kb])

        dq = lax.fori_loop(first, last, step, jnp.zeros((rows, width), F32))
        dq_ref[at, :] = dq.astype(BF)

    for piece in range(pieces):
        span = slice(piece * step_keys, (piece + 1) * step_keys)
        dkv0_ref[span, :] = dkv_scr[piece].astype(BF)
        dkv1_ref[span, :] = dkv_scr[pieces + piece].astype(BF)


def call(kernel, scalars, arrays, outs, scratch, flops):
    moved = sum(a.size * a.dtype.itemsize for a in (*arrays, *jax.tree.leaves(outs)))
    vmem = pl.BlockSpec(memory_space=pltpu.VMEM)
    return pl.pallas_call(
        kernel,
        out_shape=outs,
        in_specs=[pl.BlockSpec(memory_space=pltpu.SMEM)] + [vmem] * len(arrays),
        out_specs=jax.tree.map(lambda _: vmem, outs),
        scratch_shapes=scratch,
        compiler_params=pltpu.CompilerParams(vmem_limit_bytes=48 * 2**20),
        cost_estimate=pl.CostEstimate(flops=flops, bytes_accessed=moved, transcendentals=flops // 256),
    )(scalars, *arrays)


def self_forward(scalars, qkv, kvp, blocks):
    extent = qkv.shape[0]
    rows = extent // blocks
    width = qkv.shape[1] // 3
    heads = width // HEAD
    return call(
        functools.partial(self_forward_kernel, rows, blocks, heads),
        scalars,
        (qkv, kvp),
        [jax.ShapeDtypeStruct((extent, width), BF), jax.ShapeDtypeStruct((8, extent), F32)],
        [
            pltpu.VMEM((2 * blocks, rows, width), BF),
            pltpu.VMEM((2 * blocks, heads * rows, width), BF),
            pltpu.VMEM((2 * blocks, heads, rows, rows), F32),
            pltpu.VMEM((heads, rows, rows), F32),
            pltpu.VMEM((heads, rows, rows), F32),
        ],
        extent * extent * heads * 16 * HEAD,
    )


def cross_forward(scalars, q, kv0, kv1, blocks, real):
    extent, width = q.shape
    rows = extent // blocks
    heads = width // HEAD
    keys = kv0.shape[0]
    return call(
        functools.partial(cross_forward_kernel, rows, blocks, heads, keys // blocks, real),
        scalars,
        (q, kv0, kv1),
        [jax.ShapeDtypeStruct((extent, width), BF), jax.ShapeDtypeStruct((8, extent), F32)],
        [
            pltpu.VMEM((2, heads * keys, width), BF),
            pltpu.VMEM((2, heads, rows, keys), F32),
            pltpu.VMEM((heads, rows, keys), F32),
            pltpu.VMEM((heads, rows, keys), F32),
        ],
        extent * keys * heads * 16 * HEAD,
    )


def back_scratch(rows, heads, width, keys):
    return [
        pltpu.VMEM((heads * rows, width), BF),
        pltpu.VMEM((heads * rows, width), BF),
        pltpu.VMEM((8, rows), F32),
        pltpu.VMEM((keys, heads * rows), BF),
        pltpu.VMEM((keys, heads * rows), BF),
        pltpu.VMEM((heads * keys, rows), BF),
    ]


def self_backward(scalars, qkv, kvp, o, g, lse, blocks):
    extent = qkv.shape[0]
    rows = extent // blocks
    width = qkv.shape[1] // 3
    heads = width // HEAD
    return call(
        functools.partial(self_backward_kernel, rows, blocks, heads),
        scalars,
        (qkv, kvp, o, g, lse),
        [
            jax.ShapeDtypeStruct((extent, width), BF),
            jax.ShapeDtypeStruct((extent, 2 * width), BF),
            jax.ShapeDtypeStruct((extent, 2 * width), BF),
        ],
        [
            pltpu.VMEM((2 * blocks, rows, 2 * width), BF),
            pltpu.VMEM((2 * blocks, heads * rows, width), BF),
            pltpu.VMEM((2 * blocks, rows, 2 * width), F32),
        ]
        + back_scratch(rows, heads, width, rows),
        extent * extent * heads * 40 * HEAD,
    )


def cross_backward(scalars, q, kv0, kv1, o, g, lse, blocks, real, pieces=2):
    extent, width = q.shape
    rows = extent // blocks
    heads = width // HEAD
    keys = kv0.shape[0]
    step_keys = keys // pieces
    return call(
        functools.partial(cross_backward_kernel, rows, blocks, heads, keys // blocks, real, pieces),
        scalars,
        (q, kv0, kv1, o, g, lse),
        [
            jax.ShapeDtypeStruct((extent, width), BF),
            jax.ShapeDtypeStruct((keys, 2 * width), BF),
            jax.ShapeDtypeStruct((keys, 2 * width), BF),
        ],
        [
            pltpu.VMEM((2 * pieces, heads * step_keys, width), BF),
            pltpu.VMEM((2 * pieces, step_keys, 2 * width), F32),
        ]
        + back_scratch(rows, heads, width, step_keys),
        extent * keys * heads * 40 * HEAD,
    )


D = 1024
MICRO = 2


def product(left, right):
    return dot_nn(left, right)


def product_t(left, right):
    return dot_nt(left, right)


def outer_sum(left, right):
    return dot_tn(left, right)


def flip(block, axis, bit):
    return lax.ppermute(block, axis, [(i, i ^ bit) for i in range(lax.axis_size(axis))])


def shifted(block, distance):
    devices = range(lax.axis_size("seq"))
    route = [(i - distance, i) for i in devices if i - distance in devices]
    return lax.ppermute(block, "seq", route)


def group_pieces(own):
    far = flip(own, "mem", 2)
    near = flip(own, "mem", 1)
    return [own, near, far, flip(far, "mem", 1)]


def group_rows(own):
    return jnp.concatenate(group_pieces(own), axis=0)


def group_near(part):
    rows = part.shape[0] // 4
    slots = [part[i * rows : (i + 1) * rows] for i in range(4)]
    far = slots[2].astype(F32) + flip(slots[3], "mem", 1).astype(F32)
    near = slots[0].astype(F32) + flip(slots[1], "mem", 1).astype(F32)
    return near, far.astype(BF)


def group_far(near, far):
    return near + flip(far, "mem", 2).astype(F32)


def to_heads(pieces):
    rows = pieces[0].shape[0]
    far = flip(jnp.concatenate([pieces[2], pieces[3]], axis=0), "mem", 2)
    near = flip(pieces[1], "mem", 1)
    last = flip(far[rows:], "mem", 1)
    return [pieces[0], near, far[:rows], last]


def to_tokens(part):
    rows = part.shape[0] // 4
    far = flip(part[2 * rows :], "mem", 2)
    near = flip(part[rows : 2 * rows], "mem", 1)
    last = flip(far[rows:], "mem", 1)
    return [part[:rows], near, far[:rows], last]


def split_columns(tensor, me):
    width = tensor.shape[1] // 4
    return [lax.dynamic_slice_in_dim(tensor, (me ^ k) * width, width, 1) for k in range(4)]


def join_pieces(pieces, me, axis):
    odd = (me & 1) == 1
    high = (me & 2) == 2
    low_pair = [jnp.where(odd, pieces[1 - i], pieces[i]) for i in range(2)]
    high_pair = [jnp.where(odd, pieces[3 - i], pieces[2 + i]) for i in range(2)]
    ordered = [jnp.where(high, high_pair[i], low_pair[i]) for i in range(2)]
    ordered += [jnp.where(high, low_pair[i], high_pair[i]) for i in range(2)]
    return jnp.concatenate(ordered, axis=axis)


def seq_bits():
    count = lax.axis_size("seq")
    return [1 << i for i in reversed(range(count.bit_length() - 1))]


def seq_offsets(bits):
    offsets = [0]
    for bit in bits:
        offsets = offsets + [o ^ bit for o in offsets]
    return offsets


def seq_stage(blocks, bit):
    return blocks + [flip(b, "seq", bit) for b in blocks]


def seq_slots(block, bits):
    blocks = [block]
    for bit in bits:
        blocks = seq_stage(blocks, bit)
    return blocks


def assemble_kernel(rows, offsets, at, *refs):
    out = refs[len(offsets)]
    for ref, offset in zip(refs, offsets):
        out[pl.ds(pl.multiple_of((at[0] ^ offset) * rows, rows), rows), :] = ref[...]


def assemble(blocks, seq, bits):
    offsets = seq_offsets(bits)
    rows, columns = blocks[0].shape
    size = len(blocks) * rows
    out = jax.ShapeDtypeStruct((size, columns), blocks[0].dtype)
    return call(functools.partial(assemble_kernel, rows, offsets), seq.reshape(1), blocks, out, [], 0)


def reorder_kernel(rows, offsets, at, grad, out):
    for i, offset in enumerate(offsets):
        start = pl.multiple_of((at[0] ^ offset) * rows, rows)
        out[i * rows : (i + 1) * rows, :] = grad[pl.ds(start, rows), :].astype(BF)


def reorder(grad, seq, bits):
    offsets = seq_offsets(bits)
    rows = grad.shape[0] // len(offsets)
    out = jax.ShapeDtypeStruct(grad.shape, BF)
    return call(functools.partial(reorder_kernel, rows, offsets), seq.reshape(1), (grad,), out, [], 0)


def seq_reduce(tensor, bits):
    for bit in reversed(bits):
        cut = tensor.shape[0] // 2
        theirs = flip(tensor[cut:].astype(BF), "seq", bit)
        tensor = tensor[:cut].astype(F32) + theirs.astype(F32)
    return tensor


def normal_parts(tensor):
    average = jnp.mean(tensor, axis=-1, keepdims=True)
    centered = tensor - average
    scale = lax.rsqrt(jnp.mean(centered * centered, axis=-1, keepdims=True) + 1e-05)
    return centered * scale, scale


def normal_back(plain, scale, grad):
    inner = jnp.mean(grad * plain, axis=-1, keepdims=True)
    return scale * (grad - jnp.mean(grad, axis=-1, keepdims=True) - plain * inner)


def gelu_parts(pre):
    size = jnp.abs(pre)
    t = 1.0 / (1.0 + (0.3275911 * 0.7071067811865476) * size)
    poly = ((((1.061405429 * t - 1.453152027) * t + 1.421413741) * t - 0.284496736) * t + 0.254829592) * t
    bell = jnp.exp(-0.5 * pre * pre)
    tail = 0.5 * poly * bell
    cdf = jnp.where(pre < 0.0, tail, 1.0 - tail)
    return cdf, bell


def gelu(pre):
    cdf, _ = gelu_parts(pre)
    return pre * cdf


def gelu_slope(pre):
    cdf, bell = gelu_parts(pre)
    return cdf + pre * bell * 0.3989422804014327


def interleave(streams, aside):
    held = [next(s) for s in streams]
    results = [None] * len(streams)
    turn = 0
    ticks = 0
    while True:
        mark = None
        try:
            mark = streams[turn].send(held[turn])
        except StopIteration as end:
            results[turn] = end.value
        other = (turn + 1) % len(streams)
        if mark is not None:
            ticks += 1
            if results[other] is None:
                held[other], mark = lax.optimization_barrier((held[other], mark))
            if ticks in aside:
                mark = aside[ticks](mark)
            held[turn] = streams[turn].send(mark)
        if results[other] is None:
            turn = other
        elif results[turn] is not None:
            return results


def shards(
    inputs,
    memory,
    page_ids,
    memory_length,
    cotangent,
    gain_self,
    self_query,
    self_key,
    self_value,
    self_out,
    gain_cross,
    cross_query,
    cross_key,
    cross_value,
    cross_out,
    gain_mlp,
    mlp_in,
    mlp_out,
):
    seq = lax.axis_index("seq")
    me = lax.axis_index("mem")
    odd = me & 1
    blocks = lax.axis_size("mem")
    tok = inputs.shape[1]
    group = tok * blocks
    real = memory.shape[2]
    padded = -(-real // 16) * 16
    wrows = self_query.shape[0]
    bits = seq_bits()
    turned = bits[:-2] + [bits[-1], bits[-2]]
    half = D // 2

    def gain_rows(gain, weight):
        return (weight.astype(F32) * gain.astype(F32)[:, None]).astype(BF)

    def head_weights(parts):
        split = [split_columns(part, me) for part in parts]
        pieces = [jnp.concatenate([s[k] for s in split], axis=1) for k in range(4)]
        return join_pieces(to_heads(pieces), me, 0)

    def halves(tensor):
        return [lax.dynamic_slice_in_dim(tensor, (odd ^ k) * half, half, 1) for k in range(2)]

    def join_halves(own, other):
        return jnp.concatenate([jnp.where(odd == 0, own, other), jnp.where(odd == 0, other, own)], axis=1)

    norm_ones = [normal_parts(inputs[i].astype(F32)) for i in range(MICRO)]
    qkv_part = head_weights([gain_rows(gain_self, w) for w in (self_query, self_key, self_value)])
    low_pairs = []
    for i in range(MICRO):
        low = norm_ones[i][0].astype(BF)
        low_pairs.append(group_pieces(jnp.concatenate([low, shifted(low, 1)], axis=0)))

    extra = jnp.pad(gain_mlp[:, None], ((0, 0), (0, 127)))
    split = [halves(w) for w in (self_out, gain_rows(gain_cross, cross_query), cross_out)]
    own_half, other_half = [jnp.concatenate([s[k] for s in split] + [extra], axis=1) for k in range(2)]
    near_half = flip(other_half, "mem", 1)
    far_half = flip(jnp.concatenate([own_half, near_half], axis=0), "mem", 2)
    wide = join_pieces([own_half, near_half, far_half[:wrows], far_half[wrows:]], me, 0)
    ckv_part = head_weights([cross_key, cross_value])

    state = {}
    stages = seq_stage([qkv_part], bits[0])
    for bit in bits[1:-1]:
        stages = seq_stage(stages, bit)
    first_wide = seq_stage([wide[:, : 2 * half]], bits[0])
    for bit in bits[1:-2]:
        first_wide = seq_stage(first_wide, bit)
    stages, first_wide = lax.optimization_barrier((stages, first_wide))
    first_wide = seq_stage(first_wide, bits[-2])
    qkv_full = assemble(seq_stage(stages, bits[-1]), seq, bits)
    width = qkv_full.shape[1] // 3
    last_wide = jnp.concatenate([wide[:, 2 * half :], ckv_part], axis=1)
    hidden = mlp_in.shape[0]

    def before_self(mark):
        rows = jnp.pad(memory.reshape(MICRO, real, D), ((0, 0), (0, padded - real), (0, 0)))
        mark, first, last, rows = lax.optimization_barrier((mark, first_wide, last_wide, rows))
        state["first"] = seq_stage(first, bits[-1])
        last = seq_stage([last], bits[0])
        for bit in bits[1:-2]:
            last = seq_stage(last, bit)
        state["last"] = last
        state["rows"] = group_pieces(rows.reshape(MICRO * padded, D))
        return mark

    def after_self_one(mark):
        mark, last = lax.optimization_barrier((mark, state["last"]))
        state["last"] = seq_stage(last, bits[-2])
        return mark

    def after_self_two(mark):
        hidden_part = jnp.concatenate([mlp_in, mlp_out], axis=0)
        mark, first, last, hidden_part = lax.optimization_barrier((mark, state["first"], state["last"], hidden_part))
        state["last"] = seq_stage(last, bits[-1])
        own = assemble(first, seq, bits)
        state["first"] = own, flip(own, "mem", 1)
        state["hidden"] = seq_stage([hidden_part], turned[0])
        return mark

    def after_first_out(mark):
        mark, slots, rows, last = lax.optimization_barrier((mark, state["hidden"], state["rows"], state["last"]))
        for bit in turned[1:-1]:
            slots = seq_stage(slots, bit)
        state["hidden"] = slots
        own = assemble(last, seq, bits)
        state["ckv"] = own[:, half + 128 :]
        state["gain"] = own[:, half].astype(F32)[None, :]
        state["last"] = own[:, :half], flip(own[:, :half], "mem", 1)
        state["rows"] = [
            jnp.concatenate([r[i * padded : (i + 1) * padded] for r in rows], axis=0) for i in range(MICRO)
        ]
        state["mem_kv"] = [product(r, state["ckv"]).astype(BF) for r in state["rows"]]
        state["mem_prev"] = [shifted(kv, 1) for kv in state["mem_kv"]]
        return mark

    def after_cross_one(mark):
        mark, slots = lax.optimization_barrier((mark, state["hidden"]))
        state["hidden"] = seq_stage(slots, turned[-1])
        return mark

    def after_cross_out(mark):
        mark, slots = lax.optimization_barrier((mark, state["hidden"]))
        state["inner"] = jnp.concatenate([s[:hidden] for s in slots], axis=0)
        state["outer"] = jnp.concatenate([s[hidden:] for s in slots], axis=0)
        return mark

    def wide_weights(k):
        if k == 2:
            return state["last"]
        return [w[:, k * half : (k + 1) * half] for w in state["first"]]

    def wide_product(tensor, k):
        own, other = wide_weights(k)
        return join_halves(product(tensor, own), product(tensor, other))

    def wide_back(tensor, k):
        (left, right), (own, other) = halves(tensor), wide_weights(k)
        return product_t(left, own) + product_t(right, other)

    def wide_grads(left, right):
        own, other = halves(right)
        return outer_sum(left, own), outer_sum(left, other)

    def spill_of(micro, block):
        ids = lax.dynamic_slice_in_dim(page_ids[micro], jnp.maximum(block, 0) * group, group, 0)
        return jnp.sum((ids < block).astype(jnp.int32))

    def stream(i):
        x_rows = inputs[i].astype(F32)
        spill = spill_of(i, seq)
        self_at = jnp.stack([me, spill, spill_of(i, seq - 1)])
        before = memory_length[i][jnp.maximum(seq - 1, 0)]
        cross_at = jnp.stack([me, spill, before, memory_length[i][seq]])

        pieces = yield low_pairs[i]
        low_one = jnp.concatenate([p[:tok] for p in pieces], axis=0)
        low_before = jnp.concatenate([p[tok:] for p in pieces], axis=0)
        qkv = product(low_one, qkv_full).astype(BF)
        kv_prev = product(low_before, qkv_full[:, width:]).astype(BF)
        if i == 0:
            kv_prev = before_self(kv_prev)
        self_o, self_lse = self_forward(self_at, qkv, kv_prev, blocks)
        self_lse = yield self_lse

        pieces = yield to_tokens(self_o)
        self_low = join_pieces(pieces, me, 1)
        after_self = x_rows + wide_product(self_low, 0)
        plain_two, scale_two = normal_parts(after_self)
        low_two = plain_two.astype(BF)
        cross_q = split_columns(wide_product(low_two, 1).astype(BF), me)
        scale_two = yield scale_two

        pieces, top = yield to_heads(cross_q), group_pieces(cotangent[i])
        cross_q = jnp.concatenate(pieces, axis=0)
        mem_kv, mem_prev = state["mem_kv"][i], state["mem_prev"][i]
        cross_o, cross_lse = cross_forward(cross_at, cross_q, mem_prev, mem_kv, blocks, real)
        cross_lse = yield cross_lse

        pieces = yield to_tokens(cross_o)
        gain_three = state["gain"]
        cross_low = join_pieces(pieces, me, 1)
        after_cross = after_self + wide_product(cross_low, 2)
        plain_three, scale_three = normal_parts(after_cross)
        low_three = (plain_three * gain_three).astype(BF)
        scale_three = yield scale_three

        pieces = yield group_pieces(low_three)
        low_three = jnp.concatenate(pieces, axis=0)
        top = jnp.concatenate(top, axis=0)
        pre = product_t(low_three, state["inner"])
        pre_low = (product_t(top, state["outer"]) * gelu_slope(pre)).astype(BF)
        near, far = group_near(product(pre_low, state["inner"]).astype(BF))
        near = yield near

        grad_low_three = yield group_far(near, far)
        act = gelu(pre).astype(BF)
        grad_inner = outer_sum(pre_low, low_three)
        grad_outer = outer_sum(act, top)
        output = (after_cross + group_far(*group_near(product(act, state["outer"]).astype(BF)))).astype(BF)
        grad_gain_three = jnp.sum(grad_low_three * plain_three, axis=0)
        grad_after_cross = cotangent[i].astype(F32) + normal_back(
            plain_three, scale_three, grad_low_three * gain_three
        )
        cross_branch = grad_after_cross.astype(BF)
        pieces = split_columns(wide_back(cross_branch, 2).astype(BF), me)
        grad_gain_three = yield grad_gain_three

        pieces = yield to_heads(pieces)
        grad_cout = wide_grads(cross_low, cross_branch)
        cross_g = jnp.concatenate(pieces, axis=0)
        dcq, dmem_prev, dmem = cross_backward(
            cross_at, cross_q, mem_prev, mem_kv, cross_o, cross_g, cross_lse, blocks, real
        )
        dmem = yield dmem

        pieces = yield to_tokens(dcq)
        dmem = (dmem.astype(F32) + shifted(dmem_prev, -1).astype(F32)).astype(BF)
        grad_cq = join_pieces(pieces, me, 1)
        grad_after_self = grad_after_cross + normal_back(plain_two, scale_two, wide_back(grad_cq, 1))
        self_branch = grad_after_self.astype(BF)
        pieces = split_columns(wide_back(self_branch, 0).astype(BF), me)
        grad_after_self = yield grad_after_self

        pieces = yield to_heads(pieces)
        grad_cquery = wide_grads(low_two, grad_cq)
        grad_out = wide_grads(self_low, self_branch)
        self_g = jnp.concatenate(pieces, axis=0)
        dq, dkv, dkv_prev = self_backward(self_at, qkv, kv_prev, self_o, self_g, self_lse, blocks)
        dkv = yield dkv

        back = yield shifted(dkv_prev, -1)
        grad_qkv = outer_sum(low_one, jnp.concatenate([dq, dkv], axis=1))
        grad_prev = outer_sum(low_before, dkv_prev)
        dkv = (dkv.astype(F32) + back.astype(F32)).astype(BF)
        near, far = group_near(product_t(jnp.concatenate([dq, dkv], axis=1), qkv_full).astype(BF))
        near = yield near

        grad_plain = yield group_far(near, far)
        plain_one, scale_one = norm_ones[i]
        grad_x = grad_after_self + normal_back(plain_one, scale_one, grad_plain)
        grad_ckv = outer_sum(state["rows"][i], dmem)
        grad_mem = group_far(*group_near(product_t(dmem, state["ckv"]).astype(BF)))[:real].reshape(1, real, D)
        grad_qkv = grad_qkv + jnp.concatenate([jnp.zeros((D, width), F32), grad_prev], axis=1)
        return (output, grad_x, grad_mem, grad_gain_three, grad_inner, grad_outer, grad_qkv, grad_ckv,
                grad_out, grad_cquery, grad_cout)

    aside = {
        1: after_self_one,
        2: after_self_two,
        3: after_first_out,
        5: after_cross_one,
        8: after_cross_out,
    }
    done = interleave([stream(i) for i in range(MICRO)], aside)

    def total(k):
        return jax.tree.map(lambda a, b: a + b, done[0][k], done[1][k])

    def hidden_reduce(inner, outer):
        for bit in reversed(turned):
            cut = inner.shape[0] // 2
            theirs = flip(jnp.concatenate([inner[cut:], outer[cut:]], axis=0).astype(BF), "seq", bit).astype(F32)
            inner, outer = inner[:cut] + theirs[:cut], outer[:cut] + theirs[cut:]
        return inner, outer

    def wide_reduce(wide, extra_own, extra_other):
        own = jnp.concatenate([w[0].astype(BF) for w in wide] + extra_own, axis=1)
        other = jnp.concatenate([w[1].astype(BF) for w in wide] + extra_other, axis=1)
        return own.astype(F32) + flip(other, "mem", 1).astype(F32)

    def wide_finish(own):
        high = me >> 1
        rows_two = own.reshape(2, 2 * wrows, own.shape[1])
        theirs = lax.dynamic_index_in_dim(rows_two, 1 - high, 0, keepdims=False).astype(BF)
        own = lax.dynamic_index_in_dim(rows_two, high, 0, keepdims=False) + flip(theirs, "mem", 2).astype(F32)
        rows_two = own.reshape(2, wrows, own.shape[1])
        theirs = lax.dynamic_index_in_dim(rows_two, 1 - odd, 0, keepdims=False)
        own = lax.dynamic_index_in_dim(rows_two, odd, 0, keepdims=False)
        return own, flip(theirs.astype(BF), "mem", 1).astype(F32)

    def head_finish(summed, count):
        slots = summed.astype(BF).reshape(blocks, wrows, -1)
        ordered = [lax.dynamic_index_in_dim(slots, me ^ k, 0, keepdims=False) for k in range(4)]
        whole = join_pieces(to_tokens(jnp.concatenate(ordered, axis=0)), me, 1).astype(F32)
        whole = whole.reshape(wrows, blocks, count, -1)
        return [whole[:, :, k].reshape(wrows, D) for k in range(count)]

    def along_seq(tensor):
        return seq_reduce(reorder(tensor, seq, turned), turned)

    grad_inner, grad_outer = hidden_reduce(total(4), total(5))

    gain_terms = jnp.pad(total(3)[:, None], ((0, 0), (0, 127))).astype(BF)
    last = wide_reduce([total(10)], [gain_terms], [jnp.zeros_like(gain_terms)])
    last = along_seq(jnp.concatenate([last, total(7)], axis=1))
    own, near = wide_finish(last[:, : half + 128])
    grad_cout = join_halves(own[:, :half], near[:, :half])
    grad_gain_mlp = own[:, half] + near[:, half]
    grad_ckey, grad_cvalue = head_finish(last[:, half + 128 :], 2)

    own, near = wide_finish(along_seq(wide_reduce([total(8), total(9)], [], [])))
    grad_out, plain_cquery = [
        join_halves(own[:, k * half : (k + 1) * half], near[:, k * half : (k + 1) * half]) for k in range(2)
    ]
    plain_qkv = head_finish(along_seq(total(6)), 3)

    def gained(gain, weights, plains):
        scale = gain.astype(F32)[:, None]
        grad_gain = sum(jnp.sum(w.astype(F32) * p, axis=1) for w, p in zip(weights, plains))
        return grad_gain, [p * scale for p in plains]

    grad_gain_self, (grad_query, grad_key, grad_value) = gained(
        gain_self, (self_query, self_key, self_value), plain_qkv
    )
    grad_gain_cross, (grad_cquery,) = gained(gain_cross, (cross_query,), (plain_cquery,))
    return (
        jnp.stack([d[0] for d in done]),
        jnp.stack([d[1] for d in done]),
        jnp.stack([d[2] for d in done]),
        grad_gain_self,
        grad_query,
        grad_key,
        grad_value,
        grad_out,
        grad_gain_cross,
        grad_cquery,
        grad_ckey,
        grad_cvalue,
        grad_cout,
        grad_gain_mlp,
        grad_inner,
        grad_outer,
    )


def solution(mesh):
    rows = P(("seq", "mem"), None)
    tokens = P(None, ("seq", "mem"), None)
    pages = P(None, "seq", "mem", None)
    gains = P(("seq", "mem"))
    return jax.shard_map(
        shards,
        mesh=mesh,
        in_specs=(tokens, pages, P(), P(), tokens, gains, rows, rows, rows, rows, gains, rows, rows, rows, rows,
                  gains, rows, rows),
        out_specs=(tokens, tokens, pages, gains, rows, rows, rows, rows, gains, rows, rows, rows, rows, gains,
                   rows, rows),
        check_vma=False,
    )
```

time: 3180 us -> 841 us (0.26)
  waiting for transfers between devices: 2180 us -> 339 us
  matrix products: 404 us -> 102 us
  local copies, waits for them, and re-layouts: 301 us -> 49.2 us
  starting transfers between devices: 53 us -> 158 us
  Pallas kernels: 0 us -> 102 us
  blocking collectives: 82.3 us -> 0 us
  other arithmetic: 128 us -> 78 us
    reduce_scatter x18 -> x0, waiting for transfers between devices: 1020 us -> none  [the longest x1 140 us: shards(): lax.psum_scatter(full_grads[4], ('seq', 'mem'), scatter_dimension=0, tile...]
    all_gather x18 -> x0, waiting for transfers between devices: 398 us -> none  [the longest x1 57.5 us: shards(): lax.all_gather(self_query, ('seq', 'mem'), axis=0, tiled=True)]
    dot_general x188 -> x64, matrix products: 404 us -> 102 us  [the longest x20 41.9 us: dot_nt(): lax.dot_general(left, right, (((1,), (1,)), ((), ())), preferred_element_...]
    unnamed x44 -> x0, waiting for transfers between devices: 286 us -> none
    psum x3 -> x0, waiting for transfers between devices: 198 us -> none  [the longest x1 87.1 us: shards(): lax.psum(part_sum.astype(jnp.bfloat16), 'mem').astype(jnp.float32)]
    ppermute x16 -> x151, starting transfers between devices: 50.1 us -> 158 us  [the longest x143 139 us: flip(): lax.ppermute(block, axis, [(i, i ^ bit) for i in range(lax.axis_size(axis...]
    pallas_call x0 -> x14, Pallas kernels: none -> 102 us  [call(): pl.pallas_call(kernel, out_shape=outs, in_specs=[pl.BlockSpec(memory_spac...]
    ppermute x16 -> x151, waiting for transfers between devices: 247 us -> 339 us  [the longest x143 310 us: flip(): lax.ppermute(block, axis, [(i, i ^ bit) for i in range(lax.axis_size(axis...]
  transfers between devices with their start and end apart: 58 -> 151, of which waited for: 39 -> 57; matrix products, arithmetic and copies ran while one was open for 18% -> 25% of each run, Pallas kernels for 0% -> 12%
where the time goes in v1:
time: 841 us; the launch traced here: 834 us
  waiting for transfers between devices  339 us (40%)
  starting transfers between devices  158 us (19%)
  Pallas kernels  102 us (12%)
  matrix products  102 us (12%)
  other arithmetic  78 us (9%)
  local copies, waits for them, and re-layouts  49.2 us (6%)
    ppermute x143, waiting for transfers between devices, flip(): lax.ppermute(block, axis, [(i, i ^ bit) for i in range(lax.axis_size(axis...  310 us
    ppermute x143, starting transfers between devices, flip(): lax.ppermute(block, axis, [(i, i ^ bit) for i in range(lax.axis_size(axis...  139 us
    pallas_call x14, Pallas kernels, call(): pl.pallas_call(kernel, out_shape=outs, in_specs=[pl.BlockSpec(memory_spac...  102 us
    dot_general x20, matrix products, dot_nt(): lax.dot_general(left, right, (((1,), (1,)), ((), ())), preferred_element_...  41.9 us
    dot_general x22, matrix products, dot_tn(): lax.dot_general(left, right, (((0,), (0,)), ((), ())), preferred_element_...  32.8 us
    ppermute x8, waiting for transfers between devices, shifted(): return lax.ppermute(block, 'seq', route)  28.2 us
    unnamed x428, local copies, waits for them, and re-layouts  28.1 us
    dot_general x22, matrix products, dot_nn(): lax.dot_general(left, right, (((1,), (0,)), ((), ())), preferred_element_...  27.5 us
  transfers between devices with their start and end apart: 151, of which 57 were waited for; matrix products, arithmetic and copies ran while one was open for 25% of the time, Pallas kernels for 12%

profile of v1, /device:TPU:0, one launch (start us, length us, event | category | flops | bytes accessed | tf_op | source)
XLA Modules:
  0.0 834.4 jit_solution(11037894236978315324)
XLA Ops:
  97.4 11.9 %shard_map.298 = (bf16[1024,256]{1,0:T(8,128)(2,1)S(1)}, f32[8,1024]{1,0:T(8,128)S(1)}) custom-call(s32[3]{0:T(128)S(1)} %pad_add_fusion.sc, bf16[1024,768]{1,0:T(8,128)(2,1)S(1)} %convolution_convert_fusion.7.qkv, bf16[1024,512]{1,0:T(8,128)(2,1)S(1)} %convolution_convert_fusion.11.kvp), custom_call_target="tpu_custom_call" | custom-call | flops 4294967296 | bytes 3178496 | tf_op jit(solution)/shard_map/pallas_call | solution.py:315
  111.0 9.4 %collective-permute-start.29 = (bf16[128,1024]{1,0:T(8,128)(2,1)S(1)}, bf16[128,1024]{1,0:T(8,128)(2,1)S(1)}, u32[]{:S(2)}, u32[]{:S(2)}) collective-permute-start(bf16[128,1024]{1,0:T(8,128)(2,1)S(1)} %slice.814.refs_0_), channel_id=1, source_target_pairs={{0,4},{4,0},{8,12},{12,8},{16,20},{20,16},{24,28},{28,24},{1,5},{5... | collective-permute-start | bytes 786440 | tf_op jit(solution)/shard_map/ppermute | solution.py:443
  124.3 11.0 %collective-permute-done.33.refs_1_ = bf16[128,1152]{1,0:T(8,128)(2,1)S(1)} collective-permute-done((bf16[128,1152]{1,0:T(8,128)(2,1)S(1)}, bf16[128,1152]{1,0:T(8,128)(2,1)S(1)}, u32[]{:S(2)}, u32[]{:S(2)}) %collective-permute-start.33) | collective-permute-done | bytes 294944 | tf_op jit(solution)/shard_map/ppermute | solution.py:443
  139.5 12.1 %shard_map.299 = (bf16[1024,256]{1,0:T(8,128)(2,1)S(1)}, f32[8,1024]{1,0:T(8,128)S(1)}) custom-call(s32[3]{0:T(128)S(1)} %pad_add_fusion.1.sc, bf16[1024,768]{1,0:T(8,128)(2,1)S(1)} %convolution_convert_fusion.6.qkv, bf16[1024,512]{1,0:T(8,128)(2,1)S(1)} %convolution_convert_fusion.10.kvp), custom_call_target="tpu_custom_call" | custom-call | flops 4294967296 | bytes 3178496 | tf_op jit(solution)/shard_map/pallas_call | solution.py:315
  163.2 11.6 %collective-permute-done.44 = bf16[512,256]{1,0:T(8,128)(2,1)S(1)} collective-permute-done((bf16[512,256]{1,0:T(8,128)(2,1)}, bf16[512,256]{1,0:T(8,128)(2,1)S(1)}, u32[]{:S(2)}, u32[]{:S(2)}) %collective-permute-start.44) | collective-permute-done | bytes 262176 | tf_op jit(solution)/shard_map/ppermute | solution.py:443
  176.0 12.1 %collective-permute-done.48 = bf16[320,1024]{1,0:T(8,128)(2,1)S(1)} collective-permute-done((bf16[320,1024]{1,0:T(8,128)(2,1)}, bf16[320,1024]{1,0:T(8,128)(2,1)S(1)}, u32[]{:S(2)}, u32[]{:S(2)}) %collective-permute-start.48) | collective-permute-done | bytes 655392 | tf_op jit(solution)/shard_map/ppermute | solution.py:443
  246.5 8.8 %collective-permute-done.54.kv0 = bf16[640,512]{1,0:T(8,128)(2,1)S(1)} collective-permute-done((bf16[640,512]{1,0:T(8,128)(2,1)S(1)}, bf16[640,512]{1,0:T(8,128)(2,1)S(1)}, u32[]{:S(2)}, u32[]{:S(2)}) %collective-permute-start.54) | collective-permute-done | bytes 655392 | tf_op jit(solution)/shard_map/ppermute | solution.py:449
  255.3 10.9 %shard_map.302 = (bf16[1024,256]{1,0:T(8,128)(2,1)S(1)}, f32[8,1024]{1,0:T(8,128)S(1)}) custom-call(s32[4]{0:T(128)S(1)} %pad_add_fusion.2.sc, bf16[1024,256]{1,0:T(8,128)(2,1)S(1)} %constant_dynamic-update-slice_fusion.q_ref, bf16[640,512]{1,0:T(8,128)(2,1)S(1)} %collective-permute-done.54.kv0, bf16[640,512]{1,0:T(8,128)(2,1)S(1)} %convolution_convert_fusion.13.kv1), custom_call_target="tpu_custom_call" | custom-call | flops 2684354560 | bytes 2392064 | tf_op jit(solution)/shard_map/pallas_call | solution.py:315
  269.0 11.0 %shard_map.303 = (bf16[1024,256]{1,0:T(8,128)(2,1)S(1)}, f32[8,1024]{1,0:T(8,128)S(1)}) custom-call(s32[4]{0:T(128)S(1)} %pad_add_fusion.3.sc, bf16[1024,256]{1,0:T(8,128)(2,1)S(1)} %constant_dynamic-update-slice_fusion.4.q_ref, bf16[640,512]{1,0:T(8,128)(2,1)S(1)} %collective-permute-done.64.kv0, bf16[640,512]{1,0:T(8,128)(2,1)S(1)} %convolution_convert_fusion.12.kv1), custom_call_target="tpu_custom_call" | custom-call | flops 2684354560 | bytes 2392064 | tf_op jit(solution)/shard_map/pallas_call | solution.py:315
  312.0 10.8 %collective-permute-done.73 = bf16[256,1024]{1,0:T(8,128)(2,1)} collective-permute-done((bf16[256,1024]{1,0:T(8,128)(2,1)}, bf16[256,1024]{1,0:T(8,128)(2,1)}, u32[]{:S(2)}, u32[]{:S(2)}) %collective-permute-start.73) | collective-permute-done | bytes 524320 | tf_op jit(solution)/shard_map/ppermute | solution.py:443
  339.3 9.8 %collective-permute-done.75 = bf16[256,1024]{1,0:T(8,128)(2,1)S(1)} collective-permute-done((bf16[256,1024]{1,0:T(8,128)(2,1)}, bf16[256,1024]{1,0:T(8,128)(2,1)S(1)}, u32[]{:S(2)}, u32[]{:S(2)}) %collective-permute-start.75) | collective-permute-done | bytes 524320 | tf_op jit(solution)/shard_map/ppermute | solution.py:443
  349.1 11.2 %collective-permute-done.76 = bf16[256,1024]{1,0:T(8,128)(2,1)S(1)} collective-permute-done((bf16[256,1024]{1,0:T(8,128)(2,1)}, bf16[256,1024]{1,0:T(8,128)(2,1)S(1)}, u32[]{:S(2)}, u32[]{:S(2)}) %collective-permute-start.76) | collective-permute-done | bytes 524320 | tf_op jit(solution)/shard_map/ppermute | solution.py:443
  360.3 9.9 %collective-permute-done.77 = bf16[256,1024]{1,0:T(8,128)(2,1)S(1)} collective-permute-done((bf16[256,1024]{1,0:T(8,128)(2,1)}, bf16[256,1024]{1,0:T(8,128)(2,1)S(1)}, u32[]{:S(2)}, u32[]{:S(2)}) %collective-permute-start.77) | collective-permute-done | bytes 524320 | tf_op jit(solution)/shard_map/ppermute | solution.py:443
  438.8 10.4 %collective-permute-done.92 = bf16[256,1024]{1,0:T(8,128)(2,1)S(1)} collective-permute-done((bf16[256,1024]{1,0:T(8,128)(2,1)S(1)}, bf16[256,1024]{1,0:T(8,128)(2,1)S(1)}, u32[]{:S(2)}, u32[]{:S(2)}) %collective-permute-start.92) | collective-permute-done | bytes 524320 | tf_op jit(solution)/shard_map/ppermute | solution.py:443
  449.5 10.2 %collective-permute-done.87 = bf16[256,1024]{1,0:T(8,128)(2,1)S(1)} collective-permute-done((bf16[256,1024]{1,0:T(8,128)(2,1)S(1)}, bf16[256,1024]{1,0:T(8,128)(2,1)S(1)}, u32[]{:S(2)}, u32[]{:S(2)}) %collective-permute-start.87) | collective-permute-done | bytes 524320 | tf_op jit(solution)/shard_map/ppermute | solution.py:443
  483.3 11.9 %shard_map.304 = (bf16[1024,256]{1,0:T(8,128)(2,1)S(1)}, bf16[640,512]{1,0:T(8,128)(2,1)S(1)}, bf16[640,512]{1,0:T(8,128)(2,1)S(1)}) custom-call(s32[4]{0:T(128)S(1)} %pad_add_fusion.2.sc, bf16[1024,256]{1,0:T(8,128)(2,1)S(1)} %copy-done.15, bf16[640,512]{1,0:T(8,128)(2,1)S(1)} %copy-done.27, bf16[640,512]{1,0:T(8,128)(2,1)S(1)} %copy-done.25, ...), custom_call_target="tpu_custom_call" | custom-call | flops 6710886400 | bytes 4751360 | tf_op jit(solution)/shard_map/pallas_call | solution.py:315
  496.6 11.9 %shard_map.305 = (bf16[1024,256]{1,0:T(8,128)(2,1)S(1)}, bf16[640,512]{1,0:T(8,128)(2,1)S(1)}, bf16[640,512]{1,0:T(8,128)(2,1)S(1)}) custom-call(s32[4]{0:T(128)S(1)} %pad_add_fusion.3.sc, bf16[1024,256]{1,0:T(8,128)(2,1)S(1)} %copy-done.17, bf16[640,512]{1,0:T(8,128)(2,1)S(1)} %copy-done.29, bf16[640,512]{1,0:T(8,128)(2,1)S(1)} %copy-done.23, ...), custom_call_target="tpu_custom_call" | custom-call | flops 6710886400 | bytes 4751360 | tf_op jit(solution)/shard_map/pallas_call | solution.py:315
  572.1 13.5 %shard_map.306 = (bf16[1024,256]{1,0:T(8,128)(2,1)S(1)}, bf16[1024,512]{1,0:T(8,128)(2,1)S(1)}, bf16[1024,512]{1,0:T(8,128)(2,1)S(1)}) custom-call(s32[3]{0:T(128)S(1)} %copy-done.21, bf16[1024,768]{1,0:T(8,128)(2,1)} %copy-done.34, bf16[1024,512]{1,0:T(8,128)(2,1)S(1)} %copy-done.31, bf16[1024,256]{1,0:T(8,128)(2,1)S(1)} %copy-done.5, ...), custom_call_target="tpu_custom_call" | custom-call | flops 10737418240 | bytes 6324224 | tf_op jit(solution)/shard_map/pallas_call | solution.py:315
  587.2 13.5 %shard_map.307 = (bf16[1024,256]{1,0:T(8,128)(2,1)S(1)}, bf16[1024,512]{1,0:T(8,128)(2,1)S(1)}, bf16[1024,512]{1,0:T(8,128)(2,1)S(1)}) custom-call(s32[3]{0:T(128)S(1)} %copy-done.19, bf16[1024,768]{1,0:T(8,128)(2,1)} %copy-done.35, bf16[1024,512]{1,0:T(8,128)(2,1)S(1)} %copy-done.33, bf16[1024,256]{1,0:T(8,128)(2,1)S(1)} %get-tuple-element.223.o_ref, ...), custom_call_target="tpu_custom_call" | custom-call | flops 10737418240 | bytes 6324224 | tf_op jit(solution)/shard_map/pallas_call | solution.py:315
  626.1 17.8 %collective-permute-start.140 = (bf16[512,1152]{1,0:T(8,128)(2,1)}, bf16[512,1152]{1,0:T(8,128)(2,1)}, u32[]{:S(2)}, u32[]{:S(2)}) collective-permute-start(bf16[512,1152]{1,0:T(8,128)(2,1)} %slice.909), channel_id=1, source_target_pairs={{0,8},{4,12},{8,0},{12,4},{16,24},{20,28},{24,16},{28,20},{1,9},{5... | collective-permute-start | bytes 3538952 | tf_op jit(solution)/shard_map/ppermute | solution.py:443
  649.4 13.5 %collective-permute-done.112 = bf16[1024,512]{1,0:T(8,128)(2,1)S(1)} collective-permute-done((bf16[1024,512]{1,0:T(8,128)(2,1)S(1)}, bf16[1024,512]{1,0:T(8,128)(2,1)S(1)}, u32[]{:S(2)}, u32[]{:S(2)}) %collective-permute-start.112) | collective-permute-done | bytes 1048608 | tf_op jit(solution)/shard_map/ppermute | solution.py:449
  672.3 49.6 %collective-permute-done.140 = bf16[512,1152]{1,0:T(8,128)(2,1)} collective-permute-done((bf16[512,1152]{1,0:T(8,128)(2,1)}, bf16[512,1152]{1,0:T(8,128)(2,1)}, u32[]{:S(2)}, u32[]{:S(2)}) %collective-permute-start.140) | collective-permute-done | bytes 1179680 | tf_op jit(solution)/shard_map/ppermute | solution.py:443
  753.3 20.6 %collective-permute-done.142 = bf16[128,1152]{1,0:T(8,128)(2,1)S(1)} collective-permute-done((bf16[128,1152]{1,0:T(8,128)(2,1)S(1)}, bf16[128,1152]{1,0:T(8,128)(2,1)S(1)}, u32[]{:S(2)}, u32[]{:S(2)}) %collective-permute-start.142) | collective-permute-done | bytes 294944 | tf_op jit(solution)/shard_map/ppermute | solution.py:443
  802.5 12.2 %collective-permute-done.135 = bf16[256,1024]{1,0:T(8,128)(2,1)S(1)} collective-permute-done((bf16[256,1024]{1,0:T(8,128)(2,1)S(1)}, bf16[256,1024]{1,0:T(8,128)(2,1)S(1)}, u32[]{:S(2)}, u32[]{:S(2)}) %collective-permute-start.135) | collective-permute-done | bytes 524320 | tf_op jit(solution)/shard_map/ppermute | solution.py:443
  (1047 shorter events, 503.1 us)
Async XLA Ops:
  41.8 42.0 %collective-permute-start.1 = (bf16[512,1024]{1,0:T(8,128)(2,1)S(1)}, bf16[512,1024]{1,0:T(8,128)(2,1)S(1)}, u32[]{:S(2)}, u32[]{:S(2)}) collective-permute-start(bf16[512,1024]{1,0:T(8,128)(2,1)S(1)} %pad_maximum_fusion.19), channel_id=1, source_target_pairs={{0,1},{1,0},{2,3},{3,2},{4,5},{5,4},{6,7},{7,6},{8,9},{9,8},{10,11... | collective-permute-start | bytes 3145736 | tf_op jit(solution)/shard_map/ppermute | solution.py:443
  41.9 42.0 %collective-permute-start.27 = (bf16[512,1024]{1,0:T(8,128)(2,1)S(1)}, bf16[512,1024]{1,0:T(8,128)(2,1)S(1)}, u32[]{:S(2)}, u32[]{:S(2)}) collective-permute-start(bf16[512,1024]{1,0:T(8,128)(2,1)S(1)} %pad_maximum_fusion.20), channel_id=1, source_target_pairs={{0,2},{1,3},{2,0},{3,1},{4,6},{5,7},{6,4},{7,5},{8,10},{9,11},{10,... | collective-permute-start | bytes 3145736 | tf_op jit(solution)/shard_map/ppermute | solution.py:443
  152.8 41.4 %collective-permute-start.36 = (bf16[1024,1024]{1,0:T(8,128)(2,1)S(1)}, bf16[1024,1024]{1,0:T(8,128)(2,1)}, u32[]{:S(2)}, u32[]{:S(2)}) collective-permute-start(bf16[1024,1024]{1,0:T(8,128)(2,1)S(1)} %shard_map.300), channel_id=1, source_target_pairs={{0,1},{1,0},{2,3},{3,2},{4,5},{5,4},{6,7},{7,6},{8,9},{9,8},{10,11... | collective-permute-start | bytes 6291464 | tf_op jit(solution)/shard_map/ppermute | solution.py:443
  154.2 43.1 %collective-permute-start.41 = (bf16[256,1024]{1,0:T(8,128)(2,1)}, bf16[256,1024]{1,0:T(8,128)(2,1)}, u32[]{:S(2)}, u32[]{:S(2)}) collective-permute-start(bf16[256,1024]{1,0:T(8,128)(2,1)} %get-tuple-element.287), channel_id=1, source_target_pairs={{0,2},{1,3},{2,0},{3,1},{4,6},{5,7},{6,4},{7,5},{8,10},{9,11},{10,... | collective-permute-start | bytes 1572872 | tf_op jit(solution)/shard_map/ppermute | solution.py:443
  161.5 37.3 %collective-permute-start.47 = (bf16[320,1024]{1,0:T(8,128)(2,1)}, bf16[320,1024]{1,0:T(8,128)(2,1)S(1)}, u32[]{:S(2)}, u32[]{:S(2)}) collective-permute-start(bf16[320,1024]{1,0:T(8,128)(2,1)} %bitcast.221), channel_id=1, source_target_pairs={{0,1},{1,0},{2,3},{3,2},{4,5},{5,4},{6,7},{7,6},{8,9},{9,8},{10,11... | collective-permute-start | bytes 1966088 | tf_op jit(solution)/shard_map/ppermute | solution.py:443
  324.8 35.5 %collective-permute-start.76 = (bf16[256,1024]{1,0:T(8,128)(2,1)}, bf16[256,1024]{1,0:T(8,128)(2,1)S(1)}, u32[]{:S(2)}, u32[]{:S(2)}) collective-permute-start(bf16[256,1024]{1,0:T(8,128)(2,1)} %collective-permute-done.72), channel_id=1, source_target_pairs={{0,8},{4,12},{8,0},{12,4},{16,24},{20,28},{24,16},{28,20},{1,9},{5... | collective-permute-start | bytes 1572872 | tf_op jit(solution)/shard_map/ppermute | solution.py:443
  326.1 44.1 %collective-permute-start.77 = (bf16[256,1024]{1,0:T(8,128)(2,1)}, bf16[256,1024]{1,0:T(8,128)(2,1)S(1)}, u32[]{:S(2)}, u32[]{:S(2)}) collective-permute-start(bf16[256,1024]{1,0:T(8,128)(2,1)} %collective-permute-done.73), channel_id=1, source_target_pairs={{0,8},{4,12},{8,0},{12,4},{16,24},{20,28},{24,16},{28,20},{1,9},{5... | collective-permute-start | bytes 1572872 | tf_op jit(solution)/shard_map/ppermute | solution.py:443
  337.9 57.6 %collective-permute-start.81 = (bf16[256,1024]{1,0:T(8,128)(2,1)S(1)}, bf16[256,1024]{1,0:T(8,128)(2,1)S(1)}, u32[]{:S(2)}, u32[]{:S(2)}) collective-permute-start(bf16[256,1024]{1,0:T(8,128)(2,1)S(1)} %copy-done.74), channel_id=1, source_target_pairs={{0,1},{1,0},{2,3},{3,2},{4,5},{5,4},{6,7},{7,6},{8,9},{9,8},{10,11... | collective-permute-start | bytes 1572872 | tf_op jit(solution)/shard_map/ppermute | solution.py:443
  339.3 56.2 %collective-permute-start.83 = (bf16[256,1024]{1,0:T(8,128)(2,1)S(1)}, bf16[256,1024]{1,0:T(8,128)(2,1)S(1)}, u32[]{:S(2)}, u32[]{:S(2)}) collective-permute-start(bf16[256,1024]{1,0:T(8,128)(2,1)S(1)} %collective-permute-done.82), channel_id=1, source_target_pairs={{0,1},{1,0},{2,3},{3,2},{4,5},{5,4},{6,7},{7,6},{8,9},{9,8},{10,11... | collective-permute-start | bytes 1572872 | tf_op jit(solution)/shard_map/ppermute | solution.py:443
  394.6 40.3 %collective-permute-start.78 = (bf16[256,1024]{1,0:T(8,128)(2,1)S(1)}, bf16[256,1024]{1,0:T(8,128)(2,1)S(1)}, u32[]{:S(2)}, u32[]{:S(2)}) collective-permute-start(bf16[256,1024]{1,0:T(8,128)(2,1)S(1)} %get-tuple-element.450), channel_id=1, source_target_pairs={{0,1},{1,0},{2,3},{3,2},{4,5},{5,4},{6,7},{7,6},{8,9},{9,8},{10,11... | collective-permute-start | bytes 1572872 | tf_op jit(solution)/shard_map/ppermute | solution.py:443
  395.4 37.0 %collective-permute-start.89 = (bf16[256,1024]{1,0:T(8,128)(2,1)S(1)}, bf16[256,1024]{1,0:T(8,128)(2,1)S(1)}, u32[]{:S(2)}, u32[]{:S(2)}) collective-permute-start(bf16[256,1024]{1,0:T(8,128)(2,1)S(1)} %get-tuple-element.446), channel_id=1, source_target_pairs={{0,2},{1,3},{2,0},{3,1},{4,6},{5,7},{6,4},{7,5},{8,10},{9,11},{10,... | collective-permute-start | bytes 1572872 | tf_op jit(solution)/shard_map/ppermute | solution.py:443
  432.4 111.8 %collective-permute-start.148 = (bf16[1024,1024]{1,0:T(8,128)(2,1)}, bf16[1024,1024]{1,0:T(8,128)(2,1)}, u32[]{:S(2)}, u32[]{:S(2)}) collective-permute-start(bf16[1024,1024]{1,0:T(8,128)(2,1)} %pad_maximum_fusion.7), channel_id=1, source_target_pairs={{0,8},{4,12},{8,0},{12,4},{16,24},{20,28},{24,16},{28,20},{1,9},{5... | collective-permute-start | bytes 6291464 | tf_op jit(solution)/shard_map/ppermute | solution.py:443
  480.4 125.7 %collective-permute-start.139 = (bf16[1024,640]{1,0:T(8,128)(2,1)}, bf16[1024,640]{1,0:T(8,128)(2,1)}, u32[]{:S(2)}, u32[]{:S(2)}) collective-permute-start(bf16[1024,640]{1,0:T(8,128)(2,1)} %concatenate.327), channel_id=1, source_target_pairs={{0,1},{1,0},{2,3},{3,2},{4,5},{5,4},{6,7},{7,6},{8,9},{9,8},{10,11... | collective-permute-start | bytes 3932168 | tf_op jit(solution)/shard_map/ppermute | solution.py:443
  534.8 50.8 %collective-permute-start.105 = (bf16[256,256]{1,0:T(8,128)(2,1)}, bf16[256,256]{1,0:T(8,128)(2,1)}, u32[]{:S(2)}, u32[]{:S(2)}) collective-permute-start(bf16[256,256]{1,0:T(8,128)(2,1)} %get-tuple-element.504), channel_id=1, source_target_pairs={{0,1},{1,0},{2,3},{3,2},{4,5},{5,4},{6,7},{7,6},{8,9},{9,8},{10,11... | collective-permute-start | bytes 393224 | tf_op jit(solution)/shard_map/ppermute | solution.py:443
  563.3 83.2 %collective-permute-start.149 = (bf16[512,1024]{1,0:T(8,128)(2,1)}, bf16[512,1024]{1,0:T(8,128)(2,1)S(1)}, u32[]{:S(2)}, u32[]{:S(2)}) collective-permute-start(bf16[512,1024]{1,0:T(8,128)(2,1)} %pad_maximum_fusion.22), channel_id=1, source_target_pairs={{0,4},{4,0},{8,12},{12,8},{16,20},{20,16},{24,28},{28,24},{1,5},{5... | collective-permute-start | bytes 3145736 | tf_op jit(solution)/shard_map/ppermute | solution.py:443
  571.8 36.4 %collective-permute-start.125 = (bf16[160,1024]{1,0:T(8,128)(2,1)}, bf16[160,1024]{1,0:T(8,128)(2,1)}, u32[]{:S(2)}, u32[]{:S(2)}) collective-permute-start(bf16[160,1024]{1,0:T(8,128)(2,1)} %get-tuple-element.458), channel_id=1, source_target_pairs={{0,1},{1,0},{2,3},{3,2},{4,5},{5,4},{6,7},{7,6},{8,9},{9,8},{10,11... | collective-permute-start | bytes 983048 | tf_op jit(solution)/shard_map/ppermute | solution.py:443
  618.9 114.8 %collective-permute-start.133 = (bf16[1024,1024]{1,0:T(8,128)(2,1)}, bf16[1024,1024]{1,0:T(8,128)(2,1)}, u32[]{:S(2)}, u32[]{:S(2)}) collective-permute-start(bf16[1024,1024]{1,0:T(8,128)(2,1)} %pad_maximum_fusion.6), channel_id=1, source_target_pairs={{0,1},{1,0},{2,3},{3,2},{4,5},{5,4},{6,7},{7,6},{8,9},{9,8},{10,11... | collective-permute-start | bytes 6291464 | tf_op jit(solution)/shard_map/ppermute | solution.py:443
  619.9 43.0 %collective-permute-start.112 = (bf16[1024,512]{1,0:T(8,128)(2,1)S(1)}, bf16[1024,512]{1,0:T(8,128)(2,1)S(1)}, u32[]{:S(2)}, u32[]{:S(2)}) collective-permute-start(bf16[1024,512]{1,0:T(8,128)(2,1)S(1)} %get-tuple-element.344), channel_id=1, source_target_pairs={{4,0},{8,4},{12,8},{16,12},{20,16},{24,20},{28,24},{5,1},{9,5},{13... | collective-permute-start | bytes 3145736 | tf_op jit(solution)/shard_map/ppermute | solution.py:449
  622.3 106.6 %collective-permute-start.111 = (bf16[1024,512]{1,0:T(8,128)(2,1)S(1)}, bf16[1024,512]{1,0:T(8,128)(2,1)}, u32[]{:S(2)}, u32[]{:S(2)}) collective-permute-start(bf16[1024,512]{1,0:T(8,128)(2,1)S(1)} %get-tuple-element.341), channel_id=1, source_target_pairs={{4,0},{8,4},{12,8},{16,12},{20,16},{24,20},{28,24},{5,1},{9,5},{13... | collective-permute-start | bytes 3145736 | tf_op jit(solution)/shard_map/ppermute | solution.py:449
  626.1 95.8 %collective-permute-start.140 = (bf16[512,1152]{1,0:T(8,128)(2,1)}, bf16[512,1152]{1,0:T(8,128)(2,1)}, u32[]{:S(2)}, u32[]{:S(2)}) collective-permute-start(bf16[512,1152]{1,0:T(8,128)(2,1)} %slice.909), channel_id=1, source_target_pairs={{0,8},{4,12},{8,0},{12,4},{16,24},{20,28},{24,16},{28,20},{1,9},{5... | collective-permute-start | bytes 3538952 | tf_op jit(solution)/shard_map/ppermute | solution.py:443
  649.4 75.0 %collective-permute-start.150 = (bf16[256,1024]{1,0:T(8,128)(2,1)}, bf16[256,1024]{1,0:T(8,128)(2,1)}, u32[]{:S(2)}, u32[]{:S(2)}) collective-permute-start(bf16[256,1024]{1,0:T(8,128)(2,1)} %pad_maximum_fusion.34), channel_id=1, source_target_pairs={{0,16},{4,20},{8,24},{12,28},{16,0},{20,4},{24,8},{28,12},{1,17},{... | collective-permute-start | bytes 1572872 | tf_op jit(solution)/shard_map/ppermute | solution.py:443
  666.2 60.5 %collective-permute-start.114 = (bf16[256,1024]{1,0:T(8,128)(2,1)}, bf16[256,1024]{1,0:T(8,128)(2,1)}, u32[]{:S(2)}, u32[]{:S(2)}) collective-permute-start(bf16[256,1024]{1,0:T(8,128)(2,1)} %get-tuple-element.440), channel_id=1, source_target_pairs={{0,1},{1,0},{2,3},{3,2},{4,5},{5,4},{6,7},{7,6},{8,9},{9,8},{10,11... | collective-permute-start | bytes 1572872 | tf_op jit(solution)/shard_map/ppermute | solution.py:443
  744.4 54.5 %collective-permute-start.134 = (bf16[512,1024]{1,0:T(8,128)(2,1)}, bf16[512,1024]{1,0:T(8,128)(2,1)}, u32[]{:S(2)}, u32[]{:S(2)}) collective-permute-start(bf16[512,1024]{1,0:T(8,128)(2,1)} %slice.899), channel_id=1, source_target_pairs={{0,8},{4,12},{8,0},{12,4},{16,24},{20,28},{24,16},{28,20},{1,9},{5... | collective-permute-start | bytes 3145736 | tf_op jit(solution)/shard_map/ppermute | solution.py:443
  752.4 44.8 %collective-permute-start.118 = (bf16[256,1024]{1,0:T(8,128)(2,1)}, bf16[256,1024]{1,0:T(8,128)(2,1)}, u32[]{:S(2)}, u32[]{:S(2)}) collective-permute-start(bf16[256,1024]{1,0:T(8,128)(2,1)} %get-tuple-element.434), channel_id=1, source_target_pairs={{0,2},{1,3},{2,0},{3,1},{4,6},{5,7},{6,4},{7,5},{8,10},{9,11},{10,... | collective-permute-start | bytes 1572872 | tf_op jit(solution)/shard_map/ppermute | solution.py:443
  (325 other events, 3873.8 us)

commit v2 on v1

v2 whole, which is shorter than its diff:
```python
import functools
import jax
import jax.numpy as jnp
import numpy as np
from jax import lax
from jax.experimental import pallas as pl
from jax.experimental.pallas import tpu as pltpu
from jax.sharding import PartitionSpec as P

HEAD = 64
BF = jnp.bfloat16
F32 = jnp.float32
LOWEST = -1e30


def head_lanes(rows, width):
    return lax.broadcasted_iota(jnp.int32, (rows, width), 1) // HEAD


def one_head(block, lanes, head):
    return jnp.where(lanes == head, block, jnp.zeros_like(block))


def dot_nt(left, right):
    return lax.dot_general(left, right, (((1,), (1,)), ((), ())), preferred_element_type=F32)


def dot_nn(left, right):
    return lax.dot_general(left, right, (((1,), (0,)), ((), ())), preferred_element_type=F32)


def dot_tn(left, right):
    return lax.dot_general(left, right, (((0,), (0,)), ((), ())), preferred_element_type=F32)


def self_range(p, rows, blocks, spill, prev_spill):
    first = jnp.where(p * rows < spill, prev_spill // rows, blocks + spill // rows)
    return first, blocks + p + 1


def self_allowed(query, key, extent, spill, prev_spill):
    first = jnp.where(query < spill, prev_spill, extent + spill)
    return (key >= first) & (key <= extent + query)


def cross_allowed(query, place, side, spill, length, me, padded, real):
    part = place // padded
    inner = place - part * padded
    row = (part ^ me) * real + inner
    return (inner < real) & (row < length) & ((query < spill) == (side == 0))


def self_forward_kernel(rows, blocks, heads, sc, qkv, kvp, o_ref, lse_ref, k_scr, v_scr, s_scr, mx, tot):
    width = heads * HEAD
    extent = rows * blocks
    me, spill, prev_spill = sc[0], sc[1], sc[2]
    lanes = head_lanes(rows, width)

    def place(b):
        return pl.multiple_of((b ^ me) * rows, rows)

    first_used, _ = self_range(0, rows, blocks, spill, prev_spill)

    @pl.loop(first_used, 2 * blocks)
    def _(kb):
        def fill(keys, values):
            k_scr[kb] = keys
            for h in range(heads):
                v_scr[kb, h * rows : (h + 1) * rows, :] = one_head(values, lanes, h)

        @pl.when(kb < blocks)
        def _():
            at = pl.ds(place(kb), rows)
            fill(kvp[at, 0:width], kvp[at, width : 2 * width])

        @pl.when(kb >= blocks)
        def _():
            at = pl.ds(place(kb - blocks), rows)
            fill(qkv[at, width : 2 * width], qkv[at, 2 * width : 3 * width])

    @pl.loop(0, blocks)
    def _(p):
        q = qkv[pl.ds(place(p), rows), 0:width] * jnp.asarray(0.125, BF)
        mx[...] = jnp.full(mx.shape, LOWEST, F32)
        tot[...] = jnp.zeros(tot.shape, F32)
        first, last = self_range(p, rows, blocks, spill, prev_spill)
        query = p * rows + lax.broadcasted_iota(jnp.int32, (rows, 1), 0)

        @pl.loop(first, last)
        def _(kb):
            key = kb * rows + lax.broadcasted_iota(jnp.int32, (1, rows), 1)
            allowed = self_allowed(query, key, extent, spill, prev_spill)
            k = k_scr[kb]
            for h in range(heads):
                s = dot_nt(one_head(q, lanes, h), k)
                s = jnp.where(allowed, s, LOWEST)
                s_scr[kb, h] = s
                mx[h] = jnp.maximum(mx[h], s)

        for h in range(heads):
            mx[h, :, 0:1] = jnp.max(mx[h], axis=1, keepdims=True)

        def weigh(kb, acc):
            parts = []
            for h in range(heads):
                e = jnp.exp(s_scr[kb, h] - mx[h, :, 0:1])
                tot[h] += e
                parts.append(e.astype(BF))
            return acc + dot_nn(jnp.concatenate(parts, axis=1), v_scr[kb])

        acc = lax.fori_loop(first, last, weigh, jnp.zeros((rows, width), F32))
        finish(p, place(p), rows, heads, acc, mx, tot, lanes, o_ref, lse_ref)


def finish(p, start, rows, heads, acc, mx, tot, lanes, o_ref, lse_ref):
    over = jnp.zeros((rows, 128), F32)
    inverse = jnp.zeros(acc.shape, F32)
    slim = lax.broadcasted_iota(jnp.int32, (rows, 128), 1)
    for h in range(heads):
        total = jnp.sum(tot[h], axis=1, keepdims=True)
        inverse = jnp.where(lanes == h, 1.0 / total, inverse)
        over = jnp.where(slim == h, mx[h, :, 0:1] + jnp.log(total), over)
    o_ref[pl.ds(start, rows), :] = (acc * inverse).astype(BF)
    lse_ref[:, pl.ds(pl.multiple_of(p * rows, rows), rows)] = over.T[0:8, :]


def lay(out, own, near, far):
    rows = own.shape[0]
    out[0:rows, :] = own[...]
    out[rows : 2 * rows, :] = near[0:rows, :]
    out[2 * rows : 3 * rows, :] = far[0:rows, :]
    out[3 * rows :, :] = near[rows:, :]


def cross_forward_kernel(rows, blocks, heads, padded, real, sc, own, near, far, kv0, kv1, o_ref, lse_ref, q_ref,
                         v_scr, s_scr, mx, tot):
    lay(q_ref, own, near, far)
    width = heads * HEAD
    keys = kv0.shape[0]
    me, spill = sc[0], sc[1]
    lanes = head_lanes(rows, width)
    key_lanes = head_lanes(keys, width)
    kvs = (kv0, kv1)

    def place(b):
        return pl.multiple_of((b ^ me) * rows, rows)

    for side in range(2):
        values = kvs[side][:, width : 2 * width]
        for h in range(heads):
            v_scr[side, h * keys : (h + 1) * keys, :] = one_head(values, key_lanes, h)
    spot = lax.broadcasted_iota(jnp.int32, (1, keys), 1)

    @pl.loop(0, blocks)
    def _(p):
        q = q_ref[pl.ds(place(p), rows), :] * jnp.asarray(0.125, BF)
        mx[...] = jnp.full(mx.shape, LOWEST, F32)
        tot[...] = jnp.zeros(tot.shape, F32)
        query = p * rows + lax.broadcasted_iota(jnp.int32, (rows, 1), 0)
        reads = (p * rows < spill, (p + 1) * rows > spill)
        for side in range(2):

            @pl.when(reads[side])
            def _():
                allowed = cross_allowed(query, spot, side, spill, sc[2 + side], me, padded, real)
                k = kvs[side][:, 0:width]
                for h in range(heads):
                    s = dot_nt(one_head(q, lanes, h), k)
                    s = jnp.where(allowed, s, LOWEST)
                    s_scr[side, h] = s
                    mx[h] = jnp.maximum(mx[h], jnp.max(s, axis=1, keepdims=True))

        def weigh(side, acc):
            parts = []
            for h in range(heads):
                e = jnp.exp(s_scr[side, h] - mx[h, :, 0:1])
                tot[h] += e
                parts.append(e.astype(BF))
            return acc + dot_nn(jnp.concatenate(parts, axis=1), v_scr[side])

        first = jnp.where(reads[0], 0, 1)
        last = jnp.where(reads[1], 2, 1)
        acc = lax.fori_loop(first, last, weigh, jnp.zeros((rows, width), F32))
        finish(p, place(p), rows, heads, acc, mx, tot, lanes, o_ref, lse_ref)


def spread(p, at, rows, heads, q, g, o_ref, lse_ref, lanes, q_cat, g_cat, stat):
    weighted = (g.astype(F32) * o_ref[at, :].astype(F32)).T
    for h in range(heads):
        q_cat[h * rows : (h + 1) * rows, :] = one_head(q, lanes, h)
        g_cat[h * rows : (h + 1) * rows, :] = one_head(g, lanes, h)
        stat[heads + h : heads + h + 1, :] = jnp.sum(weighted[h * HEAD : (h + 1) * HEAD, :], axis=0, keepdims=True)
    stat[0:heads, :] = lse_ref[0:heads, pl.ds(pl.multiple_of(p * rows, rows), rows)]


def back_block(rows, heads, k, v, allowed, q_cat, g_cat, stat, w_scr, ds_wide, ds_tall):
    count = k.shape[0]
    for h in range(heads):
        span = slice(h * rows, (h + 1) * rows)
        s = dot_nt(k, q_cat[span, :])
        e = jnp.where(allowed, jnp.exp(s - stat[h : h + 1, :]), 0.0)
        de = dot_nt(v, g_cat[span, :])
        ds = (e * (de - stat[heads + h : heads + h + 1, :])).astype(BF)
        w_scr[:, span] = e.astype(BF)
        ds_wide[:, span] = ds
        ds_tall[h * count : (h + 1) * count, :] = ds


def self_backward_kernel(rows, blocks, heads, sc, qkv, kvp, o_ref, own, near, far, lse_ref, dq_ref, dkv_ref,
                         dprev_ref, g_ref, kv_scr, k_cat, dkv_scr, q_cat, g_cat, stat, w_scr, ds_wide, ds_tall):
    lay(g_ref, own, near, far)
    width = heads * HEAD
    extent = rows * blocks
    me, spill, prev_spill = sc[0], sc[1], sc[2]
    lanes = head_lanes(rows, width)

    def place(b):
        return pl.multiple_of((b ^ me) * rows, rows)

    first_used, _ = self_range(0, rows, blocks, spill, prev_spill)

    @pl.loop(0, 2 * blocks)
    def _(kb):
        dkv_scr[kb] = jnp.zeros(dkv_scr.shape[1:], F32)

    @pl.loop(first_used, 2 * blocks)
    def _(kb):
        def fill(pair):
            kv_scr[kb] = pair
            scaled = pair[:, 0:width] * jnp.asarray(0.125, BF)
            for h in range(heads):
                k_cat[kb, h * rows : (h + 1) * rows, :] = one_head(scaled, lanes, h)

        @pl.when(kb < blocks)
        def _():
            fill(kvp[pl.ds(place(kb), rows), :])

        @pl.when(kb >= blocks)
        def _():
            fill(qkv[pl.ds(place(kb - blocks), rows), width : 3 * width])

    @pl.loop(0, blocks)
    def _(p):
        at = pl.ds(place(p), rows)
        q = qkv[at, 0:width] * jnp.asarray(0.125, BF)
        g = g_ref[at, :]
        spread(p, at, rows, heads, q, g, o_ref, lse_ref, lanes, q_cat, g_cat, stat)
        first, last = self_range(p, rows, blocks, spill, prev_spill)
        query = p * rows + lax.broadcasted_iota(jnp.int32, (1, rows), 1)

        def step(kb, dq):
            key = kb * rows + lax.broadcasted_iota(jnp.int32, (rows, 1), 0)
            allowed = self_allowed(query, key, extent, spill, prev_spill)
            back_block(rows, heads, kv_scr[kb, :, 0:width], kv_scr[kb, :, width : 2 * width], allowed,
                       q_cat, g_cat, stat, w_scr, ds_wide, ds_tall)
            dkv_scr[kb, :, 0:width] += dot_nn(ds_wide[...], q_cat[...])
            dkv_scr[kb, :, width : 2 * width] += dot_nn(w_scr[...], g_cat[...])
            return dq + dot_tn(ds_tall[...], k_cat[kb])

        dq = lax.fori_loop(first, last, step, jnp.zeros((rows, width), F32))
        dq_ref[at, :] = dq.astype(BF)

    @pl.loop(0, blocks)
    def _(b):
        at = pl.ds(place(b), rows)
        dprev_ref[at, :] = dkv_scr[b].astype(BF)
        dkv_ref[at, :] = dkv_scr[blocks + b].astype(BF)


def cross_backward_kernel(rows, blocks, heads, padded, real, pieces, sc, q_ref, kv0, kv1, o_ref, own, near, far,
                          lse_ref, dq_ref, dkv0_ref, dkv1_ref, g_ref, k_cat, dkv_scr, q_cat, g_cat, stat, w_scr, ds_wide, ds_tall):
    lay(g_ref, own, near, far)
    width = heads * HEAD
    keys = kv0.shape[0]
    step_keys = keys // pieces
    me, spill = sc[0], sc[1]
    lanes = head_lanes(rows, width)
    key_lanes = head_lanes(step_keys, width)
    kvs = (kv0, kv1)

    def place(b):
        return pl.multiple_of((b ^ me) * rows, rows)

    dkv_scr[...] = jnp.zeros(dkv_scr.shape, F32)
    for side in range(2):
        for piece in range(pieces):
            scaled = kvs[side][piece * step_keys : (piece + 1) * step_keys, 0:width] * jnp.asarray(0.125, BF)
            for h in range(heads):
                k_cat[side * pieces + piece, h * step_keys : (h + 1) * step_keys, :] = one_head(scaled, key_lanes, h)

    @pl.loop(0, blocks)
    def _(p):
        at = pl.ds(place(p), rows)
        q = q_ref[at, :] * jnp.asarray(0.125, BF)
        spread(p, at, rows, heads, q, g_ref[at, :], o_ref, lse_ref, lanes, q_cat, g_cat, stat)
        query = p * rows + lax.broadcasted_iota(jnp.int32, (1, rows), 1)
        reads = (p * rows < spill, (p + 1) * rows > spill)
        first = jnp.where(reads[0], 0, pieces)
        last = jnp.where(reads[1], 2 * pieces, pieces)

        def step(kb, dq):
            side = kb // pieces
            at_key = pl.ds(pl.multiple_of((kb - side * pieces) * step_keys, step_keys), step_keys)
            spot = (kb - side * pieces) * step_keys + lax.broadcasted_iota(jnp.int32, (step_keys, 1), 0)
            length = jnp.where(side == 0, sc[2], sc[3])
            allowed = cross_allowed(query, spot, side, spill, length, me, padded, real)
            is_prev = side == 0
            pair = jnp.where(is_prev, kv0[at_key, :], kv1[at_key, :])
            back_block(rows, heads, pair[:, 0:width], pair[:, width : 2 * width], allowed,
                       q_cat, g_cat, stat, w_scr, ds_wide, ds_tall)
            dkv_scr[kb, :, 0:width] += dot_nn(ds_wide[...], q_cat[...])
            dkv_scr[kb, :, width : 2 * width] += dot_nn(w_scr[...], g_cat[...])
            return dq + dot_tn(ds_tall[...], k_cat[kb])

        dq = lax.fori_loop(first, last, step, jnp.zeros((rows, width), F32))
        dq_ref[at, :] = dq.astype(BF)

    for piece in range(pieces):
        span = slice(piece * step_keys, (piece + 1) * step_keys)
        dkv0_ref[span, :] = dkv_scr[piece].astype(BF)
        dkv1_ref[span, :] = dkv_scr[pieces + piece].astype(BF)


def call(kernel, scalars, arrays, outs, scratch=()):
    vmem = pl.BlockSpec(memory_space=pltpu.VMEM)
    return pl.pallas_call(
        kernel,
        out_shape=outs,
        in_specs=[pl.BlockSpec(memory_space=pltpu.SMEM)] + [vmem] * len(arrays),
        out_specs=jax.tree.map(lambda _: vmem, outs),
        scratch_shapes=scratch,
        compiler_params=pltpu.CompilerParams(vmem_limit_bytes=48 * 2**20),
        cost_estimate=pl.CostEstimate(flops=1024, bytes_accessed=1024, transcendentals=0),
    )(scalars, *arrays)


def self_forward(scalars, qkv, kvp, blocks):
    extent = qkv.shape[0]
    rows = extent // blocks
    width = qkv.shape[1] // 3
    heads = width // HEAD
    return call(
        functools.partial(self_forward_kernel, rows, blocks, heads),
        scalars,
        (qkv, kvp),
        [jax.ShapeDtypeStruct((extent, width), BF), jax.ShapeDtypeStruct((8, extent), F32)],
        [
            pltpu.VMEM((2 * blocks, rows, width), BF),
            pltpu.VMEM((2 * blocks, heads * rows, width), BF),
            pltpu.VMEM((2 * blocks, heads, rows, rows), F32),
            pltpu.VMEM((heads, rows, rows), F32),
            pltpu.VMEM((heads, rows, rows), F32),
        ],
    )


def cross_forward(scalars, pieces, kv0, kv1, blocks, real):
    rows, width = pieces[0].shape
    extent = rows * blocks
    heads = width // HEAD
    keys = kv0.shape[0]
    return call(
        functools.partial(cross_forward_kernel, rows, blocks, heads, keys // blocks, real),
        scalars,
        (*pieces, kv0, kv1),
        [
            jax.ShapeDtypeStruct((extent, width), BF),
            jax.ShapeDtypeStruct((8, extent), F32),
            jax.ShapeDtypeStruct((extent, width), BF),
        ],
        [
            pltpu.VMEM((2, heads * keys, width), BF),
            pltpu.VMEM((2, heads, rows, keys), F32),
            pltpu.VMEM((heads, rows, keys), F32),
            pltpu.VMEM((heads, rows, keys), F32),
        ],
    )


def back_scratch(rows, heads, width, keys):
    return [
        pltpu.VMEM((heads * rows, width), BF),
        pltpu.VMEM((heads * rows, width), BF),
        pltpu.VMEM((8, rows), F32),
        pltpu.VMEM((keys, heads * rows), BF),
        pltpu.VMEM((keys, heads * rows), BF),
        pltpu.VMEM((heads * keys, rows), BF),
    ]


def self_backward(scalars, qkv, kvp, o, g, lse, blocks):
    extent = qkv.shape[0]
    rows = extent // blocks
    width = qkv.shape[1] // 3
    heads = width // HEAD
    return call(
        functools.partial(self_backward_kernel, rows, blocks, heads),
        scalars,
        (qkv, kvp, o, *g, lse),
        [
            jax.ShapeDtypeStruct((extent, width), BF),
            jax.ShapeDtypeStruct((extent, 2 * width), BF),
            jax.ShapeDtypeStruct((extent, 2 * width), BF),
        ],
        [
            pltpu.VMEM((extent, width), BF),
            pltpu.VMEM((2 * blocks, rows, 2 * width), BF),
            pltpu.VMEM((2 * blocks, heads * rows, width), BF),
            pltpu.VMEM((2 * blocks, rows, 2 * width), F32),
        ]
        + back_scratch(rows, heads, width, rows),
    )


def cross_backward(scalars, q, kv0, kv1, o, g, lse, blocks, real, pieces=2):
    extent, width = q.shape
    rows = extent // blocks
    heads = width // HEAD
    keys = kv0.shape[0]
    step_keys = keys // pieces
    return call(
        functools.partial(cross_backward_kernel, rows, blocks, heads, keys // blocks, real, pieces),
        scalars,
        (q, kv0, kv1, o, *g, lse),
        [
            jax.ShapeDtypeStruct((extent, width), BF),
            jax.ShapeDtypeStruct((keys, 2 * width), BF),
            jax.ShapeDtypeStruct((keys, 2 * width), BF),
        ],
        [
            pltpu.VMEM((extent, width), BF),
            pltpu.VMEM((2 * pieces, heads * step_keys, width), BF),
            pltpu.VMEM((2 * pieces, step_keys, 2 * width), F32),
        ]
        + back_scratch(rows, heads, width, step_keys),
    )


def ordered_pieces(pieces, me):
    odd = (me & 1) == 1
    high = (me & 2) == 2
    low_pair = [jnp.where(odd, pieces[1 - i], pieces[i]) for i in range(2)]
    high_pair = [jnp.where(odd, pieces[3 - i], pieces[2 + i]) for i in range(2)]
    ordered = [jnp.where(high, high_pair[i], low_pair[i]) for i in range(2)]
    return ordered + [jnp.where(high, low_pair[i], high_pair[i]) for i in range(2)]


def join_pieces(pieces, me, axis):
    return jnp.concatenate(ordered_pieces(pieces, me), axis=axis)


def received(own, near, far, me):
    rows = own.shape[0]
    return join_pieces([own[...], near[0:rows, :], far[0:rows, :], near[rows:, :]], me, 1)


def send_pieces(tensor, me, first, second, rest):
    width = tensor.shape[1] // 4
    rows = tensor.shape[0]
    pieces = ordered_pieces([tensor[:, k * width : (k + 1) * width] for k in range(4)], me)
    first[...] = pieces[0]
    second[...] = pieces[1]
    rest[0:rows, :] = pieces[2]
    rest[rows:, :] = pieces[3]


def half_product(tensor, own, other, me, first):
    span = slice(first, first + own.shape[0] // 2)
    left, right = dot_nn(tensor, own[:, span]), dot_nn(tensor, other[:, span])
    odd = (me & 1) == 1
    return jnp.concatenate([jnp.where(odd, right, left), jnp.where(odd, left, right)], axis=1)


def two_halves(tensor, me):
    half = tensor.shape[1] // 2
    odd = (me & 1) == 1
    left, right = tensor[:, 0:half], tensor[:, half:]
    return jnp.where(odd, right, left), jnp.where(odd, left, right)


def half_back(mine, others, own, other, first):
    span = slice(first, first + own.shape[0] // 2)
    return dot_nt(mine, own[:, span]) + dot_nt(others, other[:, span])


def normal_parts(tensor):
    average = jnp.mean(tensor, axis=-1, keepdims=True)
    centered = tensor - average
    scale = lax.rsqrt(jnp.mean(centered * centered, axis=-1, keepdims=True) + 1e-05)
    return centered * scale, scale


def normal_back(plain, scale, grad):
    inner = jnp.mean(grad * plain, axis=-1, keepdims=True)
    return scale * (grad - jnp.mean(grad, axis=-1, keepdims=True) - plain * inner)


def gelu_parts(pre):
    size = jnp.abs(pre)
    t = 1.0 / (1.0 + (0.3275911 * 0.7071067811865476) * size)
    poly = ((((1.061405429 * t - 1.453152027) * t + 1.421413741) * t - 0.284496736) * t + 0.254829592) * t
    bell = jnp.exp(-0.5 * pre * pre)
    tail = 0.5 * poly * bell
    cdf = jnp.where(pre < 0.0, tail, 1.0 - tail)
    return pre * cdf, cdf + pre * bell * 0.3989422804014327


def qkv_kernel(at, low, far_low, near_low, ahead, far_ahead, near_ahead, weight, qkv, kvp, low_one, low_before):
    rows = low.shape[0]
    width = weight.shape[1] // 3
    for out, own, far, near in ((low_one, low, far_low, near_low), (low_before, ahead, far_ahead, near_ahead)):
        out[0:rows, :] = own[...]
        out[rows : 2 * rows, :] = near[0:rows, :]
        out[2 * rows : 3 * rows, :] = far[...]
        out[3 * rows :, :] = near[rows:, :]

    @pl.loop(0, 4)
    def _(b):
        block = pl.ds(pl.multiple_of(b * rows, rows), rows)
        qkv[block, :] = dot_nn(low_one[block, :], weight[...]).astype(BF)
        kvp[block, :] = dot_nn(low_before[block, :], weight[:, width:]).astype(BF)


def self_out_kernel(at, own, near, far, x, wide_own, wide_other,
                    low, after, plain, low_next, scale, first, second, rest):
    me = at[0]
    joined = received(own, near, far, me)
    low[...] = joined
    total = x[...].astype(F32) + half_product(joined, wide_own, wide_other, me, 0)
    after[...] = total
    normed, scaled = normal_parts(total)
    plain[...] = normed
    scale[...] = scaled
    rounded = normed.astype(BF)
    low_next[...] = rounded
    send_pieces(half_product(rounded, wide_own, wide_other, me, wide_own.shape[0] // 2).astype(BF), me, first, second, rest)


def cross_out_kernel(at, own, near, far, before, out_own, out_other, gain, low, after, plain, scale, low_next):
    me = at[0]
    joined = received(own, near, far, me)
    low[...] = joined
    total = before[...] + half_product(joined, out_own, out_other, me, 0)
    after[...] = total
    normed, scaled = normal_parts(total)
    plain[...] = normed
    scale[...] = scaled
    low_next[...] = (normed * gain[...]).astype(BF)


def mlp_kernel(at, low, near_low, far_low, top, near_top, far_top, inner, outer,
               low_all, top_all, act, pre_low, grad_keep, grad_send, out_keep, out_send):
    rows = low.shape[0]
    for out, own, near, far in ((low_all, low, near_low, far_low), (top_all, top, near_top, far_top)):
        out[0:rows, :] = own[...]
        out[rows : 2 * rows, :] = near[0:rows, :]
        out[2 * rows : 3 * rows, :] = far[...]
        out[3 * rows :, :] = near[rows:, :]
    for parity, grad, out in ((1, grad_send, out_send), (0, grad_keep, out_keep)):

        @pl.loop(0, 2)
        def _(b):
            block = pl.ds(pl.multiple_of((2 * b + parity) * rows, rows), rows)
            place = pl.ds(pl.multiple_of(b * rows, rows), rows)
            value, slope = gelu_parts(dot_nt(low_all[block, :], inner[...]))
            act_block = value.astype(BF)
            act[block, :] = act_block
            pre_block = (dot_nt(top_all[block, :], outer[...]) * slope).astype(BF)
            pre_low[block, :] = pre_block
            grad[place, :] = dot_nn(pre_block, inner[...]).astype(BF)
            out[place, :] = dot_nn(act_block, outer[...]).astype(BF)


def cross_back_kernel(at, near, far, plain, scale, gain, top, out_own, out_other,
                      grad_after, branch_own, branch_other, grad_gain, first, second, rest):
    me = at[0]
    grad = near[...] + far[...].astype(F32)
    normed = plain[...]
    grad_gain[...] = jnp.sum(grad * normed, axis=0, keepdims=True)
    total = top[...].astype(F32) + normal_back(normed, scale[...], grad * gain[...])
    grad_after[...] = total
    mine, others = two_halves(total.astype(BF), me)
    branch_own[...] = mine
    branch_other[...] = others
    send_pieces(half_back(mine, others, out_own, out_other, 0).astype(BF), me, first, second, rest)


def self_back_kernel(at, own, near, far, plain, scale, before, wide_own, wide_other,
                     grad_after, query_mine, query_others, branch_own, branch_other, first, second, rest):
    me = at[0]
    mine, others = two_halves(received(own, near, far, me), me)
    query_mine[...] = mine
    query_others[...] = others
    total = before[...] + normal_back(plain[...], scale[...], half_back(mine, others, wide_own, wide_other, wide_own.shape[0] // 2))
    grad_after[...] = total
    mine, others = two_halves(total.astype(BF), me)
    branch_own[...] = mine
    branch_other[...] = others
    send_pieces(half_back(mine, others, wide_own, wide_other, 0).astype(BF), me, first, second, rest)


def half_grads_kernel(names, at, *refs):
    own, other = refs[-2:]
    half = own.shape[1] // names
    for n in range(names):
        low_a, low_b, mine_a, mine_b, others_a, others_b = (ref[...] for ref in refs[6 * n : 6 * n + 6])
        span = slice(n * half, (n + 1) * half)
        other[:, span] = (dot_tn(low_a, others_a) + dot_tn(low_b, others_b)).astype(BF)
        own[:, span] = dot_tn(low_a, mine_a) + dot_tn(low_b, mine_b)


def qkv_back_kernel(at, dq, dkv, back, weight, keep, send):
    rows = dq.shape[0] // 4
    width = dq.shape[1]
    for parity, out in ((1, send), (0, keep)):

        @pl.loop(0, 2)
        def _(b):
            block = pl.ds(pl.multiple_of((2 * b + parity) * rows, rows), rows)
            place = pl.ds(pl.multiple_of(b * rows, rows), rows)
            kv = (dkv[block, :].astype(F32) + back[block, :].astype(F32)).astype(BF)
            grad = dot_nt(dq[block, :], weight[:, 0:width]) + dot_nt(kv, weight[:, width:])
            out[place, :] = grad.astype(BF)


def qkv_grads_kernel(at, low, before, dq, dkv, dkv_prev, out):
    width = dq.shape[1]
    out[:, 0:width] = dot_tn(low[...], dq[...])
    out[:, width:] = dot_tn(low[...], dkv[...]) + dot_tn(before[...], dkv_prev[...])


def shape(rows, columns, dtype=BF):
    return jax.ShapeDtypeStruct((rows, columns), dtype)


D = 1024
MICRO = 2


def flip(block, axis, bit):
    return lax.ppermute(block, axis, [(i, i ^ bit) for i in range(lax.axis_size(axis))])


def shifted(block, distance):
    devices = range(lax.axis_size("seq"))
    route = [(i - distance, i) for i in devices if i - distance in devices]
    return lax.ppermute(block, "seq", route)


def near_rows(own, far):
    return flip(jnp.concatenate([own, far], axis=0), "mem", 1)


def far_slots(part):
    rows = part.shape[0] // 4
    return part[:rows], part[rows : 2 * rows], flip(part[2 * rows :], "mem", 2)


def near_slots(own, side, far):
    rows = own.shape[0]
    return own, flip(jnp.concatenate([side, far[rows:]], axis=0), "mem", 1), far


def lay_slots(own, near, far):
    rows = own.shape[0]
    return jnp.concatenate([own, near[:rows], far[:rows], near[rows:]], axis=0)


def near_sum(keep, send):
    rows = keep.shape[0] // 2
    total = keep.astype(F32) + flip(send, "mem", 1).astype(F32)
    return total[:rows], total[rows:].astype(BF)


def seq_bits():
    count = lax.axis_size("seq")
    return [1 << i for i in reversed(range(count.bit_length() - 1))]


def seq_offsets(bits):
    offsets = [0]
    for bit in bits:
        offsets = offsets + [o ^ bit for o in offsets]
    return offsets


def seq_stage(block, bit):
    return jnp.concatenate([block, flip(block, "seq", bit)], axis=0)


def assemble_kernel(rows, offsets, at, first, second, *outs):
    half = len(offsets) // 2
    for i, offset in enumerate(offsets):
        ref = first if i < half else second
        start = pl.multiple_of((at[0] ^ offset) * rows, rows)
        column = 0
        for out in outs:
            columns = out.shape[1]
            place = slice((i % half) * rows, (i % half + 1) * rows)
            out[pl.ds(start, rows), :] = ref[place, column : column + columns]
            column += columns


def assemble(first, second, seq, bits, split):
    offsets = seq_offsets(bits)
    size = 2 * first.shape[0]
    outs = [shape(size, columns) for columns in split]
    return call(functools.partial(assemble_kernel, size // len(offsets), offsets), seq.reshape(1), (first, second), outs)


def reorder_kernel(rows, offsets, groups, at, *refs):
    out = refs[-1]
    for i, offset in enumerate(offsets):
        start = pl.multiple_of((at[0] ^ offset) * rows, rows)
        for column, terms in groups:
            total = None
            for term, first, columns in terms:
                part = refs[term][pl.ds(start, rows), first : first + columns].astype(F32)
                total = part if total is None else total + part
            out[i * rows : (i + 1) * rows, column : column + columns] = total.astype(BF)


def reorder(arrays, groups, seq, bits):
    offsets = seq_offsets(bits)
    size = arrays[0].shape[0]
    placed, column = [], 0
    for terms in groups:
        placed.append((column, terms))
        column += terms[0][2]
    out = jax.ShapeDtypeStruct((size, column), BF)
    kernel = functools.partial(reorder_kernel, size // len(offsets), offsets, placed)
    return call(kernel, seq.reshape(1), arrays, out)


def pack_kernel(width, half, at, *refs):
    me = at[0]
    (gain_self, gain_cross, gain_mlp), weights, (kept, message) = refs[:3], refs[3:11], refs[11:]
    query, key, value, out_w, cross_q, cross_k, cross_v, cross_o = weights

    def scaled(weight, gain):
        return (weight.astype(F32) * gain[...].astype(F32)).astype(BF)

    def piece(k):
        at_k = pl.ds(pl.multiple_of((me ^ k) * width, width), width)
        gained = [scaled(w[:, at_k], gain_self) for w in (query, key, value)]
        return jnp.concatenate(gained + [w[:, at_k] for w in (cross_k, cross_v)], axis=1)

    def side(k):
        at_k = pl.ds(pl.multiple_of(((me & 1) ^ k) * half, half), half)
        rows = gain_mlp.shape[0]
        lanes = lax.broadcasted_iota(jnp.int32, (rows, 128), 1)
        extra = jnp.where(lanes == 0, gain_mlp[...].astype(F32), 0.0).astype(BF)
        return jnp.concatenate([out_w[:, at_k], scaled(cross_q[:, at_k], gain_cross), cross_o[:, at_k], extra], axis=1)

    kept[...] = jnp.concatenate([piece(0), piece(1)], axis=1)
    message[...] = jnp.concatenate([piece(2), piece(3), side(0), side(1)], axis=1)


def repack_kernel(narrow, broad, at, kept, message, far, out):
    sides = 2 * narrow + broad
    out[:, 0:narrow] = kept[:, narrow:]
    out[:, narrow : 2 * narrow] = far[:, narrow : 2 * narrow]
    out[:, 2 * narrow : 2 * narrow + broad] = message[:, sides:]
    out[:, 2 * narrow + broad :] = far[:, sides:]


def unpack_kernel(width, narrow, broad, at, kept, message, far, near, qkv, first, last):
    me = at[0]
    start = 2 * narrow
    heads = [kept[:, 0:narrow], near[:, 0:narrow], far[:, 0:narrow], near[:, narrow:start]]
    sides = [message, near, far, near]
    sides = [ref[:, at_k : at_k + broad] for ref, at_k in zip(sides, (start, start, start, start + broad))]
    heads = join_pieces(heads, me, 0)
    sides = join_pieces(sides, me, 0)
    pair = broad - 128 - (broad - 128) // 3
    qkv[...] = heads[:, 0 : 3 * width]
    first[...] = jnp.concatenate([sides[:, 0:pair], heads[:, 3 * width :]], axis=1)
    last[...] = sides[:, pair:]


class Stay:
    def __init__(self, value):
        self.value = value


def interleave(streams, sides):
    held = [next(s) for s in streams]
    results = [None] * len(streams)
    waiting = [(side, *next(side)) for side in sides]
    turn = 0
    ticks = 0

    def serve(arrays):
        nonlocal ticks, waiting
        ticks += 1
        due = [w for w in waiting if w[1] == ticks]
        waiting = [w for w in waiting if w[1] != ticks]
        arrays, taken = lax.optimization_barrier((arrays, [w[2]() for w in due]))
        for (side, _, _), got in zip(due, taken):
            try:
                waiting.append((side, *side.send(got)))
            except StopIteration:
                pass
        return arrays

    while True:
        other = (turn + 1) % len(streams)
        try:
            mark = streams[turn].send(held[turn])
            while isinstance(mark, Stay):
                mark = streams[turn].send(serve(mark.value))
            if results[other] is None:
                held[other], mark = serve((held[other], mark))
            else:
                mark = serve(mark)
            held[turn] = streams[turn].send(mark)
        except StopIteration as end:
            results[turn] = end.value
        if results[other] is None:
            turn = other
        elif results[turn] is not None:
            assert not waiting
            return results


def shards(
    inputs,
    memory,
    page_ids,
    memory_length,
    cotangent,
    gain_self,
    self_query,
    self_key,
    self_value,
    self_out,
    gain_cross,
    cross_query,
    cross_key,
    cross_value,
    cross_out,
    gain_mlp,
    mlp_in,
    mlp_out,
):
    seq = lax.axis_index("seq")
    me = lax.axis_index("mem")
    odd = me & 1
    blocks = lax.axis_size("mem")
    tok = inputs.shape[1]
    group = tok * blocks
    real = memory.shape[2]
    padded = -(-real // 16) * 16
    wrows = self_query.shape[0]
    bits = seq_bits()
    turned = bits[:-2] + [bits[-1], bits[-2]]
    half = D // 2

    def join_halves(own, other):
        return jnp.concatenate([jnp.where(odd == 0, own, other), jnp.where(odd == 0, other, own)], axis=1)

    width = self_query.shape[1] // blocks
    narrow, broad = 5 * width, 3 * half + 128
    place = me.reshape(1)
    weights = (self_query, self_key, self_value, self_out, cross_query, cross_key, cross_value, cross_out)
    gains = [g[:, None] for g in (gain_self, gain_cross, gain_mlp)]
    kept, message = call(
        functools.partial(pack_kernel, width, half), place, (*gains, *weights),
        [shape(wrows, 2 * narrow), shape(wrows, 2 * (narrow + broad))],
    )
    far = flip(message, "mem", 2)
    norm_ones = [normal_parts(inputs[i].astype(F32)) for i in range(MICRO)]
    lows = [parts[0].astype(BF) for parts in norm_ones]
    befores = [shifted(low, 1) for low in lows]
    far_lows = [flip(lows[0], "mem", 2)]
    near = call(
        functools.partial(repack_kernel, narrow, broad), place, (kept, message, far),
        shape(*message.shape),
    )
    near = flip(near, "mem", 1)
    qkv_part, first_part, last_part = call(
        functools.partial(unpack_kernel, width, narrow, broad), place, (kept, message, far, near),
        [shape(blocks * wrows, columns) for columns in (3 * width, 2 * half + 2 * width, half + 128)],
    )

    state = {}
    hidden = mlp_in.shape[0]
    memory_own = jnp.pad(memory.reshape(MICRO, real, D), ((0, 0), (0, padded - real), (0, 0)))
    memory_own = memory_own.reshape(MICRO * padded, D)
    stage = seq_stage(qkv_part, bits[0])
    stage, first_part, befores[0] = lax.optimization_barrier((stage, first_part, befores[0]))
    far_befores = [flip(befores[0], "mem", 2)]
    for bit in bits[1:-1]:
        stage = seq_stage(stage, bit)
    stage, first_part, lows[1], befores[1] = lax.optimization_barrier((stage, first_part, lows[1], befores[1]))
    far_lows.append(flip(lows[1], "mem", 2))
    far_befores.append(flip(befores[1], "mem", 2))
    first_stage = first_part
    for bit in bits[:-2]:
        first_stage = seq_stage(first_stage, bit)
    (qkv_full,) = assemble(stage, flip(stage, "seq", bits[-1]), seq, bits, [3 * width])

    def first_side():
        (first,) = yield 1, lambda: (first_stage,)
        first = seq_stage(first, bits[-2])
        (first,) = yield 2, lambda: (first,)
        first = first, flip(first, "seq", bits[-1])
        first = yield 3, lambda: first
        state["wide_own"], state["ckv"] = assemble(*first, seq, bits, [2 * half, 2 * width])
        state["wide_other"] = flip(state["wide_own"], "mem", 1)

    def last_side():
        (last,) = yield 2, lambda: (last_part,)
        for bit in bits[:-2]:
            last = seq_stage(last, bit)
        (last,) = yield 3, lambda: (last,)
        last = seq_stage(last, bits[-2])
        (last,) = yield 5, lambda: (last,)
        last = last, flip(last, "seq", bits[-1])
        last = yield 7, lambda: last
        state["cout_own"], gain = assemble(*last, seq, bits, [half, 128])
        state["cout_other"] = flip(state["cout_own"], "mem", 1)
        state["gain"] = gain[:, 0].astype(F32)[None, :]

    def memory_side():
        (rows,) = yield 1, lambda: (memory_own,)
        rows = rows, shifted(rows, 1)
        rows = yield 2, lambda: rows
        rows = jnp.concatenate(rows, axis=0)
        far = flip(rows, "mem", 2)
        rows, far = yield 4, lambda: (rows, far)
        pieces = rows, near_rows(rows, far), far
        pieces = yield 5, lambda: pieces
        size = MICRO * padded
        near = pieces[1][: 2 * size], pieces[1][2 * size :]
        slots = pieces[0], near[0], pieces[2], near[1]
        rows = [
            jnp.concatenate([p[i * padded : (i + 1) * padded] for p in slots], axis=0) for i in range(2 * MICRO)
        ]
        state["rows"] = rows[:MICRO]
        keys = [dot_nn(r, state["ckv"]).astype(BF) for r in rows]
        state["mem_kv"], state["mem_prev"] = keys[:MICRO], keys[MICRO:]

    def hidden_side():
        (part,) = yield 1, lambda: (jnp.concatenate([mlp_in, mlp_out], axis=0),)
        whole = lax.all_gather(part, "seq", axis=0, tiled=True)
        (whole,) = yield 9, lambda: (whole,)
        whole = whole.reshape(-1, 2, hidden, D)
        state["inner"] = whole[:, 0].reshape(-1, D)
        state["outer"] = whole[:, 1].reshape(-1, D)
        grads = yield 13, lambda: (state["grad_inner"], state["grad_outer"])
        both = [sum(g).astype(BF).reshape(-1, 1, hidden, D) for g in grads]
        both = jnp.concatenate(both, axis=1).reshape(-1, D)
        both = lax.psum_scatter(both, "seq", scatter_dimension=0, tiled=True)
        state["hidden_grads"] = both[:hidden].astype(F32), both[hidden:].astype(F32)

    order = turned[::-1]

    def seq_start(tensor, bit):
        cut = tensor.shape[0] // 2
        return tensor[:cut].astype(F32), flip(tensor[cut:].astype(BF), "seq", bit)

    def seq_next(kept, received, bit):
        return seq_start(kept + received.astype(F32), bit)

    def tree_side(name, arrays, groups, ticks):
        for bit, tick in zip(order, ticks):
            if bit == order[0]:
                arrays = yield tick, lambda: arrays
                pair = seq_start(reorder(arrays, groups, seq, turned), bit)
            else:
                pair = yield tick, lambda: pair
                pair = seq_next(*pair, bit)
        for bit in order[len(ticks) :]:
            pair = seq_next(*pair, bit)
        state[name] = pair

    def half_grads(names):
        arrays = [part for low, mine, others in names for part in (*low, *mine, *others)]
        outs = [shape(D, len(names) * half, F32), shape(D, len(names) * half)]
        return call(functools.partial(half_grads_kernel, len(names)), place, arrays, outs)

    def cout_side():
        names, gains = yield 15, lambda: (state["grad_cout"], state["grad_gain_three"])
        own, other = half_grads([list(zip(*names))])
        gains = jnp.pad((gains[0] + gains[1]).reshape(D, 1), ((0, 0), (0, 127)))
        groups = [[(0, 0, half), (1, 0, half)], [(2, 0, 128)]]
        yield from tree_side("cout", (own, flip(other, "mem", 1), gains), groups, (16, 18, 20))

    def wide_side():
        out, query, ckv = yield 17, lambda: (state["grad_out"], state["grad_cquery"], state["grad_ckv"])
        own, other = half_grads([list(zip(*out)), list(zip(*query))])
        groups = [[(0, 0, 2 * half), (1, 0, 2 * half)], [(2, 0, 2 * width), (3, 0, 2 * width)]]
        yield from tree_side("wide", (own, flip(other, "mem", 1), *ckv), groups, (18, 20, 21))

    def qkv_side():
        arrays = yield 19, lambda: state["grad_qkv"]
        groups = [[(0, 0, 3 * width), (1, 0, 3 * width)]]
        pair = seq_start(reorder(arrays, groups, seq, turned), order[0])
        pair = yield 21, lambda: pair
        state["qkv"] = seq_next(*pair, order[1])

    def spill_of(micro, block):
        ids = lax.dynamic_slice_in_dim(page_ids[micro], jnp.maximum(block, 0) * group, group, 0)
        return jnp.sum((ids < block).astype(jnp.int32))

    for name in ("inner", "outer", "gain_three", "cout", "out", "cquery", "ckv", "qkv"):
        state["grad_" + name] = []
    quarter = [shape(tok, width), shape(tok, width), shape(2 * tok, width)]
    rounded, exact, column = shape(tok, D), shape(tok, D, F32), shape(tok, 1, F32)
    half_rows = shape(tok, half)

    def stream(i):
        spill = spill_of(i, seq)
        self_at = jnp.stack([me, spill, spill_of(i, seq - 1)])
        before = memory_length[i][jnp.maximum(seq - 1, 0)]
        cross_at = jnp.stack([me, spill, before, memory_length[i][seq]])

        low, far_low, ahead, far_ahead = yield lows[i], far_lows[i], befores[i], far_befores[i]
        qkv, kv_prev, low_one, low_before = call(
            qkv_kernel, place, (low, far_low, near_rows(low, far_low), ahead, far_ahead, near_rows(ahead, far_ahead), qkv_full),
            [shape(group, 3 * width), shape(group, 2 * width), shape(group, D), shape(group, D)],
        )
        if i == 0:
            qkv, kv_prev = yield Stay((qkv, kv_prev))
        self_o, self_lse = self_forward(self_at, qkv, kv_prev, blocks)
        self_lse = yield self_lse

        pieces = yield far_slots(self_o)
        self_low, after_self, plain_two, low_two, scale_two, *pieces = call(
            self_out_kernel, place, (*near_slots(*pieces), inputs[i], state["wide_own"], state["wide_other"]),
            [rounded, exact, exact, rounded, column, *quarter],
        )
        scale_two = yield scale_two

        pieces, top = yield (pieces[0], pieces[1], flip(pieces[2], "mem", 2)), cotangent[i]
        far_top = flip(top, "mem", 2)
        mem_kv, mem_prev = state["mem_kv"][i], state["mem_prev"][i]
        cross_o, cross_lse, cross_q = cross_forward(cross_at, near_slots(*pieces), mem_prev, mem_kv, blocks, real)
        cross_lse = yield cross_lse

        pieces, far_top = yield far_slots(cross_o), far_top
        cross_low, after_cross, plain_three, scale_three, low_three = call(
            cross_out_kernel, place,
            (*near_slots(*pieces), after_self, state["cout_own"], state["cout_other"], state["gain"]),
            [rounded, exact, exact, column, rounded],
        )
        near_top = near_rows(top, far_top)
        scale_three = yield scale_three

        low_three, far_three = yield low_three, flip(low_three, "mem", 2)
        whole, pair = shape(group, D), shape(2 * tok, D)
        low_all, top_all, act, pre_low, grad_keep, grad_send, out_keep, out_send = call(
            mlp_kernel, place,
            (low_three, near_rows(low_three, far_three), far_three, top, near_top, far_top, state["inner"], state["outer"]),
            [whole, whole, whole, whole, pair, pair, pair, pair],
        )
        near, far = near_sum(grad_keep, grad_send)
        near = yield near

        far, act, out_send = yield flip(far, "mem", 2), act, out_send
        grad_after_cross, mine, others, gain_three, *pieces = call(
            cross_back_kernel, place,
            (near, far, plain_three, scale_three, state["gain"], cotangent[i], state["cout_own"], state["cout_other"]),
            [exact, half_rows, half_rows, shape(1, D, F32), *quarter],
        )
        state["grad_inner"].append(dot_tn(pre_low, low_all))
        state["grad_outer"].append(dot_tn(act, top_all))
        state["grad_gain_three"].append(gain_three)
        state["grad_cout"].append((cross_low, mine, others))
        out_near, out_far = near_sum(out_keep, out_send)
        grad_after_cross = yield grad_after_cross

        pieces, out_far = yield (pieces[0], pieces[1], flip(pieces[2], "mem", 2)), out_far
        dcq, dmem_prev, dmem = cross_backward(
            cross_at, cross_q, mem_prev, mem_kv, cross_o, near_slots(*pieces), cross_lse, blocks, real
        )
        dmem = yield dmem

        back = shifted(dmem_prev, -1)
        pieces, out_far = yield far_slots(dcq), out_far
        output = (after_cross + out_near + flip(out_far, "mem", 2).astype(F32)).astype(BF)
        grad_after_self, query_mine, query_others, mine, others, *pieces = call(
            self_back_kernel, place,
            (*near_slots(*pieces), plain_two, scale_two, grad_after_cross, state["wide_own"], state["wide_other"]),
            [exact, half_rows, half_rows, half_rows, half_rows, *quarter],
        )
        state["grad_cquery"].append((low_two, query_mine, query_others))
        state["grad_out"].append((self_low, mine, others))
        dmem = (dmem.astype(F32) + back.astype(F32)).astype(BF)
        state["grad_ckv"].append(dot_tn(state["rows"][i], dmem))
        grad_after_self = yield grad_after_self

        pieces, dmem = yield (pieces[0], pieces[1], flip(pieces[2], "mem", 2)), dmem
        dq, dkv, dkv_prev = self_backward(self_at, qkv, kv_prev, self_o, near_slots(*pieces), self_lse, blocks)
        state["grad_qkv"].append(
            call(qkv_grads_kernel, place, (low_one, low_before, dq, dkv, dkv_prev), shape(D, 3 * width, F32))
        )
        mem_part = dot_nt(dmem, state["ckv"]).astype(BF)
        dkv = yield dkv

        back, mem_part = yield shifted(dkv_prev, -1), mem_part
        keep, send = call(qkv_back_kernel, place, (dq, dkv, back, qkv_full), [pair, pair])
        near, far = near_sum(keep, send)
        slots = [mem_part[k * padded : (k + 1) * padded] for k in (0, 2, 1, 3)]
        mem_near, mem_far = near_sum(jnp.concatenate(slots[:2], axis=0), jnp.concatenate(slots[2:], axis=0))
        grad_mem = (mem_near + flip(mem_far, "mem", 2).astype(F32))[:real].reshape(1, real, D)
        near = yield near

        far = yield flip(far, "mem", 2)
        plain_one, scale_one = norm_ones[i]
        grad_x = grad_after_self + normal_back(plain_one, scale_one, near + far.astype(F32))
        return output, grad_x, grad_mem

    sides = [first_side(), last_side(), memory_side(), hidden_side(), cout_side(), wide_side(), qkv_side()]
    done = interleave([stream(i) for i in range(MICRO)], sides)

    def wide_finish(own):
        high = me >> 1
        rows_two = own.reshape(2, 2 * wrows, own.shape[1])
        theirs = lax.dynamic_index_in_dim(rows_two, 1 - high, 0, keepdims=False).astype(BF)
        own = lax.dynamic_index_in_dim(rows_two, high, 0, keepdims=False) + flip(theirs, "mem", 2).astype(F32)
        rows_two = own.reshape(2, wrows, own.shape[1])
        theirs = lax.dynamic_index_in_dim(rows_two, 1 - odd, 0, keepdims=False)
        own = lax.dynamic_index_in_dim(rows_two, odd, 0, keepdims=False)
        return own, flip(theirs.astype(BF), "mem", 1).astype(F32)

    def head_finish(summed, count):
        slots = summed.astype(BF).reshape(blocks, wrows, -1)
        first, second, *rest = [lax.dynamic_index_in_dim(slots, me ^ k, 0, keepdims=False) for k in range(4)]
        far = flip(jnp.concatenate(rest, axis=0), "mem", 2)
        own, near, far = near_slots(first, second, far)
        whole = join_pieces([own, near[:wrows], far[:wrows], near[wrows:]], me, 1).astype(F32)
        whole = whole.reshape(wrows, blocks, count, -1)
        return [whole[:, :, k].reshape(wrows, D) for k in range(count)]

    def seq_finish(pair, left):
        for bit in left:
            pair = seq_next(*pair, bit)
        return pair[0] + pair[1].astype(F32)

    grad_inner, grad_outer = state["hidden_grads"]
    own, near = wide_finish(seq_finish(state["cout"], []))
    grad_cout = join_halves(own[:, :half], near[:, :half])
    grad_gain_mlp = own[:, half] + near[:, half]

    last = seq_finish(state["wide"], [])
    grad_ckey, grad_cvalue = head_finish(last[:, 2 * half :], 2)
    own, near = wide_finish(last[:, : 2 * half])
    grad_out, plain_cquery = [
        join_halves(own[:, k * half : (k + 1) * half], near[:, k * half : (k + 1) * half]) for k in range(2)
    ]
    plain_qkv = head_finish(seq_finish(state["qkv"], order[2:]), 3)

    def gained(gain, weights, plains):
        scale = gain.astype(F32)[:, None]
        grad_gain = sum(jnp.sum(w.astype(F32) * p, axis=1) for w, p in zip(weights, plains))
        return grad_gain, [p * scale for p in plains]

    grad_gain_self, (grad_query, grad_key, grad_value) = gained(
        gain_self, (self_query, self_key, self_value), plain_qkv
    )
    grad_gain_cross, (grad_cquery,) = gained(gain_cross, (cross_query,), (plain_cquery,))
    return (
        jnp.stack([d[0] for d in done]),
        jnp.stack([d[1] for d in done]),
        jnp.stack([d[2] for d in done]),
        grad_gain_self,
        grad_query,
        grad_key,
        grad_value,
        grad_out,
        grad_gain_cross,
        grad_cquery,
        grad_ckey,
        grad_cvalue,
        grad_cout,
        grad_gain_mlp,
        grad_inner,
        grad_outer,
    )


def solution(mesh):
    rows = P(("seq", "mem"), None)
    tokens = P(None, ("seq", "mem"), None)
    pages = P(None, "seq", "mem", None)
    gains = P(("seq", "mem"))
    return jax.shard_map(
        shards,
        mesh=mesh,
        in_specs=(tokens, pages, P(), P(), tokens, gains, rows, rows, rows, rows, gains, rows, rows, rows, rows,
                  gains, rows, rows),
        out_specs=(tokens, tokens, pages, gains, rows, rows, rows, rows, gains, rows, rows, rows, rows, gains,
                   rows, rows),
        check_vma=False,
    )
```

time: 841 us -> 805 us (0.957)
  Pallas kernels: 102 us -> 210 us
  waiting for transfers between devices: 339 us -> 235 us
  matrix products: 102 us -> 35.8 us
  local copies, waits for them, and re-layouts: 49.2 us -> 77.4 us
  between operations: 5.5 us -> 17.6 us
  starting transfers between devices: 158 us -> 147 us
    pallas_call x14 -> x35, Pallas kernels: 102 us -> 210 us  [call(): pl.pallas_call(kernel, out_shape=outs, in_specs=[pl.BlockSpec(memory_spac...]
    ppermute x143 -> x90, waiting for transfers between devices: 310 us -> 223 us  [flip(): lax.ppermute(block, axis, [(i, i ^ bit) for i in range(lax.axis_size(axis...]
    dot_general x20 -> x2, matrix products: 41.9 us -> 3.9 us  [dot_nt(): lax.dot_general(left, right, (((1,), (1,)), ((), ())), preferred_element_...]
    dot_general x22 -> x4, matrix products: 27.5 us -> 3.37 us  [dot_nn(): lax.dot_general(left, right, (((1,), (0,)), ((), ())), preferred_element_...]
    ppermute x8 -> x7, waiting for transfers between devices: 28.2 us -> 12.1 us  [shifted(): return lax.ppermute(block, 'seq', route)]
    unnamed x428 -> x414, local copies, waits for them, and re-layouts: 28.1 us -> 41.7 us
    ppermute x143 -> x90, starting transfers between devices: 139 us -> 127 us  [flip(): lax.ppermute(block, axis, [(i, i ^ bit) for i in range(lax.axis_size(axis...]
    slice x66 -> x58, local copies, waits for them, and re-layouts: 10.5 us -> 22.5 us  [the longest x12 5.37 us: far_slots(): return (part[:rows], part[rows:2 * rows], flip(part[2 * rows:], 'mem', 2))]
  transfers between devices with their start and end apart: 151 -> 99, of which waited for: 57 -> 32; matrix products, arithmetic and copies ran while one was open for 25% -> 18% of each run, Pallas kernels for 12% -> 22%
where the time goes in v2:
time: 805 us; the launch traced here: 794 us
  waiting for transfers between devices  235 us (29%)
  Pallas kernels  210 us (26%)
  starting transfers between devices  147 us (18%)
  local copies, waits for them, and re-layouts  77.4 us (10%)
  other arithmetic  71.6 us (9%)
  matrix products  35.8 us (4%)
  between operations  17.6 us (2%)
    ppermute x90, waiting for transfers between devices, flip(): lax.ppermute(block, axis, [(i, i ^ bit) for i in range(lax.axis_size(axis...  223 us
    pallas_call x35, Pallas kernels, call(): pl.pallas_call(kernel, out_shape=outs, in_specs=[pl.BlockSpec(memory_spac...  210 us
    ppermute x90, starting transfers between devices, flip(): lax.ppermute(block, axis, [(i, i ^ bit) for i in range(lax.axis_size(axis...  127 us
    unnamed x414, local copies, waits for them, and re-layouts  41.7 us
    dot_general x6, matrix products, dot_tn(): lax.dot_general(left, right, (((0,), (0,)), ((), ())), preferred_element_...  28.5 us
    ppermute x7, starting transfers between devices, shifted(): return lax.ppermute(block, 'seq', route)  19.4 us
  transfers between devices with their start and end apart: 99, of which 32 were waited for; matrix products, arithmetic and copies ran while one was open for 18% of the time, Pallas kernels for 22%

profile of v2, /device:TPU:0, one launch (start us, length us, event | category | flops | bytes accessed | tf_op | source)
XLA Modules:
  0.0 794.4 jit_solution(6151556190177376805)
XLA Ops:
  80.7 11.8 %collective-permute-done.11 = bf16[128,1536]{1,0:T(8,128)(2,1)} collective-permute-done((bf16[128,1536]{1,0:T(8,128)(2,1)S(1)}, bf16[128,1536]{1,0:T(8,128)(2,1)}, u32[]{:S(2)}, u32[]{:S(2)}) %collective-permute-start.11) | collective-permute-done | bytes 393248 | tf_op jit(solution)/shard_map/ppermute | solution.py:641
  114.9 11.6 %shard_map.302 = (bf16[1024,256]{1,0:T(8,128)(2,1)S(1)}, f32[8,1024]{1,0:T(8,128)S(1)}) custom-call(s32[3]{0:T(128)S(1)} %pad_add_fusion.1.sc, bf16[1024,768]{1,0:T(8,128)(2,1)S(1)} %copy-done.3, bf16[1024,512]{1,0:T(8,128)(2,1)S(1)} %get-tuple-element.305.kvp), custom_call_target="tpu_custom_call" | custom-call | flops 1024 | bytes 1024 | tf_op jit(solution)/shard_map/pallas_call | solution.py:326
  128.9 12.5 %collective-permute-start.20 = (bf16[512,1536]{1,0:T(8,128)(2,1)S(1)}, bf16[512,1536]{1,0:T(8,128)(2,1)S(1)}, u32[]{:S(2)}, u32[]{:S(2)}) collective-permute-start(bf16[512,1536]{1,0:T(8,128)(2,1)S(1)} %pad_maximum_fusion.3.first), channel_id=1, source_target_pairs={{0,4},{4,0},{8,12},{12,8},{16,20},{20,16},{24,28},{28,24},{1,5},{5... | collective-permute-start | bytes 4718600 | tf_op jit(solution)/shard_map/ppermute | solution.py:641
  167.1 11.6 %shard_map.304 = (bf16[1024,256]{1,0:T(8,128)(2,1)S(1)}, f32[8,1024]{1,0:T(8,128)S(1)}) custom-call(s32[3]{0:T(128)S(1)} %pad_add_fusion.2.sc, bf16[1024,768]{1,0:T(8,128)(2,1)S(1)} %copy-done.4, bf16[1024,512]{1,0:T(8,128)(2,1)S(1)} %get-tuple-element.318.kvp), custom_call_target="tpu_custom_call" | custom-call | flops 1024 | bytes 1024 | tf_op jit(solution)/shard_map/pallas_call | solution.py:326
  194.6 25.7 %collective-permute-done.24.far = bf16[512,256]{1,0:T(8,128)(2,1)S(1)} collective-permute-done((bf16[512,256]{1,0:T(8,128)(2,1)}, bf16[512,256]{1,0:T(8,128)(2,1)S(1)}, u32[]{:S(2)}, u32[]{:S(2)}) %collective-permute-start.24) | collective-permute-done | bytes 262176 | tf_op jit(solution)/shard_map/ppermute | solution.py:641
  238.3 20.5 %collective-permute-done.27 = bf16[256,640]{1,0:T(8,128)(2,1)S(1)} collective-permute-done((bf16[256,640]{1,0:T(8,128)(2,1)}, bf16[256,640]{1,0:T(8,128)(2,1)S(1)}, u32[]{:S(2)}, u32[]{:S(2)}) %collective-permute-start.27) | collective-permute-done | bytes 327712 | tf_op jit(solution)/shard_map/ppermute | solution.py:641
  278.4 11.0 %shard_map.308 = (bf16[1024,256]{1,0:T(8,128)(2,1)S(1)}, f32[8,1024]{1,0:T(8,128)S(1)}, bf16[1024,256]{1,0:T(8,128)(2,1)S(1)}) custom-call(s32[4]{0:T(128)S(1)} %pad_add_fusion.sc, bf16[256,256]{1,0:T(8,128)(2,1)S(1)} %copy-done.105, bf16[512,256]{1,0:T(8,128)(2,1)S(1)} %collective-permute-done.29.near, bf16[512,256]{1,0:T(8,128)(2,1)S(1)} %collective-permute-done.23.far, ...), custom_call_target="tpu_custom_call" | custom-call | flops 1024 | bytes 1024 | tf_op jit(solution)/shard_map/pallas_call | solution.py:326
  292.2 10.9 %shard_map.309 = (bf16[1024,256]{1,0:T(8,128)(2,1)S(1)}, f32[8,1024]{1,0:T(8,128)S(1)}, bf16[1024,256]{1,0:T(8,128)(2,1)S(1)}) custom-call(s32[4]{0:T(128)S(1)} %pad_add_fusion.3.sc, bf16[256,256]{1,0:T(8,128)(2,1)S(1)} %get-tuple-element.355.own, bf16[512,256]{1,0:T(8,128)(2,1)S(1)} %collective-permute-done.33.near, ...), custom_call_target="tpu_custom_call" | custom-call | flops 1024 | bytes 1024 | tf_op jit(solution)/shard_map/pallas_call | solution.py:326
  311.3 12.6 %collective-permute-done.38.far = bf16[512,256]{1,0:T(8,128)(2,1)S(1)} collective-permute-done((bf16[512,256]{1,0:T(8,128)(2,1)S(1)}, bf16[512,256]{1,0:T(8,128)(2,1)S(1)}, u32[]{:S(2)}, u32[]{:S(2)}) %collective-permute-start.38) | collective-permute-done | bytes 262176 | tf_op jit(solution)/shard_map/ppermute | solution.py:641
  341.9 15.2 %shard_map.313 = (bf16[1024,1024]{1,0:T(8,128)(2,1)}, bf16[1024,1024]{1,0:T(8,128)(2,1)}, bf16[1024,1024]{1,0:T(8,128)(2,1)}, bf16[1024,1024]{1,0:T(8,128)(2,1)}...) custom-call(s32[1]{0:T(128)} %bitcast.at, ...), custom_call_target="tpu_custom_call" | custom-call | flops 1024 | bytes 1024 | tf_op jit(solution)/shard_map/pallas_call | solution.py:326
  360.4 11.1 %collective-permute-done.45.far_low = bf16[256,1024]{1,0:T(8,128)(2,1)S(1)} collective-permute-done((bf16[256,1024]{1,0:T(8,128)(2,1)S(1)}, bf16[256,1024]{1,0:T(8,128)(2,1)S(1)}, u32[]{:S(2)}, u32[]{:S(2)}) %collective-permute-start.45) | collective-permute-done | bytes 524320 | tf_op jit(solution)/shard_map/ppermute | solution.py:641
  375.3 14.5 %shard_map.314 = (bf16[1024,1024]{1,0:T(8,128)(2,1)}, bf16[1024,1024]{1,0:T(8,128)(2,1)}, bf16[1024,1024]{1,0:T(8,128)(2,1)}, bf16[1024,1024]{1,0:T(8,128)(2,1)}...) custom-call(s32[1]{0:T(128)} %bitcast.at, ...), custom_call_target="tpu_custom_call" | custom-call | flops 1024 | bytes 1024 | tf_op jit(solution)/shard_map/pallas_call | solution.py:326
  402.4 8.6 %collective-permute-done.44.far = bf16[256,1024]{1,0:T(8,128)(2,1)S(1)} collective-permute-done((bf16[256,1024]{1,0:T(8,128)(2,1)S(1)}, bf16[256,1024]{1,0:T(8,128)(2,1)S(1)}, u32[]{:S(2)}, u32[]{:S(2)}) %collective-permute-start.44) | collective-permute-done | bytes 524320 | tf_op jit(solution)/shard_map/ppermute | solution.py:641
  439.3 11.9 %shard_map.317 = (bf16[1024,256]{1,0:T(8,128)(2,1)S(1)}, bf16[640,512]{1,0:T(8,128)(2,1)S(1)}, bf16[640,512]{1,0:T(8,128)(2,1)S(1)}) custom-call(s32[4]{0:T(128)S(1)} %pad_add_fusion.sc, bf16[1024,256]{1,0:T(8,128)(2,1)S(1)} %get-tuple-element.395.q_ref, bf16[640,512]{1,0:T(8,128)(2,1)S(1)} %copy-done.12, bf16[640,512]{1,0:T(8,128)(2,1)S(1)} %copy-done.14, ...), custom_call_target="tpu_custom_call" | custom-call | flops 1024 | bytes 1024 | tf_op jit(solution)/shard_map/pallas_call | solution.py:326
  462.1 13.3 %shard_map.318 = (bf16[1024,256]{1,0:T(8,128)(2,1)S(1)}, bf16[640,512]{1,0:T(8,128)(2,1)}, bf16[640,512]{1,0:T(8,128)(2,1)S(1)}) custom-call(s32[4]{0:T(128)S(1)} %pad_add_fusion.3.sc, bf16[1024,256]{1,0:T(8,128)(2,1)S(1)} %copy-done.75, bf16[640,512]{1,0:T(8,128)(2,1)S(1)} %copy-done.8, bf16[640,512]{1,0:T(8,128)(2,1)S(1)} %copy-done.10, ...), custom_call_target="tpu_custom_call" | custom-call | flops 1024 | bytes 1024 | tf_op jit(solution)/shard_map/pallas_call | solution.py:326
  494.9 12.1 %collective-permute-done.64 = bf16[640,512]{1,0:T(8,128)(2,1)} collective-permute-done((bf16[640,512]{1,0:T(8,128)(2,1)}, bf16[640,512]{1,0:T(8,128)(2,1)}, u32[]{:S(2)}, u32[]{:S(2)}) %collective-permute-start.64) | collective-permute-done | bytes 655392 | tf_op jit(solution)/shard_map/ppermute | solution.py:647
  540.4 13.8 %shard_map.322 = (bf16[1024,256]{1,0:T(8,128)(2,1)S(1)}, bf16[1024,512]{1,0:T(8,128)(2,1)S(1)}, bf16[1024,512]{1,0:T(8,128)(2,1)S(1)}) custom-call(s32[3]{0:T(128)S(1)} %pad_add_fusion.1.sc, bf16[1024,768]{1,0:T(8,128)(2,1)} %get-tuple-element.304.qkv, bf16[1024,512]{1,0:T(8,128)(2,1)S(1)} %get-tuple-element.305.kvp, bf16[1024,256]{1,0:T(8,128)(2,1)S(1)} %copy-done.36, ...), custom_call_target="tpu_custom_call" | custom-call | flops 1024 | bytes 1024 | tf_op jit(solution)/shard_map/pallas_call | solution.py:326
  579.6 13.6 %shard_map.325 = (bf16[1024,256]{1,0:T(8,128)(2,1)S(1)}, bf16[1024,512]{1,0:T(8,128)(2,1)S(1)}, bf16[1024,512]{1,0:T(8,128)(2,1)S(1)}) custom-call(s32[3]{0:T(128)S(1)} %pad_add_fusion.2.sc, bf16[1024,768]{1,0:T(8,128)(2,1)} %get-tuple-element.317.qkv, bf16[1024,512]{1,0:T(8,128)(2,1)S(1)} %copy-done.6, bf16[1024,256]{1,0:T(8,128)(2,1)S(1)} %copy-done.34, ...), custom_call_target="tpu_custom_call" | custom-call | flops 1024 | bytes 1024 | tf_op jit(solution)/shard_map/pallas_call | solution.py:326
  604.1 16.5 %collective-permute-start.75 = (bf16[512,1536]{1,0:T(8,128)(2,1)}, bf16[512,1536]{1,0:T(8,128)(2,1)}, u32[]{:S(2)}, u32[]{:S(2)}) collective-permute-start(bf16[512,1536]{1,0:T(8,128)(2,1)} %get-tuple-element.630), channel_id=1, source_target_pairs={{0,8},{4,12},{8,0},{12,4},{16,24},{20,28},{24,16},{28,20},{1,9},{5... | collective-permute-start | bytes 4718600 | tf_op jit(solution)/shard_map/ppermute | solution.py:641
  644.3 17.4 %collective-permute-done.74 = bf16[256,640]{1,0:T(8,128)(2,1)S(1)} collective-permute-done((bf16[256,640]{1,0:T(8,128)(2,1)S(1)}, bf16[256,640]{1,0:T(8,128)(2,1)S(1)}, u32[]{:S(2)}, u32[]{:S(2)}) %collective-permute-start.74) | collective-permute-done | bytes 327712 | tf_op jit(solution)/shard_map/ppermute | solution.py:641
  661.7 11.3 %collective-permute-done.75 = bf16[512,1536]{1,0:T(8,128)(2,1)} collective-permute-done((bf16[512,1536]{1,0:T(8,128)(2,1)}, bf16[512,1536]{1,0:T(8,128)(2,1)}, u32[]{:S(2)}, u32[]{:S(2)}) %collective-permute-start.75) | collective-permute-done | bytes 1572896 | tf_op jit(solution)/shard_map/ppermute | solution.py:641
  674.2 18.2 %collective-permute-done.94 = bf16[128,640]{1,0:T(8,128)(2,1)S(1)} collective-permute-done((bf16[128,640]{1,0:T(8,128)(2,1)S(1)}, bf16[128,640]{1,0:T(8,128)(2,1)S(1)}, u32[]{:S(2)}, u32[]{:S(2)}) %collective-permute-start.94) | collective-permute-done | bytes 163872 | tf_op jit(solution)/shard_map/ppermute | solution.py:641
  703.6 14.9 %collective-permute-start.79 = (bf16[256,1536]{1,0:T(8,128)(2,1)S(1)}, bf16[256,1536]{1,0:T(8,128)(2,1)S(1)}, u32[]{:S(2)}, u32[]{:S(2)}) collective-permute-start(bf16[256,1536]{1,0:T(8,128)(2,1)S(1)} %slice.748), channel_id=1, source_target_pairs={{0,4},{4,0},{8,12},{12,8},{16,20},{20,16},{24,28},{28,24},{1,5},{5... | collective-permute-start | bytes 2359304 | tf_op jit(solution)/shard_map/ppermute | solution.py:641
  743.0 14.5 %collective-permute-done.89 = bf16[128,1536]{1,0:T(8,128)(2,1)S(1)} collective-permute-done((bf16[128,1536]{1,0:T(8,128)(2,1)S(1)}, bf16[128,1536]{1,0:T(8,128)(2,1)S(1)}, u32[]{:S(2)}, u32[]{:S(2)}) %collective-permute-start.89) | collective-permute-done | bytes 393248 | tf_op jit(solution)/shard_map/ppermute | solution.py:641
  (835 shorter events, 441.7 us)
Async XLA Ops:
  7.2 324.3 %all-gather.2.cloned.1.call-start = ((), (), s32[]{:S(2)}) async-start(), calls=%async_computation.1 | async-start | bytes 4718592 | tf_op jit(solution)/shard_map/all_gather | solution.py:946
  60.2 39.0 %collective-permute-start.1 = (bf16[512,1024]{1,0:T(8,128)(2,1)}, bf16[512,1024]{1,0:T(8,128)(2,1)S(1)}, u32[]{:S(2)}, u32[]{:S(2)}) collective-permute-start(bf16[512,1024]{1,0:T(8,128)(2,1)} %pad_maximum_fusion.7), channel_id=1, source_target_pairs={{0,1},{1,0},{2,3},{3,2},{4,5},{5,4},{6,7},{7,6},{8,9},{9,8},{10,11... | collective-permute-start | bytes 3145736 | tf_op jit(solution)/shard_map/ppermute | solution.py:641
  61.3 38.9 %collective-permute-start.7 = (bf16[512,1024]{1,0:T(8,128)(2,1)}, bf16[512,1024]{1,0:T(8,128)(2,1)}, u32[]{:S(2)}, u32[]{:S(2)}) collective-permute-start(bf16[512,1024]{1,0:T(8,128)(2,1)} %pad_maximum_fusion.8), channel_id=1, source_target_pairs={{0,1},{1,0},{2,3},{3,2},{4,5},{5,4},{6,7},{7,6},{8,9},{9,8},{10,11... | collective-permute-start | bytes 3145736 | tf_op jit(solution)/shard_map/ppermute | solution.py:641
  79.3 48.7 %collective-permute-start.13 = (bf16[256,1024]{1,0:T(8,128)(2,1)S(1)}, bf16[256,1024]{1,0:T(8,128)(2,1)}, u32[]{:S(2)}, u32[]{:S(2)}) collective-permute-start(bf16[256,1024]{1,0:T(8,128)(2,1)S(1)} %get-tuple-element.313.low), channel_id=1, source_target_pairs={{0,2},{1,3},{2,0},{3,1},{4,6},{5,7},{6,4},{7,5},{8,10},{9,11},{10,... | collective-permute-start | bytes 1572872 | tf_op jit(solution)/shard_map/ppermute | solution.py:641
  92.6 35.5 %collective-permute-start.14 = (bf16[256,1024]{1,0:T(8,128)(2,1)}, bf16[256,1024]{1,0:T(8,128)(2,1)}, u32[]{:S(2)}, u32[]{:S(2)}) collective-permute-start(bf16[256,1024]{1,0:T(8,128)(2,1)} %collective-permute-done.9.ahead), channel_id=1, source_target_pairs={{0,2},{1,3},{2,0},{3,1},{4,6},{5,7},{6,4},{7,5},{8,10},{9,11},{10,... | collective-permute-start | bytes 1572872 | tf_op jit(solution)/shard_map/ppermute | solution.py:641
  128.9 49.8 %collective-permute-start.20 = (bf16[512,1536]{1,0:T(8,128)(2,1)S(1)}, bf16[512,1536]{1,0:T(8,128)(2,1)S(1)}, u32[]{:S(2)}, u32[]{:S(2)}) collective-permute-start(bf16[512,1536]{1,0:T(8,128)(2,1)S(1)} %pad_maximum_fusion.3.first), channel_id=1, source_target_pairs={{0,4},{4,0},{8,12},{12,8},{16,20},{20,16},{24,28},{28,24},{1,5},{5... | collective-permute-start | bytes 4718600 | tf_op jit(solution)/shard_map/ppermute | solution.py:641
  145.8 33.0 %collective-permute-start.12 = (bf16[512,256]{1,0:T(8,128)(2,1)S(1)}, bf16[512,256]{1,0:T(8,128)(2,1)S(1)}, u32[]{:S(2)}, u32[]{:S(2)}) collective-permute-start(bf16[512,256]{1,0:T(8,128)(2,1)S(1)} %slice.417), channel_id=1, source_target_pairs={{0,2},{1,3},{2,0},{3,1},{4,6},{5,7},{6,4},{7,5},{8,10},{9,11},{10,... | collective-permute-start | bytes 786440 | tf_op jit(solution)/shard_map/ppermute | solution.py:641
  183.7 36.6 %collective-permute-start.25 = (bf16[640,1024]{1,0:T(8,128)(2,1)}, bf16[640,1024]{1,0:T(8,128)(2,1)}, u32[]{:S(2)}, u32[]{:S(2)}) collective-permute-start(bf16[640,1024]{1,0:T(8,128)(2,1)} %constant_dynamic-update-slice_fusion), channel_id=1, source_target_pairs={{0,2},{1,3},{2,0},{3,1},{4,6},{5,7},{6,4},{7,5},{8,10},{9,11},{10,... | collective-permute-start | bytes 3932168 | tf_op jit(solution)/shard_map/ppermute | solution.py:641
  186.1 34.2 %collective-permute-start.24 = (bf16[512,256]{1,0:T(8,128)(2,1)}, bf16[512,256]{1,0:T(8,128)(2,1)S(1)}, u32[]{:S(2)}, u32[]{:S(2)}) collective-permute-start(bf16[512,256]{1,0:T(8,128)(2,1)} %slice.423), channel_id=1, source_target_pairs={{0,2},{1,3},{2,0},{3,1},{4,6},{5,7},{6,4},{7,5},{8,10},{9,11},{10,... | collective-permute-start | bytes 786440 | tf_op jit(solution)/shard_map/ppermute | solution.py:641
  187.3 598.0 %reduce-scatter.2.cloned.1.call-start = ((), (), s32[]{:S(2)}) async-start(), calls=%async_computation.2 | async-start | bytes 4718592 | tf_op jit(solution)/shard_map/reduce_scatter | solution.py:954
  223.9 43.7 %collective-permute-start.28 = (bf16[1280,1024]{1,0:T(8,128)(2,1)}, bf16[1280,1024]{1,0:T(8,128)(2,1)}, u32[]{:S(2)}, u32[]{:S(2)}) collective-permute-start(bf16[1280,1024]{1,0:T(8,128)(2,1)} %pad_maximum_fusion.1), channel_id=1, source_target_pairs={{0,1},{1,0},{2,3},{3,2},{4,5},{5,4},{6,7},{7,6},{8,9},{9,8},{10,11... | collective-permute-start | bytes 7864328 | tf_op jit(solution)/shard_map/ppermute | solution.py:641
  226.0 32.7 %collective-permute-start.27 = (bf16[256,640]{1,0:T(8,128)(2,1)}, bf16[256,640]{1,0:T(8,128)(2,1)S(1)}, u32[]{:S(2)}, u32[]{:S(2)}) collective-permute-start(bf16[256,640]{1,0:T(8,128)(2,1)} %pad_maximum_fusion.23), channel_id=1, source_target_pairs={{0,8},{4,12},{8,0},{12,4},{16,24},{20,28},{24,16},{28,20},{1,9},{5... | collective-permute-start | bytes 983048 | tf_op jit(solution)/shard_map/ppermute | solution.py:641
  232.8 34.8 %collective-permute-start.23 = (bf16[512,256]{1,0:T(8,128)(2,1)}, bf16[512,256]{1,0:T(8,128)(2,1)S(1)}, u32[]{:S(2)}, u32[]{:S(2)}) collective-permute-start(bf16[512,256]{1,0:T(8,128)(2,1)} %get-tuple-element.330), channel_id=1, source_target_pairs={{0,2},{1,3},{2,0},{3,1},{4,6},{5,7},{6,4},{7,5},{8,10},{9,11},{10,... | collective-permute-start | bytes 786440 | tf_op jit(solution)/shard_map/ppermute | solution.py:641
  267.7 35.3 %collective-permute-start.31 = (bf16[256,1024]{1,0:T(8,128)(2,1)S(1)}, bf16[256,1024]{1,0:T(8,128)(2,1)S(1)}, u32[]{:S(2)}, u32[]{:S(2)}) collective-permute-start(bf16[256,1024]{1,0:T(8,128)(2,1)S(1)} %get-tuple-element.350.top), channel_id=1, source_target_pairs={{0,2},{1,3},{2,0},{3,1},{4,6},{5,7},{6,4},{7,5},{8,10},{9,11},{10,... | collective-permute-start | bytes 1572872 | tf_op jit(solution)/shard_map/ppermute | solution.py:641
  268.3 34.8 %collective-permute-start.34 = (bf16[512,640]{1,0:T(8,128)(2,1)S(1)}, bf16[512,640]{1,0:T(8,128)(2,1)S(1)}, u32[]{:S(2)}, u32[]{:S(2)}) collective-permute-start(bf16[512,640]{1,0:T(8,128)(2,1)S(1)} %pad_maximum_fusion.18.first), channel_id=1, source_target_pairs={{0,4},{4,0},{8,12},{12,8},{16,20},{20,16},{24,28},{28,24},{1,5},{5... | collective-permute-start | bytes 1966088 | tf_op jit(solution)/shard_map/ppermute | solution.py:641
  521.7 43.5 %collective-permute-start.69 = (bf16[1024,1024]{1,0:T(8,128)(2,1)}, bf16[1024,1024]{1,0:T(8,128)(2,1)}, u32[]{:S(2)}, u32[]{:S(2)}) collective-permute-start(bf16[1024,1024]{1,0:T(8,128)(2,1)} %get-tuple-element.518), channel_id=1, source_target_pairs={{0,1},{1,0},{2,3},{3,2},{4,5},{5,4},{6,7},{7,6},{8,9},{9,8},{10,11... | collective-permute-start | bytes 6291464 | tf_op jit(solution)/shard_map/ppermute | solution.py:641
  532.7 32.5 %collective-permute-start.68 = (bf16[512,640]{1,0:T(8,128)(2,1)}, bf16[512,640]{1,0:T(8,128)(2,1)}, u32[]{:S(2)}, u32[]{:S(2)}) collective-permute-start(bf16[512,640]{1,0:T(8,128)(2,1)} %get-tuple-element.650), channel_id=1, source_target_pairs={{0,8},{4,12},{8,0},{12,4},{16,24},{20,28},{24,16},{28,20},{1,9},{5... | collective-permute-start | bytes 1966088 | tf_op jit(solution)/shard_map/ppermute | solution.py:641
  554.2 45.3 %collective-permute-start.72 = (bf16[1024,512]{1,0:T(8,128)(2,1)S(1)}, bf16[1024,512]{1,0:T(8,128)(2,1)S(1)}, u32[]{:S(2)}, u32[]{:S(2)}) collective-permute-start(bf16[1024,512]{1,0:T(8,128)(2,1)S(1)} %get-tuple-element.529.dkv_prev), channel_id=1, source_target_pairs={{4,0},{8,4},{12,8},{16,12},{20,16},{24,20},{28,24},{5,1},{9,5},{13... | collective-permute-start | bytes 3145736 | tf_op jit(solution)/shard_map/ppermute | solution.py:647
  604.1 68.9 %collective-permute-start.75 = (bf16[512,1536]{1,0:T(8,128)(2,1)}, bf16[512,1536]{1,0:T(8,128)(2,1)}, u32[]{:S(2)}, u32[]{:S(2)}) collective-permute-start(bf16[512,1536]{1,0:T(8,128)(2,1)} %get-tuple-element.630), channel_id=1, source_target_pairs={{0,8},{4,12},{8,0},{12,4},{16,24},{20,28},{24,16},{28,20},{1,9},{5... | collective-permute-start | bytes 4718600 | tf_op jit(solution)/shard_map/ppermute | solution.py:641
  621.8 39.9 %collective-permute-start.71 = (bf16[1024,512]{1,0:T(8,128)(2,1)S(1)}, bf16[1024,512]{1,0:T(8,128)(2,1)S(1)}, u32[]{:S(2)}, u32[]{:S(2)}) collective-permute-start(bf16[1024,512]{1,0:T(8,128)(2,1)S(1)} %get-tuple-element.525.dkv_prev), channel_id=1, source_target_pairs={{4,0},{8,4},{12,8},{16,12},{20,16},{24,20},{28,24},{5,1},{9,5},{13... | collective-permute-start | bytes 3145736 | tf_op jit(solution)/shard_map/ppermute | solution.py:647
  639.7 90.3 %collective-permute-start.78 = (bf16[512,768]{1,0:T(8,128)(2,1)S(1)}, bf16[512,768]{1,0:T(8,128)(2,1)S(1)}, u32[]{:S(2)}, u32[]{:S(2)}) collective-permute-start(bf16[512,768]{1,0:T(8,128)(2,1)S(1)} %get-tuple-element.640), channel_id=1, source_target_pairs={{0,8},{4,12},{8,0},{12,4},{16,24},{20,28},{24,16},{28,20},{1,9},{5... | collective-permute-start | bytes 2359304 | tf_op jit(solution)/shard_map/ppermute | solution.py:641
  643.0 87.0 %collective-permute-start.76 = (bf16[256,1024]{1,0:T(8,128)(2,1)}, bf16[256,1024]{1,0:T(8,128)(2,1)S(1)}, u32[]{:S(2)}, u32[]{:S(2)}) collective-permute-start(bf16[256,1024]{1,0:T(8,128)(2,1)} %slice.750), channel_id=1, source_target_pairs={{0,2},{1,3},{2,0},{3,1},{4,6},{5,7},{6,4},{7,5},{8,10},{9,11},{10,... | collective-permute-start | bytes 1572872 | tf_op jit(solution)/shard_map/ppermute | solution.py:641
  674.2 44.4 %collective-permute-start.83 = (bf16[320,1024]{1,0:T(8,128)(2,1)}, bf16[320,1024]{1,0:T(8,128)(2,1)S(1)}, u32[]{:S(2)}, u32[]{:S(2)}) collective-permute-start(bf16[320,1024]{1,0:T(8,128)(2,1)} %pad_maximum_fusion.20), channel_id=1, source_target_pairs={{0,1},{1,0},{2,3},{3,2},{4,5},{5,4},{6,7},{7,6},{8,9},{9,8},{10,11... | collective-permute-start | bytes 1966088 | tf_op jit(solution)/shard_map/ppermute | solution.py:641
  703.6 32.8 %collective-permute-start.79 = (bf16[256,1536]{1,0:T(8,128)(2,1)S(1)}, bf16[256,1536]{1,0:T(8,128)(2,1)S(1)}, u32[]{:S(2)}, u32[]{:S(2)}) collective-permute-start(bf16[256,1536]{1,0:T(8,128)(2,1)S(1)} %slice.748), channel_id=1, source_target_pairs={{0,4},{4,0},{8,12},{12,8},{16,20},{20,16},{24,28},{28,24},{1,5},{5... | collective-permute-start | bytes 2359304 | tf_op jit(solution)/shard_map/ppermute | solution.py:641
  (280 other events, 2724.4 us)
Sparse Core Ops, SparseCore 0:
  187.4 80.7 all-gather.1
  538.8 125.9 reduce-scatter.1

commit v3 on v2

--- a/solution.py
+++ b/solution.py
@@ -50,10 +50,72 @@
     return (inner < real) & (row < length) & ((query < spill) == (side == 0))
 
 
-def self_forward_kernel(rows, blocks, heads, sc, qkv, kvp, o_ref, lse_ref, k_scr, v_scr, s_scr, mx, tot):
+def fold(block, combine):
+    total = block[0:8]
+    for r in range(8, block.shape[0], 8):
+        total = combine(total, block[r : r + 8])
+    return total
+
+
+def lay_heads(out, block, lanes, heads):
+    rows = block.shape[0]
+    for h in range(heads):
+        out[h * rows : (h + 1) * rows, :] = one_head(block, lanes, h)
+
+
+def score_block(kb, k, allowed, q_cat, s_scr, tops):
+    rows = s_scr.shape[3]
+    found = []
+    for h, top in enumerate(tops):
+        s = jnp.where(allowed, dot_nt(k, q_cat[h * rows : (h + 1) * rows, :]), LOWEST)
+        s_scr[kb, h] = s
+        found.append(jnp.maximum(top, fold(s, jnp.maximum)))
+    return tuple(found)
+
+
+def weigh_block(kb, tops, totals, s_scr, p_scr, v_cat):
+    count = s_scr.shape[2]
+    summed = []
+    for h, (top, total) in enumerate(zip(tops, totals)):
+        e = jnp.exp(s_scr[kb, h] - top)
+        p_scr[h * count : (h + 1) * count, :] = e.astype(BF)
+        summed.append(total + fold(e, jnp.add))
+    return tuple(summed), dot_tn(p_scr[...], v_cat)
+
+
+def attend(first, last, heads, scores, values, s_scr, p_scr, width):
+    rows = s_scr.shape[3]
+    lowest = jnp.full((8, rows), LOWEST, F32)
+    tops = lax.fori_loop(first, last, scores, (lowest,) * heads)
+    tops = tuple(jnp.max(top, axis=0, keepdims=True) for top in tops)
+
+    def step(kb, carry):
+        totals, acc = carry
+        totals, more = weigh_block(kb, tops, totals, s_scr, p_scr, values(kb))
+        return totals, acc + more
+
+    start = (jnp.zeros((8, rows), F32),) * heads, jnp.zeros((rows, width), F32)
+    totals, acc = lax.fori_loop(first, last, step, start)
+    return tops, tuple(jnp.sum(total, axis=0, keepdims=True) for total in totals), acc
+
+
+def finish(p, start, tops, totals, acc, lanes, o_ref, lse_ref):
+    rows = acc.shape[0]
+    heads = len(tops)
+    inverse = jnp.concatenate([1.0 / total for total in totals] + [jnp.zeros((8 - heads, rows), F32)], axis=0).T
+    spread_out = jnp.zeros(acc.shape, F32)
+    for h in range(heads):
+        spread_out = jnp.where(lanes == h, inverse[:, h : h + 1], spread_out)
+    o_ref[pl.ds(start, rows), :] = (acc * spread_out).astype(BF)
+    place = pl.ds(pl.multiple_of(p * rows, rows), rows)
+    for h in range(heads):
+        lse_ref[h : h + 1, place] = tops[h] + jnp.log(totals[h])
+
+
+def self_forward_kernel(rows, blocks, heads, sc, qkv, kvp, o_ref, lse_ref, k_scr, v_scr, s_scr, q_cat, p_scr):
     width = heads * HEAD
     extent = rows * blocks
-    me, spill, prev_spill = sc[0], sc[1], sc[2]
+    me, spill, prev_spill = sc[0], sc[1], sc[4]
     lanes = head_lanes(rows, width)
 
     def place(b):
@@ -65,8 +127,7 @@
     def _(kb):
         def fill(keys, values):
             k_scr[kb] = keys
-            for h in range(heads):
-                v_scr[kb, h * rows : (h + 1) * rows, :] = one_head(values, lanes, h)
+            lay_heads(v_scr.at[kb], values, lanes, heads)
 
         @pl.when(kb < blocks)
         def _():
@@ -80,48 +141,16 @@
 
     @pl.loop(0, blocks)
     def _(p):
-        q = qkv[pl.ds(place(p), rows), 0:width] * jnp.asarray(0.125, BF)
-        mx[...] = jnp.full(mx.shape, LOWEST, F32)
-        tot[...] = jnp.zeros(tot.shape, F32)
+        lay_heads(q_cat, qkv[pl.ds(place(p), rows), 0:width] * jnp.asarray(0.125, BF), lanes, heads)
         first, last = self_range(p, rows, blocks, spill, prev_spill)
-        query = p * rows + lax.broadcasted_iota(jnp.int32, (rows, 1), 0)
-
-        @pl.loop(first, last)
-        def _(kb):
-            key = kb * rows + lax.broadcasted_iota(jnp.int32, (1, rows), 1)
-            allowed = self_allowed(query, key, extent, spill, prev_spill)
-            k = k_scr[kb]
-            for h in range(heads):
-                s = dot_nt(one_head(q, lanes, h), k)
-                s = jnp.where(allowed, s, LOWEST)
-                s_scr[kb, h] = s
-                mx[h] = jnp.maximum(mx[h], s)
-
-        for h in range(heads):
-            mx[h, :, 0:1] = jnp.max(mx[h], axis=1, keepdims=True)
-
-        def weigh(kb, acc):
-            parts = []
-            for h in range(heads):
-                e = jnp.exp(s_scr[kb, h] - mx[h, :, 0:1])
-                tot[h] += e
-                parts.append(e.astype(BF))
-            return acc + dot_nn(jnp.concatenate(parts, axis=1), v_scr[kb])
-
-        acc = lax.fori_loop(first, last, weigh, jnp.zeros((rows, width), F32))
-        finish(p, place(p), rows, heads, acc, mx, tot, lanes, o_ref, lse_ref)
-
-
-def finish(p, start, rows, heads, acc, mx, tot, lanes, o_ref, lse_ref):
-    over = jnp.zeros((rows, 128), F32)
-    inverse = jnp.zeros(acc.shape, F32)
-    slim = lax.broadcasted_iota(jnp.int32, (rows, 128), 1)
-    for h in range(heads):
-        total = jnp.sum(tot[h], axis=1, keepdims=True)
-        inverse = jnp.where(lanes == h, 1.0 / total, inverse)
-        over = jnp.where(slim == h, mx[h, :, 0:1] + jnp.log(total), over)
-    o_ref[pl.ds(start, rows), :] = (acc * inverse).astype(BF)
-    lse_ref[:, pl.ds(pl.multiple_of(p * rows, rows), rows)] = over.T[0:8, :]
+        query = p * rows + lax.broadcasted_iota(jnp.int32, (1, rows), 1)
+
+        def scores(kb, tops):
+            key = kb * rows + lax.broadcasted_iota(jnp.int32, (rows, rows), 0)
+            return score_block(kb, k_scr[kb], self_allowed(query, key, extent, spill, prev_spill), q_cat, s_scr, tops)
+
+        tops, totals, acc = attend(first, last, heads, scores, lambda kb: v_scr[kb], s_scr, p_scr, width)
+        finish(p, place(p), tops, totals, acc, lanes, o_ref, lse_ref)
 
 
 def lay(out, own, near, far):
@@ -133,7 +162,7 @@
 
 
 def cross_forward_kernel(rows, blocks, heads, padded, real, sc, own, near, far, kv0, kv1, o_ref, lse_ref, q_ref,
-                         v_scr, s_scr, mx, tot):
+                         v_scr, s_scr, q_cat, p_scr):
     lay(q_ref, own, near, far)
     width = heads * HEAD
     keys = kv0.shape[0]
@@ -146,42 +175,24 @@
         return pl.multiple_of((b ^ me) * rows, rows)
 
     for side in range(2):
-        values = kvs[side][:, width : 2 * width]
-        for h in range(heads):
-            v_scr[side, h * keys : (h + 1) * keys, :] = one_head(values, key_lanes, h)
-    spot = lax.broadcasted_iota(jnp.int32, (1, keys), 1)
+        lay_heads(v_scr.at[side], kvs[side][:, width : 2 * width], key_lanes, heads)
 
     @pl.loop(0, blocks)
     def _(p):
-        q = q_ref[pl.ds(place(p), rows), :] * jnp.asarray(0.125, BF)
-        mx[...] = jnp.full(mx.shape, LOWEST, F32)
-        tot[...] = jnp.zeros(tot.shape, F32)
-        query = p * rows + lax.broadcasted_iota(jnp.int32, (rows, 1), 0)
-        reads = (p * rows < spill, (p + 1) * rows > spill)
-        for side in range(2):
-
-            @pl.when(reads[side])
-            def _():
-                allowed = cross_allowed(query, spot, side, spill, sc[2 + side], me, padded, real)
-                k = kvs[side][:, 0:width]
-                for h in range(heads):
-                    s = dot_nt(one_head(q, lanes, h), k)
-                    s = jnp.where(allowed, s, LOWEST)
-                    s_scr[side, h] = s
-                    mx[h] = jnp.maximum(mx[h], jnp.max(s, axis=1, keepdims=True))
-
-        def weigh(side, acc):
-            parts = []
-            for h in range(heads):
-                e = jnp.exp(s_scr[side, h] - mx[h, :, 0:1])
-                tot[h] += e
-                parts.append(e.astype(BF))
-            return acc + dot_nn(jnp.concatenate(parts, axis=1), v_scr[side])
-
-        first = jnp.where(reads[0], 0, 1)
-        last = jnp.where(reads[1], 2, 1)
-        acc = lax.fori_loop(first, last, weigh, jnp.zeros((rows, width), F32))
-        finish(p, place(p), rows, heads, acc, mx, tot, lanes, o_ref, lse_ref)
+        lay_heads(q_cat, q_ref[pl.ds(place(p), rows), :] * jnp.asarray(0.125, BF), lanes, heads)
+        query = p * rows + lax.broadcasted_iota(jnp.int32, (1, rows), 1)
+
+        def scores(side, tops):
+            spot = lax.broadcasted_iota(jnp.int32, (keys, 1), 0)
+            length = jnp.where(side == 0, sc[2], sc[3])
+            allowed = cross_allowed(query, spot, side, spill, length, me, padded, real)
+            k = jnp.where(side == 0, kv0[:, 0:width], kv1[:, 0:width])
+            return score_block(side, k, allowed, q_cat, s_scr, tops)
+
+        first = jnp.where(p * rows < spill, 0, 1)
+        last = jnp.where((p + 1) * rows > spill, 2, 1)
+        tops, totals, acc = attend(first, last, heads, scores, lambda side: v_scr[side], s_scr, p_scr, width)
+        finish(p, place(p), tops, totals, acc, lanes, o_ref, lse_ref)
 
 
 def spread(p, at, rows, heads, q, g, o_ref, lse_ref, lanes, q_cat, g_cat, stat):
@@ -211,7 +222,7 @@
     lay(g_ref, own, near, far)
     width = heads * HEAD
     extent = rows * blocks
-    me, spill, prev_spill = sc[0], sc[1], sc[2]
+    me, spill, prev_spill = sc[0], sc[1], sc[4]
     lanes = head_lanes(rows, width)
 
     def place(b):
@@ -321,7 +332,7 @@
         dkv1_ref[span, :] = dkv_scr[pieces + piece].astype(BF)
 
 
-def call(kernel, scalars, arrays, outs, scratch=()):
+def call(kernel, scalars, arrays, outs, scratch=(), time=2):
     vmem = pl.BlockSpec(memory_space=pltpu.VMEM)
     return pl.pallas_call(
         kernel,
@@ -330,7 +341,7 @@
         out_specs=jax.tree.map(lambda _: vmem, outs),
         scratch_shapes=scratch,
         compiler_params=pltpu.CompilerParams(vmem_limit_bytes=48 * 2**20),
-        cost_estimate=pl.CostEstimate(flops=1024, bytes_accessed=1024, transcendentals=0),
+        cost_estimate=pl.CostEstimate(flops=1024, bytes_accessed=int(time * 640000), transcendentals=0),
     )(scalars, *arrays)
 
 
@@ -348,9 +359,10 @@
             pltpu.VMEM((2 * blocks, rows, width), BF),
             pltpu.VMEM((2 * blocks, heads * rows, width), BF),
             pltpu.VMEM((2 * blocks, heads, rows, rows), F32),
-            pltpu.VMEM((heads, rows, rows), F32),
-            pltpu.VMEM((heads, rows, rows), F32),
+            pltpu.VMEM((heads * rows, width), BF),
+            pltpu.VMEM((heads * rows, rows), BF),
         ],
+        time=18,
     )
 
 
@@ -370,10 +382,11 @@
         ],
         [
             pltpu.VMEM((2, heads * keys, width), BF),
-            pltpu.VMEM((2, heads, rows, keys), F32),
-            pltpu.VMEM((heads, rows, keys), F32),
-            pltpu.VMEM((heads, rows, keys), F32),
+            pltpu.VMEM((2, heads, keys, rows), F32),
+            pltpu.VMEM((heads * rows, width), BF),
+            pltpu.VMEM((heads * keys, rows), BF),
         ],
+        time=9,
     )
 
 
@@ -409,10 +422,11 @@
             pltpu.VMEM((2 * blocks, rows, 2 * width), F32),
         ]
         + back_scratch(rows, heads, width, rows),
+        time=22,
     )
 
 
-def cross_backward(scalars, q, kv0, kv1, o, g, lse, blocks, real, pieces=2):
+def cross_backward(scalars, q, kv0, kv1, o, g, lse, blocks, real, pieces=1):
     extent, width = q.shape
     rows = extent // blocks
     heads = width // HEAD
@@ -433,6 +447,7 @@
             pltpu.VMEM((2 * pieces, step_keys, 2 * width), F32),
         ]
         + back_scratch(rows, heads, width, step_keys),
+        time=14,
     )
 
 
@@ -505,28 +520,118 @@
     return pre * cdf, cdf + pre * bell * 0.3989422804014327
 
 
-def qkv_kernel(at, low, far_low, near_low, ahead, far_ahead, near_ahead, weight, qkv, kvp, low_one, low_before):
-    rows = low.shape[0]
+def place_kernel(group, at, lengths, ids, *outs):
+    seq, me = at[0], at[1]
+    before = jnp.maximum(seq - 1, 0)
+    for i, out in enumerate(outs):
+        out[0] = me
+        out[2] = lengths[i, before]
+        out[3] = lengths[i, seq]
+        for slot, block, number in ((1, seq, seq), (4, before, seq - 1)):
+            rows = group // 128
+            part = ids[i, pl.ds(pl.multiple_of(block * rows, rows), rows), :]
+            out[slot] = jnp.sum(jnp.where(part < number, 1.0, 0.0)).astype(jnp.int32)
+        for slot in (5, 6, 7):
+            out[slot] = 0
+
+
+def norm_kernel(at, x, low):
+    rows = 256
+    for start in range(0, low.shape[0], rows):
+        span = slice(start, min(start + rows, low.shape[0]))
+        low[span, :] = normal_parts(x[span, :].astype(F32))[0].astype(BF)
+
+
+def lay_four(out, own, near, far, last):
+    rows = own.shape[0]
+    for k, ref in enumerate((own, near, far, last)):
+        out[k * rows : (k + 1) * rows, :] = ref[...]
+
+
+def qkv_kernel(i, rows, at, *refs):
+    weight, qkv, kvp = refs[8:]
     width = weight.shape[1] // 3
-    for out, own, far, near in ((low_one, low, far_low, near_low), (low_before, ahead, far_ahead, near_ahead)):
-        out[0:rows, :] = own[...]
-        out[rows : 2 * rows, :] = near[0:rows, :]
-        out[2 * rows : 3 * rows, :] = far[...]
-        out[3 * rows :, :] = near[rows:, :]
-
-    @pl.loop(0, 4)
-    def _(b):
-        block = pl.ds(pl.multiple_of(b * rows, rows), rows)
-        qkv[block, :] = dot_nn(low_one[block, :], weight[...]).astype(BF)
-        kvp[block, :] = dot_nn(low_before[block, :], weight[:, width:]).astype(BF)
-
-
-def self_out_kernel(at, own, near, far, x, wide_own, wide_other,
+    own = slice(i * rows, (i + 1) * rows)
+    for k in range(4):
+        block = slice(k * rows, (k + 1) * rows)
+        qkv[block, :] = dot_nn(refs[k][own, :], weight[...]).astype(BF)
+        kvp[block, :] = dot_nn(refs[4 + k][own, :], weight[:, width:]).astype(BF)
+
+
+def memory_kernel(size, at, own, near, far, last, weight, *outs):
+    count = len(outs) // 2
+    rows, keys = outs[:count], outs[count:]
+    for i in range(count):
+        span = slice(i * size, (i + 1) * size)
+        block = jnp.concatenate([ref[span, :] for ref in (own, near, far, last)], axis=0)
+        rows[i][...] = block
+        keys[i][...] = dot_nn(block, weight[...]).astype(BF)
+
+
+def hidden_kernel(rows, at, whole, inner, outer):
+    slot = 2 * rows
+    for i in range(inner.shape[0] // rows):
+        inner[i * rows : (i + 1) * rows, :] = whole[i * slot : i * slot + rows, :]
+        outer[i * rows : (i + 1) * rows, :] = whole[i * slot + rows : i * slot + 2 * rows, :]
+
+
+def hidden_grads_kernel(rows, at, pre_low, low, act, top, *refs):
+    before, out = (refs[0], refs[1]) if len(refs) == 2 else (None, refs[0])
+    step, slot = 256, 2 * rows
+    for i in range(pre_low.shape[1] // step):
+        for k, (left, right) in enumerate(((pre_low, low), (act, top))):
+            grad = dot_tn(left[:, i * step : (i + 1) * step], right[...])
+            for part in range(step // rows):
+                start = (i * step // rows + part) * slot + k * rows
+                block = grad[part * rows : (part + 1) * rows]
+                if before is not None:
+                    block = block + before[start : start + rows, :].astype(F32)
+                out[start : start + rows, :] = block.astype(BF)
+
+
+def near_kernel(at, keep, received, near, far):
+    rows = near.shape[0]
+    near[...] = keep[0:rows, :].astype(F32) + received[0:rows, :].astype(F32)
+    far[...] = (keep[rows:, :].astype(F32) + received[rows:, :].astype(F32)).astype(BF)
+
+
+def tree_kernel(at, keep, received, kept, sent):
+    rows = kept.shape[0]
+    kept[...] = keep[0:rows, :] + received[0:rows, :].astype(F32)
+    sent[...] = (keep[rows:, :] + received[rows:, :].astype(F32)).astype(BF)
+
+
+def output_kernel(at, after, near, far, out):
+    out[...] = (after[...] + near[...] + far[...].astype(F32)).astype(BF)
+
+
+def grad_x_kernel(i, at, x, before, near, far, back, out):
+    rows = out.shape[0]
+    plain, scale = normal_parts(x[i * rows : (i + 1) * rows, :].astype(F32))
+    grad = near[...] + far[...].astype(F32) + back[...].astype(F32)
+    out[...] = before[...] + normal_back(plain, scale, grad)
+
+
+def far_sum_kernel(at, near, far, out):
+    out[...] = (near[...] + far[...].astype(F32)).astype(BF)
+
+
+def memory_back_kernel(at, own, prev, rows_own, rows_prev, weight, grad, keep, send):
+    grad[...] = dot_tn(rows_own[...], own[...]) + dot_tn(rows_prev[...], prev[...])
+    rows = own.shape[0] // 4
+    for k, part in enumerate((own, prev)):
+        part = dot_nt(part[...], weight[...]).astype(BF)
+        for slot, out, place in ((0, keep, 0), (1, send, 0), (2, keep, 2), (3, send, 2)):
+            out[(place + k) * rows : (place + k + 1) * rows, :] = part[slot * rows : (slot + 1) * rows]
+
+
+def self_out_kernel(i, at, own, near, far, x, wide_own, wide_other,
                     low, after, plain, low_next, scale, first, second, rest):
     me = at[0]
     joined = received(own, near, far, me)
     low[...] = joined
-    total = x[...].astype(F32) + half_product(joined, wide_own, wide_other, me, 0)
+    rows = low.shape[0]
+    total = x[i * rows : (i + 1) * rows, :].astype(F32) + half_product(joined, wide_own, wide_other, me, 0)
     after[...] = total
     normed, scaled = normal_parts(total)
     plain[...] = normed
@@ -548,14 +653,11 @@
     low_next[...] = (normed * gain[...]).astype(BF)
 
 
-def mlp_kernel(at, low, near_low, far_low, top, near_top, far_top, inner, outer,
+def mlp_kernel(i, at, low, near_low, far_low, last_low, top, near_top, far_top, last_top, inner, outer,
                low_all, top_all, act, pre_low, grad_keep, grad_send, out_keep, out_send):
     rows = low.shape[0]
-    for out, own, near, far in ((low_all, low, near_low, far_low), (top_all, top, near_top, far_top)):
-        out[0:rows, :] = own[...]
-        out[rows : 2 * rows, :] = near[0:rows, :]
-        out[2 * rows : 3 * rows, :] = far[...]
-        out[3 * rows :, :] = near[rows:, :]
+    lay_four(low_all, low, near_low, far_low, last_low)
+    lay_four(top_all, *(ref.at[i * rows : (i + 1) * rows, :] for ref in (top, near_top, far_top, last_top)))
     for parity, grad, out in ((1, grad_send, out_send), (0, grad_keep, out_keep)):
 
         @pl.loop(0, 2)
@@ -571,13 +673,14 @@
             out[place, :] = dot_nn(act_block, outer[...]).astype(BF)
 
 
-def cross_back_kernel(at, near, far, plain, scale, gain, top, out_own, out_other,
+def cross_back_kernel(i, at, near, far, plain, scale, gain, top, out_own, out_other,
                       grad_after, branch_own, branch_other, grad_gain, first, second, rest):
     me = at[0]
     grad = near[...] + far[...].astype(F32)
     normed = plain[...]
     grad_gain[...] = jnp.sum(grad * normed, axis=0, keepdims=True)
-    total = top[...].astype(F32) + normal_back(normed, scale[...], grad * gain[...])
+    rows = near.shape[0]
+    total = top[i * rows : (i + 1) * rows, :].astype(F32) + normal_back(normed, scale[...], grad * gain[...])
     grad_after[...] = total
     mine, others = two_halves(total.astype(BF), me)
     branch_own[...] = mine
@@ -609,24 +712,49 @@
         own[:, span] = dot_tn(low_a, mine_a) + dot_tn(low_b, mine_b)
 
 
-def qkv_back_kernel(at, dq, dkv, back, weight, keep, send):
+def qkv_back_kernel(at, dq, dkv, dkv_prev, weight, keep, send, keep_prev, send_prev):
     rows = dq.shape[0] // 4
     width = dq.shape[1]
-    for parity, out in ((1, send), (0, keep)):
-
-        @pl.loop(0, 2)
-        def _(b):
-            block = pl.ds(pl.multiple_of((2 * b + parity) * rows, rows), rows)
-            place = pl.ds(pl.multiple_of(b * rows, rows), rows)
-            kv = (dkv[block, :].astype(F32) + back[block, :].astype(F32)).astype(BF)
-            grad = dot_nt(dq[block, :], weight[:, 0:width]) + dot_nt(kv, weight[:, width:])
+    for parity, out, out_prev in ((1, send, send_prev), (0, keep, keep_prev)):
+        for b in range(2):
+            block = slice((2 * b + parity) * rows, (2 * b + parity + 1) * rows)
+            place = slice(b * rows, (b + 1) * rows)
+            grad = dot_nt(dq[block, :], weight[:, 0:width]) + dot_nt(dkv[block, :], weight[:, width:])
             out[place, :] = grad.astype(BF)
-
-
-def qkv_grads_kernel(at, low, before, dq, dkv, dkv_prev, out):
+            out_prev[place, :] = dot_nt(dkv_prev[block, :], weight[:, width:]).astype(BF)
+
+
+def qkv_grads(i, refs, dq, dkv, dkv_prev):
+    rows = dq.shape[0] // 4
+    own = slice(i * rows, (i + 1) * rows)
+    queries, others = None, None
+    for k in range(4):
+        block = slice(k * rows, (k + 1) * rows)
+        low, before = refs[k][own, :], refs[4 + k][own, :]
+        query = dot_tn(low, dq[block, :])
+        other = dot_tn(low, dkv[block, :]) + dot_tn(before, dkv_prev[block, :])
+        queries, others = (query, other) if k == 0 else (queries + query, others + other)
+    return queries, others
+
+
+def qkv_grads_kernel(i, at, *refs):
+    dq, dkv, dkv_prev, out = refs[8:]
     width = dq.shape[1]
-    out[:, 0:width] = dot_tn(low[...], dq[...])
-    out[:, width:] = dot_tn(low[...], dkv[...]) + dot_tn(before[...], dkv_prev[...])
+    out[:, 0:width], out[:, width:] = qkv_grads(i, refs, dq, dkv, dkv_prev)
+
+
+def last_qkv_grads_kernel(i, offsets, at, *refs):
+    dq, dkv, dkv_prev, earlier, keep, send, total = refs[8:]
+    width = dq.shape[1]
+    queries, others = qkv_grads(i, refs, dq, dkv, dkv_prev)
+    total[:, 0:width] = earlier[:, 0:width] + queries
+    total[:, width:] = earlier[:, width:] + others
+    half = len(offsets) // 2
+    rows = total.shape[0] // len(offsets)
+    for i, offset in enumerate(offsets):
+        out = keep if i < half else send
+        start = pl.multiple_of((at[0] ^ offset) * rows, rows)
+        out[(i % half) * rows : (i % half + 1) * rows, :] = total[pl.ds(start, rows), :].astype(out.dtype)
 
 
 def shape(rows, columns, dtype=BF):
@@ -647,10 +775,6 @@
     return lax.ppermute(block, "seq", route)
 
 
-def near_rows(own, far):
-    return flip(jnp.concatenate([own, far], axis=0), "mem", 1)
-
-
 def far_slots(part):
     rows = part.shape[0] // 4
     return part[:rows], part[rows : 2 * rows], flip(part[2 * rows :], "mem", 2)
@@ -661,15 +785,10 @@
     return own, flip(jnp.concatenate([side, far[rows:]], axis=0), "mem", 1), far
 
 
-def lay_slots(own, near, far):
-    rows = own.shape[0]
-    return jnp.concatenate([own, near[:rows], far[:rows], near[rows:]], axis=0)
-
-
-def near_sum(keep, send):
-    rows = keep.shape[0] // 2
-    total = keep.astype(F32) + flip(send, "mem", 1).astype(F32)
-    return total[:rows], total[rows:].astype(BF)
+def near_sum(place, keep, send):
+    rows, columns = keep.shape
+    outs = [shape(rows // 2, columns, F32), shape(rows // 2, columns)]
+    return call(near_kernel, place, (keep, flip(send, "mem", 1)), outs, time=1)
 
 
 def seq_bits():
@@ -709,15 +828,18 @@
 
 
 def reorder_kernel(rows, offsets, groups, at, *refs):
-    out = refs[-1]
+    keep, send = refs[-2:]
+    half = len(offsets) // 2
     for i, offset in enumerate(offsets):
         start = pl.multiple_of((at[0] ^ offset) * rows, rows)
+        out = keep if i < half else send
+        place = slice((i % half) * rows, (i % half + 1) * rows)
         for column, terms in groups:
             total = None
             for term, first, columns in terms:
                 part = refs[term][pl.ds(start, rows), first : first + columns].astype(F32)
                 total = part if total is None else total + part
-            out[i * rows : (i + 1) * rows, column : column + columns] = total.astype(BF)
+            out[place, column : column + columns] = total.astype(out.dtype)
 
 
 def reorder(arrays, groups, seq, bits):
@@ -727,9 +849,8 @@
     for terms in groups:
         placed.append((column, terms))
         column += terms[0][2]
-    out = jax.ShapeDtypeStruct((size, column), BF)
     kernel = functools.partial(reorder_kernel, size // len(offsets), offsets, placed)
-    return call(kernel, seq.reshape(1), arrays, out)
+    return call(kernel, seq.reshape(1), arrays, [shape(size // 2, column, F32), shape(size // 2, column)], time=column // 300)
 
 
 def pack_kernel(width, half, at, *refs):
@@ -764,7 +885,7 @@
     out[:, 2 * narrow + broad :] = far[:, sides:]
 
 
-def unpack_kernel(width, narrow, broad, at, kept, message, far, near, qkv, first, last):
+def unpack_kernel(width, narrow, broad, at, kept, message, far, near, qkv, first):
     me = at[0]
     start = 2 * narrow
     heads = [kept[:, 0:narrow], near[:, 0:narrow], far[:, 0:narrow], near[:, narrow:start]]
@@ -772,10 +893,9 @@
     sides = [ref[:, at_k : at_k + broad] for ref, at_k in zip(sides, (start, start, start, start + broad))]
     heads = join_pieces(heads, me, 0)
     sides = join_pieces(sides, me, 0)
+    qkv[...] = heads[:, 0 : 3 * width]
     pair = broad - 128 - (broad - 128) // 3
-    qkv[...] = heads[:, 0 : 3 * width]
-    first[...] = jnp.concatenate([sides[:, 0:pair], heads[:, 3 * width :]], axis=1)
-    last[...] = sides[:, pair:]
+    first[...] = jnp.concatenate([sides[:, 0:pair], heads[:, 3 * width :], sides[:, pair:]], axis=1)
 
 
 class Stay:
@@ -869,250 +989,257 @@
         [shape(wrows, 2 * narrow), shape(wrows, 2 * (narrow + broad))],
     )
     far = flip(message, "mem", 2)
-    norm_ones = [normal_parts(inputs[i].astype(F32)) for i in range(MICRO)]
-    lows = [parts[0].astype(BF) for parts in norm_ones]
-    befores = [shifted(low, 1) for low in lows]
-    far_lows = [flip(lows[0], "mem", 2)]
+    x_rows, tops = inputs.reshape(MICRO * tok, D), cotangent.reshape(MICRO * tok, D)
+    lows = call(norm_kernel, place, (x_rows,), shape(MICRO * tok, D))
+    far, lows = lax.optimization_barrier((far, lows))
+    befores = shifted(lows, 1)
+    far_lows, near_lows = flip(lows, "mem", 2), flip(lows, "mem", 1)
+    memory_own = jnp.pad(memory.reshape(MICRO, real, D), ((0, 0), (0, padded - real), (0, 0)))
+    memory_own = memory_own.reshape(MICRO * padded, D)
+    smem = pl.BlockSpec(memory_space=pltpu.SMEM)
+    ids = page_ids.reshape(MICRO, -1, 128)
+    places = pl.pallas_call(
+        functools.partial(place_kernel, group),
+        out_shape=[jax.ShapeDtypeStruct((8,), jnp.int32)] * MICRO,
+        in_specs=[smem, smem, pl.BlockSpec(memory_space=pltpu.VMEM)],
+        out_specs=[smem] * MICRO,
+    )(jnp.stack([seq, me]), memory_length, ids)
     near = call(
         functools.partial(repack_kernel, narrow, broad), place, (kept, message, far),
         shape(*message.shape),
     )
     near = flip(near, "mem", 1)
-    qkv_part, first_part, last_part = call(
+    qkv_part, first_part = call(
         functools.partial(unpack_kernel, width, narrow, broad), place, (kept, message, far, near),
-        [shape(blocks * wrows, columns) for columns in (3 * width, 2 * half + 2 * width, half + 128)],
+        [shape(blocks * wrows, columns) for columns in (3 * width, 3 * half + 128 + 2 * width)],
     )
 
     state = {}
     hidden = mlp_in.shape[0]
-    memory_own = jnp.pad(memory.reshape(MICRO, real, D), ((0, 0), (0, padded - real), (0, 0)))
-    memory_own = memory_own.reshape(MICRO * padded, D)
     stage = seq_stage(qkv_part, bits[0])
-    stage, first_part, befores[0] = lax.optimization_barrier((stage, first_part, befores[0]))
-    far_befores = [flip(befores[0], "mem", 2)]
+    hidden_part = jnp.concatenate([mlp_in, mlp_out], axis=0)
+    stage, memory_own, places, hidden_part = lax.optimization_barrier((stage, memory_own, places, hidden_part))
+    memory_before = shifted(memory_own, 1)
     for bit in bits[1:-1]:
         stage = seq_stage(stage, bit)
-    stage, first_part, lows[1], befores[1] = lax.optimization_barrier((stage, first_part, lows[1], befores[1]))
-    far_lows.append(flip(lows[1], "mem", 2))
-    far_befores.append(flip(befores[1], "mem", 2))
+    stage, first_part, befores, far_lows = lax.optimization_barrier((stage, first_part, befores, far_lows))
+    last_lows = flip(far_lows, "mem", 1)
+    far_befores, near_befores = flip(befores, "mem", 2), flip(befores, "mem", 1)
     first_stage = first_part
     for bit in bits[:-2]:
         first_stage = seq_stage(first_stage, bit)
     (qkv_full,) = assemble(stage, flip(stage, "seq", bits[-1]), seq, bits, [3 * width])
+    gathered = [lows, near_lows, far_lows, last_lows, befores, near_befores, far_befores, flip(far_befores, "mem", 1)]
 
     def first_side():
         (first,) = yield 1, lambda: (first_stage,)
         first = seq_stage(first, bits[-2])
         (first,) = yield 2, lambda: (first,)
+        cut = 2 * half + 2 * width
+        first, last = first[:, :cut], first[:, cut:]
         first = first, flip(first, "seq", bits[-1])
-        first = yield 3, lambda: first
+        *first, last = yield 3, lambda: (*first, last)
         state["wide_own"], state["ckv"] = assemble(*first, seq, bits, [2 * half, 2 * width])
         state["wide_other"] = flip(state["wide_own"], "mem", 1)
-
-    def last_side():
-        (last,) = yield 2, lambda: (last_part,)
-        for bit in bits[:-2]:
-            last = seq_stage(last, bit)
-        (last,) = yield 3, lambda: (last,)
-        last = seq_stage(last, bits[-2])
-        (last,) = yield 5, lambda: (last,)
         last = last, flip(last, "seq", bits[-1])
-        last = yield 7, lambda: last
+        last = yield 5, lambda: last
         state["cout_own"], gain = assemble(*last, seq, bits, [half, 128])
-        state["cout_other"] = flip(state["cout_own"], "mem", 1)
         state["gain"] = gain[:, 0].astype(F32)[None, :]
+        (own,) = yield 6, lambda: (state["cout_own"],)
+        state["cout_other"] = flip(own, "mem", 1)
 
     def memory_side():
-        (rows,) = yield 1, lambda: (memory_own,)
-        rows = rows, shifted(rows, 1)
-        rows = yield 2, lambda: rows
+        rows = yield 1, lambda: (memory_own, memory_before)
         rows = jnp.concatenate(rows, axis=0)
-        far = flip(rows, "mem", 2)
-        rows, far = yield 4, lambda: (rows, far)
-        pieces = rows, near_rows(rows, far), far
-        pieces = yield 5, lambda: pieces
-        size = MICRO * padded
-        near = pieces[1][: 2 * size], pieces[1][2 * size :]
-        slots = pieces[0], near[0], pieces[2], near[1]
-        rows = [
-            jnp.concatenate([p[i * padded : (i + 1) * padded] for p in slots], axis=0) for i in range(2 * MICRO)
-        ]
-        state["rows"] = rows[:MICRO]
-        keys = [dot_nn(r, state["ckv"]).astype(BF) for r in rows]
-        state["mem_kv"], state["mem_prev"] = keys[:MICRO], keys[MICRO:]
+        far, near = flip(rows, "mem", 2), flip(rows, "mem", 1)
+        rows, near, far = yield 3, lambda: (rows, near, far)
+        pieces = rows, near, far, flip(far, "mem", 1)
+        pieces = yield 4, lambda: pieces
+        whole = blocks * padded
+        outs = [shape(whole, D)] * (2 * MICRO) + [shape(whole, 2 * width)] * (2 * MICRO)
+        got = call(functools.partial(memory_kernel, padded), place, (*pieces, state["ckv"]), outs, time=6)
+        state["rows"], state["rows_prev"], state["mem_kv"], state["mem_prev"] = (
+            got[k * MICRO : (k + 1) * MICRO] for k in range(4)
+        )
+
+    def top_side():
+        (top,) = yield 2, lambda: (tops,)
+        far, near = flip(top, "mem", 2), flip(top, "mem", 1)
+        far, near = yield 4, lambda: (far, near)
+        state["top"] = tops, near, far, flip(far, "mem", 1)
 
     def hidden_side():
-        (part,) = yield 1, lambda: (jnp.concatenate([mlp_in, mlp_out], axis=0),)
+        (part,) = yield 3, lambda: (hidden_part,)
         whole = lax.all_gather(part, "seq", axis=0, tiled=True)
         (whole,) = yield 9, lambda: (whole,)
-        whole = whole.reshape(-1, 2, hidden, D)
-        state["inner"] = whole[:, 0].reshape(-1, D)
-        state["outer"] = whole[:, 1].reshape(-1, D)
-        grads = yield 13, lambda: (state["grad_inner"], state["grad_outer"])
-        both = [sum(g).astype(BF).reshape(-1, 1, hidden, D) for g in grads]
-        both = jnp.concatenate(both, axis=1).reshape(-1, D)
-        both = lax.psum_scatter(both, "seq", scatter_dimension=0, tiled=True)
-        state["hidden_grads"] = both[:hidden].astype(F32), both[hidden:].astype(F32)
+        both = [shape(whole.shape[0] // 2, D)] * 2
+        state["inner"], state["outer"] = call(functools.partial(hidden_kernel, hidden), place, (whole,), both)
+        kernel = functools.partial(hidden_grads_kernel, hidden)
+        arrays = yield 12, lambda: state["grad_hidden"][0]
+        grads = call(kernel, place, arrays, shape(2 * D, D), time=9)
+        arrays = yield 13, lambda: (*state["grad_hidden"][1], grads)
+        grads = call(kernel, place, arrays, shape(2 * D, D), time=9)
+        (grads,) = yield 14, lambda: (grads,)
+        grads = lax.psum_scatter(grads, "seq", scatter_dimension=0, tiled=True)
+        (grads,) = yield 18, lambda: (grads,)
+        state["hidden_grads"] = grads[:hidden].astype(F32), grads[hidden:].astype(F32)
 
     order = turned[::-1]
 
-    def seq_start(tensor, bit):
-        cut = tensor.shape[0] // 2
-        return tensor[:cut].astype(F32), flip(tensor[cut:].astype(BF), "seq", bit)
-
     def seq_next(kept, received, bit):
-        return seq_start(kept + received.astype(F32), bit)
+        rows, columns = kept.shape[0] // 2, kept.shape[1]
+        kept, sent = call(tree_kernel, place, (kept, received), [shape(rows, columns, F32), shape(rows, columns)])
+        return kept, flip(sent, "seq", bit)
+
+    def half_grads(names):
+        arrays = [part for low, mine, others in names for part in (*low, *mine, *others)]
+        outs = [shape(D, len(names) * half, F32), shape(D, len(names) * half)]
+        return call(functools.partial(half_grads_kernel, len(names)), place, arrays, outs, time=2 * len(names))
 
     def tree_side(name, arrays, groups, ticks):
-        for bit, tick in zip(order, ticks):
-            if bit == order[0]:
-                arrays = yield tick, lambda: arrays
-                pair = seq_start(reorder(arrays, groups, seq, turned), bit)
-            else:
-                pair = yield tick, lambda: pair
-                pair = seq_next(*pair, bit)
+        arrays = yield ticks[0], lambda: arrays
+        kept, sent = reorder(arrays, groups, seq, turned)
+        pair = kept, flip(sent, "seq", order[0])
+        for bit, tick in zip(order[1:], ticks[1:]):
+            pair = yield tick, lambda: pair
+            pair = seq_next(*pair, bit)
         for bit in order[len(ticks) :]:
             pair = seq_next(*pair, bit)
         state[name] = pair
-
-    def half_grads(names):
-        arrays = [part for low, mine, others in names for part in (*low, *mine, *others)]
-        outs = [shape(D, len(names) * half, F32), shape(D, len(names) * half)]
-        return call(functools.partial(half_grads_kernel, len(names)), place, arrays, outs)
 
     def cout_side():
         names, gains = yield 15, lambda: (state["grad_cout"], state["grad_gain_three"])
         own, other = half_grads([list(zip(*names))])
         gains = jnp.pad((gains[0] + gains[1]).reshape(D, 1), ((0, 0), (0, 127)))
         groups = [[(0, 0, half), (1, 0, half)], [(2, 0, 128)]]
-        yield from tree_side("cout", (own, flip(other, "mem", 1), gains), groups, (16, 18, 20))
+        yield from tree_side("cout", (own, flip(other, "mem", 1), gains), groups, (16, 18, 19))
 
     def wide_side():
         out, query, ckv = yield 17, lambda: (state["grad_out"], state["grad_cquery"], state["grad_ckv"])
         own, other = half_grads([list(zip(*out)), list(zip(*query))])
         groups = [[(0, 0, 2 * half), (1, 0, 2 * half)], [(2, 0, 2 * width), (3, 0, 2 * width)]]
-        yield from tree_side("wide", (own, flip(other, "mem", 1), *ckv), groups, (18, 20, 21))
+        yield from tree_side("wide", (own, flip(other, "mem", 1), *ckv), groups, (18, 19))
 
     def qkv_side():
-        arrays = yield 19, lambda: state["grad_qkv"]
-        groups = [[(0, 0, 3 * width), (1, 0, 3 * width)]]
-        pair = seq_start(reorder(arrays, groups, seq, turned), order[0])
-        pair = yield 21, lambda: pair
-        state["qkv"] = seq_next(*pair, order[1])
-
-    def spill_of(micro, block):
-        ids = lax.dynamic_slice_in_dim(page_ids[micro], jnp.maximum(block, 0) * group, group, 0)
-        return jnp.sum((ids < block).astype(jnp.int32))
-
-    for name in ("inner", "outer", "gain_three", "cout", "out", "cquery", "ckv", "qkv"):
+        kept, sent = yield 19, lambda: state["grad_qkv"][-1]
+        state["qkv"] = kept, flip(sent, "seq", order[0])
+
+    for name in ("hidden", "gain_three", "cout", "out", "cquery", "ckv", "qkv"):
         state["grad_" + name] = []
     quarter = [shape(tok, width), shape(tok, width), shape(2 * tok, width)]
     rounded, exact, column = shape(tok, D), shape(tok, D, F32), shape(tok, 1, F32)
-    half_rows = shape(tok, half)
+    half_rows, whole, pair_rows = shape(tok, half), shape(group, D), shape(2 * tok, D)
+
+    def far_pieces(pieces):
+        return pieces[0], pieces[1], flip(pieces[2], "mem", 2)
 
     def stream(i):
-        spill = spill_of(i, seq)
-        self_at = jnp.stack([me, spill, spill_of(i, seq - 1)])
-        before = memory_length[i][jnp.maximum(seq - 1, 0)]
-        cross_at = jnp.stack([me, spill, before, memory_length[i][seq]])
-
-        low, far_low, ahead, far_ahead = yield lows[i], far_lows[i], befores[i], far_befores[i]
-        qkv, kv_prev, low_one, low_before = call(
-            qkv_kernel, place, (low, far_low, near_rows(low, far_low), ahead, far_ahead, near_rows(ahead, far_ahead), qkv_full),
-            [shape(group, 3 * width), shape(group, 2 * width), shape(group, D), shape(group, D)],
+        at = places[i]
+        pieces = yield gathered
+        qkv, kv_prev = call(
+            functools.partial(qkv_kernel, i, tok), place, (*pieces, qkv_full),
+            [shape(group, 3 * width), shape(group, 2 * width)], time=5,
         )
         if i == 0:
             qkv, kv_prev = yield Stay((qkv, kv_prev))
-        self_o, self_lse = self_forward(self_at, qkv, kv_prev, blocks)
+        self_o, self_lse = self_forward(at, qkv, kv_prev, blocks)
         self_lse = yield self_lse
 
         pieces = yield far_slots(self_o)
         self_low, after_self, plain_two, low_two, scale_two, *pieces = call(
-            self_out_kernel, place, (*near_slots(*pieces), inputs[i], state["wide_own"], state["wide_other"]),
-            [rounded, exact, exact, rounded, column, *quarter],
+            functools.partial(self_out_kernel, i), place,
+            (*near_slots(*pieces), x_rows, state["wide_own"], state["wide_other"]),
+            [rounded, exact, exact, rounded, column, *quarter], time=4,
         )
         scale_two = yield scale_two
 
-        pieces, top = yield (pieces[0], pieces[1], flip(pieces[2], "mem", 2)), cotangent[i]
-        far_top = flip(top, "mem", 2)
+        pieces = yield far_pieces(pieces)
         mem_kv, mem_prev = state["mem_kv"][i], state["mem_prev"][i]
-        cross_o, cross_lse, cross_q = cross_forward(cross_at, near_slots(*pieces), mem_prev, mem_kv, blocks, real)
+        cross_o, cross_lse, cross_q = cross_forward(at, near_slots(*pieces), mem_prev, mem_kv, blocks, real)
         cross_lse = yield cross_lse
 
-        pieces, far_top = yield far_slots(cross_o), far_top
+        pieces = yield far_slots(cross_o)
         cross_low, after_cross, plain_three, scale_three, low_three = call(
             cross_out_kernel, place,
             (*near_slots(*pieces), after_self, state["cout_own"], state["cout_other"], state["gain"]),
-            [rounded, exact, exact, column, rounded],
+            [rounded, exact, exact, column, rounded], time=3,
         )
-        near_top = near_rows(top, far_top)
         scale_three = yield scale_three
 
-        low_three, far_three = yield low_three, flip(low_three, "mem", 2)
-        whole, pair = shape(group, D), shape(2 * tok, D)
+        low_three, near, far = yield low_three, flip(low_three, "mem", 1), flip(low_three, "mem", 2)
         low_all, top_all, act, pre_low, grad_keep, grad_send, out_keep, out_send = call(
-            mlp_kernel, place,
-            (low_three, near_rows(low_three, far_three), far_three, top, near_top, far_top, state["inner"], state["outer"]),
-            [whole, whole, whole, whole, pair, pair, pair, pair],
+            functools.partial(mlp_kernel, i), place,
+            (low_three, near, far, flip(far, "mem", 1), *state["top"], state["inner"], state["outer"]),
+            [whole, whole, whole, whole, pair_rows, pair_rows, pair_rows, pair_rows], time=15,
         )
-        near, far = near_sum(grad_keep, grad_send)
-        near = yield near
-
-        far, act, out_send = yield flip(far, "mem", 2), act, out_send
+        state["grad_hidden"].append((pre_low, low_all, act, top_all))
+        grad_keep = yield grad_keep
+
+        near, far = near_sum(place, grad_keep, grad_send)
+        far, out_send = yield flip(far, "mem", 2), out_send
         grad_after_cross, mine, others, gain_three, *pieces = call(
-            cross_back_kernel, place,
-            (near, far, plain_three, scale_three, state["gain"], cotangent[i], state["cout_own"], state["cout_other"]),
-            [exact, half_rows, half_rows, shape(1, D, F32), *quarter],
+            functools.partial(cross_back_kernel, i), place,
+            (near, far, plain_three, scale_three, state["gain"], tops, state["cout_own"], state["cout_other"]),
+            [exact, half_rows, half_rows, shape(1, D, F32), *quarter], time=3,
         )
-        state["grad_inner"].append(dot_tn(pre_low, low_all))
-        state["grad_outer"].append(dot_tn(act, top_all))
         state["grad_gain_three"].append(gain_three)
         state["grad_cout"].append((cross_low, mine, others))
-        out_near, out_far = near_sum(out_keep, out_send)
         grad_after_cross = yield grad_after_cross
 
-        pieces, out_far = yield (pieces[0], pieces[1], flip(pieces[2], "mem", 2)), out_far
+        pieces, out_send = yield far_pieces(pieces), out_send
         dcq, dmem_prev, dmem = cross_backward(
-            cross_at, cross_q, mem_prev, mem_kv, cross_o, near_slots(*pieces), cross_lse, blocks, real
+            at, cross_q, mem_prev, mem_kv, cross_o, near_slots(*pieces), cross_lse, blocks, real
         )
+        out_near, out_far = near_sum(place, out_keep, out_send)
         dmem = yield dmem
 
-        back = shifted(dmem_prev, -1)
         pieces, out_far = yield far_slots(dcq), out_far
-        output = (after_cross + out_near + flip(out_far, "mem", 2).astype(F32)).astype(BF)
+        out_far = flip(out_far, "mem", 2)
         grad_after_self, query_mine, query_others, mine, others, *pieces = call(
             self_back_kernel, place,
             (*near_slots(*pieces), plain_two, scale_two, grad_after_cross, state["wide_own"], state["wide_other"]),
-            [exact, half_rows, half_rows, half_rows, half_rows, *quarter],
+            [exact, half_rows, half_rows, half_rows, half_rows, *quarter], time=4,
         )
         state["grad_cquery"].append((low_two, query_mine, query_others))
         state["grad_out"].append((self_low, mine, others))
-        dmem = (dmem.astype(F32) + back.astype(F32)).astype(BF)
-        state["grad_ckv"].append(dot_tn(state["rows"][i], dmem))
+        mem_rows = shape(4 * padded, D)
+        grad_ckv, mem_keep, mem_send = call(
+            memory_back_kernel, place, (dmem, dmem_prev, state["rows"][i], state["rows_prev"][i], state["ckv"]),
+            [shape(D, 2 * width, F32), mem_rows, mem_rows], time=5,
+        )
+        state["grad_ckv"].append(grad_ckv)
         grad_after_self = yield grad_after_self
 
-        pieces, dmem = yield (pieces[0], pieces[1], flip(pieces[2], "mem", 2)), dmem
-        dq, dkv, dkv_prev = self_backward(self_at, qkv, kv_prev, self_o, near_slots(*pieces), self_lse, blocks)
-        state["grad_qkv"].append(
-            call(qkv_grads_kernel, place, (low_one, low_before, dq, dkv, dkv_prev), shape(D, 3 * width, F32))
+        pieces, out_far = yield far_pieces(pieces), out_far
+        dq, dkv, dkv_prev = self_backward(at, qkv, kv_prev, self_o, near_slots(*pieces), self_lse, blocks)
+        grads = (*gathered, dq, dkv, dkv_prev)
+        if i == 0:
+            grads = call(functools.partial(qkv_grads_kernel, i), place, grads, shape(D, 3 * width, F32), time=7)
+        else:
+            grads = call(
+                functools.partial(last_qkv_grads_kernel, i, seq_offsets(turned)), seq.reshape(1),
+                (*grads, state["grad_qkv"][0]), [shape(D // 2, 3 * width, F32), shape(D // 2, 3 * width)],
+                [pltpu.VMEM((D, 3 * width), F32)], time=8,
+            )
+        state["grad_qkv"].append(grads)
+        output = call(output_kernel, place, (after_cross, out_near, out_far), rounded)
+        keep, send, keep_prev, send_prev = call(
+            qkv_back_kernel, place, (dq, dkv, dkv_prev, qkv_full), [pair_rows] * 4, time=5
         )
-        mem_part = dot_nt(dmem, state["ckv"]).astype(BF)
-        dkv = yield dkv
-
-        back, mem_part = yield shifted(dkv_prev, -1), mem_part
-        keep, send = call(qkv_back_kernel, place, (dq, dkv, back, qkv_full), [pair, pair])
-        near, far = near_sum(keep, send)
-        slots = [mem_part[k * padded : (k + 1) * padded] for k in (0, 2, 1, 3)]
-        mem_near, mem_far = near_sum(jnp.concatenate(slots[:2], axis=0), jnp.concatenate(slots[2:], axis=0))
-        grad_mem = (mem_near + flip(mem_far, "mem", 2).astype(F32))[:real].reshape(1, real, D)
-        near = yield near
-
-        far = yield flip(far, "mem", 2)
-        plain_one, scale_one = norm_ones[i]
-        grad_x = grad_after_self + normal_back(plain_one, scale_one, near + far.astype(F32))
+        keep = yield keep
+
+        near_prev, far_prev = near_sum(place, keep_prev, send_prev)
+        near, far = near_sum(place, keep, send)
+        far_prev, far, mem_send = yield flip(far_prev, "mem", 2), flip(far, "mem", 2), mem_send
+        back = shifted(call(far_sum_kernel, place, (near_prev, far_prev), rounded), -1)
+        mem_near, mem_far = near_sum(place, mem_keep, mem_send)
+        mem_all = call(far_sum_kernel, place, (mem_near, flip(mem_far, "mem", 2)), shape(2 * padded, D))
+        mem_back = shifted(mem_all[padded:], -1)
+        grad_mem = (mem_all[:padded].astype(F32) + mem_back.astype(F32))[:real].reshape(1, real, D)
+        grad_x = call(functools.partial(grad_x_kernel, i), place, (x_rows, grad_after_self, near, far, back), exact)
         return output, grad_x, grad_mem
 
-    sides = [first_side(), last_side(), memory_side(), hidden_side(), cout_side(), wide_side(), qkv_side()]
+    sides = [first_side(), memory_side(), top_side(), hidden_side(), cout_side(), wide_side(), qkv_side()]
     done = interleave([stream(i) for i in range(MICRO)], sides)
 
     def wide_finish(own):
@@ -1150,7 +1277,7 @@
     grad_out, plain_cquery = [
         join_halves(own[:, k * half : (k + 1) * half], near[:, k * half : (k + 1) * half]) for k in range(2)
     ]
-    plain_qkv = head_finish(seq_finish(state["qkv"], order[2:]), 3)
+    plain_qkv = head_finish(seq_finish(state["qkv"], order[1:]), 3)
 
     def gained(gain, weights, plains):
         scale = gain.astype(F32)[:, None]

time: 805 us -> 743 us (0.923)
  Pallas kernels: 210 us -> 275 us
  other arithmetic: 71.6 us -> 19.5 us
  waiting for transfers between devices: 235 us -> 192 us
  matrix products: 35.8 us -> 0 us
  local copies, waits for them, and re-layouts: 77.4 us -> 102 us
  starting transfers between devices: 147 us -> 126 us
    pallas_call x35 -> x65, Pallas kernels: 210 us -> 273 us  [call(): pl.pallas_call(kernel, out_shape=outs, in_specs=[pl.BlockSpec(memory_spac...]
    ppermute x90 -> x92, waiting for transfers between devices: 223 us -> 171 us  [flip(): lax.ppermute(block, axis, [(i, i ^ bit) for i in range(lax.axis_size(axis...]
    unnamed x414 -> x481, local copies, waits for them, and re-layouts: 41.7 us -> 86.3 us
    dot_general x12 -> x0, matrix products: 35.8 us -> none  [the longest x6 28.5 us: dot_tn(): lax.dot_general(left, right, (((0,), (0,)), ((), ())), preferred_element_...]
    ppermute x90 -> x92, starting transfers between devices: 127 us -> 106 us  [flip(): lax.ppermute(block, axis, [(i, i ^ bit) for i in range(lax.axis_size(axis...]
    slice x32 -> x4, local copies, waits for them, and re-layouts: 15.9 us -> 2 us  [the longest x2 1.06 us: first_side(): first, last = (first[:, :cut], first[:, cut:])]
    concatenate x13 -> x1, other arithmetic: 12.8 us -> 1.86 us  [shards(): hidden_part = jnp.concatenate([mlp_in, mlp_out], axis=0)]
    convert_element_type x8 -> x2, other arithmetic: 11 us -> 1.22 us  [the longest x1 1.08 us: hidden_side(): grads[hidden:].astype(F32)]
  transfers between devices with their start and end apart: 99 -> 100, of which waited for: 32 -> 32; matrix products, arithmetic and copies ran while one was open for 18% -> 5% of each run, Pallas kernels for 22% -> 37%
where the time goes in v3:
time: 743 us; the launch traced here: 731 us
  Pallas kernels  275 us (37%)
  waiting for transfers between devices  192 us (26%)
  starting transfers between devices  126 us (17%)
  local copies, waits for them, and re-layouts  102 us (14%)
  other arithmetic  19.5 us (3%)
  between operations  17.2 us (2%)
    pallas_call x65, Pallas kernels, call(): pl.pallas_call(kernel, out_shape=outs, in_specs=[pl.BlockSpec(memory_spac...  273 us
    ppermute x92, waiting for transfers between devices, flip(): lax.ppermute(block, axis, [(i, i ^ bit) for i in range(lax.axis_size(axis...  171 us
    ppermute x92, starting transfers between devices, flip(): lax.ppermute(block, axis, [(i, i ^ bit) for i in range(lax.axis_size(axis...  106 us
    unnamed x481, local copies, waits for them, and re-layouts  86.3 us
    ppermute x6, waiting for transfers between devices, shifted(): return lax.ppermute(block, 'seq', route)  20.3 us
    ppermute x6, starting transfers between devices, shifted(): return lax.ppermute(block, 'seq', route)  19.5 us
  transfers between devices with their start and end apart: 100, of which 32 were waited for; matrix products, arithmetic and copies ran while one was open for 5% of the time, Pallas kernels for 37%

profile of v3, /device:TPU:0, one launch (start us, length us, event | category | flops | bytes accessed | tf_op | source)
XLA Modules:
  0.0 731.2 jit_solution(8315689708542242953)
XLA Ops:
  54.2 9.4 %collective-permute-done.4 = bf16[256,768]{1,0:T(8,128)(2,1)S(1)} collective-permute-done((bf16[256,768]{1,0:T(8,128)(2,1)S(1)}, bf16[256,768]{1,0:T(8,128)(2,1)S(1)}, u32[]{:S(2)}, u32[]{:S(2)}) %collective-permute-start.4) | collective-permute-done | bytes 393248 | tf_op jit(solution)/shard_map/ppermute | solution.py:769
  67.5 14.7 %collective-permute-start.11 = (bf16[512,768]{1,0:T(8,128)(2,1)S(1)}, bf16[512,768]{1,0:T(8,128)(2,1)S(1)}, u32[]{:S(2)}, u32[]{:S(2)}) collective-permute-start(bf16[512,768]{1,0:T(8,128)(2,1)S(1)} %pad_maximum_fusion.5.first), channel_id=1, source_target_pairs={{0,4},{4,0},{8,12},{12,8},{16,20},{20,16},{24,28},{28,24},{1,5},{5... | collective-permute-start | bytes 2359304 | tf_op jit(solution)/shard_map/ppermute | solution.py:769
  82.7 8.7 %collective-permute-done.12 = bf16[128,2176]{1,0:T(8,128)(2,1)S(1)} collective-permute-done((bf16[128,2176]{1,0:T(8,128)(2,1)S(1)}, bf16[128,2176]{1,0:T(8,128)(2,1)S(1)}, u32[]{:S(2)}, u32[]{:S(2)}) %collective-permute-start.12) | collective-permute-done | bytes 557088 | tf_op jit(solution)/shard_map/ppermute | solution.py:769
  98.4 9.8 %collective-permute-start.13 = (bf16[320,1024]{1,0:T(8,128)(2,1)S(1)}, bf16[320,1024]{1,0:T(8,128)(2,1)S(1)}, u32[]{:S(2)}, u32[]{:S(2)}) collective-permute-start(bf16[320,1024]{1,0:T(8,128)(2,1)S(1)} %bitcast.119), channel_id=1, source_target_pairs={{0,4},{4,8},{8,12},{12,16},{16,20},{20,24},{24,28},{1,5},{5,9},{9,... | collective-permute-start | bytes 1966088 | tf_op jit(solution)/shard_map/ppermute | solution.py:775
  126.0 10.0 %shard_map.304 = (bf16[1024,256]{1,0:T(8,128)(2,1)S(1)}, f32[8,1024]{1,0:T(8,128)S(1)}) custom-call(s32[8]{0:T(128)S(1)} %copy-done.208, bf16[1024,768]{1,0:T(8,128)(2,1)S(1)} %copy-done.22, bf16[1024,512]{1,0:T(8,128)(2,1)S(1)} %get-tuple-element.372.kvp), custom_call_target="tpu_custom_call" | custom-call | flops 1024 | bytes 11520000 | tf_op jit(solution)/shard_map/pallas_call | solution.py:337
  136.0 12.8 %collective-permute-done.15 = bf16[256,2176]{1,0:T(8,128)(2,1)S(1)} collective-permute-done((bf16[256,2176]{1,0:T(8,128)(2,1)S(1)}, bf16[256,2176]{1,0:T(8,128)(2,1)S(1)}, u32[]{:S(2)}, u32[]{:S(2)}) %collective-permute-start.15) | collective-permute-done | bytes 1114144 | tf_op jit(solution)/shard_map/ppermute | solution.py:769
  162.3 10.0 %shard_map.306 = (bf16[1024,256]{1,0:T(8,128)(2,1)S(1)}, f32[8,1024]{1,0:T(8,128)S(1)}) custom-call(s32[8]{0:T(128)S(1)} %copy-done.207, bf16[1024,768]{1,0:T(8,128)(2,1)S(1)} %copy-done.21, bf16[1024,512]{1,0:T(8,128)(2,1)S(1)} %get-tuple-element.386.kvp), custom_call_target="tpu_custom_call" | custom-call | flops 1024 | bytes 11520000 | tf_op jit(solution)/shard_map/pallas_call | solution.py:337
  173.3 14.7 %collective-permute-done.14.far = bf16[512,256]{1,0:T(8,128)(2,1)S(1)} collective-permute-done((bf16[512,256]{1,0:T(8,128)(2,1)S(1)}, bf16[512,256]{1,0:T(8,128)(2,1)S(1)}, u32[]{:S(2)}, u32[]{:S(2)}) %collective-permute-start.14) | collective-permute-done | bytes 262176 | tf_op jit(solution)/shard_map/ppermute | solution.py:769
  210.3 15.2 %collective-permute-done.22.far = bf16[512,256]{1,0:T(8,128)(2,1)S(1)} collective-permute-done((bf16[512,256]{1,0:T(8,128)(2,1)S(1)}, bf16[512,256]{1,0:T(8,128)(2,1)S(1)}, u32[]{:S(2)}, u32[]{:S(2)}) %collective-permute-start.22) | collective-permute-done | bytes 262176 | tf_op jit(solution)/shard_map/ppermute | solution.py:769
  290.5 15.3 %shard_map.317 = (bf16[1024,1024]{1,0:T(8,128)(2,1)}, bf16[1024,1024]{1,0:T(8,128)(2,1)}, bf16[1024,1024]{1,0:T(8,128)(2,1)}, bf16[1024,1024]{1,0:T(8,128)(2,1)}...) custom-call(s32[1]{0:T(128)} %bitcast.at, ...), custom_call_target="tpu_custom_call" | custom-call | flops 1024 | bytes 9600000 | tf_op jit(solution)/shard_map/pallas_call | solution.py:337
  310.2 26.4 %shard_map.319 = (bf16[1024,1024]{1,0:T(8,128)(2,1)}, bf16[1024,1024]{1,0:T(8,128)(2,1)}, bf16[1024,1024]{1,0:T(8,128)(2,1)}, bf16[1024,1024]{1,0:T(8,128)(2,1)}...) custom-call(s32[1]{0:T(128)} %bitcast.at, ...), custom_call_target="tpu_custom_call" | custom-call | flops 1024 | bytes 9600000 | tf_op jit(solution)/shard_map/pallas_call | solution.py:337
  338.3 12.9 %collective-permute-done.43.far = bf16[256,1024]{1,0:T(8,128)(2,1)S(1)} collective-permute-done((bf16[256,1024]{1,0:T(8,128)(2,1)S(1)}, bf16[256,1024]{1,0:T(8,128)(2,1)S(1)}, u32[]{:S(2)}, u32[]{:S(2)}) %collective-permute-start.43) | collective-permute-done | bytes 524320 | tf_op jit(solution)/shard_map/ppermute | solution.py:769
  357.3 9.1 %collective-permute-done.47.far = bf16[256,1024]{1,0:T(8,128)(2,1)S(1)} collective-permute-done((bf16[256,1024]{1,0:T(8,128)(2,1)S(1)}, bf16[256,1024]{1,0:T(8,128)(2,1)S(1)}, u32[]{:S(2)}, u32[]{:S(2)}) %collective-permute-start.47) | collective-permute-done | bytes 524320 | tf_op jit(solution)/shard_map/ppermute | solution.py:769
  366.4 9.0 %shard_map.323.refs_0_ = bf16[2048,1024]{1,0:T(8,128)(2,1)} custom-call(s32[1]{0:T(128)} %bitcast.at, bf16[1024,1024]{1,0:T(8,128)(2,1)S(1)} %copy-done.45, bf16[1024,1024]{1,0:T(8,128)(2,1)S(1)} %copy-done.44, bf16[1024,1024]{1,0:T(8,128)(2,1)} %get-tuple-element.499.act, bf16[1024,1024]{1,0:T(8,128)(2,1)} %get-tuple-element.500.top), custom_call_target="tpu_custom_call" | custom-call | flops 1024 | bytes 5760000 | tf_op jit(solution)/shard_map/pallas_call | solution.py:337
  383.6 10.1 %shard_map.326 = bf16[2048,1024]{1,0:T(8,128)(2,1)} custom-call(s32[1]{0:T(128)} %bitcast.at, bf16[1024,1024]{1,0:T(8,128)(2,1)S(1)} %copy-done.43, bf16[1024,1024]{1,0:T(8,128)(2,1)S(1)} %copy-done.42, bf16[1024,1024]{1,0:T(8,128)(2,1)} %get-tuple-element.518.act, bf16[1024,1024]{1,0:T(8,128)(2,1)} %get-tuple-element.519.top, ...), custom_call_target="tpu_custom_call" | custom-call | flops 1024 | bytes 5760000 | tf_op jit(solution)/shard_map/pallas_call | solution.py:337
  397.5 11.5 %shard_map.325 = (bf16[1024,256]{1,0:T(8,128)(2,1)S(1)}, bf16[640,512]{1,0:T(8,128)(2,1)S(1)}, bf16[640,512]{1,0:T(8,128)(2,1)S(1)}) custom-call(s32[8]{0:T(128)S(1)} %copy-done.208, bf16[1024,256]{1,0:T(8,128)(2,1)S(1)} %copy-done.152, bf16[640,512]{1,0:T(8,128)(2,1)S(1)} %copy-done.40, bf16[640,512]{1,0:T(8,128)(2,1)S(1)} %copy-done.38, ...), custom_call_target="tpu_custom_call" | custom-call | flops 1024 | bytes 8960000 | tf_op jit(solution)/shard_map/pallas_call | solution.py:337
  416.4 11.2 %shard_map.327 = (bf16[1024,256]{1,0:T(8,128)(2,1)S(1)}, bf16[640,512]{1,0:T(8,128)(2,1)S(1)}, bf16[640,512]{1,0:T(8,128)(2,1)S(1)}) custom-call(s32[8]{0:T(128)S(1)} %copy-done.207, bf16[1024,256]{1,0:T(8,128)(2,1)S(1)} %copy-done.148, bf16[640,512]{1,0:T(8,128)(2,1)S(1)} %copy-done.36, bf16[640,512]{1,0:T(8,128)(2,1)S(1)} %copy-done.34, ...), custom_call_target="tpu_custom_call" | custom-call | flops 1024 | bytes 8960000 | tf_op jit(solution)/shard_map/pallas_call | solution.py:337
  490.4 13.4 %shard_map.335 = (bf16[1024,256]{1,0:T(8,128)(2,1)S(1)}, bf16[1024,512]{1,0:T(8,128)(2,1)S(1)}, bf16[1024,512]{1,0:T(8,128)(2,1)S(1)}) custom-call(s32[8]{0:T(128)S(1)} %copy-done.208, bf16[1024,768]{1,0:T(8,128)(2,1)} %get-tuple-element.371.qkv, bf16[1024,512]{1,0:T(8,128)(2,1)S(1)} %copy-done.28, bf16[1024,256]{1,0:T(8,128)(2,1)S(1)} %copy-done.60, ...), custom_call_target="tpu_custom_call" | custom-call | flops 1024 | bytes 14080000 | tf_op jit(solution)/shard_map/pallas_call | solution.py:337
  539.3 13.4 %shard_map.342 = (bf16[1024,256]{1,0:T(8,128)(2,1)S(1)}, bf16[1024,512]{1,0:T(8,128)(2,1)S(1)}, bf16[1024,512]{1,0:T(8,128)(2,1)S(1)}) custom-call(s32[8]{0:T(128)S(1)} %copy-done.207, bf16[1024,768]{1,0:T(8,128)(2,1)} %get-tuple-element.385.qkv, bf16[1024,512]{1,0:T(8,128)(2,1)S(1)} %copy-done.26, bf16[1024,256]{1,0:T(8,128)(2,1)S(1)} %copy-done.58, ...), custom_call_target="tpu_custom_call" | custom-call | flops 1024 | bytes 14080000 | tf_op jit(solution)/shard_map/pallas_call | solution.py:337
  564.6 12.6 %collective-permute-start.70 = (bf16[256,640]{1,0:T(8,128)(2,1)}, bf16[256,640]{1,0:T(8,128)(2,1)S(1)}, u32[]{:S(2)}, u32[]{:S(2)}) collective-permute-start(bf16[256,640]{1,0:T(8,128)(2,1)} %get-tuple-element.648), channel_id=1, source_target_pairs={{0,4},{4,0},{8,12},{12,8},{16,20},{20,16},{24,28},{28,24},{1,5},{5... | collective-permute-start | bytes 983048 | tf_op jit(solution)/shard_map/ppermute | solution.py:769
  598.2 8.3 %shard_map.345 = (f32[512,768]{1,0:T(8,128)}, bf16[512,768]{1,0:T(8,128)(2,1)}) custom-call(s32[1]{0:T(128)} %bitcast.7.at, bf16[512,1024]{1,0:T(8,128)(2,1)S(1)} %shard_map.298.refs_0_, bf16[512,1024]{1,0:T(8,128)(2,1)S(1)} %copy-done.11, bf16[512,1024]{1,0:T(8,128)(2,1)S(1)} %copy-done.8, bf16[512,1024]{1,0:T(8,128)(2,1)S(1)} %copy-done.14, ...), custom_call_target="tpu_custom_call" | custom-call | flops 1024 | bytes 5120000 | tf_op jit(solution)/shard_map/pallas_call | solution.py:337
  657.7 15.6 %collective-permute-done.90 = bf16[128,1536]{1,0:T(8,128)(2,1)S(1)} collective-permute-done((bf16[128,1536]{1,0:T(8,128)(2,1)S(1)}, bf16[128,1536]{1,0:T(8,128)(2,1)S(1)}, u32[]{:S(2)}, u32[]{:S(2)}) %collective-permute-start.90) | collective-permute-done | bytes 393248 | tf_op jit(solution)/shard_map/ppermute | solution.py:769
  691.5 14.8 %collective-permute-done.87 = bf16[64,768]{1,0:T(8,128)(2,1)S(1)} collective-permute-done((bf16[64,768]{1,0:T(8,128)(2,1)S(1)}, bf16[64,768]{1,0:T(8,128)(2,1)S(1)}, u32[]{:S(2)}, u32[]{:S(2)}) %collective-permute-start.87) | collective-permute-done | bytes 98336 | tf_op jit(solution)/shard_map/ppermute | solution.py:769
  712.2 9.2 %collective-permute-done.80 = bf16[160,1024]{1,0:T(8,128)(2,1)S(1)} collective-permute-done((bf16[160,1024]{1,0:T(8,128)(2,1)S(1)}, bf16[160,1024]{1,0:T(8,128)(2,1)S(1)}, u32[]{:S(2)}, u32[]{:S(2)}) %collective-permute-start.80) | collective-permute-done | bytes 327712 | tf_op jit(solution)/shard_map/ppermute | solution.py:775
  (836 shorter events, 415.9 us)
Async XLA Ops:
  7.2 276.8 %all-gather.2.cloned.1.call-start = ((), (), s32[]{:S(2)}) async-start(), calls=%async_computation.1 | async-start | bytes 4718592 | tf_op jit(solution)/shard_map/all_gather | solution.py:1073
  29.0 34.6 %collective-permute-start.5 = (bf16[512,1024]{1,0:T(8,128)(2,1)S(1)}, bf16[512,1024]{1,0:T(8,128)(2,1)S(1)}, u32[]{:S(2)}, u32[]{:S(2)}) collective-permute-start(bf16[512,1024]{1,0:T(8,128)(2,1)S(1)} %shard_map.298.refs_0_), channel_id=1, source_target_pairs={{0,4},{4,8},{8,12},{12,16},{16,20},{20,24},{24,28},{1,5},{5,9},{9,... | collective-permute-start | bytes 3145736 | tf_op jit(solution)/shard_map/ppermute | solution.py:775
  32.7 30.9 %collective-permute-start.6 = (bf16[512,1024]{1,0:T(8,128)(2,1)S(1)}, bf16[512,1024]{1,0:T(8,128)(2,1)S(1)}, u32[]{:S(2)}, u32[]{:S(2)}) collective-permute-start(bf16[512,1024]{1,0:T(8,128)(2,1)S(1)} %shard_map.298.refs_0_), channel_id=1, source_target_pairs={{0,2},{1,3},{2,0},{3,1},{4,6},{5,7},{6,4},{7,5},{8,10},{9,11},{10,... | collective-permute-start | bytes 3145736 | tf_op jit(solution)/shard_map/ppermute | solution.py:769
  67.5 31.0 %collective-permute-start.11 = (bf16[512,768]{1,0:T(8,128)(2,1)S(1)}, bf16[512,768]{1,0:T(8,128)(2,1)S(1)}, u32[]{:S(2)}, u32[]{:S(2)}) collective-permute-start(bf16[512,768]{1,0:T(8,128)(2,1)S(1)} %pad_maximum_fusion.5.first), channel_id=1, source_target_pairs={{0,4},{4,0},{8,12},{12,8},{16,20},{20,16},{24,28},{28,24},{1,5},{5... | collective-permute-start | bytes 2359304 | tf_op jit(solution)/shard_map/ppermute | solution.py:769
  149.2 38.8 %collective-permute-start.18 = (bf16[512,1536]{1,0:T(8,128)(2,1)S(1)}, bf16[512,1536]{1,0:T(8,128)(2,1)S(1)}, u32[]{:S(2)}, u32[]{:S(2)}) collective-permute-start(bf16[512,1536]{1,0:T(8,128)(2,1)S(1)} %slice.196.first), channel_id=1, source_target_pairs={{0,4},{4,0},{8,12},{12,8},{16,20},{20,16},{24,28},{28,24},{1,5},{5... | collective-permute-start | bytes 4718600 | tf_op jit(solution)/shard_map/ppermute | solution.py:769
  151.1 36.9 %collective-permute-start.16 = (bf16[640,1024]{1,0:T(8,128)(2,1)S(1)}, bf16[640,1024]{1,0:T(8,128)(2,1)S(1)}, u32[]{:S(2)}, u32[]{:S(2)}) collective-permute-start(bf16[640,1024]{1,0:T(8,128)(2,1)S(1)} %constant_dynamic-update-slice_fusion.own), channel_id=1, source_target_pairs={{0,1},{1,0},{2,3},{3,2},{4,5},{5,4},{6,7},{7,6},{8,9},{9,8},{10,11... | collective-permute-start | bytes 3932168 | tf_op jit(solution)/shard_map/ppermute | solution.py:769
  151.1 36.8 %collective-permute-start.17 = (bf16[640,1024]{1,0:T(8,128)(2,1)S(1)}, bf16[640,1024]{1,0:T(8,128)(2,1)}, u32[]{:S(2)}, u32[]{:S(2)}) collective-permute-start(bf16[640,1024]{1,0:T(8,128)(2,1)S(1)} %constant_dynamic-update-slice_fusion.own), channel_id=1, source_target_pairs={{0,2},{1,3},{2,0},{3,1},{4,6},{5,7},{6,4},{7,5},{8,10},{9,11},{10,... | collective-permute-start | bytes 3932168 | tf_op jit(solution)/shard_map/ppermute | solution.py:769
  151.8 36.2 %collective-permute-start.14 = (bf16[512,256]{1,0:T(8,128)(2,1)S(1)}, bf16[512,256]{1,0:T(8,128)(2,1)S(1)}, u32[]{:S(2)}, u32[]{:S(2)}) collective-permute-start(bf16[512,256]{1,0:T(8,128)(2,1)S(1)} %slice.195), channel_id=1, source_target_pairs={{0,2},{1,3},{2,0},{3,1},{4,6},{5,7},{6,4},{7,5},{8,10},{9,11},{10,... | collective-permute-start | bytes 786440 | tf_op jit(solution)/shard_map/ppermute | solution.py:769
  189.6 329.5 %reduce-scatter.2.cloned.1.call-start = ((), (), s32[]{:S(2)}) async-start(), calls=%async_computation.2 | async-start | bytes 4718592 | tf_op jit(solution)/shard_map/reduce_scatter | solution.py:1083
  194.3 31.2 %collective-permute-start.25 = (bf16[640,1024]{1,0:T(8,128)(2,1)}, bf16[640,1024]{1,0:T(8,128)(2,1)}, u32[]{:S(2)}, u32[]{:S(2)}) collective-permute-start(bf16[640,1024]{1,0:T(8,128)(2,1)} %collective-permute-done.17.far), channel_id=1, source_target_pairs={{0,1},{1,0},{2,3},{3,2},{4,5},{5,4},{6,7},{7,6},{8,9},{9,8},{10,11... | collective-permute-start | bytes 3932168 | tf_op jit(solution)/shard_map/ppermute | solution.py:769
  194.8 30.7 %collective-permute-start.23 = (bf16[512,1024]{1,0:T(8,128)(2,1)S(1)}, bf16[512,1024]{1,0:T(8,128)(2,1)}, u32[]{:S(2)}, u32[]{:S(2)}) collective-permute-start(bf16[512,1024]{1,0:T(8,128)(2,1)S(1)} %bitcast.107), channel_id=1, source_target_pairs={{0,2},{1,3},{2,0},{3,1},{4,6},{5,7},{6,4},{7,5},{8,10},{9,11},{10,... | collective-permute-start | bytes 3145736 | tf_op jit(solution)/shard_map/ppermute | solution.py:769
  202.2 30.8 %collective-permute-start.27 = (bf16[512,640]{1,0:T(8,128)(2,1)S(1)}, bf16[512,640]{1,0:T(8,128)(2,1)S(1)}, u32[]{:S(2)}, u32[]{:S(2)}) collective-permute-start(bf16[512,640]{1,0:T(8,128)(2,1)S(1)} %copy-done.41), channel_id=1, source_target_pairs={{0,4},{4,0},{8,12},{12,8},{16,20},{20,16},{24,28},{28,24},{1,5},{5... | collective-permute-start | bytes 1966088 | tf_op jit(solution)/shard_map/ppermute | solution.py:769
  438.1 34.4 %collective-permute-start.55 = (bf16[256,1024]{1,0:T(8,128)(2,1)}, bf16[256,1024]{1,0:T(8,128)(2,1)}, u32[]{:S(2)}, u32[]{:S(2)}) collective-permute-start(bf16[256,1024]{1,0:T(8,128)(2,1)} %get-tuple-element.543), channel_id=1, source_target_pairs={{0,2},{1,3},{2,0},{3,1},{4,6},{5,7},{6,4},{7,5},{8,10},{9,11},{10,... | collective-permute-start | bytes 1572872 | tf_op jit(solution)/shard_map/ppermute | solution.py:769
  477.1 40.6 %collective-permute-start.64 = (bf16[1024,1024]{1,0:T(8,128)(2,1)}, bf16[1024,1024]{1,0:T(8,128)(2,1)S(1)}, u32[]{:S(2)}, u32[]{:S(2)}) collective-permute-start(bf16[1024,1024]{1,0:T(8,128)(2,1)} %get-tuple-element.622), channel_id=1, source_target_pairs={{0,1},{1,0},{2,3},{3,2},{4,5},{5,4},{6,7},{7,6},{8,9},{9,8},{10,11... | collective-permute-start | bytes 6291464 | tf_op jit(solution)/shard_map/ppermute | solution.py:769
  477.2 53.2 %collective-permute-start.81 = (bf16[640,1024]{1,0:T(8,128)(2,1)}, bf16[640,1024]{1,0:T(8,128)(2,1)}, u32[]{:S(2)}, u32[]{:S(2)}) collective-permute-start(bf16[640,1024]{1,0:T(8,128)(2,1)} %get-tuple-element.672), channel_id=1, source_target_pairs={{0,1},{1,0},{2,3},{3,2},{4,5},{5,4},{6,7},{7,6},{8,9},{9,8},{10,11... | collective-permute-start | bytes 3932168 | tf_op jit(solution)/shard_map/ppermute | solution.py:769
  480.5 36.4 %collective-permute-start.63 = (bf16[512,640]{1,0:T(8,128)(2,1)}, bf16[512,640]{1,0:T(8,128)(2,1)S(1)}, u32[]{:S(2)}, u32[]{:S(2)}) collective-permute-start(bf16[512,640]{1,0:T(8,128)(2,1)} %get-tuple-element.608), channel_id=1, source_target_pairs={{0,8},{4,12},{8,0},{12,4},{16,24},{20,28},{24,16},{28,20},{1,9},{5... | collective-permute-start | bytes 1966088 | tf_op jit(solution)/shard_map/ppermute | solution.py:769
  512.9 64.3 %collective-permute-start.65 = (bf16[512,1024]{1,0:T(8,128)(2,1)}, bf16[512,1024]{1,0:T(8,128)(2,1)}, u32[]{:S(2)}, u32[]{:S(2)}) collective-permute-start(bf16[512,1024]{1,0:T(8,128)(2,1)} %get-tuple-element.628), channel_id=1, source_target_pairs={{0,1},{1,0},{2,3},{3,2},{4,5},{5,4},{6,7},{7,6},{8,9},{9,8},{10,11... | collective-permute-start | bytes 3145736 | tf_op jit(solution)/shard_map/ppermute | solution.py:769
  528.1 78.5 %collective-permute-start.71 = (bf16[512,1536]{1,0:T(8,128)(2,1)}, bf16[512,1536]{1,0:T(8,128)(2,1)}, u32[]{:S(2)}, u32[]{:S(2)}) collective-permute-start(bf16[512,1536]{1,0:T(8,128)(2,1)} %get-tuple-element.654), channel_id=1, source_target_pairs={{0,8},{4,12},{8,0},{12,4},{16,24},{20,28},{24,16},{28,20},{1,9},{5... | collective-permute-start | bytes 4718600 | tf_op jit(solution)/shard_map/ppermute | solution.py:769
  538.2 43.6 %collective-permute-start.67 = (bf16[256,1024]{1,0:T(8,128)(2,1)S(1)}, bf16[256,1024]{1,0:T(8,128)(2,1)S(1)}, u32[]{:S(2)}, u32[]{:S(2)}) collective-permute-start(bf16[256,1024]{1,0:T(8,128)(2,1)S(1)} %get-tuple-element.632), channel_id=1, source_target_pairs={{0,2},{1,3},{2,0},{3,1},{4,6},{5,7},{6,4},{7,5},{8,10},{9,11},{10,... | collective-permute-start | bytes 1572872 | tf_op jit(solution)/shard_map/ppermute | solution.py:769
  561.4 47.4 %collective-permute-start.75 = (bf16[512,1024]{1,0:T(8,128)(2,1)}, bf16[512,1024]{1,0:T(8,128)(2,1)}, u32[]{:S(2)}, u32[]{:S(2)}) collective-permute-start(bf16[512,1024]{1,0:T(8,128)(2,1)} %get-tuple-element.664), channel_id=1, source_target_pairs={{0,1},{1,0},{2,3},{3,2},{4,5},{5,4},{6,7},{7,6},{8,9},{9,8},{10,11... | collective-permute-start | bytes 3145736 | tf_op jit(solution)/shard_map/ppermute | solution.py:769
  564.6 42.0 %collective-permute-start.70 = (bf16[256,640]{1,0:T(8,128)(2,1)}, bf16[256,640]{1,0:T(8,128)(2,1)S(1)}, u32[]{:S(2)}, u32[]{:S(2)}) collective-permute-start(bf16[256,640]{1,0:T(8,128)(2,1)} %get-tuple-element.648), channel_id=1, source_target_pairs={{0,4},{4,0},{8,12},{12,8},{16,20},{20,16},{24,28},{28,24},{1,5},{5... | collective-permute-start | bytes 983048 | tf_op jit(solution)/shard_map/ppermute | solution.py:769
  634.5 38.7 %collective-permute-start.90 = (bf16[128,1536]{1,0:T(8,128)(2,1)S(1)}, bf16[128,1536]{1,0:T(8,128)(2,1)S(1)}, u32[]{:S(2)}, u32[]{:S(2)}) collective-permute-start(bf16[128,1536]{1,0:T(8,128)(2,1)S(1)} %get-tuple-element.686), channel_id=1, source_target_pairs={{0,16},{4,20},{8,24},{12,28},{16,0},{20,4},{24,8},{28,12},{1,17},{... | collective-permute-start | bytes 1179656 | tf_op jit(solution)/shard_map/ppermute | solution.py:769
  645.6 40.1 %collective-permute-start.78 = (bf16[640,1024]{1,0:T(8,128)(2,1)}, bf16[640,1024]{1,0:T(8,128)(2,1)S(1)}, u32[]{:S(2)}, u32[]{:S(2)}) collective-permute-start(bf16[640,1024]{1,0:T(8,128)(2,1)} %copy-done.211), channel_id=1, source_target_pairs={{0,1},{1,0},{2,3},{3,2},{4,5},{5,4},{6,7},{7,6},{8,9},{9,8},{10,11... | collective-permute-start | bytes 3932168 | tf_op jit(solution)/shard_map/ppermute | solution.py:769
  647.8 31.2 %collective-permute-start.85 = (bf16[256,768]{1,0:T(8,128)(2,1)S(1)}, bf16[256,768]{1,0:T(8,128)(2,1)S(1)}, u32[]{:S(2)}, u32[]{:S(2)}) collective-permute-start(bf16[256,768]{1,0:T(8,128)(2,1)S(1)} %get-tuple-element.678), channel_id=1, source_target_pairs={{0,4},{4,0},{8,12},{12,8},{16,20},{20,16},{24,28},{28,24},{1,5},{5... | collective-permute-start | bytes 1179656 | tf_op jit(solution)/shard_map/ppermute | solution.py:769
  (312 other events, 2820.3 us)
Sparse Core Ops, SparseCore 0:
  189.7 73.0 all-gather.1
  411.7 101.5 reduce-scatter.1

commit v4 on v3

--- a/solution.py
+++ b/solution.py
@@ -1,4 +1,5 @@
 import functools
+import math
 import jax
 import jax.numpy as jnp
 import numpy as np
@@ -334,13 +335,15 @@
 
 def call(kernel, scalars, arrays, outs, scratch=(), time=2):
     vmem = pl.BlockSpec(memory_space=pltpu.VMEM)
+    held = (*arrays, *jax.tree.leaves(outs), *scratch)
+    room = sum(math.prod(a.shape) * jnp.dtype(a.dtype).itemsize for a in held) + 12 * 2**20
     return pl.pallas_call(
         kernel,
         out_shape=outs,
         in_specs=[pl.BlockSpec(memory_space=pltpu.SMEM)] + [vmem] * len(arrays),
         out_specs=jax.tree.map(lambda _: vmem, outs),
         scratch_shapes=scratch,
-        compiler_params=pltpu.CompilerParams(vmem_limit_bytes=48 * 2**20),
+        compiler_params=pltpu.CompilerParams(vmem_limit_bytes=min(room, 48 * 2**20)),
         cost_estimate=pl.CostEstimate(flops=1024, bytes_accessed=int(time * 640000), transcendentals=0),
     )(scalars, *arrays)
 
@@ -558,12 +561,14 @@
         kvp[block, :] = dot_nn(refs[4 + k][own, :], weight[:, width:]).astype(BF)
 
 
-def memory_kernel(size, at, own, near, far, last, weight, *outs):
+def memory_kernel(size, at, *refs):
+    weight, outs = refs[8], refs[9:]
     count = len(outs) // 2
     rows, keys = outs[:count], outs[count:]
     for i in range(count):
-        span = slice(i * size, (i + 1) * size)
-        block = jnp.concatenate([ref[span, :] for ref in (own, near, far, last)], axis=0)
+        span = slice((i % (count // 2)) * size, (i % (count // 2) + 1) * size)
+        pieces = refs[0:4] if i < count // 2 else refs[4:8]
+        block = jnp.concatenate([ref[span, :] for ref in pieces], axis=0)
         rows[i][...] = block
         keys[i][...] = dot_nn(block, weight[...]).astype(BF)
 
@@ -616,13 +621,18 @@
     out[...] = (near[...] + far[...].astype(F32)).astype(BF)
 
 
-def memory_back_kernel(at, own, prev, rows_own, rows_prev, weight, grad, keep, send):
-    grad[...] = dot_tn(rows_own[...], own[...]) + dot_tn(rows_prev[...], prev[...])
-    rows = own.shape[0] // 4
-    for k, part in enumerate((own, prev)):
+def memory_back_kernel(at, own_a, own_b, prev_a, prev_b, rows_a, rows_b, rows_prev_a, rows_prev_b, weight,
+                       grad, keep, send):
+    rows = own_a.shape[0] // 4
+    total = None
+    grads, places = (own_a, own_b, prev_a, prev_b), (rows_a, rows_b, rows_prev_a, rows_prev_b)
+    for k, (part, memory) in enumerate(zip(grads, places)):
+        term = dot_tn(memory[...], part[...])
+        total = term if total is None else total + term
         part = dot_nt(part[...], weight[...]).astype(BF)
-        for slot, out, place in ((0, keep, 0), (1, send, 0), (2, keep, 2), (3, send, 2)):
+        for slot, out, place in ((0, keep, 0), (1, send, 0), (2, keep, 4), (3, send, 4)):
             out[(place + k) * rows : (place + k + 1) * rows, :] = part[slot * rows : (slot + 1) * rows]
+    grad[...] = total
 
 
 def self_out_kernel(i, at, own, near, far, x, wide_own, wide_other,
@@ -706,10 +716,11 @@
     own, other = refs[-2:]
     half = own.shape[1] // names
     for n in range(names):
-        low_a, low_b, mine_a, mine_b, others_a, others_b = (ref[...] for ref in refs[6 * n : 6 * n + 6])
+        parts = [ref[...] for ref in refs[6 * n : 6 * n + 6]]
+        low, mine, others = (jnp.concatenate(parts[k : k + 2], axis=0) for k in (0, 2, 4))
         span = slice(n * half, (n + 1) * half)
-        other[:, span] = (dot_tn(low_a, others_a) + dot_tn(low_b, others_b)).astype(BF)
-        own[:, span] = dot_tn(low_a, mine_a) + dot_tn(low_b, mine_b)
+        other[:, span] = dot_tn(low, others).astype(BF)
+        own[:, span] = dot_tn(low, mine)
 
 
 def qkv_back_kernel(at, dq, dkv, dkv_prev, weight, keep, send, keep_prev, send_prev):
@@ -724,37 +735,36 @@
             out_prev[place, :] = dot_nt(dkv_prev[block, :], weight[:, width:]).astype(BF)
 
 
-def qkv_grads(i, refs, dq, dkv, dkv_prev):
-    rows = dq.shape[0] // 4
+def lay_own(i, refs, low_all, before_all):
+    rows = low_all.shape[0] // 4
     own = slice(i * rows, (i + 1) * rows)
-    queries, others = None, None
-    for k in range(4):
-        block = slice(k * rows, (k + 1) * rows)
-        low, before = refs[k][own, :], refs[4 + k][own, :]
-        query = dot_tn(low, dq[block, :])
-        other = dot_tn(low, dkv[block, :]) + dot_tn(before, dkv_prev[block, :])
-        queries, others = (query, other) if k == 0 else (queries + query, others + other)
-    return queries, others
+    for out, pieces in ((low_all, refs[0:4]), (before_all, refs[4:8])):
+        for k, ref in enumerate(pieces):
+            out[k * rows : (k + 1) * rows, :] = ref[own, :]
 
 
 def qkv_grads_kernel(i, at, *refs):
-    dq, dkv, dkv_prev, out = refs[8:]
+    dq, dkv, dkv_prev, out, low, before, own = refs[8:]
     width = dq.shape[1]
-    out[:, 0:width], out[:, width:] = qkv_grads(i, refs, dq, dkv, dkv_prev)
+    lay_own(i, refs, low, before)
+    out[:, 0:width] = dot_tn(low[...], dq[...])
+    own[...] = dot_tn(low[...], dkv[...])
+    out[:, width:] = own[...] + dot_tn(before[...], dkv_prev[...])
 
 
 def last_qkv_grads_kernel(i, offsets, at, *refs):
-    dq, dkv, dkv_prev, earlier, keep, send, total = refs[8:]
+    dq, dkv, dkv_prev, earlier, keep, send, low, before, total = refs[8:]
     width = dq.shape[1]
-    queries, others = qkv_grads(i, refs, dq, dkv, dkv_prev)
-    total[:, 0:width] = earlier[:, 0:width] + queries
-    total[:, width:] = earlier[:, width:] + others
+    lay_own(i, refs, low, before)
+    total[:, 0:width] = earlier[:, 0:width] + dot_tn(low[...], dq[...])
+    total[:, width:] = earlier[:, width:] + dot_tn(low[...], dkv[...])
+    total[:, width:] += dot_tn(before[...], dkv_prev[...])
     half = len(offsets) // 2
     rows = total.shape[0] // len(offsets)
-    for i, offset in enumerate(offsets):
-        out = keep if i < half else send
+    for n, offset in enumerate(offsets):
+        out = keep if n < half else send
         start = pl.multiple_of((at[0] ^ offset) * rows, rows)
-        out[(i % half) * rows : (i % half + 1) * rows, :] = total[pl.ds(start, rows), :].astype(out.dtype)
+        out[(n % half) * rows : (n % half + 1) * rows, :] = total[pl.ds(start, rows), :].astype(out.dtype)
 
 
 def shape(rows, columns, dtype=BF):
@@ -991,11 +1001,8 @@
     far = flip(message, "mem", 2)
     x_rows, tops = inputs.reshape(MICRO * tok, D), cotangent.reshape(MICRO * tok, D)
     lows = call(norm_kernel, place, (x_rows,), shape(MICRO * tok, D))
-    far, lows = lax.optimization_barrier((far, lows))
     befores = shifted(lows, 1)
     far_lows, near_lows = flip(lows, "mem", 2), flip(lows, "mem", 1)
-    memory_own = jnp.pad(memory.reshape(MICRO, real, D), ((0, 0), (0, padded - real), (0, 0)))
-    memory_own = memory_own.reshape(MICRO * padded, D)
     smem = pl.BlockSpec(memory_space=pltpu.SMEM)
     ids = page_ids.reshape(MICRO, -1, 128)
     places = pl.pallas_call(
@@ -1017,24 +1024,33 @@
     state = {}
     hidden = mlp_in.shape[0]
     stage = seq_stage(qkv_part, bits[0])
+    stage, first_part, befores, memory_here = lax.optimization_barrier((stage, first_part, befores, memory))
+    far_befores, near_befores = flip(befores, "mem", 2), flip(befores, "mem", 1)
+    first_stage = first_part
+    for bit in bits[:-3]:
+        first_stage = seq_stage(first_stage, bit)
+    first_pair = first_stage, flip(first_stage, "seq", bits[-3])
+    memory_own = jnp.pad(memory_here.reshape(MICRO, real, D), ((0, 0), (0, padded - real), (0, 0)))
+    memory_own = memory_own.reshape(MICRO * padded, D)
     hidden_part = jnp.concatenate([mlp_in, mlp_out], axis=0)
-    stage, memory_own, places, hidden_part = lax.optimization_barrier((stage, memory_own, places, hidden_part))
-    memory_before = shifted(memory_own, 1)
     for bit in bits[1:-1]:
         stage = seq_stage(stage, bit)
-    stage, first_part, befores, far_lows = lax.optimization_barrier((stage, first_part, befores, far_lows))
+    stage, far_lows, memory_own, hidden_part, places = lax.optimization_barrier(
+        (stage, far_lows, memory_own, hidden_part, places)
+    )
     last_lows = flip(far_lows, "mem", 1)
-    far_befores, near_befores = flip(befores, "mem", 2), flip(befores, "mem", 1)
-    first_stage = first_part
-    for bit in bits[:-2]:
-        first_stage = seq_stage(first_stage, bit)
-    (qkv_full,) = assemble(stage, flip(stage, "seq", bits[-1]), seq, bits, [3 * width])
+    last_stage, first_pair, far_befores, memory_own, tops = lax.optimization_barrier(
+        (flip(stage, "seq", bits[-1]), first_pair, far_befores, memory_own, tops)
+    )
+    first_stage = seq_stage(jnp.concatenate(first_pair, axis=0), bits[-2])
+    memory_before = shifted(memory_own, 1)
+    memory_far = flip(memory_own, "mem", 2)
+    far_tops, near_tops = flip(tops, "mem", 2), flip(tops, "mem", 1)
+    (qkv_full,) = assemble(stage, last_stage, seq, bits, [3 * width])
     gathered = [lows, near_lows, far_lows, last_lows, befores, near_befores, far_befores, flip(far_befores, "mem", 1)]
 
     def first_side():
-        (first,) = yield 1, lambda: (first_stage,)
-        first = seq_stage(first, bits[-2])
-        (first,) = yield 2, lambda: (first,)
+        (first,) = yield 2, lambda: (first_stage,)
         cut = 2 * half + 2 * width
         first, last = first[:, :cut], first[:, cut:]
         first = first, flip(first, "seq", bits[-1])
@@ -1042,18 +1058,18 @@
         state["wide_own"], state["ckv"] = assemble(*first, seq, bits, [2 * half, 2 * width])
         state["wide_other"] = flip(state["wide_own"], "mem", 1)
         last = last, flip(last, "seq", bits[-1])
-        last = yield 5, lambda: last
+        last = yield 6, lambda: last
         state["cout_own"], gain = assemble(*last, seq, bits, [half, 128])
         state["gain"] = gain[:, 0].astype(F32)[None, :]
-        (own,) = yield 6, lambda: (state["cout_own"],)
-        state["cout_other"] = flip(own, "mem", 1)
+        state["cout_other"] = flip(state["cout_own"], "mem", 1)
 
     def memory_side():
-        rows = yield 1, lambda: (memory_own, memory_before)
-        rows = jnp.concatenate(rows, axis=0)
-        far, near = flip(rows, "mem", 2), flip(rows, "mem", 1)
-        rows, near, far = yield 3, lambda: (rows, near, far)
-        pieces = rows, near, far, flip(far, "mem", 1)
+        before, near_own = yield 2, lambda: (memory_before, flip(memory_own, "mem", 1))
+        far_prev, near_prev = flip(before, "mem", 2), flip(before, "mem", 1)
+        *gone, far_own = yield 3, lambda: (before, near_own, far_prev, near_prev, memory_far)
+        before, near_own, far_prev, near_prev = gone
+        last_own, last_prev = flip(far_own, "mem", 1), flip(far_prev, "mem", 1)
+        pieces = memory_own, near_own, far_own, last_own, before, near_prev, far_prev, last_prev
         pieces = yield 4, lambda: pieces
         whole = blocks * padded
         outs = [shape(whole, D)] * (2 * MICRO) + [shape(whole, 2 * width)] * (2 * MICRO)
@@ -1063,25 +1079,24 @@
         )
 
     def top_side():
-        (top,) = yield 2, lambda: (tops,)
-        far, near = flip(top, "mem", 2), flip(top, "mem", 1)
-        far, near = yield 4, lambda: (far, near)
+        far, near = yield 2, lambda: (far_tops, near_tops)
         state["top"] = tops, near, far, flip(far, "mem", 1)
 
     def hidden_side():
-        (part,) = yield 3, lambda: (hidden_part,)
+        (part,) = yield 2, lambda: (hidden_part,)
         whole = lax.all_gather(part, "seq", axis=0, tiled=True)
-        (whole,) = yield 9, lambda: (whole,)
+        (whole,) = yield 8, lambda: (whole,)
         both = [shape(whole.shape[0] // 2, D)] * 2
-        state["inner"], state["outer"] = call(functools.partial(hidden_kernel, hidden), place, (whole,), both)
+        both = call(functools.partial(hidden_kernel, hidden), place, (whole,), both)
+        state["inner"], state["outer"] = yield 9, lambda: both
         kernel = functools.partial(hidden_grads_kernel, hidden)
-        arrays = yield 12, lambda: state["grad_hidden"][0]
+        arrays = yield 11, lambda: state["grad_hidden"][0]
         grads = call(kernel, place, arrays, shape(2 * D, D), time=9)
-        arrays = yield 13, lambda: (*state["grad_hidden"][1], grads)
+        arrays = yield 12, lambda: (*state["grad_hidden"][1], grads)
         grads = call(kernel, place, arrays, shape(2 * D, D), time=9)
-        (grads,) = yield 14, lambda: (grads,)
+        (grads,) = yield 13, lambda: (grads,)
         grads = lax.psum_scatter(grads, "seq", scatter_dimension=0, tiled=True)
-        (grads,) = yield 18, lambda: (grads,)
+        (grads,) = yield 19, lambda: (grads,)
         state["hidden_grads"] = grads[:hidden].astype(F32), grads[hidden:].astype(F32)
 
     order = turned[::-1]
@@ -1103,8 +1118,6 @@
         for bit, tick in zip(order[1:], ticks[1:]):
             pair = yield tick, lambda: pair
             pair = seq_next(*pair, bit)
-        for bit in order[len(ticks) :]:
-            pair = seq_next(*pair, bit)
         state[name] = pair
 
     def cout_side():
@@ -1112,20 +1125,31 @@
         own, other = half_grads([list(zip(*names))])
         gains = jnp.pad((gains[0] + gains[1]).reshape(D, 1), ((0, 0), (0, 127)))
         groups = [[(0, 0, half), (1, 0, half)], [(2, 0, 128)]]
-        yield from tree_side("cout", (own, flip(other, "mem", 1), gains), groups, (16, 18, 19))
+        yield from tree_side("cout", (own, flip(other, "mem", 1), gains), groups, (16, 20))
 
     def wide_side():
-        out, query, ckv = yield 17, lambda: (state["grad_out"], state["grad_cquery"], state["grad_ckv"])
+        out, query, dmem = yield 17, lambda: (state["grad_out"], state["grad_cquery"], state["dmem"])
         own, other = half_grads([list(zip(*out)), list(zip(*query))])
-        groups = [[(0, 0, 2 * half), (1, 0, 2 * half)], [(2, 0, 2 * width), (3, 0, 2 * width)]]
-        yield from tree_side("wide", (own, flip(other, "mem", 1), *ckv), groups, (18, 19))
-
-    def qkv_side():
-        kept, sent = yield 19, lambda: state["grad_qkv"][-1]
-        state["qkv"] = kept, flip(sent, "seq", order[0])
-
-    for name in ("hidden", "gain_three", "cout", "out", "cquery", "ckv", "qkv"):
+        other = flip(other, "mem", 1)
+        mem_rows = shape(8 * padded, D)
+        arrays = (*(part for pair in zip(*dmem) for part in pair), *state["rows"], *state["rows_prev"], state["ckv"])
+        ckv, mem_keep, mem_send = call(
+            memory_back_kernel, place, arrays, [shape(D, 2 * width, F32), mem_rows, mem_rows], time=10
+        )
+        state["memory_parts"] = mem_keep, flip(mem_send, "mem", 1)
+        groups = [[(0, 0, 2 * half), (1, 0, 2 * half)], [(2, 0, 2 * width)]]
+        yield from tree_side("wide", (own, other, ckv), groups, (18, 19, 20))
+
+    def memory_grads_side():
+        parts = yield 18, lambda: state["memory_parts"]
+        rows = 4 * padded
+        near, far = call(near_kernel, place, parts, [shape(rows, D, F32), shape(rows, D)], time=1)
+        near, far = yield 20, lambda: (near, far)
+        state["memory_sums"] = near, flip(far, "mem", 2)
+
+    for name in ("hidden", "gain_three", "cout", "out", "cquery", "qkv"):
         state["grad_" + name] = []
+    state["dmem"] = []
     quarter = [shape(tok, width), shape(tok, width), shape(2 * tok, width)]
     rounded, exact, column = shape(tok, D), shape(tok, D, F32), shape(tok, 1, F32)
     half_rows, whole, pair_rows = shape(tok, half), shape(group, D), shape(2 * tok, D)
@@ -1173,7 +1197,7 @@
             [whole, whole, whole, whole, pair_rows, pair_rows, pair_rows, pair_rows], time=15,
         )
         state["grad_hidden"].append((pre_low, low_all, act, top_all))
-        grad_keep = yield grad_keep
+        grad_keep, grad_send = yield grad_keep, grad_send
 
         near, far = near_sum(place, grad_keep, grad_send)
         far, out_send = yield flip(far, "mem", 2), out_send
@@ -1202,44 +1226,53 @@
         )
         state["grad_cquery"].append((low_two, query_mine, query_others))
         state["grad_out"].append((self_low, mine, others))
-        mem_rows = shape(4 * padded, D)
-        grad_ckv, mem_keep, mem_send = call(
-            memory_back_kernel, place, (dmem, dmem_prev, state["rows"][i], state["rows_prev"][i], state["ckv"]),
-            [shape(D, 2 * width, F32), mem_rows, mem_rows], time=5,
-        )
-        state["grad_ckv"].append(grad_ckv)
+        state["dmem"].append((dmem, dmem_prev))
         grad_after_self = yield grad_after_self
 
         pieces, out_far = yield far_pieces(pieces), out_far
-        dq, dkv, dkv_prev = self_backward(at, qkv, kv_prev, self_o, near_slots(*pieces), self_lse, blocks)
+        pieces = near_slots(*pieces)
+        if i == 0:
+            pieces = yield Stay(pieces)
+        dq, dkv, dkv_prev = self_backward(at, qkv, kv_prev, self_o, pieces, self_lse, blocks)
         grads = (*gathered, dq, dkv, dkv_prev)
+        lows_scratch = [pltpu.VMEM((group, D), BF)] * 2
         if i == 0:
-            grads = call(functools.partial(qkv_grads_kernel, i), place, grads, shape(D, 3 * width, F32), time=7)
+            grads = call(
+                functools.partial(qkv_grads_kernel, i), place, grads, shape(D, 3 * width, F32),
+                [*lows_scratch, pltpu.VMEM((D, 2 * width), F32)], time=6,
+            )
+            state["grad_qkv"].append(grads)
         else:
             grads = call(
                 functools.partial(last_qkv_grads_kernel, i, seq_offsets(turned)), seq.reshape(1),
                 (*grads, state["grad_qkv"][0]), [shape(D // 2, 3 * width, F32), shape(D // 2, 3 * width)],
-                [pltpu.VMEM((D, 3 * width), F32)], time=8,
+                [*lows_scratch, pltpu.VMEM((D, 3 * width), F32)], time=7,
             )
-        state["grad_qkv"].append(grads)
         output = call(output_kernel, place, (after_cross, out_near, out_far), rounded)
-        keep, send, keep_prev, send_prev = call(
-            qkv_back_kernel, place, (dq, dkv, dkv_prev, qkv_full), [pair_rows] * 4, time=5
-        )
-        keep = yield keep
-
-        near_prev, far_prev = near_sum(place, keep_prev, send_prev)
-        near, far = near_sum(place, keep, send)
-        far_prev, far, mem_send = yield flip(far_prev, "mem", 2), flip(far, "mem", 2), mem_send
-        back = shifted(call(far_sum_kernel, place, (near_prev, far_prev), rounded), -1)
-        mem_near, mem_far = near_sum(place, mem_keep, mem_send)
-        mem_all = call(far_sum_kernel, place, (mem_near, flip(mem_far, "mem", 2)), shape(2 * padded, D))
-        mem_back = shifted(mem_all[padded:], -1)
-        grad_mem = (mem_all[:padded].astype(F32) + mem_back.astype(F32))[:real].reshape(1, real, D)
-        grad_x = call(functools.partial(grad_x_kernel, i), place, (x_rows, grad_after_self, near, far, back), exact)
-        return output, grad_x, grad_mem
-
-    sides = [first_side(), memory_side(), top_side(), hidden_side(), cout_side(), wide_side(), qkv_side()]
+        if i < MICRO - 1:
+            back = call(qkv_back_kernel, place, (dq, dkv, dkv_prev, qkv_full), [pair_rows] * 4, time=5)
+            back, state["grad_qkv"][0] = yield last_near(*back), grads
+            back = yield last_far(*back)
+        else:
+            state["last_qkv"], dq, dkv, dkv_prev = yield grads, dq, dkv, dkv_prev
+            back = call(qkv_back_kernel, place, (dq, dkv, dkv_prev, qkv_full), [pair_rows] * 4, time=5)
+            yield ()
+        return output, grad_after_self, back
+
+    def last_near(keep, send, keep_prev, send_prev):
+        return [near_sum(place, *pair) for pair in ((keep_prev, send_prev), (keep, send))]
+
+    def last_far(*pairs):
+        return [part for near, far in pairs for part in (near, flip(far, "mem", 2))]
+
+    def back_rows(near_prev, far_prev, near, far):
+        return shifted(call(far_sum_kernel, place, (near_prev, far_prev), rounded), -1)
+
+    def final_rows(i, sums, back):
+        grads = x_rows, done[i][1], sums[2], sums[3], back
+        return call(functools.partial(grad_x_kernel, i), place, grads, exact)
+
+    sides = [first_side(), memory_side(), top_side(), hidden_side(), cout_side(), wide_side(), memory_grads_side()]
     done = interleave([stream(i) for i in range(MICRO)], sides)
 
     def wide_finish(own):
@@ -1266,18 +1299,39 @@
             pair = seq_next(*pair, bit)
         return pair[0] + pair[1].astype(F32)
 
+    tie = lax.optimization_barrier
+    kept, sent = state["last_qkv"]
+    qkv_pair = kept, flip(sent, "seq", order[0])
+    sums = [done[0][2]]
+    backs = [back_rows(*sums[0])]
+    nears, memory_sums = tie((last_near(*done[1][2]), state["memory_sums"]))
+    sums.append(last_far(*nears))
+    qkv_pair, sums, backs, memory_sums, cout_pair = tie((qkv_pair, sums, backs, memory_sums, state["cout"]))
+    qkv_pair = seq_next(*qkv_pair, order[1])
+    backs.append(back_rows(*sums[1]))
+    memory_near, memory_far = memory_sums
+    both = call(far_sum_kernel, place, (memory_near, memory_far), shape(4 * padded, D))
+    mem_own, mem_back = both[: 2 * padded], shifted(both[2 * padded :], -1)
+    wide_pair, cout_pair = state["wide"], seq_next(*cout_pair, order[2])
+    for bit in order[3:]:
+        wide_pair, cout_pair = seq_next(*wide_pair, bit), seq_next(*cout_pair, bit)
+    qkv_pair, wide_pair, cout_pair = tie((qkv_pair, wide_pair, cout_pair))
+    qkv_pair = seq_next(*qkv_pair, order[2])
+    for bit in order[3:]:
+        qkv_pair = seq_next(*qkv_pair, bit)
+    grad_rows = [final_rows(i, sums[i], backs[i]) for i in range(MICRO)]
+    grad_mem = mem_own.reshape(MICRO, 1, padded, D).astype(F32) + mem_back.reshape(MICRO, 1, padded, D).astype(F32)
     grad_inner, grad_outer = state["hidden_grads"]
-    own, near = wide_finish(seq_finish(state["cout"], []))
+    own, near = wide_finish(seq_finish(cout_pair, []))
     grad_cout = join_halves(own[:, :half], near[:, :half])
     grad_gain_mlp = own[:, half] + near[:, half]
-
-    last = seq_finish(state["wide"], [])
+    last = seq_finish(wide_pair, [])
     grad_ckey, grad_cvalue = head_finish(last[:, 2 * half :], 2)
     own, near = wide_finish(last[:, : 2 * half])
     grad_out, plain_cquery = [
         join_halves(own[:, k * half : (k + 1) * half], near[:, k * half : (k + 1) * half]) for k in range(2)
     ]
-    plain_qkv = head_finish(seq_finish(state["qkv"], order[1:]), 3)
+    plain_qkv = head_finish(seq_finish(qkv_pair, []), 3)
 
     def gained(gain, weights, plains):
         scale = gain.astype(F32)[:, None]
@@ -1290,8 +1344,8 @@
     grad_gain_cross, (grad_cquery,) = gained(gain_cross, (cross_query,), (plain_cquery,))
     return (
         jnp.stack([d[0] for d in done]),
-        jnp.stack([d[1] for d in done]),
-        jnp.stack([d[2] for d in done]),
+        jnp.stack(grad_rows),
+        grad_mem[:, :, :real],
         grad_gain_self,
         grad_query,
         grad_key,

time: 743 us -> 650 us (0.87)
  Pallas kernels: 275 us -> 196 us
  waiting for transfers between devices: 192 us -> 138 us
  local copies, waits for them, and re-layouts: 102 us -> 124 us
  starting transfers between devices: 126 us -> 141 us
    pallas_call x65 -> x62, Pallas kernels: 273 us -> 194 us  [call(): pl.pallas_call(kernel, out_shape=outs, in_specs=[pl.BlockSpec(memory_spac...]
    ppermute x92 -> x93, waiting for transfers between devices: 171 us -> 134 us  [flip(): lax.ppermute(block, axis, [(i, i ^ bit) for i in range(lax.axis_size(axis...]
    ppermute x92 -> x93, starting transfers between devices: 106 us -> 131 us  [flip(): lax.ppermute(block, axis, [(i, i ^ bit) for i in range(lax.axis_size(axis...]
    ppermute x6 -> x5, waiting for transfers between devices: 20.3 us -> 3.79 us  [shifted(): return lax.ppermute(block, 'seq', route)]
    unnamed x481 -> x512, local copies, waits for them, and re-layouts: 86.3 us -> 102 us
    ppermute x6 -> x5, starting transfers between devices: 19.5 us -> 10.2 us  [shifted(): return lax.ppermute(block, 'seq', route)]
  transfers between devices with their start and end apart: 100 -> 100, of which waited for: 32 -> 31; matrix products, arithmetic and copies ran while one was open for 5% -> 7% of each run, Pallas kernels for 37% -> 31%
where the time goes in v4:
time: 650 us; the launch traced here: 638 us
  Pallas kernels  196 us (30%)
  starting transfers between devices  141 us (22%)
  waiting for transfers between devices  138 us (21%)
  local copies, waits for them, and re-layouts  124 us (19%)
  other arithmetic  22 us (3%)
  between operations  17.5 us (3%)
    pallas_call x62, Pallas kernels, call(): pl.pallas_call(kernel, out_shape=outs, in_specs=[pl.BlockSpec(memory_spac...  194 us
    ppermute x93, waiting for transfers between devices, flip(): lax.ppermute(block, axis, [(i, i ^ bit) for i in range(lax.axis_size(axis...  134 us
    ppermute x93, starting transfers between devices, flip(): lax.ppermute(block, axis, [(i, i ^ bit) for i in range(lax.axis_size(axis...  131 us
    unnamed x512, local copies, waits for them, and re-layouts  102 us
  transfers between devices with their start and end apart: 100, of which 31 were waited for; matrix products, arithmetic and copies ran while one was open for 7% of the time, Pallas kernels for 31%

profile of v4, /device:TPU:0, one launch (start us, length us, event | category | flops | bytes accessed | tf_op | source)
XLA Modules:
  0.0 638.0 jit_solution(16632832089001645888)
XLA Ops:
  32.9 9.4 %collective-permute-done.2 = bf16[128,768]{1,0:T(8,128)(2,1)S(1)} collective-permute-done((bf16[128,768]{1,0:T(8,128)(2,1)S(1)}, bf16[128,768]{1,0:T(8,128)(2,1)S(1)}, u32[]{:S(2)}, u32[]{:S(2)}) %collective-permute-start.2) | collective-permute-done | bytes 196640 | tf_op jit(solution)/shard_map/ppermute | solution.py:779
  60.5 8.9 %collective-permute-start.9 = (bf16[512,768]{1,0:T(8,128)(2,1)S(1)}, bf16[512,768]{1,0:T(8,128)(2,1)S(1)}, u32[]{:S(2)}, u32[]{:S(2)}) collective-permute-start(bf16[512,768]{1,0:T(8,128)(2,1)S(1)} %pad_maximum_fusion.4.first), channel_id=1, source_target_pairs={{0,4},{4,0},{8,12},{12,8},{16,20},{20,16},{24,28},{28,24},{1,5},{5... | collective-permute-start | bytes 2359304 | tf_op jit(solution)/shard_map/ppermute | solution.py:779
  73.3 22.0 %collective-permute-done.10 = bf16[128,2176]{1,0:T(8,128)(2,1)S(1)} collective-permute-done((bf16[128,2176]{1,0:T(8,128)(2,1)S(1)}, bf16[128,2176]{1,0:T(8,128)(2,1)S(1)}, u32[]{:S(2)}, u32[]{:S(2)}) %collective-permute-start.10) | collective-permute-done | bytes 557088 | tf_op jit(solution)/shard_map/ppermute | solution.py:779
  105.5 10.0 %shard_map.304 = (bf16[1024,256]{1,0:T(8,128)(2,1)S(1)}, f32[8,1024]{1,0:T(8,128)S(1)}) custom-call(s32[8]{0:T(128)S(1)} %copy-done.237, bf16[1024,768]{1,0:T(8,128)(2,1)S(1)} %get-tuple-element.415.qkv, bf16[1024,512]{1,0:T(8,128)(2,1)S(1)} %get-tuple-element.416.kvp), custom_call_target="tpu_custom_call" | custom-call | flops 1024 | bytes 11520000 | tf_op jit(solution)/shard_map/pallas_call | solution.py:340
  115.5 7.1 %collective-permute-done.14 = bf16[256,2176]{1,0:T(8,128)(2,1)S(1)} collective-permute-done((bf16[256,2176]{1,0:T(8,128)(2,1)S(1)}, bf16[256,2176]{1,0:T(8,128)(2,1)S(1)}, u32[]{:S(2)}, u32[]{:S(2)}) %collective-permute-start.14) | collective-permute-done | bytes 1114144 | tf_op jit(solution)/shard_map/ppermute | solution.py:779
  128.0 11.2 %collective-permute-start.19 = (bf16[512,1536]{1,0:T(8,128)(2,1)S(1)}, bf16[512,1536]{1,0:T(8,128)(2,1)S(1)}, u32[]{:S(2)}, u32[]{:S(2)}) collective-permute-start(bf16[512,1536]{1,0:T(8,128)(2,1)S(1)} %slice.187.first), channel_id=1, source_target_pairs={{0,4},{4,0},{8,12},{12,8},{16,20},{20,16},{24,28},{28,24},{1,5},{5... | collective-permute-start | bytes 4718600 | tf_op jit(solution)/shard_map/ppermute | solution.py:779
  149.7 10.2 %shard_map.306 = (bf16[1024,256]{1,0:T(8,128)(2,1)S(1)}, f32[8,1024]{1,0:T(8,128)S(1)}) custom-call(s32[8]{0:T(128)S(1)} %copy-done.236, bf16[1024,768]{1,0:T(8,128)(2,1)S(1)} %get-tuple-element.433.qkv, bf16[1024,512]{1,0:T(8,128)(2,1)S(1)} %get-tuple-element.434.kvp), custom_call_target="tpu_custom_call" | custom-call | flops 1024 | bytes 11520000 | tf_op jit(solution)/shard_map/pallas_call | solution.py:340
  161.3 13.1 %collective-permute-done.13.far = bf16[512,256]{1,0:T(8,128)(2,1)S(1)} collective-permute-done((bf16[512,256]{1,0:T(8,128)(2,1)S(1)}, bf16[512,256]{1,0:T(8,128)(2,1)S(1)}, u32[]{:S(2)}, u32[]{:S(2)}) %collective-permute-start.13) | collective-permute-done | bytes 262176 | tf_op jit(solution)/shard_map/ppermute | solution.py:779
  174.5 8.2 %collective-permute-done.19.second = bf16[512,1536]{1,0:T(8,128)(2,1)S(1)} collective-permute-done((bf16[512,1536]{1,0:T(8,128)(2,1)S(1)}, bf16[512,1536]{1,0:T(8,128)(2,1)S(1)}, u32[]{:S(2)}, u32[]{:S(2)}) %collective-permute-start.19) | collective-permute-done | bytes 1572896 | tf_op jit(solution)/shard_map/ppermute | solution.py:779
  211.0 7.7 %shard_map.311 = (bf16[1024,256]{1,0:T(8,128)(2,1)S(1)}, f32[8,1024]{1,0:T(8,128)S(1)}, bf16[1024,256]{1,0:T(8,128)(2,1)S(1)}) custom-call(s32[8]{0:T(128)S(1)} %copy-done.237, bf16[256,256]{1,0:T(8,128)(2,1)S(1)} %get-tuple-element.459.own, bf16[512,256]{1,0:T(8,128)(2,1)S(1)} %collective-permute-done.30.near, ...), custom_call_target="tpu_custom_call" | custom-call | flops 1024 | bytes 5760000 | tf_op jit(solution)/shard_map/pallas_call | solution.py:340
  223.4 8.1 %shard_map.312 = (bf16[1024,256]{1,0:T(8,128)(2,1)S(1)}, f32[8,1024]{1,0:T(8,128)S(1)}, bf16[1024,256]{1,0:T(8,128)(2,1)S(1)}) custom-call(s32[8]{0:T(128)S(1)} %copy-done.236, bf16[256,256]{1,0:T(8,128)(2,1)S(1)} %get-tuple-element.479.own, bf16[512,256]{1,0:T(8,128)(2,1)S(1)} %collective-permute-done.34.near, ...), custom_call_target="tpu_custom_call" | custom-call | flops 1024 | bytes 5760000 | tf_op jit(solution)/shard_map/pallas_call | solution.py:340
  256.2 13.6 %shard_map.317 = (bf16[1024,1024]{1,0:T(8,128)(2,1)S(1)}, bf16[1024,1024]{1,0:T(8,128)(2,1)S(1)}, bf16[1024,1024]{1,0:T(8,128)(2,1)S(1)}, bf16[1024,1024]{1,0:T(...) custom-call(s32[1]{0:T(128)} %bitcast.at, ...), custom_call_target="tpu_custom_call" | custom-call | flops 1024 | bytes 9600000 | tf_op jit(solution)/shard_map/pallas_call | solution.py:340
  276.4 13.4 %shard_map.319 = (bf16[1024,1024]{1,0:T(8,128)(2,1)S(1)}, bf16[1024,1024]{1,0:T(8,128)(2,1)S(1)}, bf16[1024,1024]{1,0:T(8,128)(2,1)S(1)}, bf16[1024,1024]{1,0:T(...) custom-call(s32[1]{0:T(128)} %bitcast.at, ...), custom_call_target="tpu_custom_call" | custom-call | flops 1024 | bytes 9600000 | tf_op jit(solution)/shard_map/pallas_call | solution.py:340
  339.7 11.2 %shard_map.326 = (bf16[1024,256]{1,0:T(8,128)(2,1)S(1)}, bf16[640,512]{1,0:T(8,128)(2,1)S(1)}, bf16[640,512]{1,0:T(8,128)(2,1)S(1)}) custom-call(s32[8]{0:T(128)S(1)} %copy-done.237, bf16[1024,256]{1,0:T(8,128)(2,1)S(1)} %copy-done.177, bf16[640,512]{1,0:T(8,128)(2,1)S(1)} %copy-done.69, bf16[640,512]{1,0:T(8,128)(2,1)S(1)} %copy-done.67, ...), custom_call_target="tpu_custom_call" | custom-call | flops 1024 | bytes 8960000 | tf_op jit(solution)/shard_map/pallas_call | solution.py:340
  355.1 10.8 %shard_map.327 = (bf16[1024,256]{1,0:T(8,128)(2,1)S(1)}, bf16[640,512]{1,0:T(8,128)(2,1)S(1)}, bf16[640,512]{1,0:T(8,128)(2,1)S(1)}) custom-call(s32[8]{0:T(128)S(1)} %copy-done.236, bf16[1024,256]{1,0:T(8,128)(2,1)S(1)} %copy-done.179, bf16[640,512]{1,0:T(8,128)(2,1)S(1)} %copy-done.65, bf16[640,512]{1,0:T(8,128)(2,1)S(1)} %get-tuple-element.483.kv1, ...), custom_call_target="tpu_custom_call" | custom-call | flops 1024 | bytes 8960000 | tf_op jit(solution)/shard_map/pallas_call | solution.py:340
  398.5 6.2 shard_map.333
  418.1 9.6 %collective-permute-start.70 = (bf16[512,1536]{1,0:T(8,128)(2,1)S(1)}, bf16[512,1536]{1,0:T(8,128)(2,1)S(1)}, u32[]{:S(2)}, u32[]{:S(2)}) collective-permute-start(bf16[512,1536]{1,0:T(8,128)(2,1)S(1)} %get-tuple-element.692), channel_id=1, source_target_pairs={{0,8},{4,12},{8,0},{12,4},{16,24},{20,28},{24,16},{28,20},{1,9},{5... | collective-permute-start | bytes 4718600 | tf_op jit(solution)/shard_map/ppermute | solution.py:779
  427.8 12.5 %shard_map.335 = (bf16[1024,256]{1,0:T(8,128)(2,1)S(1)}, bf16[1024,512]{1,0:T(8,128)(2,1)S(1)}, bf16[1024,512]{1,0:T(8,128)(2,1)S(1)}) custom-call(s32[8]{0:T(128)S(1)} %copy-done.237, bf16[1024,768]{1,0:T(8,128)(2,1)S(1)} %copy-done.48, bf16[1024,512]{1,0:T(8,128)(2,1)S(1)} %copy-done.57, bf16[1024,256]{1,0:T(8,128)(2,1)S(1)} %copy-done.95, ...), custom_call_target="tpu_custom_call" | custom-call | flops 1024 | bytes 14080000 | tf_op jit(solution)/shard_map/pallas_call | solution.py:340
  454.0 9.3 %collective-permute-done.63.far = bf16[512,256]{1,0:T(8,128)(2,1)S(1)} collective-permute-done((bf16[512,256]{1,0:T(8,128)(2,1)S(1)}, bf16[512,256]{1,0:T(8,128)(2,1)S(1)}, u32[]{:S(2)}, u32[]{:S(2)}) %collective-permute-start.63) | collective-permute-done | bytes 262176 | tf_op jit(solution)/shard_map/ppermute | solution.py:779
  469.0 8.5 %collective-permute-start.75 = (bf16[256,1536]{1,0:T(8,128)(2,1)S(1)}, bf16[256,1536]{1,0:T(8,128)(2,1)S(1)}, u32[]{:S(2)}, u32[]{:S(2)}) collective-permute-start(bf16[256,1536]{1,0:T(8,128)(2,1)S(1)} %get-tuple-element.721), channel_id=1, source_target_pairs={{0,4},{4,0},{8,12},{12,8},{16,20},{20,16},{24,28},{28,24},{1,5},{5... | collective-permute-start | bytes 2359304 | tf_op jit(solution)/shard_map/ppermute | solution.py:779
  485.8 12.7 %shard_map.342 = (bf16[1024,256]{1,0:T(8,128)(2,1)S(1)}, bf16[1024,512]{1,0:T(8,128)(2,1)S(1)}, bf16[1024,512]{1,0:T(8,128)(2,1)S(1)}) custom-call(s32[8]{0:T(128)S(1)} %copy-done.236, bf16[1024,768]{1,0:T(8,128)(2,1)S(1)} %copy-done.46, bf16[1024,512]{1,0:T(8,128)(2,1)S(1)} %copy-done.55, bf16[1024,256]{1,0:T(8,128)(2,1)S(1)} %copy-done.93, ...), custom_call_target="tpu_custom_call" | custom-call | flops 1024 | bytes 14080000 | tf_op jit(solution)/shard_map/pallas_call | solution.py:340
  519.5 15.9 %collective-permute-done.79.far = bf16[640,1024]{1,0:T(8,128)(2,1)S(1)} collective-permute-done((bf16[640,1024]{1,0:T(8,128)(2,1)S(1)}, bf16[640,1024]{1,0:T(8,128)(2,1)S(1)}, u32[]{:S(2)}, u32[]{:S(2)}) %collective-permute-start.79) | collective-permute-done | bytes 1310752 | tf_op jit(solution)/shard_map/ppermute | solution.py:779
  538.3 11.9 %collective-permute-start.83 = (bf16[256,640]{1,0:T(8,128)(2,1)}, bf16[256,640]{1,0:T(8,128)(2,1)}, u32[]{:S(2)}, u32[]{:S(2)}) collective-permute-start(bf16[256,640]{1,0:T(8,128)(2,1)} %get-tuple-element.750), channel_id=1, source_target_pairs={{0,4},{4,0},{8,12},{12,8},{16,20},{20,16},{24,28},{28,24},{1,5},{5... | collective-permute-start | bytes 983048 | tf_op jit(solution)/shard_map/ppermute | solution.py:779
  561.5 13.2 %collective-permute-start.88 = (bf16[128,640]{1,0:T(8,128)(2,1)S(1)}, bf16[128,640]{1,0:T(8,128)(2,1)S(1)}, u32[]{:S(2)}, u32[]{:S(2)}) collective-permute-start(bf16[128,640]{1,0:T(8,128)(2,1)S(1)} %get-tuple-element.772), channel_id=1, source_target_pairs={{0,16},{4,20},{8,24},{12,28},{16,0},{20,4},{24,8},{28,12},{1,17},{... | collective-permute-start | bytes 491528 | tf_op jit(solution)/shard_map/ppermute | solution.py:779
  (861 shorter events, 355.5 us)
Async XLA Ops:
  7.2 233.6 %all-gather.2.cloned.1.call-start = ((), (), s32[]{:S(2)}) async-start(), calls=%async_computation.1 | async-start | bytes 4718592 | tf_op jit(solution)/shard_map/all_gather | solution.py:1087
  28.2 32.3 %collective-permute-start.5 = (bf16[512,1024]{1,0:T(8,128)(2,1)S(1)}, bf16[512,1024]{1,0:T(8,128)(2,1)}, u32[]{:S(2)}, u32[]{:S(2)}) collective-permute-start(bf16[512,1024]{1,0:T(8,128)(2,1)S(1)} %shard_map.300.refs_0_), channel_id=1, source_target_pairs={{0,2},{1,3},{2,0},{3,1},{4,6},{5,7},{6,4},{7,5},{8,10},{9,11},{10,... | collective-permute-start | bytes 3145736 | tf_op jit(solution)/shard_map/ppermute | solution.py:779
  52.8 42.6 %collective-permute-start.11 = (bf16[512,1024]{1,0:T(8,128)(2,1)}, bf16[512,1024]{1,0:T(8,128)(2,1)}, u32[]{:S(2)}, u32[]{:S(2)}) collective-permute-start(bf16[512,1024]{1,0:T(8,128)(2,1)} %copy-done.16), channel_id=1, source_target_pairs={{0,2},{1,3},{2,0},{3,1},{4,6},{5,7},{6,4},{7,5},{8,10},{9,11},{10,... | collective-permute-start | bytes 3145736 | tf_op jit(solution)/shard_map/ppermute | solution.py:779
  60.5 34.9 %collective-permute-start.9 = (bf16[512,768]{1,0:T(8,128)(2,1)S(1)}, bf16[512,768]{1,0:T(8,128)(2,1)S(1)}, u32[]{:S(2)}, u32[]{:S(2)}) collective-permute-start(bf16[512,768]{1,0:T(8,128)(2,1)S(1)} %pad_maximum_fusion.4.first), channel_id=1, source_target_pairs={{0,4},{4,0},{8,12},{12,8},{16,20},{20,16},{24,28},{28,24},{1,5},{5... | collective-permute-start | bytes 2359304 | tf_op jit(solution)/shard_map/ppermute | solution.py:779
  96.0 26.6 %collective-permute-start.14 = (bf16[256,2176]{1,0:T(8,128)(2,1)S(1)}, bf16[256,2176]{1,0:T(8,128)(2,1)S(1)}, u32[]{:S(2)}, u32[]{:S(2)}) collective-permute-start(bf16[256,2176]{1,0:T(8,128)(2,1)S(1)} %pad_maximum_fusion.2), channel_id=1, source_target_pairs={{0,8},{4,12},{8,0},{12,4},{16,24},{20,28},{24,16},{28,20},{1,9},{5... | collective-permute-start | bytes 3342344 | tf_op jit(solution)/shard_map/ppermute | solution.py:779
  96.8 28.5 %collective-permute-start.17 = (bf16[512,1024]{1,0:T(8,128)(2,1)S(1)}, bf16[512,1024]{1,0:T(8,128)(2,1)}, u32[]{:S(2)}, u32[]{:S(2)}) collective-permute-start(bf16[512,1024]{1,0:T(8,128)(2,1)S(1)} %bitcast.102), channel_id=1, source_target_pairs={{0,2},{1,3},{2,0},{3,1},{4,6},{5,7},{6,4},{7,5},{8,10},{9,11},{10,... | collective-permute-start | bytes 3145736 | tf_op jit(solution)/shard_map/ppermute | solution.py:779
  97.4 27.9 %collective-permute-start.18 = (bf16[512,1024]{1,0:T(8,128)(2,1)S(1)}, bf16[512,1024]{1,0:T(8,128)(2,1)S(1)}, u32[]{:S(2)}, u32[]{:S(2)}) collective-permute-start(bf16[512,1024]{1,0:T(8,128)(2,1)S(1)} %bitcast.103), channel_id=1, source_target_pairs={{0,1},{1,0},{2,3},{3,2},{4,5},{5,4},{6,7},{7,6},{8,9},{9,8},{10,11... | collective-permute-start | bytes 3145736 | tf_op jit(solution)/shard_map/ppermute | solution.py:779
  126.3 339.1 %reduce-scatter.2.cloned.1.call-start = ((), (), s32[]{:S(2)}) async-start(), calls=%async_computation.2 | async-start | bytes 4718592 | tf_op jit(solution)/shard_map/reduce_scatter | solution.py:1098
  128.0 54.6 %collective-permute-start.19 = (bf16[512,1536]{1,0:T(8,128)(2,1)S(1)}, bf16[512,1536]{1,0:T(8,128)(2,1)S(1)}, u32[]{:S(2)}, u32[]{:S(2)}) collective-permute-start(bf16[512,1536]{1,0:T(8,128)(2,1)S(1)} %slice.187.first), channel_id=1, source_target_pairs={{0,4},{4,0},{8,12},{12,8},{16,20},{20,16},{24,28},{28,24},{1,5},{5... | collective-permute-start | bytes 4718600 | tf_op jit(solution)/shard_map/ppermute | solution.py:779
  139.7 34.7 %collective-permute-start.20 = (bf16[320,1024]{1,0:T(8,128)(2,1)}, bf16[320,1024]{1,0:T(8,128)(2,1)S(1)}, u32[]{:S(2)}, u32[]{:S(2)}) collective-permute-start(bf16[320,1024]{1,0:T(8,128)(2,1)} %copy-done.162), channel_id=1, source_target_pairs={{0,2},{1,3},{2,0},{3,1},{4,6},{5,7},{6,4},{7,5},{8,10},{9,11},{10,... | collective-permute-start | bytes 1966088 | tf_op jit(solution)/shard_map/ppermute | solution.py:779
  141.2 33.2 %collective-permute-start.21 = (bf16[320,1024]{1,0:T(8,128)(2,1)}, bf16[320,1024]{1,0:T(8,128)(2,1)S(1)}, u32[]{:S(2)}, u32[]{:S(2)}) collective-permute-start(bf16[320,1024]{1,0:T(8,128)(2,1)} %copy-done.162), channel_id=1, source_target_pairs={{0,1},{1,0},{2,3},{3,2},{4,5},{5,4},{6,7},{7,6},{8,9},{9,8},{10,11... | collective-permute-start | bytes 1966088 | tf_op jit(solution)/shard_map/ppermute | solution.py:779
  142.2 32.3 %collective-permute-start.13 = (bf16[512,256]{1,0:T(8,128)(2,1)S(1)}, bf16[512,256]{1,0:T(8,128)(2,1)S(1)}, u32[]{:S(2)}, u32[]{:S(2)}) collective-permute-start(bf16[512,256]{1,0:T(8,128)(2,1)S(1)} %slice.186), channel_id=1, source_target_pairs={{0,2},{1,3},{2,0},{3,1},{4,6},{5,7},{6,4},{7,5},{8,10},{9,11},{10,... | collective-permute-start | bytes 786440 | tf_op jit(solution)/shard_map/ppermute | solution.py:779
  189.3 30.9 %collective-permute-start.33 = (bf16[512,640]{1,0:T(8,128)(2,1)S(1)}, bf16[512,640]{1,0:T(8,128)(2,1)S(1)}, u32[]{:S(2)}, u32[]{:S(2)}) collective-permute-start(bf16[512,640]{1,0:T(8,128)(2,1)S(1)} %slice.188.first), channel_id=1, source_target_pairs={{0,4},{4,0},{8,12},{12,8},{16,20},{20,16},{24,28},{28,24},{1,5},{5... | collective-permute-start | bytes 1966088 | tf_op jit(solution)/shard_map/ppermute | solution.py:779
  299.6 31.0 %collective-permute-start.48 = (bf16[512,256]{1,0:T(8,128)(2,1)}, bf16[512,256]{1,0:T(8,128)(2,1)S(1)}, u32[]{:S(2)}, u32[]{:S(2)}) collective-permute-start(bf16[512,256]{1,0:T(8,128)(2,1)} %get-tuple-element.536), channel_id=1, source_target_pairs={{0,2},{1,3},{2,0},{3,1},{4,6},{5,7},{6,4},{7,5},{8,10},{9,11},{10,... | collective-permute-start | bytes 786440 | tf_op jit(solution)/shard_map/ppermute | solution.py:779
  330.7 35.3 %collective-permute-start.51 = (bf16[512,1024]{1,0:T(8,128)(2,1)}, bf16[512,1024]{1,0:T(8,128)(2,1)S(1)}, u32[]{:S(2)}, u32[]{:S(2)}) collective-permute-start(bf16[512,1024]{1,0:T(8,128)(2,1)} %copy-done.240), channel_id=1, source_target_pairs={{0,1},{1,0},{2,3},{3,2},{4,5},{5,4},{6,7},{7,6},{8,9},{9,8},{10,11... | collective-permute-start | bytes 3145736 | tf_op jit(solution)/shard_map/ppermute | solution.py:779
  418.1 46.1 %collective-permute-start.70 = (bf16[512,1536]{1,0:T(8,128)(2,1)S(1)}, bf16[512,1536]{1,0:T(8,128)(2,1)S(1)}, u32[]{:S(2)}, u32[]{:S(2)}) collective-permute-start(bf16[512,1536]{1,0:T(8,128)(2,1)S(1)} %get-tuple-element.692), channel_id=1, source_target_pairs={{0,8},{4,12},{8,0},{12,4},{16,24},{20,28},{24,16},{28,20},{1,9},{5... | collective-permute-start | bytes 4718600 | tf_op jit(solution)/shard_map/ppermute | solution.py:779
  469.0 36.7 %collective-permute-start.75 = (bf16[256,1536]{1,0:T(8,128)(2,1)S(1)}, bf16[256,1536]{1,0:T(8,128)(2,1)S(1)}, u32[]{:S(2)}, u32[]{:S(2)}) collective-permute-start(bf16[256,1536]{1,0:T(8,128)(2,1)S(1)} %get-tuple-element.721), channel_id=1, source_target_pairs={{0,4},{4,0},{8,12},{12,8},{16,20},{20,16},{24,28},{28,24},{1,5},{5... | collective-permute-start | bytes 2359304 | tf_op jit(solution)/shard_map/ppermute | solution.py:779
  505.7 29.7 %collective-permute-start.79 = (bf16[640,1024]{1,0:T(8,128)(2,1)S(1)}, bf16[640,1024]{1,0:T(8,128)(2,1)S(1)}, u32[]{:S(2)}, u32[]{:S(2)}) collective-permute-start(bf16[640,1024]{1,0:T(8,128)(2,1)S(1)} %get-tuple-element.740), channel_id=1, source_target_pairs={{0,2},{1,3},{2,0},{3,1},{4,6},{5,7},{6,4},{7,5},{8,10},{9,11},{10,... | collective-permute-start | bytes 3932168 | tf_op jit(solution)/shard_map/ppermute | solution.py:779
  510.1 50.3 %collective-permute-start.76 = (bf16[512,768]{1,0:T(8,128)(2,1)}, bf16[512,768]{1,0:T(8,128)(2,1)}, u32[]{:S(2)}, u32[]{:S(2)}) collective-permute-start(bf16[512,768]{1,0:T(8,128)(2,1)} %get-tuple-element.723), channel_id=1, source_target_pairs={{0,8},{4,12},{8,0},{12,4},{16,24},{20,28},{24,16},{28,20},{1,9},{5... | collective-permute-start | bytes 2359304 | tf_op jit(solution)/shard_map/ppermute | solution.py:779
  515.2 45.2 %collective-permute-start.82 = (bf16[256,1024]{1,0:T(8,128)(2,1)}, bf16[256,1024]{1,0:T(8,128)(2,1)}, u32[]{:S(2)}, u32[]{:S(2)}) collective-permute-start(bf16[256,1024]{1,0:T(8,128)(2,1)} %shard_map.350), channel_id=1, source_target_pairs={{4,0},{8,4},{12,8},{16,12},{20,16},{24,20},{28,24},{5,1},{9,5},{13... | collective-permute-start | bytes 1572872 | tf_op jit(solution)/shard_map/ppermute | solution.py:785
  557.5 30.3 %collective-permute-start.87 = (bf16[128,1536]{1,0:T(8,128)(2,1)S(1)}, bf16[128,1536]{1,0:T(8,128)(2,1)S(1)}, u32[]{:S(2)}, u32[]{:S(2)}) collective-permute-start(bf16[128,1536]{1,0:T(8,128)(2,1)S(1)} %get-tuple-element.768), channel_id=1, source_target_pairs={{0,16},{4,20},{8,24},{12,28},{16,0},{20,4},{24,8},{28,12},{1,17},{... | collective-permute-start | bytes 1179656 | tf_op jit(solution)/shard_map/ppermute | solution.py:779
  561.5 26.3 %collective-permute-start.88 = (bf16[128,640]{1,0:T(8,128)(2,1)S(1)}, bf16[128,640]{1,0:T(8,128)(2,1)S(1)}, u32[]{:S(2)}, u32[]{:S(2)}) collective-permute-start(bf16[128,640]{1,0:T(8,128)(2,1)S(1)} %get-tuple-element.772), channel_id=1, source_target_pairs={{0,16},{4,20},{8,24},{12,28},{16,0},{20,4},{24,8},{28,12},{1,17},{... | collective-permute-start | bytes 491528 | tf_op jit(solution)/shard_map/ppermute | solution.py:779
  581.8 42.7 %collective-permute-start.85 = (bf16[320,1024]{1,0:T(8,128)(2,1)}, bf16[320,1024]{1,0:T(8,128)(2,1)}, u32[]{:S(2)}, u32[]{:S(2)}) collective-permute-start(bf16[320,1024]{1,0:T(8,128)(2,1)} %slice.246), channel_id=1, source_target_pairs={{4,0},{8,4},{12,8},{16,12},{20,16},{24,20},{28,24},{5,1},{9,5},{13... | collective-permute-start | bytes 1966088 | tf_op jit(solution)/shard_map/ppermute | solution.py:785
  584.4 26.9 %collective-permute-start.84 = (bf16[256,1024]{1,0:T(8,128)(2,1)S(1)}, bf16[256,1024]{1,0:T(8,128)(2,1)}, u32[]{:S(2)}, u32[]{:S(2)}) collective-permute-start(bf16[256,1024]{1,0:T(8,128)(2,1)S(1)} %shard_map.353), channel_id=1, source_target_pairs={{4,0},{8,4},{12,8},{16,12},{20,16},{24,20},{28,24},{5,1},{9,5},{13... | collective-permute-start | bytes 1572872 | tf_op jit(solution)/shard_map/ppermute | solution.py:785
  (328 other events, 2897.1 us)
Sparse Core Ops, SparseCore 0:
  126.4 98.5 all-gather.1
  330.8 94.9 reduce-scatter.1

commit v5 on v4

--- a/solution.py
+++ b/solution.py
@@ -1064,13 +1064,13 @@
         state["cout_other"] = flip(state["cout_own"], "mem", 1)
 
     def memory_side():
-        before, near_own = yield 2, lambda: (memory_before, flip(memory_own, "mem", 1))
+        before, near_own, far_own = yield 3, lambda: (memory_before, flip(memory_own, "mem", 1), memory_far)
         far_prev, near_prev = flip(before, "mem", 2), flip(before, "mem", 1)
-        *gone, far_own = yield 3, lambda: (before, near_own, far_prev, near_prev, memory_far)
-        before, near_own, far_prev, near_prev = gone
-        last_own, last_prev = flip(far_own, "mem", 1), flip(far_prev, "mem", 1)
+        last_own = flip(far_own, "mem", 1)
+        *gone, far_prev = yield 5, lambda: (before, near_own, far_own, last_own, near_prev, far_prev)
+        before, near_own, far_own, last_own, near_prev = gone
+        last_prev = flip(far_prev, "mem", 1)
         pieces = memory_own, near_own, far_own, last_own, before, near_prev, far_prev, last_prev
-        pieces = yield 4, lambda: pieces
         whole = blocks * padded
         outs = [shape(whole, D)] * (2 * MICRO) + [shape(whole, 2 * width)] * (2 * MICRO)
         got = call(functools.partial(memory_kernel, padded), place, (*pieces, state["ckv"]), outs, time=6)

time: 650 us -> 672 us (1.034)
  waiting for transfers between devices: 138 us -> 178 us
  starting transfers between devices: 141 us -> 126 us
    ppermute x5, waiting for transfers between devices: 3.79 us -> 49.6 us  [shifted(): return lax.ppermute(block, 'seq', route)]
    ppermute x93, starting transfers between devices: 131 us -> 116 us  [flip(): lax.ppermute(block, axis, [(i, i ^ bit) for i in range(lax.axis_size(axis...]
    unnamed x512 -> x510, local copies, waits for them, and re-layouts: 102 us -> 100 us
  transfers between devices with their start and end apart: 100 -> 100, of which waited for: 31 -> 34; matrix products, arithmetic and copies ran while one was open for 7% -> 7% of each run, Pallas kernels for 31% -> 30%
where the time goes in v5:
time: 672 us; the launch traced here: 662 us
  Pallas kernels  196 us (29%)
  waiting for transfers between devices  178 us (26%)
  starting transfers between devices  126 us (19%)
  local copies, waits for them, and re-layouts  122 us (18%)
  other arithmetic  21.3 us (3%)
  between operations  17.6 us (3%)
    pallas_call x62, Pallas kernels, call(): pl.pallas_call(kernel, out_shape=outs, in_specs=[pl.BlockSpec(memory_spac...  195 us
    ppermute x93, waiting for transfers between devices, flip(): lax.ppermute(block, axis, [(i, i ^ bit) for i in range(lax.axis_size(axis...  128 us
    ppermute x93, starting transfers between devices, flip(): lax.ppermute(block, axis, [(i, i ^ bit) for i in range(lax.axis_size(axis...  116 us
    unnamed x510, local copies, waits for them, and re-layouts  100 us
    ppermute x5, waiting for transfers between devices, shifted(): return lax.ppermute(block, 'seq', route)  49.6 us
  transfers between devices with their start and end apart: 100, of which 34 were waited for; matrix products, arithmetic and copies ran while one was open for 7% of the time, Pallas kernels for 30%

profile of v5, /device:TPU:0, one launch (start us, length us, event | category | flops | bytes accessed | tf_op | source)
XLA Modules:
  0.0 662.2 jit_solution(17875581015107813805)
XLA Ops:
  32.9 9.4 %collective-permute-done.2 = bf16[128,768]{1,0:T(8,128)(2,1)S(1)} collective-permute-done((bf16[128,768]{1,0:T(8,128)(2,1)S(1)}, bf16[128,768]{1,0:T(8,128)(2,1)S(1)}, u32[]{:S(2)}, u32[]{:S(2)}) %collective-permute-start.2) | collective-permute-done | bytes 196640 | tf_op jit(solution)/shard_map/ppermute | solution.py:779
  60.4 8.2 %collective-permute-start.9 = (bf16[512,768]{1,0:T(8,128)(2,1)S(1)}, bf16[512,768]{1,0:T(8,128)(2,1)S(1)}, u32[]{:S(2)}, u32[]{:S(2)}) collective-permute-start(bf16[512,768]{1,0:T(8,128)(2,1)S(1)} %pad_maximum_fusion.4.first), channel_id=1, source_target_pairs={{0,4},{4,0},{8,12},{12,8},{16,20},{20,16},{24,28},{28,24},{1,5},{5... | collective-permute-start | bytes 2359304 | tf_op jit(solution)/shard_map/ppermute | solution.py:779
  72.5 21.9 %collective-permute-done.10 = bf16[128,2176]{1,0:T(8,128)(2,1)S(1)} collective-permute-done((bf16[128,2176]{1,0:T(8,128)(2,1)S(1)}, bf16[128,2176]{1,0:T(8,128)(2,1)S(1)}, u32[]{:S(2)}, u32[]{:S(2)}) %collective-permute-start.10) | collective-permute-done | bytes 557088 | tf_op jit(solution)/shard_map/ppermute | solution.py:779
  106.1 10.0 %shard_map.304 = (bf16[1024,256]{1,0:T(8,128)(2,1)S(1)}, f32[8,1024]{1,0:T(8,128)S(1)}) custom-call(s32[8]{0:T(128)S(1)} %copy-done.237, bf16[1024,768]{1,0:T(8,128)(2,1)S(1)} %get-tuple-element.409.qkv, bf16[1024,512]{1,0:T(8,128)(2,1)S(1)} %get-tuple-element.410.kvp), custom_call_target="tpu_custom_call" | custom-call | flops 1024 | bytes 11520000 | tf_op jit(solution)/shard_map/pallas_call | solution.py:340
  140.3 10.2 %shard_map.306 = (bf16[1024,256]{1,0:T(8,128)(2,1)S(1)}, f32[8,1024]{1,0:T(8,128)S(1)}) custom-call(s32[8]{0:T(128)S(1)} %copy-done.236, bf16[1024,768]{1,0:T(8,128)(2,1)S(1)} %get-tuple-element.426.qkv, bf16[1024,512]{1,0:T(8,128)(2,1)S(1)} %get-tuple-element.427.kvp), custom_call_target="tpu_custom_call" | custom-call | flops 1024 | bytes 11520000 | tf_op jit(solution)/shard_map/pallas_call | solution.py:340
  151.8 45.1 %collective-permute-done.17.refs_4_ = bf16[320,1024]{1,0:T(8,128)(2,1)S(1)} collective-permute-done((bf16[320,1024]{1,0:T(8,128)(2,1)S(1)}, bf16[320,1024]{1,0:T(8,128)(2,1)S(1)}, u32[]{:S(2)}, u32[]{:S(2)}) %collective-permute-start.17) | collective-permute-done | bytes 655392 | tf_op jit(solution)/shard_map/ppermute | solution.py:785
  205.5 15.3 %collective-permute-done.24.far = bf16[512,256]{1,0:T(8,128)(2,1)S(1)} collective-permute-done((bf16[512,256]{1,0:T(8,128)(2,1)S(1)}, bf16[512,256]{1,0:T(8,128)(2,1)S(1)}, u32[]{:S(2)}, u32[]{:S(2)}) %collective-permute-start.24) | collective-permute-done | bytes 262176 | tf_op jit(solution)/shard_map/ppermute | solution.py:779
  238.9 7.7 %shard_map.311 = (bf16[1024,256]{1,0:T(8,128)(2,1)S(1)}, f32[8,1024]{1,0:T(8,128)S(1)}, bf16[1024,256]{1,0:T(8,128)(2,1)S(1)}) custom-call(s32[8]{0:T(128)S(1)} %copy-done.237, bf16[256,256]{1,0:T(8,128)(2,1)S(1)} %get-tuple-element.449.own, bf16[512,256]{1,0:T(8,128)(2,1)S(1)} %collective-permute-done.29.near, ...), custom_call_target="tpu_custom_call" | custom-call | flops 1024 | bytes 5760000 | tf_op jit(solution)/shard_map/pallas_call | solution.py:340
  250.7 8.1 %shard_map.312 = (bf16[1024,256]{1,0:T(8,128)(2,1)S(1)}, f32[8,1024]{1,0:T(8,128)S(1)}, bf16[1024,256]{1,0:T(8,128)(2,1)S(1)}) custom-call(s32[8]{0:T(128)S(1)} %copy-done.236, bf16[256,256]{1,0:T(8,128)(2,1)S(1)} %get-tuple-element.467.own, bf16[512,256]{1,0:T(8,128)(2,1)S(1)} %collective-permute-done.34.near, ...), custom_call_target="tpu_custom_call" | custom-call | flops 1024 | bytes 5760000 | tf_op jit(solution)/shard_map/pallas_call | solution.py:340
  283.3 13.8 %shard_map.317 = (bf16[1024,1024]{1,0:T(8,128)(2,1)S(1)}, bf16[1024,1024]{1,0:T(8,128)(2,1)S(1)}, bf16[1024,1024]{1,0:T(8,128)(2,1)S(1)}, bf16[1024,1024]{1,0:T(...) custom-call(s32[1]{0:T(128)} %bitcast.at, ...), custom_call_target="tpu_custom_call" | custom-call | flops 1024 | bytes 9600000 | tf_op jit(solution)/shard_map/pallas_call | solution.py:340
  304.7 13.4 %shard_map.319 = (bf16[1024,1024]{1,0:T(8,128)(2,1)S(1)}, bf16[1024,1024]{1,0:T(8,128)(2,1)S(1)}, bf16[1024,1024]{1,0:T(8,128)(2,1)S(1)}, bf16[1024,1024]{1,0:T(...) custom-call(s32[1]{0:T(128)} %bitcast.at, ...), custom_call_target="tpu_custom_call" | custom-call | flops 1024 | bytes 9600000 | tf_op jit(solution)/shard_map/pallas_call | solution.py:340
  366.9 11.2 %shard_map.326 = (bf16[1024,256]{1,0:T(8,128)(2,1)S(1)}, bf16[640,512]{1,0:T(8,128)(2,1)S(1)}, bf16[640,512]{1,0:T(8,128)(2,1)S(1)}) custom-call(s32[8]{0:T(128)S(1)} %copy-done.237, bf16[1024,256]{1,0:T(8,128)(2,1)S(1)} %copy-done.175, bf16[640,512]{1,0:T(8,128)(2,1)S(1)} %copy-done.69, bf16[640,512]{1,0:T(8,128)(2,1)S(1)} %copy-done.67, ...), custom_call_target="tpu_custom_call" | custom-call | flops 1024 | bytes 8960000 | tf_op jit(solution)/shard_map/pallas_call | solution.py:340
  382.3 10.8 %shard_map.327 = (bf16[1024,256]{1,0:T(8,128)(2,1)S(1)}, bf16[640,512]{1,0:T(8,128)(2,1)S(1)}, bf16[640,512]{1,0:T(8,128)(2,1)S(1)}) custom-call(s32[8]{0:T(128)S(1)} %copy-done.236, bf16[1024,256]{1,0:T(8,128)(2,1)S(1)} %copy-done.177, bf16[640,512]{1,0:T(8,128)(2,1)S(1)} %copy-done.65, bf16[640,512]{1,0:T(8,128)(2,1)S(1)} %get-tuple-element.471.kv1, ...), custom_call_target="tpu_custom_call" | custom-call | flops 1024 | bytes 8960000 | tf_op jit(solution)/shard_map/pallas_call | solution.py:340
  425.6 6.2 shard_map.333
  446.4 12.5 %shard_map.335 = (bf16[1024,256]{1,0:T(8,128)(2,1)S(1)}, bf16[1024,512]{1,0:T(8,128)(2,1)S(1)}, bf16[1024,512]{1,0:T(8,128)(2,1)S(1)}) custom-call(s32[8]{0:T(128)S(1)} %copy-done.237, bf16[1024,768]{1,0:T(8,128)(2,1)S(1)} %copy-done.48, bf16[1024,512]{1,0:T(8,128)(2,1)S(1)} %copy-done.57, bf16[1024,256]{1,0:T(8,128)(2,1)S(1)} %copy-done.95, ...), custom_call_target="tpu_custom_call" | custom-call | flops 1024 | bytes 14080000 | tf_op jit(solution)/shard_map/pallas_call | solution.py:340
  472.8 9.3 %collective-permute-done.63.far = bf16[512,256]{1,0:T(8,128)(2,1)S(1)} collective-permute-done((bf16[512,256]{1,0:T(8,128)(2,1)S(1)}, bf16[512,256]{1,0:T(8,128)(2,1)S(1)}, u32[]{:S(2)}, u32[]{:S(2)}) %collective-permute-start.63) | collective-permute-done | bytes 262176 | tf_op jit(solution)/shard_map/ppermute | solution.py:779
  487.6 17.8 %collective-permute-start.75 = (bf16[256,1536]{1,0:T(8,128)(2,1)S(1)}, bf16[256,1536]{1,0:T(8,128)(2,1)S(1)}, u32[]{:S(2)}, u32[]{:S(2)}) collective-permute-start(bf16[256,1536]{1,0:T(8,128)(2,1)S(1)} %get-tuple-element.709), channel_id=1, source_target_pairs={{0,4},{4,0},{8,12},{12,8},{16,20},{20,16},{24,28},{28,24},{1,5},{5... | collective-permute-start | bytes 2359304 | tf_op jit(solution)/shard_map/ppermute | solution.py:779
  513.2 12.7 %shard_map.342 = (bf16[1024,256]{1,0:T(8,128)(2,1)S(1)}, bf16[1024,512]{1,0:T(8,128)(2,1)S(1)}, bf16[1024,512]{1,0:T(8,128)(2,1)S(1)}) custom-call(s32[8]{0:T(128)S(1)} %copy-done.236, bf16[1024,768]{1,0:T(8,128)(2,1)S(1)} %copy-done.46, bf16[1024,512]{1,0:T(8,128)(2,1)S(1)} %copy-done.55, bf16[1024,256]{1,0:T(8,128)(2,1)S(1)} %copy-done.93, ...), custom_call_target="tpu_custom_call" | custom-call | flops 1024 | bytes 14080000 | tf_op jit(solution)/shard_map/pallas_call | solution.py:340
  526.0 5.6 shard_map.343
  548.0 14.8 %collective-permute-done.79.far = bf16[640,1024]{1,0:T(8,128)(2,1)S(1)} collective-permute-done((bf16[640,1024]{1,0:T(8,128)(2,1)S(1)}, bf16[640,1024]{1,0:T(8,128)(2,1)S(1)}, u32[]{:S(2)}, u32[]{:S(2)}) %collective-permute-start.79) | collective-permute-done | bytes 1310752 | tf_op jit(solution)/shard_map/ppermute | solution.py:779
  566.6 7.2 %collective-permute-start.83 = (bf16[256,640]{1,0:T(8,128)(2,1)}, bf16[256,640]{1,0:T(8,128)(2,1)}, u32[]{:S(2)}, u32[]{:S(2)}) collective-permute-start(bf16[256,640]{1,0:T(8,128)(2,1)} %get-tuple-element.738), channel_id=1, source_target_pairs={{0,4},{4,0},{8,12},{12,8},{16,20},{20,16},{24,28},{28,24},{1,5},{5... | collective-permute-start | bytes 983048 | tf_op jit(solution)/shard_map/ppermute | solution.py:779
  581.2 5.2 collective-permute-done.81.far
  591.1 6.9 %collective-permute-start.86 = (bf16[256,768]{1,0:T(8,128)(2,1)S(1)}, bf16[256,768]{1,0:T(8,128)(2,1)S(1)}, u32[]{:S(2)}, u32[]{:S(2)}) collective-permute-start(bf16[256,768]{1,0:T(8,128)(2,1)S(1)} %get-tuple-element.752), channel_id=1, source_target_pairs={{0,4},{4,0},{8,12},{12,8},{16,20},{20,16},{24,28},{28,24},{1,5},{5... | collective-permute-start | bytes 1179656 | tf_op jit(solution)/shard_map/ppermute | solution.py:779
  617.2 6.4 collective-permute-start.89
  (859 shorter events, 354.8 us)
Async XLA Ops:
  7.2 260.8 %all-gather.2.cloned.1.call-start = ((), (), s32[]{:S(2)}) async-start(), calls=%async_computation.1 | async-start | bytes 4718592 | tf_op jit(solution)/shard_map/all_gather | solution.py:1087
  28.2 32.2 %collective-permute-start.5 = (bf16[512,1024]{1,0:T(8,128)(2,1)S(1)}, bf16[512,1024]{1,0:T(8,128)(2,1)}, u32[]{:S(2)}, u32[]{:S(2)}) collective-permute-start(bf16[512,1024]{1,0:T(8,128)(2,1)S(1)} %shard_map.300.refs_0_), channel_id=1, source_target_pairs={{0,2},{1,3},{2,0},{3,1},{4,6},{5,7},{6,4},{7,5},{8,10},{9,11},{10,... | collective-permute-start | bytes 3145736 | tf_op jit(solution)/shard_map/ppermute | solution.py:779
  52.8 41.7 %collective-permute-start.11 = (bf16[512,1024]{1,0:T(8,128)(2,1)}, bf16[512,1024]{1,0:T(8,128)(2,1)}, u32[]{:S(2)}, u32[]{:S(2)}) collective-permute-start(bf16[512,1024]{1,0:T(8,128)(2,1)} %copy-done.16), channel_id=1, source_target_pairs={{0,2},{1,3},{2,0},{3,1},{4,6},{5,7},{6,4},{7,5},{8,10},{9,11},{10,... | collective-permute-start | bytes 3145736 | tf_op jit(solution)/shard_map/ppermute | solution.py:779
  60.4 34.0 %collective-permute-start.9 = (bf16[512,768]{1,0:T(8,128)(2,1)S(1)}, bf16[512,768]{1,0:T(8,128)(2,1)S(1)}, u32[]{:S(2)}, u32[]{:S(2)}) collective-permute-start(bf16[512,768]{1,0:T(8,128)(2,1)S(1)} %pad_maximum_fusion.4.first), channel_id=1, source_target_pairs={{0,4},{4,0},{8,12},{12,8},{16,20},{20,16},{24,28},{28,24},{1,5},{5... | collective-permute-start | bytes 2359304 | tf_op jit(solution)/shard_map/ppermute | solution.py:779
  95.8 25.8 %collective-permute-start.15 = (bf16[512,1024]{1,0:T(8,128)(2,1)S(1)}, bf16[512,1024]{1,0:T(8,128)(2,1)}, u32[]{:S(2)}, u32[]{:S(2)}) collective-permute-start(bf16[512,1024]{1,0:T(8,128)(2,1)S(1)} %bitcast.102), channel_id=1, source_target_pairs={{0,2},{1,3},{2,0},{3,1},{4,6},{5,7},{6,4},{7,5},{8,10},{9,11},{10,... | collective-permute-start | bytes 3145736 | tf_op jit(solution)/shard_map/ppermute | solution.py:779
  122.7 361.4 %reduce-scatter.2.cloned.1.call-start = ((), (), s32[]{:S(2)}) async-start(), calls=%async_computation.2 | async-start | bytes 4718592 | tf_op jit(solution)/shard_map/reduce_scatter | solution.py:1098
  124.5 72.5 %collective-permute-start.20 = (bf16[512,1536]{1,0:T(8,128)(2,1)S(1)}, bf16[512,1536]{1,0:T(8,128)(2,1)S(1)}, u32[]{:S(2)}, u32[]{:S(2)}) collective-permute-start(bf16[512,1536]{1,0:T(8,128)(2,1)S(1)} %slice.187.first), channel_id=1, source_target_pairs={{0,4},{4,0},{8,12},{12,8},{16,20},{20,16},{24,28},{28,24},{1,5},{5... | collective-permute-start | bytes 4718600 | tf_op jit(solution)/shard_map/ppermute | solution.py:779
  128.3 68.6 %collective-permute-start.17 = (bf16[320,1024]{1,0:T(8,128)(2,1)S(1)}, bf16[320,1024]{1,0:T(8,128)(2,1)S(1)}, u32[]{:S(2)}, u32[]{:S(2)}) collective-permute-start(bf16[320,1024]{1,0:T(8,128)(2,1)S(1)} %bitcast.110), channel_id=1, source_target_pairs={{0,4},{4,8},{8,12},{12,16},{16,20},{20,24},{24,28},{1,5},{5,9},{9,... | collective-permute-start | bytes 1966088 | tf_op jit(solution)/shard_map/ppermute | solution.py:785
  130.3 66.7 %collective-permute-start.18 = (bf16[320,1024]{1,0:T(8,128)(2,1)S(1)}, bf16[320,1024]{1,0:T(8,128)(2,1)S(1)}, u32[]{:S(2)}, u32[]{:S(2)}) collective-permute-start(bf16[320,1024]{1,0:T(8,128)(2,1)S(1)} %bitcast.111), channel_id=1, source_target_pairs={{0,1},{1,0},{2,3},{3,2},{4,5},{5,4},{6,7},{7,6},{8,9},{9,8},{10,11... | collective-permute-start | bytes 1966088 | tf_op jit(solution)/shard_map/ppermute | solution.py:779
  130.4 66.6 %collective-permute-start.19 = (bf16[320,1024]{1,0:T(8,128)(2,1)S(1)}, bf16[320,1024]{1,0:T(8,128)(2,1)S(1)}, u32[]{:S(2)}, u32[]{:S(2)}) collective-permute-start(bf16[320,1024]{1,0:T(8,128)(2,1)S(1)} %bitcast.112), channel_id=1, source_target_pairs={{0,2},{1,3},{2,0},{3,1},{4,6},{5,7},{6,4},{7,5},{8,10},{9,11},{10,... | collective-permute-start | bytes 1966088 | tf_op jit(solution)/shard_map/ppermute | solution.py:779
  131.5 65.5 %collective-permute-start.13 = (bf16[512,256]{1,0:T(8,128)(2,1)S(1)}, bf16[512,256]{1,0:T(8,128)(2,1)S(1)}, u32[]{:S(2)}, u32[]{:S(2)}) collective-permute-start(bf16[512,256]{1,0:T(8,128)(2,1)S(1)} %slice.186), channel_id=1, source_target_pairs={{0,2},{1,3},{2,0},{3,1},{4,6},{5,7},{6,4},{7,5},{8,10},{9,11},{10,... | collective-permute-start | bytes 786440 | tf_op jit(solution)/shard_map/ppermute | solution.py:779
  197.9 29.1 %collective-permute-start.26 = (bf16[320,1024]{1,0:T(8,128)(2,1)S(1)}, bf16[320,1024]{1,0:T(8,128)(2,1)S(1)}, u32[]{:S(2)}, u32[]{:S(2)}) collective-permute-start(bf16[320,1024]{1,0:T(8,128)(2,1)S(1)} %collective-permute-done.19.refs_2_), channel_id=1, source_target_pairs={{0,1},{1,0},{2,3},{3,2},{4,5},{5,4},{6,7},{7,6},{8,9},{9,8},{10,11... | collective-permute-start | bytes 1966088 | tf_op jit(solution)/shard_map/ppermute | solution.py:779
  198.0 29.0 %collective-permute-start.27 = (bf16[320,1024]{1,0:T(8,128)(2,1)S(1)}, bf16[320,1024]{1,0:T(8,128)(2,1)S(1)}, u32[]{:S(2)}, u32[]{:S(2)}) collective-permute-start(bf16[320,1024]{1,0:T(8,128)(2,1)S(1)} %collective-permute-done.17.refs_4_), channel_id=1, source_target_pairs={{0,1},{1,0},{2,3},{3,2},{4,5},{5,4},{6,7},{7,6},{8,9},{9,8},{10,11... | collective-permute-start | bytes 1966088 | tf_op jit(solution)/shard_map/ppermute | solution.py:779
  198.4 28.6 %collective-permute-start.28 = (bf16[320,1024]{1,0:T(8,128)(2,1)S(1)}, bf16[320,1024]{1,0:T(8,128)(2,1)S(1)}, u32[]{:S(2)}, u32[]{:S(2)}) collective-permute-start(bf16[320,1024]{1,0:T(8,128)(2,1)S(1)} %collective-permute-done.17.refs_4_), channel_id=1, source_target_pairs={{0,2},{1,3},{2,0},{3,1},{4,6},{5,7},{6,4},{7,5},{8,10},{9,11},{10,... | collective-permute-start | bytes 1966088 | tf_op jit(solution)/shard_map/ppermute | solution.py:779
  325.5 32.3 %collective-permute-start.48 = (bf16[512,256]{1,0:T(8,128)(2,1)}, bf16[512,256]{1,0:T(8,128)(2,1)S(1)}, u32[]{:S(2)}, u32[]{:S(2)}) collective-permute-start(bf16[512,256]{1,0:T(8,128)(2,1)} %get-tuple-element.524), channel_id=1, source_target_pairs={{0,2},{1,3},{2,0},{3,1},{4,6},{5,7},{6,4},{7,5},{8,10},{9,11},{10,... | collective-permute-start | bytes 786440 | tf_op jit(solution)/shard_map/ppermute | solution.py:779
  357.8 35.3 %collective-permute-start.51 = (bf16[512,1024]{1,0:T(8,128)(2,1)}, bf16[512,1024]{1,0:T(8,128)(2,1)S(1)}, u32[]{:S(2)}, u32[]{:S(2)}) collective-permute-start(bf16[512,1024]{1,0:T(8,128)(2,1)} %copy-done.240), channel_id=1, source_target_pairs={{0,1},{1,0},{2,3},{3,2},{4,5},{5,4},{6,7},{7,6},{8,9},{9,8},{10,11... | collective-permute-start | bytes 3145736 | tf_op jit(solution)/shard_map/ppermute | solution.py:779
  445.2 37.7 %collective-permute-start.70 = (bf16[512,1536]{1,0:T(8,128)(2,1)S(1)}, bf16[512,1536]{1,0:T(8,128)(2,1)S(1)}, u32[]{:S(2)}, u32[]{:S(2)}) collective-permute-start(bf16[512,1536]{1,0:T(8,128)(2,1)S(1)} %get-tuple-element.680), channel_id=1, source_target_pairs={{0,8},{4,12},{8,0},{12,4},{16,24},{20,28},{24,16},{28,20},{1,9},{5... | collective-permute-start | bytes 4718600 | tf_op jit(solution)/shard_map/ppermute | solution.py:779
  487.6 45.5 %collective-permute-start.75 = (bf16[256,1536]{1,0:T(8,128)(2,1)S(1)}, bf16[256,1536]{1,0:T(8,128)(2,1)S(1)}, u32[]{:S(2)}, u32[]{:S(2)}) collective-permute-start(bf16[256,1536]{1,0:T(8,128)(2,1)S(1)} %get-tuple-element.709), channel_id=1, source_target_pairs={{0,4},{4,0},{8,12},{12,8},{16,20},{20,16},{24,28},{28,24},{1,5},{5... | collective-permute-start | bytes 2359304 | tf_op jit(solution)/shard_map/ppermute | solution.py:779
  533.1 29.7 %collective-permute-start.79 = (bf16[640,1024]{1,0:T(8,128)(2,1)S(1)}, bf16[640,1024]{1,0:T(8,128)(2,1)S(1)}, u32[]{:S(2)}, u32[]{:S(2)}) collective-permute-start(bf16[640,1024]{1,0:T(8,128)(2,1)S(1)} %get-tuple-element.728), channel_id=1, source_target_pairs={{0,2},{1,3},{2,0},{3,1},{4,6},{5,7},{6,4},{7,5},{8,10},{9,11},{10,... | collective-permute-start | bytes 3932168 | tf_op jit(solution)/shard_map/ppermute | solution.py:779
  538.0 43.2 %collective-permute-start.76 = (bf16[512,768]{1,0:T(8,128)(2,1)}, bf16[512,768]{1,0:T(8,128)(2,1)}, u32[]{:S(2)}, u32[]{:S(2)}) collective-permute-start(bf16[512,768]{1,0:T(8,128)(2,1)} %get-tuple-element.711), channel_id=1, source_target_pairs={{0,8},{4,12},{8,0},{12,4},{16,24},{20,28},{24,16},{28,20},{1,9},{5... | collective-permute-start | bytes 2359304 | tf_op jit(solution)/shard_map/ppermute | solution.py:779
  543.7 37.5 %collective-permute-start.82 = (bf16[256,1024]{1,0:T(8,128)(2,1)}, bf16[256,1024]{1,0:T(8,128)(2,1)}, u32[]{:S(2)}, u32[]{:S(2)}) collective-permute-start(bf16[256,1024]{1,0:T(8,128)(2,1)} %shard_map.350), channel_id=1, source_target_pairs={{4,0},{8,4},{12,8},{16,12},{20,16},{24,20},{28,24},{5,1},{9,5},{13... | collective-permute-start | bytes 1572872 | tf_op jit(solution)/shard_map/ppermute | solution.py:785
  581.2 28.5 %collective-permute-start.87 = (bf16[128,1536]{1,0:T(8,128)(2,1)S(1)}, bf16[128,1536]{1,0:T(8,128)(2,1)S(1)}, u32[]{:S(2)}, u32[]{:S(2)}) collective-permute-start(bf16[128,1536]{1,0:T(8,128)(2,1)S(1)} %get-tuple-element.756), channel_id=1, source_target_pairs={{0,16},{4,20},{8,24},{12,28},{16,0},{20,4},{24,8},{28,12},{1,17},{... | collective-permute-start | bytes 1179656 | tf_op jit(solution)/shard_map/ppermute | solution.py:779
  603.8 44.9 %collective-permute-start.85 = (bf16[320,1024]{1,0:T(8,128)(2,1)}, bf16[320,1024]{1,0:T(8,128)(2,1)}, u32[]{:S(2)}, u32[]{:S(2)}) collective-permute-start(bf16[320,1024]{1,0:T(8,128)(2,1)} %slice.246), channel_id=1, source_target_pairs={{4,0},{8,4},{12,8},{16,12},{20,16},{24,20},{28,24},{5,1},{9,5},{13... | collective-permute-start | bytes 1966088 | tf_op jit(solution)/shard_map/ppermute | solution.py:785
  606.3 30.5 %collective-permute-start.84 = (bf16[256,1024]{1,0:T(8,128)(2,1)S(1)}, bf16[256,1024]{1,0:T(8,128)(2,1)}, u32[]{:S(2)}, u32[]{:S(2)}) collective-permute-start(bf16[256,1024]{1,0:T(8,128)(2,1)S(1)} %shard_map.353), channel_id=1, source_target_pairs={{4,0},{8,4},{12,8},{16,12},{20,16},{24,20},{28,24},{5,1},{9,5},{13... | collective-permute-start | bytes 1572872 | tf_op jit(solution)/shard_map/ppermute | solution.py:785
  (327 other events, 2974.2 us)
Sparse Core Ops, SparseCore 0:
  122.8 96.5 all-gather.1
  357.9 87.5 reduce-scatter.1

commit v6 on v4

--- a/solution.py
+++ b/solution.py
@@ -336,7 +336,7 @@
 def call(kernel, scalars, arrays, outs, scratch=(), time=2):
     vmem = pl.BlockSpec(memory_space=pltpu.VMEM)
     held = (*arrays, *jax.tree.leaves(outs), *scratch)
-    room = sum(math.prod(a.shape) * jnp.dtype(a.dtype).itemsize for a in held) + 12 * 2**20
+    room = sum(math.prod(a.shape) * jnp.dtype(a.dtype).itemsize for a in held) + 7 * 2**20
     return pl.pallas_call(
         kernel,
         out_shape=outs,

time: 650 us -> 654 us (level)
    unnamed x512 -> x530, local copies, waits for them, and re-layouts: 102 us -> 107 us
  transfers between devices with their start and end apart: 100 -> 100, of which waited for: 31 -> 32; matrix products, arithmetic and copies ran while one was open for 7% -> 7% of each run, Pallas kernels for 31% -> 30%
where the time goes in v6:
time: 654 us; the launch traced here: 641 us
  Pallas kernels  194 us (30%)
  waiting for transfers between devices  140 us (21%)
  starting transfers between devices  138 us (21%)
  local copies, waits for them, and re-layouts  129 us (20%)
  other arithmetic  21.9 us (3%)
  between operations  17.5 us (3%)
    pallas_call x62, Pallas kernels, call(): pl.pallas_call(kernel, out_shape=outs, in_specs=[pl.BlockSpec(memory_spac...  193 us
    ppermute x93, waiting for transfers between devices, flip(): lax.ppermute(block, axis, [(i, i ^ bit) for i in range(lax.axis_size(axis...  137 us
    ppermute x93, starting transfers between devices, flip(): lax.ppermute(block, axis, [(i, i ^ bit) for i in range(lax.axis_size(axis...  128 us
    unnamed x530, local copies, waits for them, and re-layouts  107 us
  transfers between devices with their start and end apart: 100, of which 32 were waited for; matrix products, arithmetic and copies ran while one was open for 7% of the time, Pallas kernels for 30%

profile of v6, /device:TPU:0, one launch (start us, length us, event | category | flops | bytes accessed | tf_op | source)
XLA Modules:
  0.0 641.4 jit_solution(2846621341775755603)
XLA Ops:
  32.9 9.4 %collective-permute-done.2 = bf16[128,768]{1,0:T(8,128)(2,1)S(1)} collective-permute-done((bf16[128,768]{1,0:T(8,128)(2,1)S(1)}, bf16[128,768]{1,0:T(8,128)(2,1)S(1)}, u32[]{:S(2)}, u32[]{:S(2)}) %collective-permute-start.2) | collective-permute-done | bytes 196640 | tf_op jit(solution)/shard_map/ppermute | solution.py:779
  60.5 8.9 %collective-permute-start.9 = (bf16[512,768]{1,0:T(8,128)(2,1)S(1)}, bf16[512,768]{1,0:T(8,128)(2,1)S(1)}, u32[]{:S(2)}, u32[]{:S(2)}) collective-permute-start(bf16[512,768]{1,0:T(8,128)(2,1)S(1)} %pad_maximum_fusion.4.first), channel_id=1, source_target_pairs={{0,4},{4,0},{8,12},{12,8},{16,20},{20,16},{24,28},{28,24},{1,5},{5... | collective-permute-start | bytes 2359304 | tf_op jit(solution)/shard_map/ppermute | solution.py:779
  73.3 22.0 %collective-permute-done.10 = bf16[128,2176]{1,0:T(8,128)(2,1)S(1)} collective-permute-done((bf16[128,2176]{1,0:T(8,128)(2,1)S(1)}, bf16[128,2176]{1,0:T(8,128)(2,1)S(1)}, u32[]{:S(2)}, u32[]{:S(2)}) %collective-permute-start.10) | collective-permute-done | bytes 557088 | tf_op jit(solution)/shard_map/ppermute | solution.py:779
  105.4 10.0 %shard_map.304 = (bf16[1024,256]{1,0:T(8,128)(2,1)S(1)}, f32[8,1024]{1,0:T(8,128)S(1)}) custom-call(s32[8]{0:T(128)S(1)} %copy-done.247, bf16[1024,768]{1,0:T(8,128)(2,1)S(1)} %get-tuple-element.415.qkv, bf16[1024,512]{1,0:T(8,128)(2,1)S(1)} %get-tuple-element.416.kvp), custom_call_target="tpu_custom_call" | custom-call | flops 1024 | bytes 11520000 | tf_op jit(solution)/shard_map/pallas_call | solution.py:340
  117.0 5.6 collective-permute-done.14
  128.0 11.1 %collective-permute-start.19 = (bf16[512,1536]{1,0:T(8,128)(2,1)S(1)}, bf16[512,1536]{1,0:T(8,128)(2,1)S(1)}, u32[]{:S(2)}, u32[]{:S(2)}) collective-permute-start(bf16[512,1536]{1,0:T(8,128)(2,1)S(1)} %slice.187.first), channel_id=1, source_target_pairs={{0,4},{4,0},{8,12},{12,8},{16,20},{20,16},{24,28},{28,24},{1,5},{5... | collective-permute-start | bytes 4718600 | tf_op jit(solution)/shard_map/ppermute | solution.py:779
  149.7 10.2 %shard_map.306 = (bf16[1024,256]{1,0:T(8,128)(2,1)S(1)}, f32[8,1024]{1,0:T(8,128)S(1)}) custom-call(s32[8]{0:T(128)S(1)} %copy-done.246, bf16[1024,768]{1,0:T(8,128)(2,1)S(1)} %get-tuple-element.433.qkv, bf16[1024,512]{1,0:T(8,128)(2,1)S(1)} %get-tuple-element.434.kvp), custom_call_target="tpu_custom_call" | custom-call | flops 1024 | bytes 11520000 | tf_op jit(solution)/shard_map/pallas_call | solution.py:340
  161.3 13.1 %collective-permute-done.13.far = bf16[512,256]{1,0:T(8,128)(2,1)S(1)} collective-permute-done((bf16[512,256]{1,0:T(8,128)(2,1)S(1)}, bf16[512,256]{1,0:T(8,128)(2,1)S(1)}, u32[]{:S(2)}, u32[]{:S(2)}) %collective-permute-start.13) | collective-permute-done | bytes 262176 | tf_op jit(solution)/shard_map/ppermute | solution.py:779
  174.4 8.2 %collective-permute-done.19.second = bf16[512,1536]{1,0:T(8,128)(2,1)S(1)} collective-permute-done((bf16[512,1536]{1,0:T(8,128)(2,1)S(1)}, bf16[512,1536]{1,0:T(8,128)(2,1)S(1)}, u32[]{:S(2)}, u32[]{:S(2)}) %collective-permute-start.19) | collective-permute-done | bytes 1572896 | tf_op jit(solution)/shard_map/ppermute | solution.py:779
  211.0 7.7 %shard_map.311 = (bf16[1024,256]{1,0:T(8,128)(2,1)S(1)}, f32[8,1024]{1,0:T(8,128)S(1)}, bf16[1024,256]{1,0:T(8,128)(2,1)S(1)}) custom-call(s32[8]{0:T(128)S(1)} %copy-done.247, bf16[256,256]{1,0:T(8,128)(2,1)S(1)} %get-tuple-element.459.own, bf16[512,256]{1,0:T(8,128)(2,1)S(1)} %collective-permute-done.30.near, ...), custom_call_target="tpu_custom_call" | custom-call | flops 1024 | bytes 5760000 | tf_op jit(solution)/shard_map/pallas_call | solution.py:340
  223.4 8.1 %shard_map.312 = (bf16[1024,256]{1,0:T(8,128)(2,1)S(1)}, f32[8,1024]{1,0:T(8,128)S(1)}, bf16[1024,256]{1,0:T(8,128)(2,1)S(1)}) custom-call(s32[8]{0:T(128)S(1)} %copy-done.246, bf16[256,256]{1,0:T(8,128)(2,1)S(1)} %get-tuple-element.479.own, bf16[512,256]{1,0:T(8,128)(2,1)S(1)} %collective-permute-done.34.near, ...), custom_call_target="tpu_custom_call" | custom-call | flops 1024 | bytes 5760000 | tf_op jit(solution)/shard_map/pallas_call | solution.py:340
  256.2 12.3 %shard_map.317 = (bf16[1024,1024]{1,0:T(8,128)(2,1)S(1)}, bf16[1024,1024]{1,0:T(8,128)(2,1)S(1)}, bf16[1024,1024]{1,0:T(8,128)(2,1)S(1)}, bf16[1024,1024]{1,0:T(...) custom-call(s32[1]{0:T(128)} %bitcast.at, ...), custom_call_target="tpu_custom_call" | custom-call | flops 1024 | bytes 9600000 | tf_op jit(solution)/shard_map/pallas_call | solution.py:340
  279.4 12.0 %shard_map.319 = (bf16[1024,1024]{1,0:T(8,128)(2,1)S(1)}, bf16[1024,1024]{1,0:T(8,128)(2,1)S(1)}, bf16[1024,1024]{1,0:T(8,128)(2,1)S(1)}, bf16[1024,1024]{1,0:T(...) custom-call(s32[1]{0:T(128)} %bitcast.at, ...), custom_call_target="tpu_custom_call" | custom-call | flops 1024 | bytes 9600000 | tf_op jit(solution)/shard_map/pallas_call | solution.py:340
  342.5 11.2 %shard_map.326 = (bf16[1024,256]{1,0:T(8,128)(2,1)S(1)}, bf16[640,512]{1,0:T(8,128)(2,1)S(1)}, bf16[640,512]{1,0:T(8,128)(2,1)S(1)}) custom-call(s32[8]{0:T(128)S(1)} %copy-done.247, bf16[1024,256]{1,0:T(8,128)(2,1)S(1)} %copy-done.179, bf16[640,512]{1,0:T(8,128)(2,1)S(1)} %copy-done.67, bf16[640,512]{1,0:T(8,128)(2,1)S(1)} %copy-done.65, ...), custom_call_target="tpu_custom_call" | custom-call | flops 1024 | bytes 8960000 | tf_op jit(solution)/shard_map/pallas_call | solution.py:340
  357.9 10.8 %shard_map.327 = (bf16[1024,256]{1,0:T(8,128)(2,1)S(1)}, bf16[640,512]{1,0:T(8,128)(2,1)S(1)}, bf16[640,512]{1,0:T(8,128)(2,1)S(1)}) custom-call(s32[8]{0:T(128)S(1)} %copy-done.246, bf16[1024,256]{1,0:T(8,128)(2,1)S(1)} %copy-done.181, bf16[640,512]{1,0:T(8,128)(2,1)S(1)} %copy-done.63, bf16[640,512]{1,0:T(8,128)(2,1)S(1)} %get-tuple-element.483.kv1, ...), custom_call_target="tpu_custom_call" | custom-call | flops 1024 | bytes 8960000 | tf_op jit(solution)/shard_map/pallas_call | solution.py:340
  401.2 6.2 shard_map.333
  420.9 9.6 %collective-permute-start.70 = (bf16[512,1536]{1,0:T(8,128)(2,1)S(1)}, bf16[512,1536]{1,0:T(8,128)(2,1)S(1)}, u32[]{:S(2)}, u32[]{:S(2)}) collective-permute-start(bf16[512,1536]{1,0:T(8,128)(2,1)S(1)} %get-tuple-element.692), channel_id=1, source_target_pairs={{0,8},{4,12},{8,0},{12,4},{16,24},{20,28},{24,16},{28,20},{1,9},{5... | collective-permute-start | bytes 4718600 | tf_op jit(solution)/shard_map/ppermute | solution.py:779
  430.5 12.5 %shard_map.335 = (bf16[1024,256]{1,0:T(8,128)(2,1)S(1)}, bf16[1024,512]{1,0:T(8,128)(2,1)S(1)}, bf16[1024,512]{1,0:T(8,128)(2,1)S(1)}) custom-call(s32[8]{0:T(128)S(1)} %copy-done.247, bf16[1024,768]{1,0:T(8,128)(2,1)S(1)} %copy-done.46, bf16[1024,512]{1,0:T(8,128)(2,1)S(1)} %copy-done.55, bf16[1024,256]{1,0:T(8,128)(2,1)S(1)} %copy-done.97, ...), custom_call_target="tpu_custom_call" | custom-call | flops 1024 | bytes 14080000 | tf_op jit(solution)/shard_map/pallas_call | solution.py:340
  456.8 9.3 %collective-permute-done.63.far = bf16[512,256]{1,0:T(8,128)(2,1)S(1)} collective-permute-done((bf16[512,256]{1,0:T(8,128)(2,1)S(1)}, bf16[512,256]{1,0:T(8,128)(2,1)S(1)}, u32[]{:S(2)}, u32[]{:S(2)}) %collective-permute-start.63) | collective-permute-done | bytes 262176 | tf_op jit(solution)/shard_map/ppermute | solution.py:779
  471.7 8.6 %collective-permute-start.75 = (bf16[256,1536]{1,0:T(8,128)(2,1)S(1)}, bf16[256,1536]{1,0:T(8,128)(2,1)S(1)}, u32[]{:S(2)}, u32[]{:S(2)}) collective-permute-start(bf16[256,1536]{1,0:T(8,128)(2,1)S(1)} %get-tuple-element.721), channel_id=1, source_target_pairs={{0,4},{4,0},{8,12},{12,8},{16,20},{20,16},{24,28},{28,24},{1,5},{5... | collective-permute-start | bytes 2359304 | tf_op jit(solution)/shard_map/ppermute | solution.py:779
  489.7 12.7 %shard_map.342 = (bf16[1024,256]{1,0:T(8,128)(2,1)S(1)}, bf16[1024,512]{1,0:T(8,128)(2,1)S(1)}, bf16[1024,512]{1,0:T(8,128)(2,1)S(1)}) custom-call(s32[8]{0:T(128)S(1)} %copy-done.246, bf16[1024,768]{1,0:T(8,128)(2,1)S(1)} %copy-done.44, bf16[1024,512]{1,0:T(8,128)(2,1)S(1)} %copy-done.53, bf16[1024,256]{1,0:T(8,128)(2,1)S(1)} %copy-done.95, ...), custom_call_target="tpu_custom_call" | custom-call | flops 1024 | bytes 14080000 | tf_op jit(solution)/shard_map/pallas_call | solution.py:340
  522.2 17.2 %collective-permute-done.79.far = bf16[640,1024]{1,0:T(8,128)(2,1)S(1)} collective-permute-done((bf16[640,1024]{1,0:T(8,128)(2,1)S(1)}, bf16[640,1024]{1,0:T(8,128)(2,1)S(1)}, u32[]{:S(2)}, u32[]{:S(2)}) %collective-permute-start.79) | collective-permute-done | bytes 1310752 | tf_op jit(solution)/shard_map/ppermute | solution.py:779
  542.3 11.4 %collective-permute-start.83 = (bf16[256,640]{1,0:T(8,128)(2,1)}, bf16[256,640]{1,0:T(8,128)(2,1)}, u32[]{:S(2)}, u32[]{:S(2)}) collective-permute-start(bf16[256,640]{1,0:T(8,128)(2,1)} %get-tuple-element.750), channel_id=1, source_target_pairs={{0,4},{4,0},{8,12},{12,8},{16,20},{20,16},{24,28},{28,24},{1,5},{5... | collective-permute-start | bytes 983048 | tf_op jit(solution)/shard_map/ppermute | solution.py:779
  564.2 8.7 %collective-permute-start.88 = (bf16[128,640]{1,0:T(8,128)(2,1)S(1)}, bf16[128,640]{1,0:T(8,128)(2,1)S(1)}, u32[]{:S(2)}, u32[]{:S(2)}) collective-permute-start(bf16[128,640]{1,0:T(8,128)(2,1)S(1)} %get-tuple-element.772), channel_id=1, source_target_pairs={{0,16},{4,20},{8,24},{12,28},{16,0},{20,4},{24,8},{28,12},{1,17},{... | collective-permute-start | bytes 491528 | tf_op jit(solution)/shard_map/ppermute | solution.py:779
  (879 shorter events, 367.0 us)
Async XLA Ops:
  7.2 233.5 %all-gather.2.cloned.1.call-start = ((), (), s32[]{:S(2)}) async-start(), calls=%async_computation.1 | async-start | bytes 4718592 | tf_op jit(solution)/shard_map/all_gather | solution.py:1087
  28.2 32.3 %collective-permute-start.5 = (bf16[512,1024]{1,0:T(8,128)(2,1)S(1)}, bf16[512,1024]{1,0:T(8,128)(2,1)}, u32[]{:S(2)}, u32[]{:S(2)}) collective-permute-start(bf16[512,1024]{1,0:T(8,128)(2,1)S(1)} %shard_map.300.refs_0_), channel_id=1, source_target_pairs={{0,2},{1,3},{2,0},{3,1},{4,6},{5,7},{6,4},{7,5},{8,10},{9,11},{10,... | collective-permute-start | bytes 3145736 | tf_op jit(solution)/shard_map/ppermute | solution.py:779
  52.8 42.6 %collective-permute-start.11 = (bf16[512,1024]{1,0:T(8,128)(2,1)}, bf16[512,1024]{1,0:T(8,128)(2,1)}, u32[]{:S(2)}, u32[]{:S(2)}) collective-permute-start(bf16[512,1024]{1,0:T(8,128)(2,1)} %copy-done.16), channel_id=1, source_target_pairs={{0,2},{1,3},{2,0},{3,1},{4,6},{5,7},{6,4},{7,5},{8,10},{9,11},{10,... | collective-permute-start | bytes 3145736 | tf_op jit(solution)/shard_map/ppermute | solution.py:779
  60.5 34.9 %collective-permute-start.9 = (bf16[512,768]{1,0:T(8,128)(2,1)S(1)}, bf16[512,768]{1,0:T(8,128)(2,1)S(1)}, u32[]{:S(2)}, u32[]{:S(2)}) collective-permute-start(bf16[512,768]{1,0:T(8,128)(2,1)S(1)} %pad_maximum_fusion.4.first), channel_id=1, source_target_pairs={{0,4},{4,0},{8,12},{12,8},{16,20},{20,16},{24,28},{28,24},{1,5},{5... | collective-permute-start | bytes 2359304 | tf_op jit(solution)/shard_map/ppermute | solution.py:779
  96.0 26.6 %collective-permute-start.14 = (bf16[256,2176]{1,0:T(8,128)(2,1)S(1)}, bf16[256,2176]{1,0:T(8,128)(2,1)S(1)}, u32[]{:S(2)}, u32[]{:S(2)}) collective-permute-start(bf16[256,2176]{1,0:T(8,128)(2,1)S(1)} %pad_maximum_fusion.2), channel_id=1, source_target_pairs={{0,8},{4,12},{8,0},{12,4},{16,24},{20,28},{24,16},{28,20},{1,9},{5... | collective-permute-start | bytes 3342344 | tf_op jit(solution)/shard_map/ppermute | solution.py:779
  96.8 28.5 %collective-permute-start.17 = (bf16[512,1024]{1,0:T(8,128)(2,1)S(1)}, bf16[512,1024]{1,0:T(8,128)(2,1)}, u32[]{:S(2)}, u32[]{:S(2)}) collective-permute-start(bf16[512,1024]{1,0:T(8,128)(2,1)S(1)} %bitcast.102), channel_id=1, source_target_pairs={{0,2},{1,3},{2,0},{3,1},{4,6},{5,7},{6,4},{7,5},{8,10},{9,11},{10,... | collective-permute-start | bytes 3145736 | tf_op jit(solution)/shard_map/ppermute | solution.py:779
  97.4 27.9 %collective-permute-start.18 = (bf16[512,1024]{1,0:T(8,128)(2,1)S(1)}, bf16[512,1024]{1,0:T(8,128)(2,1)S(1)}, u32[]{:S(2)}, u32[]{:S(2)}) collective-permute-start(bf16[512,1024]{1,0:T(8,128)(2,1)S(1)} %bitcast.103), channel_id=1, source_target_pairs={{0,1},{1,0},{2,3},{3,2},{4,5},{5,4},{6,7},{7,6},{8,9},{9,8},{10,11... | collective-permute-start | bytes 3145736 | tf_op jit(solution)/shard_map/ppermute | solution.py:779
  126.2 341.8 %reduce-scatter.2.cloned.1.call-start = ((), (), s32[]{:S(2)}) async-start(), calls=%async_computation.2 | async-start | bytes 4718592 | tf_op jit(solution)/shard_map/reduce_scatter | solution.py:1098
  128.0 54.6 %collective-permute-start.19 = (bf16[512,1536]{1,0:T(8,128)(2,1)S(1)}, bf16[512,1536]{1,0:T(8,128)(2,1)S(1)}, u32[]{:S(2)}, u32[]{:S(2)}) collective-permute-start(bf16[512,1536]{1,0:T(8,128)(2,1)S(1)} %slice.187.first), channel_id=1, source_target_pairs={{0,4},{4,0},{8,12},{12,8},{16,20},{20,16},{24,28},{28,24},{1,5},{5... | collective-permute-start | bytes 4718600 | tf_op jit(solution)/shard_map/ppermute | solution.py:779
  139.7 34.7 %collective-permute-start.20 = (bf16[320,1024]{1,0:T(8,128)(2,1)}, bf16[320,1024]{1,0:T(8,128)(2,1)S(1)}, u32[]{:S(2)}, u32[]{:S(2)}) collective-permute-start(bf16[320,1024]{1,0:T(8,128)(2,1)} %copy-done.164), channel_id=1, source_target_pairs={{0,2},{1,3},{2,0},{3,1},{4,6},{5,7},{6,4},{7,5},{8,10},{9,11},{10,... | collective-permute-start | bytes 1966088 | tf_op jit(solution)/shard_map/ppermute | solution.py:779
  141.2 33.2 %collective-permute-start.21 = (bf16[320,1024]{1,0:T(8,128)(2,1)}, bf16[320,1024]{1,0:T(8,128)(2,1)S(1)}, u32[]{:S(2)}, u32[]{:S(2)}) collective-permute-start(bf16[320,1024]{1,0:T(8,128)(2,1)} %copy-done.164), channel_id=1, source_target_pairs={{0,1},{1,0},{2,3},{3,2},{4,5},{5,4},{6,7},{7,6},{8,9},{9,8},{10,11... | collective-permute-start | bytes 1966088 | tf_op jit(solution)/shard_map/ppermute | solution.py:779
  142.1 32.3 %collective-permute-start.13 = (bf16[512,256]{1,0:T(8,128)(2,1)S(1)}, bf16[512,256]{1,0:T(8,128)(2,1)S(1)}, u32[]{:S(2)}, u32[]{:S(2)}) collective-permute-start(bf16[512,256]{1,0:T(8,128)(2,1)S(1)} %slice.186), channel_id=1, source_target_pairs={{0,2},{1,3},{2,0},{3,1},{4,6},{5,7},{6,4},{7,5},{8,10},{9,11},{10,... | collective-permute-start | bytes 786440 | tf_op jit(solution)/shard_map/ppermute | solution.py:779
  189.3 30.8 %collective-permute-start.33 = (bf16[512,640]{1,0:T(8,128)(2,1)S(1)}, bf16[512,640]{1,0:T(8,128)(2,1)S(1)}, u32[]{:S(2)}, u32[]{:S(2)}) collective-permute-start(bf16[512,640]{1,0:T(8,128)(2,1)S(1)} %slice.188.first), channel_id=1, source_target_pairs={{0,4},{4,0},{8,12},{12,8},{16,20},{20,16},{24,28},{28,24},{1,5},{5... | collective-permute-start | bytes 1966088 | tf_op jit(solution)/shard_map/ppermute | solution.py:779
  302.4 31.1 %collective-permute-start.48 = (bf16[512,256]{1,0:T(8,128)(2,1)}, bf16[512,256]{1,0:T(8,128)(2,1)S(1)}, u32[]{:S(2)}, u32[]{:S(2)}) collective-permute-start(bf16[512,256]{1,0:T(8,128)(2,1)} %get-tuple-element.536), channel_id=1, source_target_pairs={{0,2},{1,3},{2,0},{3,1},{4,6},{5,7},{6,4},{7,5},{8,10},{9,11},{10,... | collective-permute-start | bytes 786440 | tf_op jit(solution)/shard_map/ppermute | solution.py:779
  333.5 35.3 %collective-permute-start.51 = (bf16[512,1024]{1,0:T(8,128)(2,1)}, bf16[512,1024]{1,0:T(8,128)(2,1)S(1)}, u32[]{:S(2)}, u32[]{:S(2)}) collective-permute-start(bf16[512,1024]{1,0:T(8,128)(2,1)} %copy-done.250), channel_id=1, source_target_pairs={{0,1},{1,0},{2,3},{3,2},{4,5},{5,4},{6,7},{7,6},{8,9},{9,8},{10,11... | collective-permute-start | bytes 3145736 | tf_op jit(solution)/shard_map/ppermute | solution.py:779
  420.9 46.1 %collective-permute-start.70 = (bf16[512,1536]{1,0:T(8,128)(2,1)S(1)}, bf16[512,1536]{1,0:T(8,128)(2,1)S(1)}, u32[]{:S(2)}, u32[]{:S(2)}) collective-permute-start(bf16[512,1536]{1,0:T(8,128)(2,1)S(1)} %get-tuple-element.692), channel_id=1, source_target_pairs={{0,8},{4,12},{8,0},{12,4},{16,24},{20,28},{24,16},{28,20},{1,9},{5... | collective-permute-start | bytes 4718600 | tf_op jit(solution)/shard_map/ppermute | solution.py:779
  471.7 37.7 %collective-permute-start.75 = (bf16[256,1536]{1,0:T(8,128)(2,1)S(1)}, bf16[256,1536]{1,0:T(8,128)(2,1)S(1)}, u32[]{:S(2)}, u32[]{:S(2)}) collective-permute-start(bf16[256,1536]{1,0:T(8,128)(2,1)S(1)} %get-tuple-element.721), channel_id=1, source_target_pairs={{0,4},{4,0},{8,12},{12,8},{16,20},{20,16},{24,28},{28,24},{1,5},{5... | collective-permute-start | bytes 2359304 | tf_op jit(solution)/shard_map/ppermute | solution.py:779
  509.4 30.0 %collective-permute-start.79 = (bf16[640,1024]{1,0:T(8,128)(2,1)S(1)}, bf16[640,1024]{1,0:T(8,128)(2,1)S(1)}, u32[]{:S(2)}, u32[]{:S(2)}) collective-permute-start(bf16[640,1024]{1,0:T(8,128)(2,1)S(1)} %get-tuple-element.740), channel_id=1, source_target_pairs={{0,2},{1,3},{2,0},{3,1},{4,6},{5,7},{6,4},{7,5},{8,10},{9,11},{10,... | collective-permute-start | bytes 3932168 | tf_op jit(solution)/shard_map/ppermute | solution.py:779
  513.7 47.3 %collective-permute-start.76 = (bf16[512,768]{1,0:T(8,128)(2,1)}, bf16[512,768]{1,0:T(8,128)(2,1)}, u32[]{:S(2)}, u32[]{:S(2)}) collective-permute-start(bf16[512,768]{1,0:T(8,128)(2,1)} %get-tuple-element.723), channel_id=1, source_target_pairs={{0,8},{4,12},{8,0},{12,4},{16,24},{20,28},{24,16},{28,20},{1,9},{5... | collective-permute-start | bytes 2359304 | tf_op jit(solution)/shard_map/ppermute | solution.py:779
  517.9 43.1 %collective-permute-start.82 = (bf16[256,1024]{1,0:T(8,128)(2,1)}, bf16[256,1024]{1,0:T(8,128)(2,1)}, u32[]{:S(2)}, u32[]{:S(2)}) collective-permute-start(bf16[256,1024]{1,0:T(8,128)(2,1)} %shard_map.350), channel_id=1, source_target_pairs={{4,0},{8,4},{12,8},{16,12},{20,16},{24,20},{28,24},{5,1},{9,5},{13... | collective-permute-start | bytes 1572872 | tf_op jit(solution)/shard_map/ppermute | solution.py:785
  561.0 30.3 %collective-permute-start.87 = (bf16[128,1536]{1,0:T(8,128)(2,1)S(1)}, bf16[128,1536]{1,0:T(8,128)(2,1)S(1)}, u32[]{:S(2)}, u32[]{:S(2)}) collective-permute-start(bf16[128,1536]{1,0:T(8,128)(2,1)S(1)} %get-tuple-element.768), channel_id=1, source_target_pairs={{0,16},{4,20},{8,24},{12,28},{16,0},{20,4},{24,8},{28,12},{1,17},{... | collective-permute-start | bytes 1179656 | tf_op jit(solution)/shard_map/ppermute | solution.py:779
  564.2 27.0 %collective-permute-start.88 = (bf16[128,640]{1,0:T(8,128)(2,1)S(1)}, bf16[128,640]{1,0:T(8,128)(2,1)S(1)}, u32[]{:S(2)}, u32[]{:S(2)}) collective-permute-start(bf16[128,640]{1,0:T(8,128)(2,1)S(1)} %get-tuple-element.772), channel_id=1, source_target_pairs={{0,16},{4,20},{8,24},{12,28},{16,0},{20,4},{24,8},{28,12},{1,17},{... | collective-permute-start | bytes 491528 | tf_op jit(solution)/shard_map/ppermute | solution.py:779
  584.3 43.7 %collective-permute-start.85 = (bf16[320,1024]{1,0:T(8,128)(2,1)}, bf16[320,1024]{1,0:T(8,128)(2,1)}, u32[]{:S(2)}, u32[]{:S(2)}) collective-permute-start(bf16[320,1024]{1,0:T(8,128)(2,1)} %slice.246), channel_id=1, source_target_pairs={{4,0},{8,4},{12,8},{16,12},{20,16},{24,20},{28,24},{5,1},{9,5},{13... | collective-permute-start | bytes 1966088 | tf_op jit(solution)/shard_map/ppermute | solution.py:785
  586.8 28.1 %collective-permute-start.84 = (bf16[256,1024]{1,0:T(8,128)(2,1)S(1)}, bf16[256,1024]{1,0:T(8,128)(2,1)}, u32[]{:S(2)}, u32[]{:S(2)}) collective-permute-start(bf16[256,1024]{1,0:T(8,128)(2,1)S(1)} %shard_map.353), channel_id=1, source_target_pairs={{4,0},{8,4},{12,8},{16,12},{20,16},{24,20},{28,24},{5,1},{9,5},{13... | collective-permute-start | bytes 1572872 | tf_op jit(solution)/shard_map/ppermute | solution.py:785
  (337 other events, 2937.4 us)
Sparse Core Ops, SparseCore 0:
  126.4 98.4 all-gather.1
  333.6 94.7 reduce-scatter.1
